TPU v7x, 32 devices: a whole 2x2x4 slice. The times are simulated.
32 devices in a mesh: exp: 8 (over z, y), hid: 4 (over x, core).
Axes of the slice: x: 2, y: 2, z: 4, core: 2. Of those that a mesh axis runs over, the one named last changes fastest.
Arguments:
- tokens: bfloat16 [8, 2048, 768], P('exp', 'hid'), may hold values from -6 to 6
- cotangent: bfloat16 [8, 2048, 768], P('exp', 'hid'), may hold values from -6 to 6
- routes: int32 [8, 2048, 2], P('exp', 'hid'), may hold values from 0 to 7, all different within a row; in each aligned block of 512 rows (0 to 511, 512 to 1023, ..., all dimensions but the last counted through in order) at most 288 rows name the same one
- segments: int32 [8, 2048], P('exp'), may hold values from 0 to 2, as said below
- lengths: int32 [8], P('exp'), may hold values from 1920 to 2048
- gain_attn: float32 [768], replicated, may hold values from 0.5 to 1.5
- gain_moe: float32 [768], replicated, may hold values from 0.5 to 1.5
- w_qkv: bfloat16 [768, 2304], replicated, may hold values from -0.21875 to 0.21875
- w_out: bfloat16 [768, 768], replicated, may hold values from -1.75 to 1.75
- router_w: float32 [768, 8], replicated, may hold values from -0.15 to 0.15
- router_first: float32 [768, 4], replicated, may hold values from -6 to 6
- router_second: float32 [768, 4], replicated, may hold values from 0.01 to 1
- up_w: float32 [8, 768, 3072], P('exp', None, 'hid'), may hold values from -0.21875 to 0.21875
- down_w: float32 [8, 3072, 768], P('exp', 'hid'), may hold values from -0.109375 to 0.109375
- up_first: float32 [8, 768, 3072], P('exp', None, 'hid'), may hold values from -6 to 6
- up_second: float32 [8, 768, 3072], P('exp', None, 'hid'), may hold values from 0.01 to 1
- down_first: float32 [8, 3072, 768], P('exp', 'hid'), may hold values from -6 to 6
- down_second: float32 [8, 3072, 768], P('exp', 'hid'), may hold values from 0.01 to 1
Outputs:
- out_tokens: bfloat16 [8, 2048, 768], P('exp', 'hid')
- grad_tokens: bfloat16 [8, 2048, 768], P('exp', 'hid')
- grad_qkv: float32 [768, 2304], replicated
- grad_out_proj: float32 [768, 768], replicated
- grad_gain_attn: float32 [768], replicated
- grad_gain_moe: float32 [768], replicated
- grad_router: float32 [768, 8], replicated
- router_next: float32 [768, 8], replicated
- router_first_next: float32 [768, 4], replicated
- router_second_next: float32 [768, 4], replicated
- grad_up: float32 [8, 768, 3072], P('exp', None, 'hid')
- grad_down: float32 [8, 3072, 768], P('exp', 'hid')
- up_next: float32 [8, 768, 3072], P('exp', None, 'hid')
- down_next: float32 [8, 3072, 768], P('exp', 'hid')
- up_first_next: float32 [8, 768, 3072], P('exp', None, 'hid')
- up_second_next: float32 [8, 768, 3072], P('exp', None, 'hid')
- down_first_next: float32 [8, 3072, 768], P('exp', 'hid')
- down_second_next: float32 [8, 3072, 768], P('exp', 'hid')
Inputs may be any that keep to these rules, and one draw needn't show every extreme that they name: `routes`: each token names two different experts. Among the tokens of one device no expert is named by more than 288 tokens, and in some devices one is named by exactly 288. `segments`: each row holds three documents in order, numbered 0, 1, 2; document 1 begins within the first 256 positions and ends within the last 256.
All inputs are finite; a program needn't handle non-finite values.
Results may differ from a plain program's by a relative error of at most 0.014.
Values may be sent and summed in bfloat16 or wider, within the bound.
No kernel may reach another device: no remote copies, remote signals or barrier semaphores. Data moves between devices by JAX's collectives and lax.ppermute only.
A program may use at most 384 MiB of HBM per device.

v0:
```python
import jax
import jax.numpy as jnp
from jax import lax
from jax.sharding import PartitionSpec as P

HEADS = 12
HEAD_DIM = 64


precise = lax.Precision.HIGHEST
norm_eps = 1e-06
beta_one = 0.9
beta_two = 0.999
learn_rate = 0.01
adam_eps = 1e-08
adam_steps = 10.0
masked_score = -1e30


def rms_scale(values_in, gain_vec):
    mean_square = jnp.mean(values_in * values_in, axis=-1, keepdims=True)
    return values_in * lax.rsqrt(mean_square + norm_eps) * gain_vec


def gelu_tanh(values_in):
    return jax.nn.gelu(values_in, approximate=True)


def adam_update(weight, gradient, first_moment, second_moment, live_mask):
    first_next = beta_one * first_moment + (1.0 - beta_one) * gradient
    second_next = beta_two * second_moment + (1.0 - beta_two) * gradient * gradient
    first_hat = first_next / (1.0 - beta_one**adam_steps)
    second_hat = second_next / (1.0 - beta_two**adam_steps)
    weight_next = weight - learn_rate * first_hat / (jnp.sqrt(second_hat) + adam_eps)
    return (
        jnp.where(live_mask, weight_next, weight),
        jnp.where(live_mask, first_next, first_moment),
        jnp.where(live_mask, second_next, second_moment),
    )


def contract_rows(left, right):
    return lax.dot_general(
        left, right, (((0,), (0,)), ((), ())), preferred_element_type=jnp.float32
    )


def contract_cols(left, right):
    return lax.dot_general(
        left, right, (((1,), (1,)), ((), ())), preferred_element_type=jnp.float32
    )


def body(
    tokens,
    cotangent,
    routes,
    segments,
    lengths,
    gain_attn,
    gain_moe,
    w_qkv,
    w_out,
    router_w,
    router_first,
    router_second,
    up_w,
    down_w,
    up_first,
    up_second,
    down_first,
    down_second,
):
    exp_count = lax.axis_size("exp")
    hid_index = lax.axis_index("hid")
    exp_index = lax.axis_index("exp")
    tok_count = tokens.shape[1]
    model_width = tokens.shape[2]
    row_len = segments.shape[1]
    experts = router_w.shape[1]
    frozen_count = experts // 2
    capacity = max(2, 3 * tok_count // experts)
    own_rows = exp_count * capacity
    token_vals = tokens[0].astype(jnp.float32)
    normed_one, norm_one_back = jax.vjp(rms_scale, token_vals, gain_attn)
    a_one = normed_one.astype(jnp.bfloat16)
    qkv_vals = jnp.dot(a_one, w_qkv, preferred_element_type=jnp.float32).astype(jnp.bfloat16)
    query_rows = qkv_vals[:, :model_width]
    key_own = qkv_vals[:, model_width : 2 * model_width]
    value_own = qkv_vals[:, 2 * model_width :]
    key_rows, value_rows = (
        lax.all_gather(key_own, "hid", axis=0, tiled=True),
        lax.all_gather(value_own, "hid", axis=0, tiled=True),
    )
    query_heads = query_rows.reshape(tok_count, HEADS, HEAD_DIM)
    key_heads = key_rows.reshape(row_len, HEADS, HEAD_DIM)
    value_heads = value_rows.reshape(row_len, HEADS, HEAD_DIM)
    seg_row = segments[0]
    key_pos = jnp.arange(row_len, dtype=jnp.int32)
    query_pos = hid_index * tok_count + jnp.arange(tok_count, dtype=jnp.int32)
    query_seg = lax.dynamic_slice_in_dim(seg_row, hid_index * tok_count, tok_count, 0)
    allowed = (
        (query_seg[:, None] == seg_row[None, :])
        & (key_pos[None, :] <= query_pos[:, None])
        & ((key_pos[None, :] < lengths[0]) | (key_pos[None, :] == query_pos[:, None]))
    )

    def masked_scores():
        raw_scores = 0.125 * jnp.einsum(
            "qhd,khd->hqk", query_heads, key_heads, preferred_element_type=jnp.float32
        )
        return jnp.where(allowed[None], raw_scores, masked_score)

    scores = masked_scores()
    row_top = jnp.max(scores, axis=-1, keepdims=True)
    log_total = row_top + jnp.log(jnp.sum(jnp.exp(scores - row_top), axis=-1, keepdims=True))
    prob_low = jnp.exp(scores - log_total).astype(jnp.bfloat16)
    attended = jnp.einsum("hqk,khd->qhd", prob_low, value_heads, preferred_element_type=jnp.float32)
    attended_low = attended.reshape(tok_count, model_width).astype(jnp.bfloat16)
    residual = token_vals + jnp.dot(attended_low, w_out, preferred_element_type=jnp.float32)
    normed_two, norm_two_back = jax.vjp(rms_scale, residual, gain_moe)
    logits = jnp.dot(normed_two, router_w, precision=precise)
    expert_ids = jnp.arange(experts, dtype=jnp.int32)
    hit_table = (routes[0][:, :, None] == expert_ids).astype(jnp.int32)
    choose = hit_table.astype(jnp.float32)
    picked = jnp.einsum("te,tje->tj", logits, choose, precision=precise)
    gate_vals = jax.nn.softmax(picked, axis=-1)
    flat_hits = hit_table.reshape(tok_count * 2, experts)
    before = jnp.cumsum(flat_hits, axis=0, dtype=jnp.int32) - flat_hits
    slot_pos = jnp.sum(before * flat_hits, axis=-1, dtype=jnp.int32)
    flat_expert = routes[0].reshape(tok_count * 2)
    kept_mask = slot_pos < capacity
    slot_index = jnp.where(kept_mask, slot_pos, capacity)
    fetch_index = jnp.minimum(slot_pos, capacity - 1)
    kept_float = kept_mask.astype(jnp.float32)[:, None]
    is_new = exp_index >= frozen_count
    a_two = normed_two.astype(jnp.bfloat16)
    pair_rows = jnp.repeat(a_two, 2, axis=0)
    send_rows = jnp.zeros((experts, capacity, model_width), jnp.bfloat16)
    send_rows = send_rows.at[flat_expert, slot_index].set(pair_rows, mode="drop")
    arrived = lax.all_to_all(send_rows, "exp", split_axis=0, concat_axis=0, tiled=True)
    arrived_rows = arrived.reshape(own_rows, model_width)
    up_low = up_w[0].astype(jnp.bfloat16)
    down_low = down_w[0].astype(jnp.bfloat16)
    expert_rows = lax.all_gather(arrived_rows, "hid", axis=0, tiled=True)
    pre_act = jnp.dot(expert_rows, up_low, preferred_element_type=jnp.float32)
    act_low = gelu_tanh(pre_act).astype(jnp.bfloat16)
    whole_sum = lax.psum(jnp.dot(act_low, down_low, preferred_element_type=jnp.float32), "hid")
    expert_sum = lax.dynamic_slice_in_dim(whole_sum, hid_index * own_rows, own_rows, 0)
    returned = lax.all_to_all(
        expert_sum.astype(jnp.bfloat16).reshape(exp_count, capacity, model_width),
        "exp",
        split_axis=0,
        concat_axis=0,
        tiled=True,
    )
    fetched = returned[flat_expert, fetch_index].astype(jnp.float32) * kept_float
    fetched = fetched.reshape(tok_count, 2, model_width)
    moe_out = jnp.sum(gate_vals[:, :, None] * fetched, axis=1)
    out_tokens = (residual + moe_out).astype(jnp.bfloat16)
    grad_out = cotangent[0].astype(jnp.float32)
    grad_gates = jnp.einsum("td,tjd->tj", grad_out, fetched, precision=precise)
    grad_pair = (gate_vals[:, :, None] * grad_out[:, None, :]).astype(jnp.bfloat16)
    grad_send = jnp.zeros((experts, capacity, model_width), jnp.bfloat16)
    grad_send = grad_send.at[flat_expert, slot_index].set(
        grad_pair.reshape(tok_count * 2, model_width), mode="drop"
    )
    grad_arrived = lax.all_to_all(grad_send, "exp", split_axis=0, concat_axis=0, tiled=True)
    grad_arrived_rows = grad_arrived.reshape(own_rows, model_width)
    gelu_back = jax.vjp(gelu_tanh, pre_act)[1]
    grad_slots = lax.all_gather(grad_arrived_rows, "hid", axis=0, tiled=True)
    grad_act = contract_cols(grad_slots, down_low)
    grad_pre = gelu_back(grad_act)[0].astype(jnp.bfloat16)

    def weight_grads(unused):
        return (contract_rows(expert_rows, grad_pre), contract_rows(act_low, grad_slots))

    def zero_grads(unused):
        return (jnp.zeros(up_low.shape, jnp.float32), jnp.zeros(down_low.shape, jnp.float32))

    grad_up_local, grad_down_local = lax.cond(is_new, weight_grads, zero_grads, 0)
    grad_inputs = lax.psum_scatter(
        contract_cols(grad_pre, up_low), "hid", scatter_dimension=0, tiled=True
    )
    grad_returned = lax.all_to_all(
        grad_inputs.astype(jnp.bfloat16).reshape(exp_count, capacity, model_width),
        "exp",
        split_axis=0,
        concat_axis=0,
        tiled=True,
    )
    grad_fetched = grad_returned[flat_expert, fetch_index].astype(jnp.float32) * kept_float
    grad_normed_two = jnp.sum(grad_fetched.reshape(tok_count, 2, model_width), axis=1)
    grad_picked = gate_vals * (grad_gates - jnp.sum(gate_vals * grad_gates, axis=-1, keepdims=True))
    grad_logits = jnp.einsum("tj,tje->te", grad_picked, choose, precision=precise)
    grad_router_local = lax.dot_general(
        normed_two, grad_logits, (((0,), (0,)), ((), ())), precision=precise
    )
    grad_normed_two = grad_normed_two + lax.dot_general(
        grad_logits, router_w, (((1,), (1,)), ((), ())), precision=precise
    )
    grad_residual_norm, grad_gain_moe_local = norm_two_back(grad_normed_two)
    grad_residual = grad_out + grad_residual_norm
    grad_branch = grad_residual.astype(jnp.bfloat16)
    grad_out_local = contract_rows(attended_low, grad_branch)
    grad_attended = contract_cols(grad_branch, w_out).astype(jnp.bfloat16)
    grad_attended = grad_attended.reshape(tok_count, HEADS, HEAD_DIM)
    prob_again = jnp.exp(masked_scores() - log_total)
    grad_prob = jnp.einsum(
        "qhd,khd->hqk", grad_attended, value_heads, preferred_element_type=jnp.float32
    )
    grad_scores = prob_again * (grad_prob - jnp.sum(prob_again * grad_prob, axis=-1, keepdims=True))
    grad_scores = grad_scores.astype(jnp.bfloat16)
    grad_query = 0.125 * jnp.einsum(
        "hqk,khd->qhd", grad_scores, key_heads, preferred_element_type=jnp.float32
    )
    grad_key = 0.125 * jnp.einsum(
        "hqk,qhd->khd", grad_scores, query_heads, preferred_element_type=jnp.float32
    )
    grad_value = jnp.einsum(
        "hqk,qhd->khd",
        prob_again.astype(jnp.bfloat16),
        grad_attended,
        preferred_element_type=jnp.float32,
    )
    grad_key_own, grad_value_own = (
        lax.psum_scatter(
            grad_key.reshape(row_len, model_width), "hid", scatter_dimension=0, tiled=True
        ),
        lax.psum_scatter(
            grad_value.reshape(row_len, model_width), "hid", scatter_dimension=0, tiled=True
        ),
    )
    grad_qkv_low = jnp.concatenate(
        [grad_query.reshape(tok_count, model_width), grad_key_own, grad_value_own], axis=1
    ).astype(jnp.bfloat16)
    grad_qkv_local = contract_rows(a_one, grad_qkv_low)
    grad_normed_one = contract_cols(grad_qkv_low, w_qkv)
    grad_token_norm, grad_gain_attn_local = norm_one_back(grad_normed_one)
    grad_tokens = (grad_residual + grad_token_norm).astype(jnp.bfloat16)
    grad_qkv, grad_out_proj, grad_router_all, grad_gain_attn, grad_gain_moe = lax.psum(
        (
            grad_qkv_local,
            grad_out_local,
            grad_router_local,
            grad_gain_attn_local,
            grad_gain_moe_local,
        ),
        ("exp", "hid"),
    )
    live_columns = (expert_ids >= frozen_count)[None, :]
    grad_router = jnp.where(live_columns, grad_router_all, 0.0)
    router_new, router_first_next, router_second_next = adam_update(
        router_w[:, frozen_count:], grad_router[:, frozen_count:], router_first, router_second, True
    )
    router_next = jnp.concatenate([router_w[:, :frozen_count], router_new], axis=1)
    up_next, up_first_next, up_second_next = adam_update(
        up_w[0], grad_up_local, up_first[0], up_second[0], is_new
    )
    down_next, down_first_next, down_second_next = adam_update(
        down_w[0], grad_down_local, down_first[0], down_second[0], is_new
    )
    return (
        out_tokens[None],
        grad_tokens[None],
        grad_qkv,
        grad_out_proj,
        grad_gain_attn,
        grad_gain_moe,
        grad_router,
        router_next,
        router_first_next,
        router_second_next,
        grad_up_local[None],
        grad_down_local[None],
        up_next[None],
        down_next[None],
        up_first_next[None],
        up_second_next[None],
        down_first_next[None],
        down_second_next[None],
    )


def solution(mesh):
    return jax.shard_map(
        body,
        mesh=mesh,
        in_specs=(
            P("exp", "hid", None),
            P("exp", "hid", None),
            P("exp", "hid", None),
            P("exp", None),
            P("exp"),
            P(),
            P(),
            P(),
            P(),
            P(),
            P(),
            P(),
            P("exp", None, "hid"),
            P("exp", "hid", None),
            P("exp", None, "hid"),
            P("exp", None, "hid"),
            P("exp", "hid", None),
            P("exp", "hid", None),
        ),
        out_specs=(
            P("exp", "hid", None),
            P("exp", "hid", None),
            P(),
            P(),
            P(),
            P(),
            P(),
            P(),
            P(),
            P(),
            P("exp", None, "hid"),
            P("exp", "hid", None),
            P("exp", None, "hid"),
            P("exp", "hid", None),
            P("exp", None, "hid"),
            P("exp", None, "hid"),
            P("exp", "hid", None),
            P("exp", "hid", None),
        ),
        check_vma=False,
    )
```

profile of v0, /device:TPU:1, one launch (start us, length us, event | category | flops | bytes accessed | tf_op | source)
XLA Modules:
  0.0 1573.2 jit_solution(18164360073597449113)
XLA Ops:
  38.7 6.7 all-gather.7.cloned.1.call-done
  50.1 23.4 %fusion = (f32[12,512]{1,0:T(8,128)}, f32[12,512,2048]{2,1,0:T(8,128)}) fusion(pred[512,2048]{1,0:T(8,128)(4,1)} %fusion.10, bf16[512,12,64]{0,2,1:T(8,128)(2,1)} %bitcast.228, bf16[2048,12,64]{0,2,1:T(8,128)(2,1)} %bitcast.217), kind=kOutput, calls=%fused_computation.9 | convolution fusion | flops 1648355328 | bytes 55336960 | tf_op jit(solution)/shard_map/qhd,khd->hqk/dot_general | solution.py:109
  73.5 22.1 %exponential_reduce_fusion = f32[12,512]{1,0:T(8,128)S(1)} fusion(f32[12,512,2048]{2,1,0:T(8,128)} %get-tuple-element.72, f32[12,512]{1,0:T(8,128)} %get-tuple-element.71, pred[512,2048]{1,0:T(8,128)(4,1)} %fusion.10), kind=kLoop, calls=%fused_computation.7 | loop fusion | flops 50325504 | bytes 51429376 | tf_op jit(solution)/shard_map/reduce_sum | solution.py:116
  100.9 20.7 %convolution_convert_fusion.1 = bf16[12,64,512]{2,1,0:T(8,128)(2,1)S(1)} fusion(bf16[2048,12,64]{0,2,1:T(8,128)(2,1)} %bitcast.220, f32[12,512,2048]{2,1,0:T(8,128)} %get-tuple-element.72, f32[12,512]{1,0:T(8,128)} %log_add_fusion, pred[512,2048]{1,0:T(8,128)(4,1)} %fusion.10), kind=kOutput, calls=%fused_computation.86 | convolution fusion | flops 1661337600 | bytes 55336960 | tf_op jit(solution)/shard_map/hqk,khd->qhd/dot_general | solution.py:118
  130.6 7.5 scatter_custom_fusion
  138.0 59.2 %all_to_all.20 = bf16[8,192,768]{2,1,0:T(8,128)(2,1)} all-to-all(bf16[8,192,768]{2,1,0:T(8,128)(2,1)} %bitcast.227), channel_id=1, replica_groups=mesh['exp'=8,'hid'=4] {'exp'}, dimensions={0} | all-to-all | bytes 4718592 | tf_op jit(solution)/shard_map/all_to_all | solution.py:141
  197.2 63.8 %all-gather.9.cloned.1.call-done = bf16[6144,768]{1,0:T(8,128)(2,1)} async-done(((bf16[1536,768]{1,0:T(8,128)(2,1)}), bf16[6144,768]{1,0:T(8,128)(2,1)}) %all-gather.9.cloned.1.call-update) | async-done | bytes 9437200 | tf_op jit(solution)/shard_map/all_gather | solution.py:145
  261.0 19.1 %multiply_convert_fusion.1 = (bf16[6144,768]{1,0:T(8,128)(2,1)}, f32[6144,768]{1,0:T(8,128)}) fusion(bf16[6144,768]{1,0:T(8,128)(2,1)} %all-gather.9.cloned.1.call-done, f32[1,768,768]{2,1,0:T(8,128)} %param.32), kind=kOutput, calls=%fused_computation.20 | convolution fusion | flops 7290224640 | bytes 40108032 | tf_op jit(solution)/shard_map/dot_general | solution.py:146
  280.1 14.4 fusion.95
  294.4 321.4 %all-reduce.6 = bf16[6144,768]{1,0:T(8,128)(2,1)} all-reduce(f32[6144,768]{1,0:T(8,128)} %fusion.95), channel_id=1, replica_groups=mesh['exp'=8,'hid'=4] {'hid'}, use_global_device_ids=true, to_apply=%region_10.11 | all-reduce | flops 4718592 | bytes 28311552 | tf_op jit(solution)/shard_map/psum | solution.py:148
  648.7 29.3 %all-to-all-done.1 = bf16[8,192,768]{2,1,0:T(8,128)(2,1)} async-done(((bf16[8,192,768]{2,1,0:T(8,128)(2,1)}), bf16[8,192,768]{2,1,0:T(8,128)(2,1)}, u32[]{:S(2)}, u32[]{:S(2)}) %all-to-all-start.1) | async-done | bytes 2359328 | tf_op jit(solution)/shard_map/all_to_all | solution.py:150
  678.1 21.6 %gather_fusion = bf16[1024,768]{1,0:T(8,128)(2,1)} fusion(bf16[8,192,768]{2,1,0:T(8,128)(2,1)} %all-to-all-done.1, s32[1024]{0:T(1024)S(1)} %bitcast.215), kind=kCustom, calls=%fused_computation | custom fusion | bytes 3153920 | tf_op jit(solution)/shard_map/gather | solution.py:157
  704.8 14.5 fusion.12
  721.9 8.5 scatter_custom_fusion.1
  730.4 58.8 %all_to_all.21 = bf16[8,192,768]{2,1,0:T(8,128)(2,1)} all-to-all(bf16[8,192,768]{2,1,0:T(8,128)(2,1)} %bitcast.226), channel_id=1, replica_groups=mesh['exp'=8,'hid'=4] {'exp'}, dimensions={0} | all-to-all | bytes 4718592 | tf_op jit(solution)/shard_map/all_to_all | solution.py:168
  789.2 62.8 %all-gather.11.cloned.1.call-done = bf16[6144,768]{1,0:T(8,128)(2,1)} async-done(((bf16[1536,768]{1,0:T(8,128)(2,1)}), bf16[6144,768]{1,0:T(8,128)(2,1)}) %all-gather.11.cloned.1.call-update) | async-done | bytes 9437200 | tf_op jit(solution)/shard_map/all_gather | solution.py:171
  852.0 21.9 %fusion.8 = bf16[6144,768]{1,0:T(8,128)(2,1)S(1)} fusion(f32[6144,768]{1,0:T(8,128)} %get-tuple-element.76, bf16[6144,768]{1,0:T(8,128)(2,1)} %all-gather.11.cloned.1.call-done, f32[1,768,768]{2,1,0:T(8,128)} %param.33), kind=kOutput, calls=%fused_computation.19 | convolution fusion | flops 7342129152 | bytes 40108032 | tf_op jit(solution)/shard_map/dot_general | solution.py:49
  877.5 11.1 fusion.98
  888.7 139.2 %reduce-scatter.4.cloned.1.call-done = f32[1536,768]{1,0:T(8,128)} async-done(((f32[6144,768]{1,0:T(8,128)}), f32[1536,768]{1,0:T(8,128)}) %reduce-scatter.4.cloned.1.call-update) | async-done | bytes 4718608 | tf_op jit(solution)/shard_map/reduce_scatter | solution.py:182
  1043.9 46.4 %all-to-all-done.3 = bf16[8,192,768]{2,1,0:T(8,128)(2,1)} async-done(((bf16[8,192,768]{2,1,0:T(8,128)(2,1)}), bf16[8,192,768]{2,1,0:T(8,128)(2,1)}, u32[]{:S(2)}, u32[]{:S(2)}) %all-to-all-start.3) | async-done | bytes 2359328 | tf_op jit(solution)/shard_map/all_to_all | solution.py:185
  1090.3 21.6 %gather_fusion.1 = bf16[1024,768]{1,0:T(8,128)(2,1)} fusion(bf16[8,192,768]{2,1,0:T(8,128)(2,1)} %all-to-all-done.3, s32[1024]{0:T(1024)S(1)} %bitcast.216), kind=kCustom, calls=%fused_computation.1 | custom fusion | bytes 3153920 | tf_op jit(solution)/shard_map/gather | solution.py:192
  1116.8 18.6 %multiply_reduce_fusion.1 = (f32[512,768]{1,0:T(8,128)S(1)}, f32[512,768]{1,0:T(8,128)S(1)}) fusion(f32[512,2,768]{2,1,0:T(2,128)} %reshape.370, f32[512,2]{1,0:T(8,128)} %reshape.369, f32[512,2,768]{2,1,0:T(2,128)} %reshape.368, f32[512,2]{1,0:T(8,128)} %get-tuple-element.55), kind=kLoop, calls=%fused_computation.38 | loop fusion | flops 3145728 | bytes 9445376 | tf_op jit(solution)/shard_map/reduce_sum | solution.py:193
  1144.4 38.2 %multiply_reduce_fusion = (f32[12,512]{1,0:T(8,128)}, f32[12,512,2048]{2,1,0:T(8,128)}) fusion(f32[12,512,2048]{2,1,0:T(8,128)} %get-tuple-element.72, f32[12,512]{1,0:T(8,128)} %log_add_fusion, pred[512,2048]{1,0:T(8,128)(4,1)} %fusion.10, bf16[512,12,64]{0,2,1:T(8,128)(2,1)} %bitcast.231, bf16[2048,12,64]{0,2,1:T(8,128)(2,1)} %bitcast.221), kind=kOutput, calls=%fused_computation.5 | convolution fusion | flops 1673521152 | bytes 105693184 | tf_op jit(solution)/shard_map/qhd,khd->hqk/dot_general | solution.py:209
  1182.6 41.5 %multiply_convert_fusion = bf16[12,512,2048]{2,1,0:T(8,128)(2,1)} fusion(f32[12,512,2048]{2,1,0:T(8,128)} %get-tuple-element.79, f32[12,512,2048]{2,1,0:T(8,128)} %get-tuple-element.72, f32[12,512]{1,0:T(8,128)} %get-tuple-element.78, f32[12,512]{1,0:T(8,128)} %log_add_fusion, pred[512,2048]{1,0:T(8,128)(4,1)} %fusion.10), kind=kLoop, calls=%fused_computation.4 | loop fusion | flops 75497472 | bytes 126926848 | tf_op jit(solution)/shard_map/convert_element_type | solution.py:213
  1224.1 15.5 convolution_multiply_fusion
  1239.6 26.1 %fusion.69 = f32[12,64,2048]{2,1,0:T(8,128)} fusion(bf16[512,12,64]{0,2,1:T(8,128)(2,1)} %bitcast.232, f32[12,512,2048]{2,1,0:T(8,128)} %get-tuple-element.72, f32[12,512]{1,0:T(8,128)} %log_add_fusion, pred[512,2048]{1,0:T(8,128)(4,1)} %fusion.10), kind=kOutput, calls=%fused_computation.121 | convolution fusion | flops 1660944384 | bytes 58482688 | tf_op jit(solution)/shard_map/hqk,qhd->khd/dot_general | solution.py:220
  1269.7 14.3 multiply_convert_fusion.4
  1284.0 13.3 reduce-scatter.6.cloned.1.call-done
  1299.7 59.0 %reduce-scatter.8.cloned.1.call-done = f32[512,768]{0,1:T(8,128)} async-done(((f32[2048,768]{0,1:T(8,128)}), f32[512,768]{0,1:T(8,128)}) %reduce-scatter.8.cloned.1.call-update) | async-done | bytes 1572880 | tf_op jit(solution)/shard_map/reduce_scatter | solution.py:230
  1376.3 13.4 fusion.18
  1393.7 65.1 %all-reduce = (f32[768]{0:T(1024)}, f32[768]{0:T(1024)}, f32[768,8]{0,1:T(8,128)}) all-reduce(f32[768]{0:T(1024)} %get-tuple-element.42, f32[768]{0:T(1024)S(1)} %copy-done.30, f32[768,8]{0,1:T(8,128)} %fusion.37), channel_id=1, replica_groups=mesh['exp'=8,'hid'=4] {'exp','hid'}, use_global_device_ids=true, to_apply=%region_24.25 | all-reduce | flops 7680 | bytes 61440 | tf_op jit(solution)/shard_map/psum | solution.py:241
  1466.4 91.7 %all-reduce.5.cloned.1.call-done = (f32[768,2304]{1,0:T(8,128)}, f32[768,768]{1,0:T(8,128)}) async-done(((f32[768,2304]{1,0:T(8,128)}, f32[768,768]{1,0:T(8,128)}), (f32[768,2304]{1,0:T(8,128)}, f32[768,768]{1,0:T(8,128)})) %all-reduce.5.cloned.1.call-update) | async-done | bytes 9437200 | tf_op jit(solution)/shard_map/psum | solution.py:241
  (176 shorter events, 170.7 us)
Async XLA Ops:
  7.2 38.1 %all-gather.7.cloned.1.call-start = ((), (), s32[]{:S(2)}) async-start(), calls=%async_computation.8 | async-start | bytes 3932160 | tf_op jit(solution)/shard_map/all_gather | solution.py:92
  8.8 3.9 copy-start.27
  14.2 82.1 %all-gather.5.cloned.1.call-start = ((), (), s32[]{:S(2)}) async-start(), calls=%async_computation.7 | async-start | bytes 3932160 | tf_op jit(solution)/shard_map/all_gather | solution.py:93
  14.9 246.1 %all-gather.9.cloned.1.call-start = ((), (), s32[]{:S(2)}) async-start(), calls=%async_computation.9 | async-start | bytes 11796480 | tf_op jit(solution)/shard_map/all_gather | solution.py:145
  73.5 22.1 %copy-start.23 = (f32[12,512]{1,0:T(8,128)S(1)}, f32[12,512]{1,0:T(8,128)}, u32[]{:S(2)}) copy-start(f32[12,512]{1,0:T(8,128)} %get-tuple-element.71) | copy-start | bytes 73732
  100.9 20.8 %copy-start.4 = (bf16[1,512,768]{2,1,0:T(8,128)(2,1)S(1)}, bf16[1,512,768]{2,1,0:T(8,128)(2,1)}, u32[]{:S(2)}) copy-start(bf16[1,512,768]{2,1,0:T(8,128)(2,1)} %param.20) | copy-start | bytes 2359300
  100.9 20.8 %copy-start.40 = (bf16[768,768]{1,0:T(8,128)(2,1)S(1)}, bf16[768,768]{1,0:T(8,128)(2,1)}, u32[]{:S(2)}) copy-start(bf16[768,768]{1,0:T(8,128)(2,1)} %param.28) | copy-start | bytes 3538948
  261.0 19.1 %copy-start.9 = (f32[1,768,768]{2,1,0:T(8,128)S(1)}, f32[1,768,768]{2,1,0:T(8,128)}, u32[]{:S(2)}) copy-start(f32[1,768,768]{2,1,0:T(8,128)} %param.33) | copy-start | bytes 7077892
  619.0 59.0 %all-to-all-start.1 = ((bf16[8,192,768]{2,1,0:T(8,128)(2,1)}), bf16[8,192,768]{2,1,0:T(8,128)(2,1)}, u32[]{:S(2)}, u32[]{:S(2)}) async-start(bf16[8,192,768]{2,1,0:T(8,128)(2,1)} %bitcast.223), calls=%async_computation.1 | async-start | bytes 4718592 | tf_op jit(solution)/shard_map/all_to_all | solution.py:150
  624.4 227.6 %all-gather.11.cloned.1.call-start = ((), (), s32[]{:S(2)}) async-start(), calls=%async_computation.10 | async-start | bytes 11796480 | tf_op jit(solution)/shard_map/all_gather | solution.py:171
  704.7 14.6 copy-start.12
  704.7 14.6 copy-start.32
  789.2 238.7 %reduce-scatter.4.cloned.1.call-start = ((), (), s32[]{:S(2)}) async-start(), calls=%async_computation.11 | async-start | bytes 23592960 | tf_op jit(solution)/shard_map/reduce_scatter | solution.py:182
  852.0 25.5 %copy-start.8 = (f32[1,768,768]{2,1,0:T(8,128)S(1)}, f32[1,768,768]{2,1,0:T(8,128)}, u32[]{:S(2)}) copy-start(f32[1,768,768]{2,1,0:T(8,128)} %param.32) | copy-start | bytes 7077892
  1031.8 5.6 copy-start.31
  1031.8 58.5 %all-to-all-start.3 = ((bf16[8,192,768]{2,1,0:T(8,128)(2,1)}), bf16[8,192,768]{2,1,0:T(8,128)(2,1)}, u32[]{:S(2)}, u32[]{:S(2)}) async-start(bf16[8,192,768]{2,1,0:T(8,128)(2,1)} %bitcast.222), calls=%async_computation.4 | async-start | bytes 4718592 | tf_op jit(solution)/shard_map/all_to_all | solution.py:185
  1037.2 260.1 %reduce-scatter.6.cloned.1.call-start = ((), (), s32[]{:S(2)}) async-start(), calls=%async_computation.12 | async-start | bytes 7864320 | tf_op jit(solution)/shard_map/reduce_scatter | solution.py:227
  1116.8 18.6 %copy-start.2 = (f32[512,768]{1,0:T(8,128)S(1)}, f32[512,768]{1,0:T(8,128)}, u32[]{:S(2)}) copy-start(f32[512,768]{1,0:T(8,128)} %copy-done.1) | copy-start | bytes 4718596
  1116.8 18.6 %copy-start.17 = (f32[512,1,8]{2,1,0:T(1,128)S(1)}, f32[512,1,8]{2,1,0:T(1,128)}, u32[]{:S(2)}) copy-start(f32[512,1,8]{2,1,0:T(1,128)} %fusion.56) | copy-start | bytes 49156
  1116.8 18.6 %copy-start.24 = (f32[768,8]{0,1:T(8,128)S(1)}, f32[768,8]{0,1:T(8,128)}, u32[]{:S(2)}) copy-start(f32[768,8]{0,1:T(8,128)} %param.29) | copy-start | bytes 73732
  1239.6 119.2 %reduce-scatter.8.cloned.1.call-start = ((), (), s32[]{:S(2)}) async-start(), calls=%async_computation.13 | async-start | bytes 7864320 | tf_op jit(solution)/shard_map/reduce_scatter | solution.py:230
  1265.8 292.4 %all-reduce.5.cloned.1.call-start = ((), (), s32[]{:S(2)}) async-start(), calls=%async_computation.14 | async-start | bytes 18874368 | tf_op jit(solution)/shard_map/psum | solution.py:241
  1284.0 77.4 %copy-start.34 = (f32[512]{0:T(512)S(1)}, f32[512]{0:T(512)}, u32[]{:S(2)}) copy-start(f32[512]{0:T(512)} %copy-done.33) | copy-start | bytes 6148
  1284.0 77.4 %copy-start.37 = (f32[768]{0:T(1024)S(1)}, f32[768]{0:T(1024)}, u32[]{:S(2)}) copy-start(f32[768]{0:T(1024)} %param.25) | copy-start | bytes 9220
  1376.3 13.4 copy-start.6
  1376.3 13.4 copy-start.15
  1376.3 13.4 copy-start.20
  1376.3 13.4 copy-start.22
  1376.3 13.4 copy-start.38
  1389.7 4.0 copy-start.30
  1389.7 72.6 %copy-start.28 = (f32[512]{0:T(512)S(1)}, f32[512]{0:T(512)}, u32[]{:S(2)}) copy-start(f32[512]{0:T(512)} %copy-done.27) | copy-start | bytes 6148
  1558.1 6.6 copy-start.13
  (20 other events, 39.1 us)
Sparse Core Ops, SparseCore 0:
  14.3 31.0 all-gather.6
  47.5 28.5 all-gather.4
  197.4 63.6 all-gather.8
  789.3 62.6 all-gather.10
  888.8 139.0 reduce-scatter.3
  1239.7 57.5 reduce-scatter.5
  1300.4 58.3 reduce-scatter.7
  1366.7 191.3 all-reduce.4
where the time goes:
time: 1580 us; the launch traced here: 1570 us
  waiting for transfers between devices  513 us (32%)
  blocking collectives  504 us (32%)
  matrix products  257 us (16%)
  other arithmetic  145 us (9%)
  local copies, waits for them, and re-layouts  126 us (8%)
    psum x1, blocking collectives, body(): lax.psum(jnp.dot(act_low, down_low, preferred_element_type=jnp.float32),...  321 us
    reduce_scatter x1, waiting for transfers between devices, body(): lax.psum_scatter(contract_cols(grad_pre, up_low), 'hid', scatter_dimensio...  139 us
    psum x1, waiting for transfers between devices, body(): lax.psum((grad_qkv_local, grad_out_local, grad_router_local, grad_gain_at...  91.7 us
    psum x1, blocking collectives, body(): lax.psum((grad_qkv_local, grad_out_local, grad_router_local, grad_gain_at...  65.1 us
    all_gather x1, waiting for transfers between devices, body(): expert_rows = lax.all_gather(arrived_rows, 'hid', axis=0, tiled=True)  63.8 us
    all_gather x1, waiting for transfers between devices, body(): grad_slots = lax.all_gather(grad_arrived_rows, 'hid', axis=0, tiled=True)  62.8 us
    all_to_all x1, blocking collectives, body(): lax.all_to_all(send_rows, 'exp', split_axis=0, concat_axis=0, tiled=True)  59.2 us
    reduce_scatter x1, waiting for transfers between devices, body(): lax.psum_scatter(grad_value.reshape(row_len, model_width), 'hid', scatter...  59 us
  transfers between devices with their start and end apart: 10, of which 9 were waited for; matrix products, arithmetic and copies ran while one was open for 12% of the time, Pallas kernels for 0%

commit v1 on v0

v1 whole, which is shorter than its diff:
```python
import functools

import jax
import jax.numpy as jnp
from jax import lax
from jax.experimental import pallas as pl
from jax.experimental.pallas import tpu as pltpu
from jax.sharding import PartitionSpec as P

HEADS = 12
HEAD_DIM = 64

precise = lax.Precision.HIGHEST
norm_eps = 1e-06
beta_one = 0.9
beta_two = 0.999
learn_rate = 0.01
adam_eps = 1e-08
adam_steps = 10.0
masked_score = -1e30

bf16 = jnp.bfloat16
f32 = jnp.float32
MIB = 1 << 20


def mm(left, right, contract=((1,), (0,)), precision=None):
    return lax.dot_general(
        left, right, (contract, ((), ())), preferred_element_type=f32, precision=precision
    )


NT = ((1,), (1,))
TN = ((0,), (0,))


def swap(value, axis, distance):
    count = lax.axis_size(axis)
    return lax.ppermute(value, axis, [(i, i ^ distance) for i in range(count)])


def iota(shape, dim):
    return lax.broadcasted_iota(jnp.int32, shape, dim)


def split_three(value):
    high = value.astype(bf16)
    rest = value - high.astype(f32)
    mid = rest.astype(bf16)
    low = (rest - mid.astype(f32)).astype(bf16)
    return high, mid, low


def vmem_spec():
    return pl.BlockSpec(memory_space=pltpu.VMEM)


def smem_spec():
    return pl.BlockSpec(memory_space=pltpu.SMEM)


def params(mib):
    return pltpu.CompilerParams(vmem_limit_bytes=mib * MIB)


def cost(micros):
    return pl.CostEstimate(
        flops=int(micros * 1.1e9), bytes_accessed=int(micros * 3e6), transcendentals=0
    )


def tables_kernel(capacity, own_ref, routes_ref, dy_ref, hot_ref, pick0, pick1, *sends):
    experts = len(sends)
    count = routes_ref.shape[1]
    expert_row = iota((experts, count), 0) ^ own_ref[1]
    route_rows = [routes_ref[k : k + 1, :] for k in range(2)]
    hits = [expert_row == row for row in route_rows]
    hit = hits[0] | hits[1]
    hit_low = jnp.where(hit, 1.0, 0.0).astype(bf16)
    upper = jnp.where(iota((count, count), 0) < iota((count, count), 1), 1.0, 0.0).astype(bf16)
    slot = mm(hit_low, upper)
    slot = jnp.where(hit & (slot < capacity), slot, -1.0)
    row_id = iota((capacity, count), 0).astype(f32)
    for e in range(experts):
        hot_ref[e * capacity : (e + 1) * capacity, :] = jnp.where(
            row_id == slot[e : e + 1, :], 1.0, 0.0
        ).astype(bf16)
    rows = mm(hot_ref[...], dy_ref[...]).astype(bf16)
    for e, send in enumerate(sends):
        send[...] = rows[e * capacity : (e + 1) * capacity, :]
    index_rows = []
    for k in range(2):
        own_slot = jnp.sum(jnp.where(hits[k], slot, 0.0), axis=0, keepdims=True)
        place = (route_rows[k] ^ own_ref[1]).astype(f32) * capacity + own_slot
        index_rows.append(jnp.where(own_slot >= 0, place, -1.0))
    index_cols = jnp.concatenate(index_rows * 4, axis=0).T
    for k, pick in enumerate((pick0, pick1)):
        lane = iota(pick.shape, 1).astype(f32)
        pick[...] = jnp.where(lane == index_cols[:, k : k + 1], 1.0, 0.0).astype(bf16)


def make_tables(own, routes_t, dy, experts, capacity):
    count, width = dy.shape
    slots = experts * capacity
    shapes = [jax.ShapeDtypeStruct((slots, count), bf16)]
    shapes += [jax.ShapeDtypeStruct((count, slots), bf16)] * 2
    shapes += [jax.ShapeDtypeStruct((capacity, width), bf16)] * experts
    results = pl.pallas_call(
        functools.partial(tables_kernel, capacity),
        out_shape=shapes,
        in_specs=[smem_spec()] + [vmem_spec()] * 2,
        out_specs=[vmem_spec()] * len(shapes),
        compiler_params=params(48),
        name="slot_tables",
        cost_estimate=cost(4),
    )(own, routes_t, dy)
    return results[0], results[1:3], results[3:]


def qkv_kernel(
    own_ref, x0, x1, x2, x3, gain_ref, w_ref, a_ref, qkv_ref, k_ref, v_ref, heads_ref, x_buf, w_buf
):
    step = pl.program_id(0)
    width, cols = heads_ref.shape
    third = cols // 3

    @pl.when(step == 0)
    def turn():
        for h in range(width // third):

            @pl.when(own_ref[0] == h)
            def pick(h=h):
                for t in range(3):
                    start = t * width + h * third
                    heads_ref[:, t * third : (t + 1) * third] = w_ref[:, start : start + third]

        w_buf[...] = heads_ref[...].T

    for j, block in enumerate((x0, x1, x2, x3)):

        @pl.when(step == j)
        def take(block=block):
            x_buf[...] = block[...].astype(f32)

    x = x_buf[...]
    scale = lax.rsqrt(jnp.mean(x * x, axis=1, keepdims=True) + norm_eps)
    a = (x * scale * gain_ref[...]).astype(bf16)
    a_ref[...] = a
    qkv_t = mm(w_buf[...], a, NT).astype(bf16)
    qkv_ref[0:third, :] = qkv_t[0:third, :] * jnp.asarray(0.125, bf16)
    qkv_ref[third:, :] = qkv_t[third:, :]
    both = mm(a, heads_ref[:, third:]).astype(bf16)
    k_ref[...] = both[:, :third]
    v_ref[...] = both[:, third:]


def project_qkv(own, blocks, gain, w_qkv):
    count, width = blocks[0].shape
    parts = len(blocks)
    cols = w_qkv.shape[1] // parts
    third = cols // 3

    def whole(shape):
        return pl.BlockSpec(shape, lambda g, own_ref: (0, 0), pipeline_mode=pl.Buffered(1))

    return pl.pallas_call(
        qkv_kernel,
        out_shape=[
            jax.ShapeDtypeStruct((parts * count, width), bf16),
            jax.ShapeDtypeStruct((cols, parts * count), bf16),
            jax.ShapeDtypeStruct((parts * count, third), bf16),
            jax.ShapeDtypeStruct((parts * count, third), bf16),
            jax.ShapeDtypeStruct((width, cols), bf16),
        ],
        grid_spec=pltpu.PrefetchScalarGridSpec(
            num_scalar_prefetch=1,
            grid=(parts,),
            in_specs=[whole((count, width))] * parts
            + [whole((1, width)), whole((width, parts * cols))],
            out_specs=[
                pl.BlockSpec((count, width), lambda g, own_ref: (own_ref[0] ^ g, 0)),
                pl.BlockSpec((cols, count), lambda g, own_ref: (0, own_ref[0] ^ g)),
                pl.BlockSpec((count, third), lambda g, own_ref: (own_ref[0] ^ g, 0)),
                pl.BlockSpec((count, third), lambda g, own_ref: (own_ref[0] ^ g, 0)),
                whole((width, cols)),
            ],
            scratch_shapes=[pltpu.VMEM((count, width), f32), pltpu.VMEM((cols, width), bf16)],
        ),
        compiler_params=params(40),
        name="norm_qkv",
        cost_estimate=cost(7),
    )(own, *blocks, gain, w_qkv)


def mask_scores(scores, key_start, start_row, last_row, query_row, diagonal):
    key_col = key_start + iota(scores.shape, 0)
    valid = key_col >= start_row
    if diagonal:
        valid = (valid & (key_col <= last_row)) | (key_col == query_row)
    return jnp.where(valid, scores, masked_score)


def query_rows(info_ref, query_start, size):
    query_row = query_start + iota((1, size), 1)
    first_cut, last_cut, length = info_ref[0], info_ref[1], info_ref[2]
    start_row = jnp.where(
        query_row >= last_cut, last_cut, jnp.where(query_row >= first_cut, first_cut, 0)
    )
    last_row = jnp.minimum(query_row, length - 1)
    return query_row, start_row, last_row


def attend_kernel(block, info_ref, k_ref, q_ref, v_ref, o_ref, low_ref, log_ref, q_pad, s_buf):
    head = pl.program_id(0)
    qb = pl.program_id(1)
    q_pad[...] = jnp.zeros_like(q_pad)
    q_pad[pl.ds(pl.multiple_of(head * HEAD_DIM, HEAD_DIM), HEAD_DIM), :] = q_ref[...]
    query_row, start_row, last_row = query_rows(info_ref, qb * block, block)

    def score(j, diagonal):
        rows = pl.ds(pl.multiple_of(j * block, block), block)
        s = mm(k_ref[rows, :], q_pad[...])
        s = mask_scores(s, j * block, start_row, last_row, query_row, diagonal)
        s_buf[rows, :] = s
        return jnp.max(s, axis=0, keepdims=True)

    top = score(qb, True)
    top = lax.fori_loop(0, qb, lambda j, t: jnp.maximum(t, score(j, False)), top)

    def weigh(j, carry):
        total, out = carry
        rows = pl.ds(pl.multiple_of(j * block, block), block)
        p = jnp.exp(s_buf[rows, :] - top)
        total = total + jnp.sum(p, axis=0, keepdims=True)
        return total, out + mm(v_ref[:, rows], p.astype(bf16))

    zero = (jnp.zeros((1, block), f32), jnp.zeros((HEAD_DIM, block), f32))
    total, out = lax.fori_loop(0, qb + 1, weigh, zero)
    out = out / total
    o_ref[...] = out
    low_ref[...] = out.astype(bf16)
    log_ref[0] = top + jnp.log(total)


def attend(info, keys, qkv_t, block=512):
    row_len, group = keys.shape
    heads = group // HEAD_DIM
    return pl.pallas_call(
        functools.partial(attend_kernel, block),
        out_shape=[
            jax.ShapeDtypeStruct((group, row_len), f32),
            jax.ShapeDtypeStruct((group, row_len), bf16),
            jax.ShapeDtypeStruct((heads, 1, row_len), f32),
        ],
        grid=(heads, row_len // block),
        in_specs=[
            smem_spec(),
            pl.BlockSpec((row_len, group), lambda h, i: (0, 0)),
            pl.BlockSpec((HEAD_DIM, block), lambda h, i: (h, i)),
            pl.BlockSpec((HEAD_DIM, row_len), lambda h, i: (2 * heads + h, 0)),
        ],
        out_specs=[
            pl.BlockSpec((HEAD_DIM, block), lambda h, i: (h, i)),
            pl.BlockSpec((HEAD_DIM, block), lambda h, i: (h, i)),
            pl.BlockSpec((1, 1, block), lambda h, i: (h, 0, i)),
        ],
        scratch_shapes=[pltpu.VMEM((group, block), bf16), pltpu.VMEM((row_len, block), f32)],
        compiler_params=params(40),
        name="attend",
        cost_estimate=cost(21),
    )(info, keys, qkv_t, qkv_t)


def attend_back_kernel(
    block, info_ref, own_ref, k_ref, v_ref, q_ref, kt_ref, g0, g1, g2, g3, o_ref, log_ref,
    dq_ref, dk_ref, dv_ref, q_pad, g_pad, dk_acc, dv_acc,
):
    head = pl.program_id(0)
    qb = pl.program_id(1)
    blocks = pl.num_programs(1)
    rows_of_head = pl.ds(pl.multiple_of(head * HEAD_DIM, HEAD_DIM), HEAD_DIM)

    @pl.when(qb == 0)
    def clear():
        dk_acc[...] = jnp.zeros_like(dk_acc)
        dv_acc[...] = jnp.zeros_like(dv_acc)

    q = q_ref[...]
    q_pad[...] = jnp.zeros_like(q_pad)
    g_pad[...] = jnp.zeros_like(g_pad)
    q_pad[rows_of_head, :] = q
    for j, part in enumerate((g0, g1, g2, g3)):

        @pl.when((own_ref[0] ^ j) == qb)
        def take(part=part):
            g_pad[rows_of_head, :] = part[...]

    g = g_pad[rows_of_head, :]
    delta = jnp.sum(g.astype(f32) * o_ref[...], axis=0, keepdims=True)
    log_total = log_ref[0]
    query_row, start_row, last_row = query_rows(info_ref, qb * block, block)

    def one(j, dq, diagonal):
        rows = pl.ds(pl.multiple_of(j * block, block), block)
        s = mm(k_ref[rows, :], q_pad[...])
        s = mask_scores(s, j * block, start_row, last_row, query_row, diagonal)
        p = jnp.exp(s - log_total)
        dp = mm(v_ref[rows, :], g_pad[...])
        ds = (p * (dp - delta)).astype(bf16)
        dv_acc[:, rows] += mm(g, p.astype(bf16), NT)
        dk_acc[:, rows] += mm(q, ds, NT)
        return dq + mm(kt_ref[:, rows], ds)

    dq = one(qb, jnp.zeros((HEAD_DIM, block), f32), True)
    dq = lax.fori_loop(0, qb, lambda j, t: one(j, t, False), dq)
    dq_ref[...] = (0.125 * dq).astype(bf16)

    @pl.when(qb == blocks - 1)
    def finish():
        dk_ref[...] = dk_acc[...].astype(bf16)
        dv_ref[...] = dv_acc[...].astype(bf16)


def attend_back(info, own, keys, values, qkv_t, grads, out, logs, block=512):
    row_len, group = keys.shape
    heads = group // HEAD_DIM
    whole = pl.BlockSpec((row_len, group), lambda h, i: (0, 0))
    piece = pl.BlockSpec((HEAD_DIM, block), lambda h, i: (h, 0))
    tile = pl.BlockSpec((HEAD_DIM, block), lambda h, i: (h, i))
    full = pl.BlockSpec((HEAD_DIM, row_len), lambda h, i: (h, 0))
    return pl.pallas_call(
        functools.partial(attend_back_kernel, block),
        out_shape=[jax.ShapeDtypeStruct((group, row_len), bf16)] * 3,
        grid=(heads, row_len // block),
        in_specs=[
            smem_spec(),
            smem_spec(),
            whole,
            whole,
            tile,
            pl.BlockSpec((HEAD_DIM, row_len), lambda h, i: (heads + h, 0)),
            piece,
            piece,
            piece,
            piece,
            tile,
            pl.BlockSpec((1, 1, block), lambda h, i: (h, 0, i)),
        ],
        out_specs=[tile, full, full],
        scratch_shapes=[
            pltpu.VMEM((group, block), bf16),
            pltpu.VMEM((group, block), bf16),
            pltpu.VMEM((HEAD_DIM, row_len), f32),
            pltpu.VMEM((HEAD_DIM, row_len), f32),
        ],
        compiler_params=params(40),
        name="attend_back",
        cost_estimate=cost(30),
    )(info, own, keys, values, qkv_t, qkv_t, *grads, out, logs)


def gates_of(normed, router, route_rows):
    logits = mm(router, normed, NT, precise)
    expert_row = iota(logits.shape, 0)
    picked = [
        jnp.sum(jnp.where(expert_row == row, logits, 0.0), axis=0, keepdims=True)
        for row in route_rows
    ]
    top = jnp.maximum(picked[0], picked[1])
    raw = [jnp.exp(p - top) for p in picked]
    return [r / (raw[0] + raw[1]) for r in raw]


def dispatch_kernel(
    own_ref, t0, t1, t2, t3, x_ref, w_ref, gain_ref, router_ref, routes_ref, hot_ref,
    residual_ref, gates_ref, slot_gates_ref, *sends,
):
    residual = x_ref[...].astype(f32)
    group = t0.shape[0]
    for j, part in enumerate((t0, t1, t2, t3)):
        rows = pl.ds(pl.multiple_of((own_ref[0] ^ j) * group, group), group)
        residual = residual + mm(part[...], w_ref[rows, :], TN)
    residual_ref[...] = residual
    scale = lax.rsqrt(jnp.mean(residual * residual, axis=1, keepdims=True) + norm_eps)
    normed = residual * scale * gain_ref[...]
    capacity = sends[0].shape[0]
    one_hot = hot_ref[...]
    rows = mm(one_hot, normed.astype(bf16)).astype(bf16)
    for e, send in enumerate(sends):
        send[...] = rows[e * capacity : (e + 1) * capacity, :]
    route_rows = [routes_ref[k : k + 1, :] for k in range(2)]
    gates = gates_of(normed, router_ref[...], route_rows)
    gates_ref[0:1, :] = gates[0]
    gates_ref[1:2, :] = gates[1]
    experts = router_ref.shape[0]
    expert_row = iota((experts, x_ref.shape[0]), 0) ^ own_ref[1]
    table = jnp.where(expert_row == route_rows[0], gates[0], 0.0) + jnp.where(
        expert_row == route_rows[1], gates[1], 0.0
    )
    spread = sum(mm(piece, one_hot, NT) for piece in split_three(table))
    own = iota(spread.shape, 1) // capacity == iota(spread.shape, 0)
    slot_gates_ref[...] = jnp.sum(jnp.where(own, spread, 0.0), axis=0, keepdims=True)


def make_dispatch(own, parts, x, w_out, gain, router_t, routes_t, hot, capacity):
    count, width = x.shape
    slots = hot.shape[0]
    experts = slots // capacity
    shapes = [
        jax.ShapeDtypeStruct((count, width), f32),
        jax.ShapeDtypeStruct((2, count), f32),
        jax.ShapeDtypeStruct((1, slots), f32),
    ]
    shapes += [jax.ShapeDtypeStruct((capacity, width), bf16)] * experts
    results = pl.pallas_call(
        dispatch_kernel,
        out_shape=shapes,
        in_specs=[smem_spec()] + [vmem_spec()] * 10,
        out_specs=[vmem_spec()] * len(shapes),
        compiler_params=params(48),
        name="project_dispatch",
        cost_estimate=cost(8),
    )(own, *parts, x, w_out, gain, router_t, routes_t, hot)
    return results[0], results[1], results[2], results[3:]


def column_of(row):
    return jnp.broadcast_to(row, (128, row.shape[1])).T[:, 0:1]


def row_of(column):
    return jnp.broadcast_to(column, (column.shape[0], 128)).T[0:1, :]


GELU_SCALE = 0.7978845608028654
GELU_CUBE = 0.044715


def expert_kernel(sources, block, *refs):
    xs, dys = refs[:sources], refs[sources : 2 * sources]
    ups, downs = refs[2 * sources : 2 * sources + 4], refs[2 * sources + 4 : 2 * sources + 8]
    refs = refs[2 * sources + 8 :]
    outs, slots = refs[:sources], refs[sources : 2 * sources]
    dgate_ref, act_ref, dpre_ref, x_buf, dy_buf, up_buf, down_buf, out_acc, slot_acc, sems = refs[
        2 * sources :
    ]
    capacity = xs[0].shape[0]
    step = pl.program_id(0)
    parts = len(ups)

    def copies(j):
        return (
            pltpu.make_async_copy(ups[j], up_buf.at[j % 2], sems.at[0, j % 2]),
            pltpu.make_async_copy(downs[j], down_buf.at[j % 2], sems.at[1, j % 2]),
        )

    @pl.when(step == 0)
    def first():
        for copy in copies(0):
            copy.start()
        for n in range(sources):
            x_buf[n * capacity : (n + 1) * capacity, :] = xs[n][...]
            dy_buf[n * capacity : (n + 1) * capacity, :] = dys[n][...]
        out_acc[...] = jnp.zeros_like(out_acc)
        slot_acc[...] = jnp.zeros_like(slot_acc)

    for j in range(parts):

        @pl.when(step == j)
        def arrive(j=j):
            if j + 1 < parts:
                for copy in copies(j + 1):
                    copy.start()
            for copy in copies(j):
                copy.wait()

    which = lax.rem(step, 2)

    @pl.loop(0, x_buf.shape[0] // block)
    def rows_of(r):
        rows = pl.ds(pl.multiple_of(r * block, block), block)
        up, down = up_buf[which], down_buf[which]
        pre = mm(x_buf[rows, :], up)
        square = pre * pre
        tanh = jnp.tanh(GELU_SCALE * (pre * (1.0 + GELU_CUBE * square)))
        half = 0.5 * (1.0 + tanh)
        act = (pre * half).astype(bf16)
        act_ref[0, rows, :] = act
        out_acc[rows, :] += mm(act, down)
        slope = half + (0.5 * GELU_SCALE) * pre * (1.0 - tanh * tanh) * (
            1.0 + (3.0 * GELU_CUBE) * square
        )
        dpre = (mm(dy_buf[rows, :], down, NT) * slope).astype(bf16)
        dpre_ref[0, rows, :] = dpre
        slot_acc[rows, :] += mm(dpre, up, NT)

    @pl.when(step == parts - 1)
    def last():
        out = out_acc[...].astype(bf16)
        slot = slot_acc[...].astype(bf16)
        dgate = row_of(
            jnp.sum(dy_buf[...].astype(f32) * out.astype(f32), axis=1, keepdims=True)
        )
        dgate_ref[...] = dgate
        for n in range(sources):
            outs[n][...] = out[n * capacity : (n + 1) * capacity, :]
            slots[n][...] = slot[n * capacity : (n + 1) * capacity, :]


def row_block(rows, most=256):
    return max(b for b in range(16, most + 1, 16) if rows % b == 0)


def run_experts(xs, dys, ups, downs):
    sources = len(xs)
    capacity, width = xs[0].shape
    rows = sources * capacity
    units = ups[0].shape[1]
    parts = len(ups)

    def whole(shape):
        return pl.BlockSpec(shape, lambda g: (0, 0))

    hbm = pl.BlockSpec(memory_space=pl.ANY)
    piece = whole((capacity, width))
    shape = jax.ShapeDtypeStruct((capacity, width), bf16)
    kept = jax.ShapeDtypeStruct((parts, rows, units), bf16)
    kept_spec = pl.BlockSpec((1, rows, units), lambda g: (g, 0, 0))
    results = pl.pallas_call(
        functools.partial(expert_kernel, sources, row_block(rows)),
        out_shape=[shape] * (2 * sources) + [jax.ShapeDtypeStruct((1, rows), f32), kept, kept],
        grid=(parts,),
        in_specs=[piece] * (2 * sources) + [hbm] * (2 * parts),
        out_specs=[piece] * (2 * sources) + [whole((1, rows)), kept_spec, kept_spec],
        scratch_shapes=[
            pltpu.VMEM((rows, width), bf16),
            pltpu.VMEM((rows, width), bf16),
            pltpu.VMEM((2, width, units), bf16),
            pltpu.VMEM((2, units, width), bf16),
            pltpu.VMEM((rows, width), f32),
            pltpu.VMEM((rows, width), f32),
            pltpu.SemaphoreType.DMA((2, 2)),
        ],
        compiler_params=params(40),
        name="experts",
        cost_estimate=cost(16),
    )(*xs, *dys, *ups, *downs)
    return (
        results[:sources], results[sources : 2 * sources], results[2 * sources],
        results[2 * sources + 1], results[2 * sources + 2],
    )


def weight_kernel(experts, groups, gate_ref, *refs):
    xs, dys = refs[:experts], refs[experts : 2 * experts]
    acts, dpres = refs[2 * experts : 2 * experts + groups], refs[2 * experts + groups : 2 * experts + 2 * groups]
    refs = refs[2 * experts + 2 * groups :]
    ups, downs, (x_turn, dy_turn) = refs[:4], refs[4:8], refs[8:]
    step = pl.program_id(0)
    capacity = xs[0].shape[0]

    @pl.when(step == 0)
    def turn():
        for n in range(experts):
            cols = slice(n * capacity, (n + 1) * capacity)
            gate = gate_ref[0:1, cols]
            x_turn[:, cols] = (xs[n][...].astype(f32).T * gate).astype(bf16)
            dy_turn[:, cols] = (dys[n][...].astype(f32).T * gate).astype(bf16)

    act = jnp.concatenate([a[0] for a in acts], axis=0)
    dpre = jnp.concatenate([d[0] for d in dpres], axis=0)
    up = mm(x_turn[...], dpre)
    down = mm(dy_turn[...], act).T
    for j in range(4):

        @pl.when(step == j)
        def keep(j=j):
            ups[j][...] = up.astype(ups[j].dtype)
            downs[j][...] = down.astype(downs[j].dtype)


def weight_grads(gates, xs, dys, acts, dpres):
    experts, groups = len(xs), len(acts)
    capacity, width = xs[0].shape
    parts, rows, units = acts[0].shape

    def whole(shape):
        return pl.BlockSpec(shape, lambda g: (0, 0), pipeline_mode=pl.Buffered(1))

    kept = pl.BlockSpec((1, rows, units), lambda g: (g, 0, 0))
    types = (f32, bf16, f32, bf16)
    results = pl.pallas_call(
        functools.partial(weight_kernel, experts, groups),
        out_shape=[jax.ShapeDtypeStruct((width, units), t) for t in types]
        + [jax.ShapeDtypeStruct((units, width), t) for t in types],
        grid=(parts,),
        in_specs=[whole((1, experts * capacity))] + [whole((capacity, width))] * (2 * experts)
        + [kept] * (2 * groups),
        out_specs=[whole((width, units))] * parts + [whole((units, width))] * parts,
        scratch_shapes=[pltpu.VMEM((width, experts * capacity), bf16)] * 2,
        compiler_params=params(56),
        name="expert_weight_grads",
        cost_estimate=cost(30),
    )(gates, *xs, *dys, *acts, *dpres)
    return results[:parts], results[parts:]


def combine_back_kernel(
    own_ref, dgate_ref, hot_ref, pick0, pick1, residual_ref, dy_ref, gates_ref, routes_ref,
    router_ref, gain_ref, w_ref, t0, t1, t2, t3, *refs,
):
    experts = router_ref.shape[0]
    slots, (dres_ref, datt_ref, gout_ref, small_ref, slot_buf) = refs[:experts], refs[experts:]
    capacity = slots[0].shape[0]
    for n, slot in enumerate(slots):
        slot_buf[n * capacity : (n + 1) * capacity, :] = slot[...]
    residual = residual_ref[...]
    count = residual.shape[0]
    scale = lax.rsqrt(jnp.mean(residual * residual, axis=1, keepdims=True) + norm_eps)
    unit = residual * scale
    gain = gain_ref[...]
    row = dgate_ref[...]
    shape = (experts, row.shape[1])
    spread = jnp.where(iota(shape, 1) // capacity == iota(shape, 0), row, 0.0)
    table = sum(mm(piece, hot_ref[...]) for piece in split_three(spread))
    place_row = iota((experts, count), 0) ^ own_ref[1]
    routes = [routes_ref[k : k + 1, :] for k in range(2)]
    gates = [gates_ref[k : k + 1, :] for k in range(2)]
    dgates = [
        jnp.sum(jnp.where(place_row == r, table, 0.0), axis=0, keepdims=True) for r in routes
    ]
    mean = gates[0] * dgates[0] + gates[1] * dgates[1]
    expert_row = iota((experts, count), 0)
    dlogit = sum(
        jnp.where(expert_row == r, g * (d - mean), 0.0) for r, g, d in zip(routes, gates, dgates)
    )
    small_ref[...] = jnp.zeros_like(small_ref)
    small_ref[0:experts, :] = mm(dlogit, unit * gain, precision=precise)
    slot_rows = slot_buf[...]
    dnormed = mm(dlogit, router_ref[...], TN, precise)
    for gate, pick in zip(gates, (pick0, pick1)):
        dnormed = dnormed + column_of(gate) * mm(pick[...], slot_rows)
    small_ref[experts : experts + 1, :] = jnp.sum(dnormed * unit, axis=0, keepdims=True)
    scaled = dnormed * gain
    dres = dy_ref[...].astype(f32) + scale * (
        scaled - unit * jnp.mean(scaled * unit, axis=1, keepdims=True)
    )
    dres_ref[...] = dres
    branch = dres.astype(bf16)
    datt_ref[...] = mm(w_ref[...], branch, NT).astype(bf16)
    group = t0.shape[0]
    for j, part in enumerate((t0, t1, t2, t3)):
        rows = pl.ds(pl.multiple_of((own_ref[0] ^ j) * group, group), group)
        gout_ref[rows, :] = mm(part[...], branch)


def combine_back(own, slots, dgate, hot, picks, residual, dy, gates, routes_t, router_t, gain, w_out, parts):
    count, width = residual.shape
    experts = router_t.shape[0]
    shapes = [
        jax.ShapeDtypeStruct((count, width), f32),
        jax.ShapeDtypeStruct((width, count), bf16),
        jax.ShapeDtypeStruct((width, width), f32),
        jax.ShapeDtypeStruct((experts + 8, width), f32),
    ]
    return pl.pallas_call(
        combine_back_kernel,
        out_shape=shapes,
        in_specs=[smem_spec()] + [vmem_spec()] * (15 + experts),
        out_specs=[vmem_spec()] * len(shapes),
        scratch_shapes=[pltpu.VMEM((hot.shape[0], width), bf16)],
        compiler_params=params(56),
        name="combine_back",
        cost_estimate=cost(12),
    )(own, dgate, hot, *picks, residual, dy, gates, routes_t, router_t, gain, w_out, *parts, *slots)


def combine_kernel(pick0, pick1, residual_ref, gates_ref, *refs):
    outs, (y_ref, out_buf) = refs[:-2], refs[-2:]
    capacity = outs[0].shape[0]
    for n, out in enumerate(outs):
        out_buf[n * capacity : (n + 1) * capacity, :] = out[...]
    rows = out_buf[...]
    total = None
    for k, pick in enumerate((pick0, pick1)):
        term = column_of(gates_ref[k : k + 1, :]) * mm(pick[...], rows)
        total = term if total is None else total + term
    y_ref[...] = (residual_ref[...] + total).astype(bf16)


def combine(outs, picks, residual, gates):
    capacity, width = outs[0].shape
    return pl.pallas_call(
        combine_kernel,
        out_shape=jax.ShapeDtypeStruct(residual.shape, bf16),
        in_specs=[vmem_spec()] * (4 + len(outs)),
        out_specs=vmem_spec(),
        scratch_shapes=[pltpu.VMEM((len(outs) * capacity, width), bf16)],
        compiler_params=params(48),
        name="combine",
        cost_estimate=cost(5),
    )(*picks, residual, gates, *outs)


def lay_out_kernel(sizes, qkv_ref, out_ref, grad_qkv_ref, gain_ref, grad_out_ref, small_ref):
    exps, hids, rows, out_rows = sizes
    width = grad_out_ref.shape[1]
    bits = exps.bit_length() - 1

    def at(h, e):
        return (h & 1, h >> 1) + tuple((e >> b) & 1 for b in range(bits))

    third = exps * rows // 3
    gain = 0.0
    small_ref[...] = jnp.zeros_like(small_ref)
    for h in range(hids):
        block = jnp.concatenate([qkv_ref[at(h, e)][:rows] for e in range(exps)], axis=0)
        turned = block.astype(f32).T
        for t in range(3):
            start = t * width + h * third
            grad_qkv_ref[:, start : start + third] = turned[:, t * third : (t + 1) * third]
        gain = gain + qkv_ref[at(h, 0)][rows : rows + 1].astype(f32)
        for e in range(exps):
            n = h * exps + e
            piece = out_ref[at(h, e)].astype(f32)
            grad_out_ref[n * out_rows : (n + 1) * out_rows, :] = piece[:out_rows]
            if n < small_ref.shape[0]:
                small_ref[n : n + 1, :] = piece[out_rows : out_rows + 1]
    gain_ref[...] = gain


def lay_out(qkv, out, rows, out_rows, small_rows):
    hids, exps = 4, 1 << (qkv.ndim - 4)
    width = qkv.shape[-1]
    return pl.pallas_call(
        functools.partial(lay_out_kernel, (exps, hids, rows, out_rows)),
        out_shape=[
            jax.ShapeDtypeStruct((width, 3 * width), f32),
            jax.ShapeDtypeStruct((1, width), f32),
            jax.ShapeDtypeStruct((width, width), f32),
            jax.ShapeDtypeStruct((small_rows, width), f32),
        ],
        in_specs=[vmem_spec()] * 2,
        out_specs=[vmem_spec()] * 4,
        compiler_params=params(48),
        name="lay_out_sums",
        cost_estimate=cost(6),
    )(qkv, out)


def adam_update(weight, gradient, first_moment, second_moment, live_mask):
    first_next = beta_one * first_moment + (1.0 - beta_one) * gradient
    second_next = beta_two * second_moment + (1.0 - beta_two) * gradient * gradient
    first_hat = first_next / (1.0 - beta_one**adam_steps)
    second_hat = second_next / (1.0 - beta_two**adam_steps)
    weight_next = weight - learn_rate * first_hat / (jnp.sqrt(second_hat) + adam_eps)
    return (
        jnp.where(live_mask, weight_next, weight),
        jnp.where(live_mask, first_next, first_moment),
        jnp.where(live_mask, second_next, second_moment),
    )


def tie(value, other):
    return lax.optimization_barrier((value, other))[0]


def exchange(value, axis):
    return lax.all_to_all(value, axis, split_axis=0, concat_axis=0, tiled=True)


def send_all(pieces, axis):
    far_first = sorted(range(1, len(pieces)), reverse=True)
    order = [d for d in far_first if d * 2 >= len(pieces)][::-1]
    order += [d for d in far_first if d * 2 < len(pieces)]
    moved = {d: swap(pieces[d], axis, d) for d in order}
    return [pieces[0]] + [moved[d] for d in range(1, len(pieces))]


def reorder(value, index):
    count = value.shape[0]
    match = (jnp.arange(count) ^ index)[:, None] == jnp.arange(count)[None, :]
    return jnp.sum(jnp.where(match[:, :, None], value[None], 0.0), axis=1)


def split_sum(value, axis, distance):
    pairs = value.reshape((value.shape[0] // 2, 2) + value.shape[1:])
    low = (lax.axis_index(axis) & distance) == 0
    keep = jnp.where(low, pairs[:, 0], pairs[:, 1])
    give = jnp.where(low, pairs[:, 1], pairs[:, 0]).astype(bf16)
    return keep + swap(give, axis, distance).astype(f32)


def swap_stack(value, axis, distance):
    other = swap(value, axis, distance)
    low = (lax.axis_index(axis) & distance) == 0
    return jnp.stack([jnp.where(low, value, other), jnp.where(low, other, value)])


def gather_all(value, distances):
    for d in reversed(distances):
        value = swap_stack(value, "exp", d)
    for d in (2, 1):
        value = swap_stack(value, "hid", d)
    return value


def body(
    tokens, cotangent, routes, segments, lengths, gain_attn, gain_moe, w_qkv, w_out, router_w,
    router_first, router_second, up_w, down_w, up_first, up_second, down_first, down_second,
):
    exp_count = lax.axis_size("exp")
    hid_count = lax.axis_size("hid")
    hid = lax.axis_index("hid")
    exp_index = lax.axis_index("exp")
    own = jnp.stack([hid, exp_index]).astype(jnp.int32)
    x_own = tokens[0]
    dy = cotangent[0]
    count, width = x_own.shape
    experts = router_w.shape[1]
    frozen_count = experts // 2
    capacity = max(2, 3 * count // experts)
    group = width // hid_count
    is_new = exp_index >= frozen_count

    x_far = swap(x_own, "hid", 2)
    x_near = swap(x_own, "hid", 1)
    routes_t = routes[0].T
    hot, picks, dy_sends = make_tables(own, routes_t, dy, experts, capacity)
    seg_row = segments[0]
    info = jnp.stack(
        [
            jnp.sum((seg_row < 1).astype(jnp.int32)),
            jnp.sum((seg_row < 2).astype(jnp.int32)),
            lengths[0],
        ]
    )
    up_low = up_w[0].astype(bf16)
    down_low = down_w[0].astype(bf16)
    router_t = router_w.T
    x_far, (info, dy_sends, up_low, down_low, router_t, routes_t) = lax.optimization_barrier(
        (x_far, (info, dy_sends, up_low, down_low, router_t, routes_t))
    )
    x_last = swap(x_far, "hid", 1)
    blocks = (x_own, x_near, x_far, x_last)
    dy_rows = send_all(dy_sends, "exp")

    up_far, down_far = swap(up_low, "hid", 2), swap(down_low, "hid", 2)
    up_near, down_near = swap(up_low, "hid", 1), swap(down_low, "hid", 1)
    up_last, down_last = swap(up_far, "hid", 1), swap(down_far, "hid", 1)
    ups = (up_low, up_near, up_far, up_last)
    downs = (down_low, down_near, down_far, down_last)

    a_one, qkv_t, keys, values, w_heads = project_qkv(own, blocks, gain_attn[None], w_qkv)
    out_heads, out_low, logs = attend(info, keys, qkv_t)

    def piece_of(value, j):
        return lax.dynamic_slice_in_dim(value, (hid ^ j) * count, count, 1)

    att_parts = [piece_of(out_low, 0)] + [
        swap(piece_of(out_low, j), "hid", j) for j in range(1, hid_count)
    ]
    att_parts, dy_rows = lax.optimization_barrier((att_parts, dy_rows))

    residual, gates, slot_gates, sends = make_dispatch(
        own, att_parts, x_own, w_out, gain_moe[None], router_t, routes_t, hot, capacity
    )
    x_rows = send_all(sends, "exp")
    gate_rows = exchange(reorder(slot_gates.reshape(experts, capacity), exp_index), "exp")
    gate_rows = reorder(gate_rows, exp_index).reshape(1, experts * capacity)

    in_group = exp_count // 4
    groups = [range(g * in_group, (g + 1) * in_group) for g in (0, 2, 1, 3)]
    results = {}
    for members in groups:
        outs, slots, dgate, act, dpre = run_experts(
            [x_rows[d] for d in members], [dy_rows[d] for d in members], ups, downs
        )
        results[members[0] // in_group] = (outs, slots, dgate, act, dpre)
    results = [results[g] for g in range(4)]
    slot_back = send_all([s for r in results for s in r[1]], "exp")
    dgates = jnp.concatenate([r[2].reshape(in_group, capacity) for r in results], axis=0)
    dgates = reorder(exchange(reorder(dgates, exp_index), "exp"), exp_index)
    dgates = dgates.reshape(1, experts * capacity)

    part_ups, part_downs = weight_grads(
        gate_rows, x_rows, dy_rows, [r[3] for r in results], [r[4] for r in results]
    )
    near_up, near_down = swap(part_ups[1], "hid", 1), swap(part_downs[1], "hid", 1)
    last_up, last_down = swap(part_ups[3], "hid", 1), swap(part_downs[3], "hid", 1)
    far_up = (part_ups[2] + last_up.astype(f32)).astype(bf16)
    far_down = (part_downs[2] + last_down.astype(f32)).astype(bf16)
    far_up, far_down = swap(far_up, "hid", 2), swap(far_down, "hid", 2)
    grad_up = part_ups[0] + near_up.astype(f32) + far_up.astype(f32)
    grad_down = part_downs[0] + near_down.astype(f32) + far_down.astype(f32)
    grad_up = jnp.where(is_new, grad_up, 0.0)
    grad_down = jnp.where(is_new, grad_down, 0.0)

    dres, datt, gout, small = combine_back(
        own, slot_back, dgates, hot, picks, residual, dy, gates, routes_t, router_t,
        gain_moe[None], w_out, att_parts,
    )

    def heads_of(value, j):
        return lax.dynamic_slice_in_dim(value, (hid ^ j) * group, group, 0)

    datt_parts = [heads_of(datt, 0)] + [
        swap(heads_of(datt, j), "hid", j) for j in range(1, hid_count)
    ]

    out_back = send_all([o for r in results for o in r[0]], "exp")
    out_tokens = combine(out_back, picks, residual, gates)

    dqkv_t = jnp.concatenate(
        attend_back(info, own, keys, values, qkv_t, datt_parts, out_heads, logs), axis=0
    )
    grad_t = mm(dqkv_t, a_one)
    dnormed = mm(dqkv_t, w_heads, ((0,), (1,)))

    def rows_of(j):
        return lax.dynamic_slice_in_dim(dnormed, (hid ^ j) * count, count, 0)

    near = swap(rows_of(1).astype(bf16), "hid", 1)
    last = swap(rows_of(3).astype(bf16), "hid", 1)
    far = swap((rows_of(2) + last.astype(f32)).astype(bf16), "hid", 2)
    dnormed_own = rows_of(0) + near.astype(f32) + far.astype(f32)
    x = x_own.astype(f32)
    scale = lax.rsqrt(jnp.mean(x * x, axis=-1, keepdims=True) + norm_eps)
    unit = x * scale
    scaled = dnormed_own * gain_attn
    grad_tokens = (
        dres + scale * (scaled - unit * jnp.mean(scaled * unit, axis=-1, keepdims=True))
    ).astype(bf16)
    ggain_part = jnp.sum(dnormed * a_one.astype(f32), axis=0) / gain_attn

    rows = 3 * group // exp_count
    tail = -(rows + 1) % 8 + 1
    pad = jnp.broadcast_to(ggain_part, (exp_count, tail, width))
    piece = jnp.concatenate([grad_t.reshape(exp_count, rows, width), pad], axis=1)
    distances = [1 << b for b in range(exp_count.bit_length() - 1)]
    for d in distances:
        piece = split_sum(piece, "exp", d)
    whole = gather_all(piece[0].astype(bf16), distances)

    devices = exp_count * hid_count
    out_rows = width // devices
    extra = -(out_rows + 1) % 8 + 1
    small = jnp.pad(small[:devices], ((0, max(0, devices - small.shape[0])), (0, 0)))
    part = jnp.concatenate(
        [
            gout.reshape(devices, out_rows, width),
            small[:, None],
            jnp.zeros((devices, extra - 1, width), f32),
        ],
        axis=1,
    ).reshape(hid_count, exp_count * (out_rows + extra), width)
    for d in (1, 2):
        part = split_sum(part, "hid", d)
    part = part.reshape(exp_count, out_rows + extra, width)
    for d in distances:
        part = split_sum(part, "exp", d)
    out_whole = gather_all(part[0].astype(bf16), distances)

    grad_qkv, grad_gain_attn, grad_out_proj, small = lay_out(
        whole, out_whole, rows, out_rows, (experts + 8) // 8 * 8
    )
    grad_gain_attn = grad_gain_attn[0]
    grad_gain_moe = small[experts]
    live_columns = (jnp.arange(experts, dtype=jnp.int32) >= frozen_count)[None, :]
    grad_router = jnp.where(live_columns, small[:experts].T, 0.0)
    router_new, router_first_next, router_second_next = adam_update(
        router_w[:, frozen_count:], grad_router[:, frozen_count:], router_first, router_second, True
    )
    router_next = jnp.concatenate([router_w[:, :frozen_count], router_new], axis=1)
    up_next, up_first_next, up_second_next = adam_update(
        up_w[0], grad_up, up_first[0], up_second[0], is_new
    )
    down_next, down_first_next, down_second_next = adam_update(
        down_w[0], grad_down, down_first[0], down_second[0], is_new
    )
    return (
        out_tokens[None],
        grad_tokens[None],
        grad_qkv,
        grad_out_proj,
        grad_gain_attn,
        grad_gain_moe,
        grad_router,
        router_next,
        router_first_next,
        router_second_next,
        grad_up[None],
        grad_down[None],
        up_next[None],
        down_next[None],
        up_first_next[None],
        up_second_next[None],
        down_first_next[None],
        down_second_next[None],
    )


def solution(mesh):
    tok = P("exp", "hid", None)
    up = P("exp", None, "hid")
    return jax.shard_map(
        body,
        mesh=mesh,
        in_specs=(tok, tok, tok, P("exp", None), P("exp")) + (P(),) * 7
        + (up, tok, up, up, tok, tok),
        out_specs=(tok, tok) + (P(),) * 8 + (up, tok, up, tok, up, up, tok, tok),
        check_vma=False,
    )
```

time: 1580 us -> 574 us (0.36)
  blocking collectives: 504 us -> 0 us
  waiting for transfers between devices: 513 us -> 175 us
  matrix products: 257 us -> 6.8 us
  Pallas kernels: 0 us -> 188 us
  other arithmetic: 145 us -> 36.1 us
  starting transfers between devices: 11.4 us -> 112 us
  local copies, waits for them, and re-layouts: 126 us -> 47.6 us
    psum x2 -> x0, blocking collectives: 386 us -> none  [the longest x1 321 us: body(): lax.psum(jnp.dot(act_low, down_low, preferred_element_type=jnp.float32),...]
    dot_general x22 -> x2, matrix products: 257 us -> 6.8 us  [mm(): lax.dot_general(left, right, (contract, ((), ())), preferred_element_type...]
    reduce_scatter x3 -> x0, waiting for transfers between devices: 212 us -> none  [the longest x1 139 us: body(): lax.psum_scatter(contract_cols(grad_pre, up_low), 'hid', scatter_dimensio...]
    pallas_call x0 -> x13, Pallas kernels: none -> 188 us  [the longest x4 60.3 us: run_experts(): pl.pallas_call(functools.partial(expert_kernel, sources, row_block(rows))...]
    ppermute x0 -> x70, waiting for transfers between devices: none -> 172 us  [swap(): return lax.ppermute(value, axis, [(i, i ^ distance) for i in range(count)])]
    all_gather x4 -> x0, waiting for transfers between devices: 133 us -> none  [the longest x1 63.8 us: body(): expert_rows = lax.all_gather(arrived_rows, 'hid', axis=0, tiled=True)]
    all_to_all x2 -> x0, blocking collectives: 118 us -> none  [the longest x1 59.2 us: body(): lax.all_to_all(send_rows, 'exp', split_axis=0, concat_axis=0, tiled=True)]
    ppermute x0 -> x70, starting transfers between devices: none -> 105 us  [swap(): return lax.ppermute(value, axis, [(i, i ^ distance) for i in range(count)])]
  transfers between devices with their start and end apart: 10 -> 72, of which waited for: 9 -> 25; matrix products, arithmetic and copies ran while one was open for 12% -> 8% of each run, Pallas kernels for 0% -> 29%
where the time goes in v1:
time: 574 us; the launch traced here: 568 us
  Pallas kernels  188 us (33%)
  waiting for transfers between devices  175 us (30%)
  starting transfers between devices  112 us (20%)
  local copies, waits for them, and re-layouts  47.6 us (8%)
  other arithmetic  36.1 us (6%)
  matrix products  6.8 us (1%)
    ppermute x70, waiting for transfers between devices, swap(): return lax.ppermute(value, axis, [(i, i ^ distance) for i in range(count)])  172 us
    ppermute x70, starting transfers between devices, swap(): return lax.ppermute(value, axis, [(i, i ^ distance) for i in range(count)])  105 us
    pallas_call x4, Pallas kernels, run_experts(): pl.pallas_call(functools.partial(expert_kernel, sources, row_block(rows))...  60.3 us
    unnamed x240, local copies, waits for them, and re-layouts  41.4 us
    pallas_call x1, Pallas kernels, weight_grads(): pl.pallas_call(functools.partial(weight_kernel, experts, groups), out_sha...  30.5 us
    pallas_call x1, Pallas kernels, attend_back(): pl.pallas_call(functools.partial(attend_back_kernel, block), out_shape=[j...  29.8 us
    pallas_call x1, Pallas kernels, attend(): pl.pallas_call(functools.partial(attend_kernel, block), out_shape=[jax.Sh...  21.4 us
    pallas_call x1, Pallas kernels, combine_back(): pl.pallas_call(combine_back_kernel, out_shape=shapes, in_specs=[smem_spec...  13.2 us
  transfers between devices with their start and end apart: 72, of which 25 were waited for; matrix products, arithmetic and copies ran while one was open for 8% of the time, Pallas kernels for 29%

profile of v1, /device:TPU:1, one launch (start us, length us, event | category | flops | bytes accessed | tf_op | source)
XLA Modules:
  0.0 568.1 jit_solution(951268660135237539)
XLA Ops:
  9.9 4.1 slot_tables.1
  27.9 10.2 %norm_qkv.1 = (bf16[2048,768]{1,0:T(8,128)(2,1)S(1)}, bf16[576,2048]{1,0:T(8,128)(2,1)S(1)}, bf16[2048,192]{1,0:T(8,128)(2,1)S(1)}, bf16[2048,192]{1,0:T(8,128)(2,1)S(1)}, bf16[768,576]{1,0:T(8,128)(2,1)S(1)}) custom-call(s32[2]{0:T(128)S(1)} %pad_add_fusion.own_ref, bf16[512,768]{1,0:T(8,128)(2,1)S(1)} %bitcast.266, ...), custom_call_target="tpu_custom_call" | custom-call | flops 7699999744 | bytes 21000000 | tf_op jit(solution)/shard_map/norm_qkv/pallas_call | solution.py:166
  50.7 21.4 %attend.1 = (f32[192,2048]{1,0:T(8,128)S(1)}, bf16[192,2048]{1,0:T(8,128)(2,1)S(1)}, f32[3,1,2048]{2,1,0:T(1,128)S(1)}) custom-call(s32[3]{0:T(128)S(1)} %pad_add_fusion.1.info_ref, bf16[2048,192]{1,0:T(8,128)(2,1)S(1)} %get-tuple-element.133.k_ref, bf16[576,2048]{1,0:T(8,128)(2,1)S(1)} %get-tuple-element.134.q_ref.v_ref.kt_ref, ...), custom_call_target="tpu_custom_call" | custom-call | flops 23100000256 | bytes 63000000 | tf_op jit(solution)/shard_map/attend/pallas_call | solution.py:248
  79.0 26.2 %collective-permute-done.4.t2 = bf16[192,512]{1,0:T(8,128)(2,1)S(1)} collective-permute-done((bf16[192,512]{1,0:T(8,128)(2,1)S(1)}, bf16[192,512]{1,0:T(8,128)(2,1)S(1)}, u32[]{:S(2)}, u32[]{:S(2)}) %collective-permute-start.4) | collective-permute-done | bytes 196640 | tf_op jit(solution)/shard_map/ppermute | solution.py:39
  110.7 7.7 %project_dispatch.1 = (f32[512,768]{1,0:T(8,128)}, f32[2,512]{1,0:T(2,128)S(1)}, f32[1,1536]{1,0:T(1,128)S(1)}, bf16[192,768]{1,0:T(8,128)(2,1)S(1)}, bf16[192,7...) custom-call(s32[2]{0:T(128)S(1)} %pad_add_fusion.own_ref, ...), custom_call_target="tpu_custom_call" | custom-call | flops 8800000000 | bytes 24000000 | tf_op jit(solution)/shard_map/project_dispatch/pallas_call | solution.py:415
  124.6 4.4 collective-permute-done.21.refs_0_.refs_2_
  129.3 10.1 %collective-permute-done.22.refs_1_.refs_3_ = bf16[192,768]{1,0:T(8,128)(2,1)} collective-permute-done((bf16[192,768]{1,0:T(8,128)(2,1)S(1)}, bf16[192,768]{1,0:T(8,128)(2,1)}, u32[]{:S(2)}, u32[]{:S(2)}) %collective-permute-start.22) | collective-permute-done | bytes 294944 | tf_op jit(solution)/shard_map/ppermute | solution.py:39
  145.7 15.6 %experts.5 = (bf16[192,768]{1,0:T(8,128)(2,1)S(1)}, bf16[192,768]{1,0:T(8,128)(2,1)S(1)}, bf16[192,768]{1,0:T(8,128)(2,1)S(1)}, bf16[192,768]{1,0:T(8,128)(2,1)S...) custom-call(bf16[192,768]{1,0:T(8,128)(2,1)} %collective-permute-done.21.refs_0_.refs_2_, ...), custom_call_target="tpu_custom_call" | custom-call | flops 17600000000 | bytes 48000000 | tf_op jit(solution)/shard_map/experts/pallas_call | solution.py:529
  164.2 7.7 %collective-permute-done.26.refs_1_.refs_5_ = bf16[192,768]{1,0:T(8,128)(2,1)S(1)} collective-permute-done((bf16[192,768]{1,0:T(8,128)(2,1)}, bf16[192,768]{1,0:T(8,128)(2,1)S(1)}, u32[]{:S(2)}, u32[]{:S(2)}) %collective-permute-start.26) | collective-permute-done | bytes 294944 | tf_op jit(solution)/shard_map/ppermute | solution.py:39
  171.9 14.7 %experts.6 = (bf16[192,768]{1,0:T(8,128)(2,1)S(1)}, bf16[192,768]{1,0:T(8,128)(2,1)S(1)}, bf16[192,768]{1,0:T(8,128)(2,1)S(1)}, bf16[192,768]{1,0:T(8,128)(2,1)S...) custom-call(bf16[192,768]{1,0:T(8,128)(2,1)S(1)} %collective-permute-done.25.refs_0_.refs_, ...), custom_call_target="tpu_custom_call" | custom-call | flops 17600000000 | bytes 48000000 | tf_op jit(solution)/shard_map/experts/pallas_call | solution.py:529
  189.5 14.5 %experts.7 = (bf16[192,768]{1,0:T(8,128)(2,1)S(1)}, bf16[192,768]{1,0:T(8,128)(2,1)S(1)}, bf16[192,768]{1,0:T(8,128)(2,1)S(1)}, bf16[192,768]{1,0:T(8,128)(2,1)S...) custom-call(bf16[192,768]{1,0:T(8,128)(2,1)S(1)} %collective-permute-done.29.refs_0_.refs_, ...), custom_call_target="tpu_custom_call" | custom-call | flops 17600000000 | bytes 48000000 | tf_op jit(solution)/shard_map/experts/pallas_call | solution.py:529
  212.8 15.5 %experts.4 = (bf16[192,768]{1,0:T(8,128)(2,1)S(1)}, bf16[192,768]{1,0:T(8,128)(2,1)S(1)}, bf16[192,768]{1,0:T(8,128)(2,1)S(1)}, bf16[192,768]{1,0:T(8,128)(2,1)S...) custom-call(bf16[192,768]{1,0:T(8,128)(2,1)S(1)} %copy-done.83, ...), custom_call_target="tpu_custom_call" | custom-call | flops 17600000000 | bytes 48000000 | tf_op jit(solution)/shard_map/experts/pallas_call | solution.py:529
  255.2 30.5 %expert_weight_grads.1 = (f32[768,768]{1,0:T(8,128)}, bf16[768,768]{1,0:T(8,128)(2,1)}, f32[768,768]{1,0:T(8,128)}, bf16[768,768]{1,0:T(8,128)(2,1)}, f32[768,76...) custom-call(f32[1,1536]{1,0:T(1,128)} %reshape.319.gate_ref, ...), custom_call_target="tpu_custom_call" | custom-call | flops 32999999488 | bytes 90000000 | tf_op jit(solution)/shard_map/expert_weight_grads/pallas_call | solution.py:592
  288.3 13.2 %combine_back.1 = (f32[512,768]{1,0:T(8,128)}, bf16[768,512]{1,0:T(8,128)(2,1)}, f32[768,768]{1,0:T(8,128)}, f32[16,768]{1,0:T(8,128)}) custom-call(s32[2]{0:T(128)} %copy-done.63, f32[1,1536]{1,0:T(1,128)} %reshape.312.dgate_ref, bf16[1536,512]{1,0:T(8,128)(2,1)} %copy-done.67, bf16[512,1536]{1,0:T(8,128)(2,1)} %get-tuple-element.121.pick0, ...), custom_call_target="tpu_custom_call" | custom-call | flops 13200000000 | bytes 36000000 | tf_op jit(solution)/shard_map/combine_back/pallas_call | solution.py:666
  302.8 5.8 %collective-permute-start.40 = (bf16[192,512]{1,0:T(8,128)(2,1)S(1)}, bf16[192,512]{1,0:T(8,128)(2,1)S(1)}, u32[]{:S(2)}, u32[]{:S(2)}) collective-permute-start(bf16[192,512]{1,0:T(8,128)(2,1)S(1)} %get-tuple-element.255), channel_id=1, source_target_pairs={{0,1},{1,0},{2,3},{3,2},{4,5},{5,4},{6,7},{7,6},{8,9},{9,8},{10,11... | collective-permute-start | bytes 589832 | tf_op jit(solution)/shard_map/ppermute | solution.py:39
  314.6 10.4 %collective-permute-start.24 = (bf16[192,768]{1,0:T(8,128)(2,1)S(1)}, bf16[192,768]{1,0:T(8,128)(2,1)S(1)}, u32[]{:S(2)}, u32[]{:S(2)}) collective-permute-start(bf16[192,768]{1,0:T(8,128)(2,1)S(1)} %copy-done.25), channel_id=1, source_target_pairs={{0,12},{4,8},{8,4},{12,0},{16,28},{20,24},{24,20},{28,16},{1,13},{... | collective-permute-start | bytes 884744 | tf_op jit(solution)/shard_map/ppermute | solution.py:39
  325.8 5.4 collective-permute-start.28
  331.3 29.8 %attend_back.1 = (bf16[192,2048]{1,0:T(8,128)(2,1)S(1)}, bf16[192,2048]{1,0:T(8,128)(2,1)S(1)}, bf16[192,2048]{1,0:T(8,128)(2,1)S(1)}) custom-call(s32[3]{0:T(128)S(1)} %pad_add_fusion.1.info_ref, s32[2]{0:T(128)S(1)} %copy-done.64, bf16[2048,192]{1,0:T(8,128)(2,1)S(1)} %copy-done.71, bf16[2048,192]{1,0:T(8,128)(2,1)S(1)} %copy-done.73, ...), custom_call_target="tpu_custom_call" | custom-call | flops 32999999488 | bytes 90000000 | tf_op jit(solution)/shard_map/attend_back/pallas_call | solution.py:331
  363.2 4.8 multiply_reduce_fusion
  385.6 5.1 combine.1
  390.9 4.9 collective-permute-done.46
  401.1 10.4 %collective-permute-start.47 = (bf16[2,80,768]{2,1,0:T(8,128)(2,1)S(1)}, bf16[2,80,768]{2,1,0:T(8,128)(2,1)S(1)}, u32[]{:S(2)}, u32[]{:S(2)}) collective-permute-start(bf16[2,80,768]{2,1,0:T(8,128)(2,1)S(1)} %fusion.29), channel_id=1, source_target_pairs={{0,8},{4,12},{8,0},{12,4},{16,24},{20,28},{24,16},{28,20},{1,9},{5... | collective-permute-start | bytes 737288 | tf_op jit(solution)/shard_map/ppermute | solution.py:39
  413.3 4.1 collective-permute-done.47
  429.4 7.8 %collective-permute-done.49 = bf16[80,768]{1,0:T(8,128)(2,1)S(1)} collective-permute-done((bf16[80,768]{1,0:T(8,128)(2,1)S(1)}, bf16[80,768]{1,0:T(8,128)(2,1)S(1)}, u32[]{:S(2)}, u32[]{:S(2)}) %collective-permute-start.49) | collective-permute-done | bytes 122912 | tf_op jit(solution)/shard_map/ppermute | solution.py:39
  437.2 6.0 %collective-permute-done.56 = bf16[4,32,768]{2,1,0:T(8,128)(2,1)S(1)} collective-permute-done((bf16[4,32,768]{2,1,0:T(8,128)(2,1)S(1)}, bf16[4,32,768]{2,1,0:T(8,128)(2,1)S(1)}, u32[]{:S(2)}, u32[]{:S(2)}) %collective-permute-start.56) | collective-permute-done | bytes 196640 | tf_op jit(solution)/shard_map/ppermute | solution.py:39
  457.1 4.2 collective-permute-done.60
  461.5 4.8 collective-permute-done.45
  468.5 4.1 collective-permute-done.61
  476.6 15.0 %collective-permute-done.66 = bf16[768,768]{1,0:T(8,128)(2,1)S(1)} collective-permute-done((bf16[768,768]{1,0:T(8,128)(2,1)S(1)}, bf16[768,768]{1,0:T(8,128)(2,1)S(1)}, u32[]{:S(2)}, u32[]{:S(2)}) %collective-permute-start.66) | collective-permute-done | bytes 1179680 | tf_op jit(solution)/shard_map/ppermute | solution.py:39
  499.1 47.3 %collective-permute-done.52 = bf16[2,2,2,80,768]{4,3,2,1,0:T(8,128)(2,1)S(1)} collective-permute-done((bf16[2,2,2,80,768]{4,3,2,1,0:T(8,128)(2,1)S(1)}, bf16[2,2,2,80,768]{4,3,2,1,0:T(8,128)(2,1)S(1)}, u32[]{:S(2)}, u32[]{:S(2)}) %collective-permute-start.52) | collective-permute-done | bytes 983072 | tf_op jit(solution)/shard_map/ppermute | solution.py:39
  546.9 4.6 collective-permute-start.53
  559.9 5.5 lay_out_sums.1
  (458 shorter events, 189.4 us)
Async XLA Ops:
  26.9 47.8 %collective-permute-start.10 = (bf16[192,768]{1,0:T(8,128)(2,1)}, bf16[192,768]{1,0:T(8,128)(2,1)S(1)}, u32[]{:S(2)}, u32[]{:S(2)}) collective-permute-start(bf16[192,768]{1,0:T(8,128)(2,1)} %copy-done.54), channel_id=1, source_target_pairs={{0,20},{4,16},{8,28},{12,24},{16,4},{20,0},{24,12},{28,8},{1,21},{... | collective-permute-start | bytes 884744 | tf_op jit(solution)/shard_map/ppermute | solution.py:39
  41.6 34.7 %collective-permute-start.11 = (bf16[192,768]{1,0:T(8,128)(2,1)S(1)}, bf16[192,768]{1,0:T(8,128)(2,1)S(1)}, u32[]{:S(2)}, u32[]{:S(2)}) collective-permute-start(bf16[192,768]{1,0:T(8,128)(2,1)S(1)} %copy-done.53), channel_id=1, source_target_pairs={{0,24},{4,28},{8,16},{12,20},{16,8},{20,12},{24,0},{28,4},{1,25},{... | collective-permute-start | bytes 884744 | tf_op jit(solution)/shard_map/ppermute | solution.py:39
  45.6 32.1 %collective-permute-start.12 = (bf16[192,768]{1,0:T(8,128)(2,1)S(1)}, bf16[192,768]{1,0:T(8,128)(2,1)S(1)}, u32[]{:S(2)}, u32[]{:S(2)}) collective-permute-start(bf16[192,768]{1,0:T(8,128)(2,1)S(1)} %get-tuple-element.143), channel_id=1, source_target_pairs={{0,28},{4,24},{8,20},{12,16},{16,12},{20,8},{24,4},{28,0},{1,29},{... | collective-permute-start | bytes 884744 | tf_op jit(solution)/shard_map/ppermute | solution.py:39
  49.3 59.4 %collective-permute-start.15 = (bf16[768,768]{1,0:T(8,128)(2,1)S(1)}, bf16[768,768]{1,0:T(8,128)(2,1)}, u32[]{:S(2)}, u32[]{:S(2)}) collective-permute-start(bf16[768,768]{1,0:T(8,128)(2,1)S(1)} %get-tuple-element.157.refs_4_), channel_id=1, source_target_pairs={{0,2},{1,3},{2,0},{3,1},{4,6},{5,7},{6,4},{7,5},{8,10},{9,11},{10,... | collective-permute-start | bytes 3538952 | tf_op jit(solution)/shard_map/ppermute | solution.py:39
  50.5 58.2 %collective-permute-start.18 = (bf16[768,768]{1,0:T(8,128)(2,1)S(1)}, bf16[768,768]{1,0:T(8,128)(2,1)}, u32[]{:S(2)}, u32[]{:S(2)}) collective-permute-start(bf16[768,768]{1,0:T(8,128)(2,1)S(1)} %get-tuple-element.158.refs_8_), channel_id=1, source_target_pairs={{0,2},{1,3},{2,0},{3,1},{4,6},{5,7},{6,4},{7,5},{8,10},{9,11},{10,... | collective-permute-start | bytes 3538952 | tf_op jit(solution)/shard_map/ppermute | solution.py:39
  78.4 42.0 %collective-permute-start.14 = (bf16[768,768]{1,0:T(8,128)(2,1)S(1)}, bf16[768,768]{1,0:T(8,128)(2,1)S(1)}, u32[]{:S(2)}, u32[]{:S(2)}) collective-permute-start(bf16[768,768]{1,0:T(8,128)(2,1)S(1)} %get-tuple-element.157.refs_4_), channel_id=1, source_target_pairs={{0,1},{1,0},{2,3},{3,2},{4,5},{5,4},{6,7},{7,6},{8,9},{9,8},{10,11... | collective-permute-start | bytes 3538952 | tf_op jit(solution)/shard_map/ppermute | solution.py:39
  78.7 31.9 %collective-permute-start.5 = (bf16[192,512]{1,0:T(8,128)(2,1)S(1)}, bf16[192,512]{1,0:T(8,128)(2,1)S(1)}, u32[]{:S(2)}, u32[]{:S(2)}) collective-permute-start(bf16[192,512]{1,0:T(8,128)(2,1)S(1)} %get-tuple-element.257), channel_id=1, source_target_pairs={{0,3},{1,2},{2,1},{3,0},{4,7},{5,6},{6,5},{7,4},{8,11},{9,10},{10,... | collective-permute-start | bytes 589832 | tf_op jit(solution)/shard_map/ppermute | solution.py:39
  108.7 31.0 %collective-permute-start.16 = (bf16[768,768]{1,0:T(8,128)(2,1)}, bf16[768,768]{1,0:T(8,128)(2,1)}, u32[]{:S(2)}, u32[]{:S(2)}) collective-permute-start(bf16[768,768]{1,0:T(8,128)(2,1)} %collective-permute-done.15.refs_6_), channel_id=1, source_target_pairs={{0,1},{1,0},{2,3},{3,2},{4,5},{5,4},{6,7},{7,6},{8,9},{9,8},{10,11... | collective-permute-start | bytes 3538952 | tf_op jit(solution)/shard_map/ppermute | solution.py:39
  108.8 32.9 %collective-permute-start.19 = (bf16[768,768]{1,0:T(8,128)(2,1)}, bf16[768,768]{1,0:T(8,128)(2,1)}, u32[]{:S(2)}, u32[]{:S(2)}) collective-permute-start(bf16[768,768]{1,0:T(8,128)(2,1)} %collective-permute-done.18.refs_10_), channel_id=1, source_target_pairs={{0,1},{1,0},{2,3},{3,2},{4,5},{5,4},{6,7},{7,6},{8,9},{9,8},{10,11... | collective-permute-start | bytes 3538952 | tf_op jit(solution)/shard_map/ppermute | solution.py:39
  124.5 84.1 %collective-permute-start.13 = (bf16[192,768]{1,0:T(8,128)(2,1)}, bf16[192,768]{1,0:T(8,128)(2,1)}, u32[]{:S(2)}, u32[]{:S(2)}) collective-permute-start(bf16[192,768]{1,0:T(8,128)(2,1)} %get-tuple-element.154), channel_id=1, source_target_pairs={{0,4},{4,0},{8,12},{12,8},{16,20},{20,16},{24,28},{28,24},{1,5},{5... | collective-permute-start | bytes 884744 | tf_op jit(solution)/shard_map/ppermute | solution.py:39
  129.0 35.2 %collective-permute-start.25 = (bf16[192,768]{1,0:T(8,128)(2,1)}, bf16[192,768]{1,0:T(8,128)(2,1)S(1)}, u32[]{:S(2)}, u32[]{:S(2)}) collective-permute-start(bf16[192,768]{1,0:T(8,128)(2,1)} %get-tuple-element.167), channel_id=1, source_target_pairs={{0,16},{4,20},{8,24},{12,28},{16,0},{20,4},{24,8},{28,12},{1,17},{... | collective-permute-start | bytes 884744 | tf_op jit(solution)/shard_map/ppermute | solution.py:39
  139.5 32.4 %collective-permute-start.26 = (bf16[192,768]{1,0:T(8,128)(2,1)}, bf16[192,768]{1,0:T(8,128)(2,1)S(1)}, u32[]{:S(2)}, u32[]{:S(2)}) collective-permute-start(bf16[192,768]{1,0:T(8,128)(2,1)} %get-tuple-element.168), channel_id=1, source_target_pairs={{0,20},{4,16},{8,28},{12,24},{16,4},{20,0},{24,12},{28,8},{1,21},{... | collective-permute-start | bytes 884744 | tf_op jit(solution)/shard_map/ppermute | solution.py:39
  139.7 49.8 %collective-permute-start.29 = (bf16[192,768]{1,0:T(8,128)(2,1)}, bf16[192,768]{1,0:T(8,128)(2,1)S(1)}, u32[]{:S(2)}, u32[]{:S(2)}) collective-permute-start(bf16[192,768]{1,0:T(8,128)(2,1)} %get-tuple-element.173), channel_id=1, source_target_pairs={{0,24},{4,28},{8,16},{12,20},{16,8},{20,12},{24,0},{28,4},{1,25},{... | collective-permute-start | bytes 884744 | tf_op jit(solution)/shard_map/ppermute | solution.py:39
  141.7 47.7 %collective-permute-start.30 = (bf16[192,768]{1,0:T(8,128)(2,1)}, bf16[192,768]{1,0:T(8,128)(2,1)S(1)}, u32[]{:S(2)}, u32[]{:S(2)}) collective-permute-start(bf16[192,768]{1,0:T(8,128)(2,1)} %get-tuple-element.174), channel_id=1, source_target_pairs={{0,28},{4,24},{8,20},{12,16},{16,12},{20,8},{24,4},{28,0},{1,29},{... | collective-permute-start | bytes 884744 | tf_op jit(solution)/shard_map/ppermute | solution.py:39
  245.7 40.7 %collective-permute-start.35 = (bf16[192,768]{1,0:T(8,128)(2,1)S(1)}, bf16[192,768]{1,0:T(8,128)(2,1)S(1)}, u32[]{:S(2)}, u32[]{:S(2)}) collective-permute-start(bf16[192,768]{1,0:T(8,128)(2,1)S(1)} %get-tuple-element.186), channel_id=1, source_target_pairs={{0,12},{4,8},{8,4},{12,0},{16,28},{20,24},{24,20},{28,16},{1,13},{... | collective-permute-start | bytes 884744 | tf_op jit(solution)/shard_map/ppermute | solution.py:39
  247.9 39.5 %collective-permute-start.36 = (bf16[192,768]{1,0:T(8,128)(2,1)}, bf16[192,768]{1,0:T(8,128)(2,1)S(1)}, u32[]{:S(2)}, u32[]{:S(2)}) collective-permute-start(bf16[192,768]{1,0:T(8,128)(2,1)} %copy-done.46), channel_id=1, source_target_pairs={{0,16},{4,20},{8,24},{12,28},{16,0},{20,4},{24,8},{28,12},{1,17},{... | collective-permute-start | bytes 884744 | tf_op jit(solution)/shard_map/ppermute | solution.py:39
  250.0 37.5 %collective-permute-start.37 = (bf16[192,768]{1,0:T(8,128)(2,1)}, bf16[192,768]{1,0:T(8,128)(2,1)S(1)}, u32[]{:S(2)}, u32[]{:S(2)}) collective-permute-start(bf16[192,768]{1,0:T(8,128)(2,1)} %copy-done.44), channel_id=1, source_target_pairs={{0,20},{4,16},{8,28},{12,24},{16,4},{20,0},{24,12},{28,8},{1,21},{... | collective-permute-start | bytes 884744 | tf_op jit(solution)/shard_map/ppermute | solution.py:39
  251.7 35.8 %collective-permute-start.38 = (bf16[192,768]{1,0:T(8,128)(2,1)}, bf16[192,768]{1,0:T(8,128)(2,1)S(1)}, u32[]{:S(2)}, u32[]{:S(2)}) collective-permute-start(bf16[192,768]{1,0:T(8,128)(2,1)} %copy-done.49), channel_id=1, source_target_pairs={{0,24},{4,28},{8,16},{12,20},{16,8},{20,12},{24,0},{28,4},{1,25},{... | collective-permute-start | bytes 884744 | tf_op jit(solution)/shard_map/ppermute | solution.py:39
  253.1 34.4 %collective-permute-start.39 = (bf16[192,768]{1,0:T(8,128)(2,1)}, bf16[192,768]{1,0:T(8,128)(2,1)}, u32[]{:S(2)}, u32[]{:S(2)}) collective-permute-start(bf16[192,768]{1,0:T(8,128)(2,1)} %copy-done.48), channel_id=1, source_target_pairs={{0,28},{4,24},{8,20},{12,16},{16,12},{20,8},{24,4},{28,0},{1,29},{... | collective-permute-start | bytes 884744 | tf_op jit(solution)/shard_map/ppermute | solution.py:39
  286.4 81.6 %collective-permute-start.20 = (bf16[192,768]{1,0:T(8,128)(2,1)S(1)}, bf16[192,768]{1,0:T(8,128)(2,1)S(1)}, u32[]{:S(2)}, u32[]{:S(2)}) collective-permute-start(bf16[192,768]{1,0:T(8,128)(2,1)S(1)} %copy-done.41), channel_id=1, source_target_pairs={{0,4},{4,0},{8,12},{12,8},{16,20},{20,16},{24,28},{28,24},{1,5},{5... | collective-permute-start | bytes 884744 | tf_op jit(solution)/shard_map/ppermute | solution.py:39
  287.4 81.9 %collective-permute-start.23 = (bf16[192,768]{1,0:T(8,128)(2,1)S(1)}, bf16[192,768]{1,0:T(8,128)(2,1)S(1)}, u32[]{:S(2)}, u32[]{:S(2)}) collective-permute-start(bf16[192,768]{1,0:T(8,128)(2,1)S(1)} %copy-done.37), channel_id=1, source_target_pairs={{0,8},{4,12},{8,0},{12,4},{16,24},{20,28},{24,16},{28,20},{1,9},{5... | collective-permute-start | bytes 884744 | tf_op jit(solution)/shard_map/ppermute | solution.py:39
  314.6 59.0 %collective-permute-start.24 = (bf16[192,768]{1,0:T(8,128)(2,1)S(1)}, bf16[192,768]{1,0:T(8,128)(2,1)S(1)}, u32[]{:S(2)}, u32[]{:S(2)}) collective-permute-start(bf16[192,768]{1,0:T(8,128)(2,1)S(1)} %copy-done.25), channel_id=1, source_target_pairs={{0,12},{4,8},{8,4},{12,0},{16,28},{20,24},{24,20},{28,16},{1,13},{... | collective-permute-start | bytes 884744 | tf_op jit(solution)/shard_map/ppermute | solution.py:39
  325.0 49.7 %collective-permute-start.27 = (bf16[192,768]{1,0:T(8,128)(2,1)S(1)}, bf16[192,768]{1,0:T(8,128)(2,1)S(1)}, u32[]{:S(2)}, u32[]{:S(2)}) collective-permute-start(bf16[192,768]{1,0:T(8,128)(2,1)S(1)} %copy-done.31), channel_id=1, source_target_pairs={{0,16},{4,20},{8,24},{12,28},{16,0},{20,4},{24,8},{28,12},{1,17},{... | collective-permute-start | bytes 884744 | tf_op jit(solution)/shard_map/ppermute | solution.py:39
  325.8 49.0 %collective-permute-start.28 = (bf16[192,768]{1,0:T(8,128)(2,1)S(1)}, bf16[192,768]{1,0:T(8,128)(2,1)S(1)}, u32[]{:S(2)}, u32[]{:S(2)}) collective-permute-start(bf16[192,768]{1,0:T(8,128)(2,1)S(1)} %copy-done.27), channel_id=1, source_target_pairs={{0,20},{4,16},{8,28},{12,24},{16,4},{20,0},{24,12},{28,8},{1,21},{... | collective-permute-start | bytes 884744 | tf_op jit(solution)/shard_map/ppermute | solution.py:39
  374.7 100.4 %collective-permute-start.64 = (bf16[768,768]{1,0:T(8,128)(2,1)}, bf16[768,768]{1,0:T(8,128)(2,1)}, u32[]{:S(2)}, u32[]{:S(2)}) collective-permute-start(bf16[768,768]{1,0:T(8,128)(2,1)} %get-tuple-element.217), channel_id=1, source_target_pairs={{0,1},{1,0},{2,3},{3,2},{4,5},{5,4},{6,7},{7,6},{8,9},{9,8},{10,11... | collective-permute-start | bytes 3538952 | tf_op jit(solution)/shard_map/ppermute | solution.py:39
  374.8 44.4 %collective-permute-start.68 = (bf16[768,768]{1,0:T(8,128)(2,1)}, bf16[768,768]{1,0:T(8,128)(2,1)}, u32[]{:S(2)}, u32[]{:S(2)}) collective-permute-start(bf16[768,768]{1,0:T(8,128)(2,1)} %get-tuple-element.223), channel_id=1, source_target_pairs={{0,1},{1,0},{2,3},{3,2},{4,5},{5,4},{6,7},{7,6},{8,9},{9,8},{10,11... | collective-permute-start | bytes 3538952 | tf_op jit(solution)/shard_map/ppermute | solution.py:39
  395.8 156.0 %collective-permute-start.67 = (bf16[768,768]{1,0:T(8,128)(2,1)}, bf16[768,768]{1,0:T(8,128)(2,1)S(1)}, u32[]{:S(2)}, u32[]{:S(2)}) collective-permute-start(bf16[768,768]{1,0:T(8,128)(2,1)} %get-tuple-element.221), channel_id=1, source_target_pairs={{0,1},{1,0},{2,3},{3,2},{4,5},{5,4},{6,7},{7,6},{8,9},{9,8},{10,11... | collective-permute-start | bytes 3538952 | tf_op jit(solution)/shard_map/ppermute | solution.py:39
  399.4 47.5 %collective-permute-start.44 = (bf16[512,768]{1,0:T(8,128)(2,1)S(1)}, bf16[512,768]{1,0:T(8,128)(2,1)S(1)}, u32[]{:S(2)}, u32[]{:S(2)}) collective-permute-start(bf16[512,768]{1,0:T(8,128)(2,1)S(1)} %get-tuple-element.238), channel_id=1, source_target_pairs={{0,1},{1,0},{2,3},{3,2},{4,5},{5,4},{6,7},{7,6},{8,9},{9,8},{10,11... | collective-permute-start | bytes 2359304 | tf_op jit(solution)/shard_map/ppermute | solution.py:39
  425.8 35.5 %collective-permute-start.43 = (bf16[512,768]{1,0:T(8,128)(2,1)S(1)}, bf16[512,768]{1,0:T(8,128)(2,1)S(1)}, u32[]{:S(2)}, u32[]{:S(2)}) collective-permute-start(bf16[512,768]{1,0:T(8,128)(2,1)S(1)} %get-tuple-element.237), channel_id=1, source_target_pairs={{0,1},{1,0},{2,3},{3,2},{4,5},{5,4},{6,7},{7,6},{8,9},{9,8},{10,11... | collective-permute-start | bytes 2359304 | tf_op jit(solution)/shard_map/ppermute | solution.py:39
  472.6 79.1 %collective-permute-start.69 = (bf16[768,768]{1,0:T(8,128)(2,1)S(1)}, bf16[768,768]{1,0:T(8,128)(2,1)S(1)}, u32[]{:S(2)}, u32[]{:S(2)}) collective-permute-start(bf16[768,768]{1,0:T(8,128)(2,1)S(1)} %add_convert_fusion), channel_id=1, source_target_pairs={{0,2},{1,3},{2,0},{3,1},{4,6},{5,7},{6,4},{7,5},{8,10},{9,11},{10,... | collective-permute-start | bytes 3538952 | tf_op jit(solution)/shard_map/ppermute | solution.py:39
  474.8 76.7 %collective-permute-start.62 = (bf16[2,2,2,32,768]{4,3,2,1,0:T(8,128)(2,1)S(1)}, bf16[2,2,2,32,768]{4,3,2,1,0:T(8,128)(2,1)S(1)}, u32[]{:S(2)}, u32[]{:S(2)}) collective-permute-start(bf16[2,2,2,32,768]{4,3,2,1,0:T(8,128)(2,1)S(1)} %pad_maximum_fusion.7), channel_id=1, source_target_pairs={{0,2},{1,3},{2,0},{3,1},{4,6},{5,7},{6,4},{7,5},{8,10},{9,11},{10,... | collective-permute-start | bytes 1179656 | tf_op jit(solution)/shard_map/ppermute | solution.py:39
  475.1 71.3 %collective-permute-start.52 = (bf16[2,2,2,80,768]{4,3,2,1,0:T(8,128)(2,1)S(1)}, bf16[2,2,2,80,768]{4,3,2,1,0:T(8,128)(2,1)S(1)}, u32[]{:S(2)}, u32[]{:S(2)}) collective-permute-start(bf16[2,2,2,80,768]{4,3,2,1,0:T(8,128)(2,1)S(1)} %pad_maximum_fusion.4), channel_id=1, source_target_pairs={{0,2},{1,3},{2,0},{3,1},{4,6},{5,7},{6,4},{7,5},{8,10},{9,11},{10,... | collective-permute-start | bytes 2949128 | tf_op jit(solution)/shard_map/ppermute | solution.py:39
  (158 other events, 1856.3 us)

commit v2 on v1

v2 whole, which is shorter than its diff:
```python
import functools

import jax
import jax.numpy as jnp
from jax import lax
from jax.experimental import pallas as pl
from jax.experimental.pallas import tpu as pltpu
from jax.sharding import PartitionSpec as P

HEADS = 12
HEAD_DIM = 64

precise = lax.Precision.HIGHEST
norm_eps = 1e-06
beta_one = 0.9
beta_two = 0.999
learn_rate = 0.01
adam_eps = 1e-08
adam_steps = 10.0
masked_score = -1e30

bf16 = jnp.bfloat16
f32 = jnp.float32
MIB = 1 << 20
COST_SCALE = 0.25


def mm(left, right, contract=((1,), (0,)), precision=None):
    return lax.dot_general(
        left, right, (contract, ((), ())), preferred_element_type=f32, precision=precision
    )


NT = ((1,), (1,))
TN = ((0,), (0,))


def swap(value, axis, distance):
    count = lax.axis_size(axis)
    return lax.ppermute(value, axis, [(i, i ^ distance) for i in range(count)])


def iota(shape, dim):
    return lax.broadcasted_iota(jnp.int32, shape, dim)


def split_three(value):
    high = value.astype(bf16)
    rest = value - high.astype(f32)
    mid = rest.astype(bf16)
    low = (rest - mid.astype(f32)).astype(bf16)
    return high, mid, low


EXTRA = 8


def three_rows(row):
    high, mid, low = (piece.astype(f32) for piece in split_three(row))
    return jnp.concatenate([high, mid, low, jnp.zeros((EXTRA - 3, row.shape[1]), f32)], axis=0).astype(bf16)


def vmem_spec():
    return pl.BlockSpec(memory_space=pltpu.VMEM)


def smem_spec():
    return pl.BlockSpec(memory_space=pltpu.SMEM)


def params(mib):
    return pltpu.CompilerParams(vmem_limit_bytes=mib * MIB)


def cost(micros):
    micros = micros * COST_SCALE
    return pl.CostEstimate(
        flops=int(micros * 1.1e9), bytes_accessed=int(micros * 3e6), transcendentals=0
    )


def halves_of(capacity):
    first = (capacity // 2 + 15) // 16 * 16
    return ((0, first), (first, capacity - first))


def tables_kernel(routes_ref, dy_ref, hot_a, hot_b, *outs):
    picks, send_ref = outs[:4], outs[4]
    experts, capacity, _ = send_ref.shape
    count = routes_ref.shape[1]
    expert_row = iota((experts, count), 0)
    route_rows = [routes_ref[k : k + 1, :] for k in range(2)]
    hits = [expert_row == row for row in route_rows]
    hit = hits[0] | hits[1]
    hit_low = jnp.where(hit, 1.0, 0.0).astype(bf16)
    upper = jnp.where(iota((count, count), 0) < iota((count, count), 1), 1.0, 0.0).astype(bf16)
    slot = mm(hit_low, upper)
    slot = jnp.where(hit & (slot < capacity), slot, -1.0)
    index_rows = []
    for (start, size), hot in zip(halves_of(capacity), (hot_a, hot_b)):
        row_id = iota((size, count), 0).astype(f32) + float(start)
        for e in range(experts):
            hot[e * size : (e + 1) * size, :] = jnp.where(
                row_id == slot[e : e + 1, :], 1.0, 0.0
            ).astype(bf16)
        rows = mm(hot[...], dy_ref[...]).astype(bf16)
        for e in range(experts):
            send_ref[e, start : start + size, :] = rows[e * size : (e + 1) * size, :]
        for k in range(2):
            own_slot = jnp.sum(jnp.where(hits[k], slot, 0.0), axis=0, keepdims=True)
            inside = (own_slot >= start) & (own_slot < start + size)
            place = route_rows[k].astype(f32) * size + own_slot - start
            index_rows.append(jnp.where(inside, place, -1.0))
    index_cols = jnp.concatenate(index_rows * 2, axis=0).T
    for n, pick in enumerate(picks):
        lane = iota(pick.shape, 1).astype(f32)
        pick[...] = jnp.where(lane == index_cols[:, n : n + 1], 1.0, 0.0).astype(bf16)


def make_tables(routes_t, dy, experts, capacity):
    count, width = dy.shape
    sizes = [experts * size for _, size in halves_of(capacity)]
    shapes = [jax.ShapeDtypeStruct((size, count), bf16) for size in sizes]
    shapes += [jax.ShapeDtypeStruct((count, size), bf16) for size in sizes for _ in range(2)]
    shapes += [jax.ShapeDtypeStruct((experts, capacity, width), bf16)]
    results = pl.pallas_call(
        tables_kernel,
        out_shape=shapes,
        in_specs=[vmem_spec()] * 2,
        out_specs=[vmem_spec()] * len(shapes),
        compiler_params=params(60),
        name="slot_tables",
        cost_estimate=cost(5),
    )(routes_t, dy)
    return results[0:2], results[2:6], results[6]


def qkv_kernel(
    own_ref, x0, x1, x2, x3, gain_ref, w_ref, a_ref, qkv_ref, k_ref, v_ref, w_buf, x_buf, heads_ref
):
    step = pl.program_id(0)
    width, cols = heads_ref.shape
    third = cols // 3

    @pl.when(step == 0)
    def turn():
        for h in range(width // third):

            @pl.when(own_ref[0] == h)
            def pick(h=h):
                for t in range(3):
                    start = t * width + h * third
                    heads_ref[:, t * third : (t + 1) * third] = w_ref[:, start : start + third]

        w_buf[...] = heads_ref[...].T

    for j, block in enumerate((x0, x1, x2, x3)):

        @pl.when(step == j)
        def take(block=block):
            x_buf[...] = block[...].astype(f32)

    x = x_buf[...]
    scale = lax.rsqrt(jnp.mean(x * x, axis=1, keepdims=True) + norm_eps)
    a = (x * scale * gain_ref[...]).astype(bf16)
    a_ref[...] = a
    qkv_t = mm(w_buf[...], a, NT).astype(bf16)
    qkv_ref[0:third, :] = qkv_t[0:third, :] * jnp.asarray(0.125, bf16)
    qkv_ref[third:, :] = qkv_t[third:, :]
    both = mm(a, heads_ref[:, third:]).astype(bf16)
    k_ref[...] = both[:, :third]
    v_ref[...] = both[:, third:]


def project_qkv(own, blocks, gain, w_qkv):
    count, width = blocks[0].shape
    parts = len(blocks)
    cols = w_qkv.shape[1] // parts
    third = cols // 3

    def whole(shape):
        return pl.BlockSpec(shape, lambda g, own_ref: (0, 0), pipeline_mode=pl.Buffered(1))

    return pl.pallas_call(
        qkv_kernel,
        out_shape=[
            jax.ShapeDtypeStruct((parts * count, width), bf16),
            jax.ShapeDtypeStruct((cols, parts * count), bf16),
            jax.ShapeDtypeStruct((parts * count, third), bf16),
            jax.ShapeDtypeStruct((parts * count, third), bf16),
            jax.ShapeDtypeStruct((cols, width), bf16),
        ],
        grid_spec=pltpu.PrefetchScalarGridSpec(
            num_scalar_prefetch=1,
            grid=(parts,),
            in_specs=[whole((count, width))] * parts
            + [whole((1, width)), whole((width, parts * cols))],
            out_specs=[
                pl.BlockSpec((count, width), lambda g, own_ref: (own_ref[0] ^ g, 0)),
                pl.BlockSpec((cols, count), lambda g, own_ref: (0, own_ref[0] ^ g)),
                pl.BlockSpec((count, third), lambda g, own_ref: (own_ref[0] ^ g, 0)),
                pl.BlockSpec((count, third), lambda g, own_ref: (own_ref[0] ^ g, 0)),
                whole((cols, width)),
            ],
            scratch_shapes=[pltpu.VMEM((count, width), f32), pltpu.VMEM((width, cols), bf16)],
        ),
        compiler_params=params(60),
        name="norm_qkv",
        cost_estimate=cost(11),
    )(own, *blocks, gain, w_qkv)


EDGE = 256


def query_rows(info_ref, query_start, size):
    query_row = query_start + iota((1, size), 1)
    first_cut, last_cut, length = info_ref[0], info_ref[1], info_ref[2]
    start_row = jnp.where(
        query_row >= last_cut, last_cut, jnp.where(query_row >= first_cut, first_cut, 0)
    )
    last_row = jnp.minimum(query_row, length - 1)
    return query_row, start_row, last_row


def score_parts(info_ref, keys_ref, queries, block, number, row_len):
    query_start = number * block
    query_row, start_row, last_row = query_rows(info_ref, query_start, block)
    free_from = query_start if query_start + block > row_len - EDGE else min(EDGE, query_start)
    parts = []
    for first, last in ((0, free_from), (free_from, query_start), (query_start, query_start + block)):
        if first == last:
            continue
        scores = mm(keys_ref[first:last, :], queries)
        key_col = first + iota(scores.shape, 0)
        if first == query_start:
            valid = (key_col >= start_row) & (key_col <= last_row) | (key_col == query_row)
            scores = jnp.where(valid, scores, masked_score)
        elif last == free_from:
            scores = jnp.where(key_col >= start_row, scores, masked_score)
        parts.append((first, last, scores))
    return parts


def attend_kernel(block, info_ref, k_ref, q_ref, v_ref, o_ref, low_ref, log_ref, q_pad):
    head = pl.program_id(0)
    row_len = k_ref.shape[0]
    q_pad[...] = jnp.zeros_like(q_pad)
    q_pad[pl.ds(pl.multiple_of(head * HEAD_DIM, HEAD_DIM), HEAD_DIM), :] = q_ref[...]
    for i in range(row_len // block):
        cols = slice(i * block, (i + 1) * block)
        parts = score_parts(info_ref, k_ref, q_pad[:, cols], block, i, row_len)
        top = functools.reduce(
            jnp.maximum, [jnp.max(s, axis=0, keepdims=True) for _, _, s in parts]
        )
        total, out = 0.0, 0.0
        for first, last, s in parts:
            p = jnp.exp(s - top)
            total = total + jnp.sum(p, axis=0, keepdims=True)
            out = out + mm(v_ref[:, first:last], p.astype(bf16))
        out = out / total
        o_ref[:, cols] = out
        low_ref[:, cols] = out.astype(bf16)
        log_ref[0, :, cols] = top + jnp.log(total)


def attend(info, keys, qkv_t, block=512):
    row_len, group = keys.shape
    heads = group // HEAD_DIM
    tile = pl.BlockSpec((HEAD_DIM, row_len), lambda h: (h, 0))
    return pl.pallas_call(
        functools.partial(attend_kernel, block),
        out_shape=[
            jax.ShapeDtypeStruct((group, row_len), f32),
            jax.ShapeDtypeStruct((group, row_len), bf16),
            jax.ShapeDtypeStruct((heads, 1, row_len), f32),
        ],
        grid=(heads,),
        in_specs=[
            smem_spec(),
            pl.BlockSpec((row_len, group), lambda h: (0, 0)),
            tile,
            pl.BlockSpec((HEAD_DIM, row_len), lambda h: (2 * heads + h, 0)),
        ],
        out_specs=[tile, tile, pl.BlockSpec((1, 1, row_len), lambda h: (h, 0, 0))],
        scratch_shapes=[pltpu.VMEM((group, row_len), bf16)],
        compiler_params=params(60),
        name="attend",
        cost_estimate=cost(17),
    )(info, keys, qkv_t, qkv_t)


def attend_back_kernel(
    block, head, info_ref, own_ref, k_ref, v_ref, q_ref, kt_ref, g0, g1, g2, g3, o_ref, log_ref,
    a_ref, dqkv_ref, grad_ref, q_pad, g_pad, dk_acc, dv_acc,
):
    row_len = k_ref.shape[0]
    own_rows = slice(head * HEAD_DIM, (head + 1) * HEAD_DIM)
    dk_acc[...] = jnp.zeros_like(dk_acc)
    dv_acc[...] = jnp.zeros_like(dv_acc)
    q_pad[...] = jnp.zeros_like(q_pad)
    g_pad[...] = jnp.zeros_like(g_pad)
    q_pad[own_rows, :] = q_ref[...]
    for j, part in enumerate((g0, g1, g2, g3)):
        size = part.shape[1]
        g_pad[own_rows, pl.ds(pl.multiple_of((own_ref[0] ^ j) * size, size), size)] = part[...]
    for i in range(row_len // block):
        cols = slice(i * block, (i + 1) * block)
        q, g = q_ref[:, cols], g_pad[own_rows, cols]
        g_wide = g_pad[:, cols]
        delta = jnp.sum(g.astype(f32) * o_ref[:, cols], axis=0, keepdims=True)
        log_total = log_ref[0, :, cols]
        dq = 0.0
        for first, last, s in score_parts(info_ref, k_ref, q_pad[:, cols], block, i, row_len):
            p = jnp.exp(s - log_total)
            dp = mm(v_ref[first:last, :], g_wide)
            ds = (p * (dp - delta)).astype(bf16)
            dv_acc[:, first:last] += mm(g, p.astype(bf16), NT)
            dk_acc[:, first:last] += mm(q, ds, NT)
            dq = dq + mm(kt_ref[:, first:last], ds)
        dqkv_ref[0:HEAD_DIM, cols] = (0.125 * dq).astype(bf16)
    dqkv_ref[HEAD_DIM : 2 * HEAD_DIM, :] = dk_acc[...].astype(bf16)
    dqkv_ref[2 * HEAD_DIM :, :] = dv_acc[...].astype(bf16)
    grad = mm(dqkv_ref[...], a_ref[...])
    rows = grad_ref.shape[1]
    for e in range(grad_ref.shape[0]):
        grad_ref[e] = grad[e * rows : (e + 1) * rows, :].astype(bf16)


def attend_back(head, pieces, info, own, keys, values, qkv_t, grads, out, logs, a_one, block=256):
    row_len, group = keys.shape
    heads = group // HEAD_DIM
    width = a_one.shape[1]
    whole = pl.BlockSpec((row_len, group), lambda g: (0, 0))
    piece = pl.BlockSpec((HEAD_DIM, grads[0].shape[1]), lambda g: (head, 0))
    tile = pl.BlockSpec((HEAD_DIM, row_len), lambda g: (head, 0))
    return pl.pallas_call(
        functools.partial(attend_back_kernel, block, head),
        out_shape=[
            jax.ShapeDtypeStruct((3 * HEAD_DIM, row_len), bf16),
            jax.ShapeDtypeStruct((pieces, 3 * HEAD_DIM // pieces, width), bf16),
        ],
        grid=(1,),
        in_specs=[
            smem_spec(),
            smem_spec(),
            whole,
            whole,
            tile,
            pl.BlockSpec((HEAD_DIM, row_len), lambda g: (heads + head, 0)),
            piece,
            piece,
            piece,
            piece,
            tile,
            pl.BlockSpec((1, 1, row_len), lambda g: (head, 0, 0)),
            pl.BlockSpec((row_len, width), lambda g: (0, 0)),
        ],
        out_specs=[
            pl.BlockSpec((3 * HEAD_DIM, row_len), lambda g: (0, 0)),
            pl.BlockSpec((pieces, 3 * HEAD_DIM // pieces, width), lambda g: (0, 0, 0)),
        ],
        scratch_shapes=[
            pltpu.VMEM((group, row_len), bf16),
            pltpu.VMEM((group, row_len), bf16),
            pltpu.VMEM((HEAD_DIM, row_len), f32),
            pltpu.VMEM((HEAD_DIM, row_len), f32),
        ],
        compiler_params=params(60),
        name="attend_back",
        cost_estimate=cost(11),
    )(info, own, keys, values, qkv_t, qkv_t, *grads, out, logs, a_one)


def gates_of(normed, router, route_rows):
    logits = mm(router, normed, NT, precise)
    expert_row = iota(logits.shape, 0)
    picked = [
        jnp.sum(jnp.where(expert_row == row, logits, 0.0), axis=0, keepdims=True)
        for row in route_rows
    ]
    top = jnp.maximum(picked[0], picked[1])
    raw = [jnp.exp(p - top) for p in picked]
    return [r / (raw[0] + raw[1]) for r in raw]


def dispatch_kernel(
    own_ref, t0, t1, t2, t3, x_ref, w_ref, gain_ref, router_ref, routes_ref, hot_a, hot_b,
    residual_ref, gates_ref, send_a, send_b,
):
    residual = x_ref[...].astype(f32)
    group = t0.shape[0]
    for j, part in enumerate((t0, t1, t2, t3)):
        rows = pl.ds(pl.multiple_of((own_ref[0] ^ j) * group, group), group)
        residual = residual + mm(part[...], w_ref[rows, :], TN)
    residual_ref[...] = residual
    scale = lax.rsqrt(jnp.mean(residual * residual, axis=1, keepdims=True) + norm_eps)
    normed = residual * scale * gain_ref[...]
    a_two = normed.astype(bf16)
    route_rows = [routes_ref[k : k + 1, :] for k in range(2)]
    gates = gates_of(normed, router_ref[...], route_rows)
    gates_ref[0:1, :] = gates[0]
    gates_ref[1:2, :] = gates[1]
    experts = router_ref.shape[0]
    expert_row = iota((experts, x_ref.shape[0]), 0)
    table = jnp.where(expert_row == route_rows[0], gates[0], 0.0) + jnp.where(
        expert_row == route_rows[1], gates[1], 0.0
    )
    stacked = jnp.concatenate([piece.astype(f32) for piece in split_three(table)], axis=0)
    stacked = stacked.astype(bf16)
    for hot, send in ((hot_a, send_a), (hot_b, send_b)):
        size = send.shape[1] - EXTRA
        rows = mm(hot[...], a_two).astype(bf16)
        for e in range(experts):
            own_rows = slice(e * size, (e + 1) * size)
            send[e, 0:size, :] = rows[own_rows, :]
            picked = mm(stacked, hot[own_rows, :], NT)
            three = [picked[k * experts + e : k * experts + e + 1, :] for k in range(3)]
            three = jnp.concatenate(three + [jnp.zeros((EXTRA - 3, size), f32)], axis=0)
            send[e, size:, :] = jnp.zeros((EXTRA, send.shape[2]), bf16)
            send[e, size:, 0:size] = three.astype(bf16)


def make_dispatch(own, parts, x, w_out, gain, router_t, routes_t, hots):
    count, width = x.shape
    experts = router_t.shape[0]
    shapes = [
        jax.ShapeDtypeStruct((count, width), f32),
        jax.ShapeDtypeStruct((2, count), f32),
    ]
    shapes += [
        jax.ShapeDtypeStruct((experts, hot.shape[0] // experts + EXTRA, width), bf16) for hot in hots
    ]
    return pl.pallas_call(
        dispatch_kernel,
        out_shape=shapes,
        in_specs=[smem_spec()] + [vmem_spec()] * 11,
        out_specs=[vmem_spec()] * len(shapes),
        compiler_params=params(60),
        name="project_dispatch",
        cost_estimate=cost(9),
    )(own, *parts, x, w_out, gain, router_t, routes_t, *hots)


def column_of(row):
    return jnp.broadcast_to(row, (128, row.shape[1])).T[:, 0:1]


def row_of(column):
    return jnp.broadcast_to(column, (column.shape[0], 128)).T[0:1, :]


GELU_SCALE = 0.7978845608028654
GELU_CUBE = 0.044715


def expert_kernel(start, x_ref, dy_ref, *refs):
    weights, refs = refs[:8], refs[8:]
    out_ref, slot_ref, act_ref, dpre_ref = refs[:4]
    x_buf, dy_buf, up_buf, down_buf, out_acc, slot_acc, sems = refs[4:]
    sources, size, width = out_ref.shape
    step = pl.program_id(0)
    parts = len(weights) // 2

    def copies(j):
        return (
            pltpu.make_async_copy(weights[2 * j], up_buf.at[j % 2], sems.at[0, j % 2]),
            pltpu.make_async_copy(weights[2 * j + 1], down_buf.at[j % 2], sems.at[1, j % 2]),
        )

    @pl.when(step == 0)
    def first():
        for copy in copies(0):
            copy.start()
        for n in range(sources):
            x_buf[n * size : (n + 1) * size, :] = x_ref[n, 0:size, :]
            dy_buf[n * size : (n + 1) * size, :] = dy_ref[n, start : start + size, :]
        out_acc[...] = jnp.zeros_like(out_acc)
        slot_acc[...] = jnp.zeros_like(slot_acc)

    for j in range(parts):

        @pl.when(step == j)
        def arrive(j=j):
            if j + 1 < parts:
                for copy in copies(j + 1):
                    copy.start()
            for copy in copies(j):
                copy.wait()

    which = lax.rem(step, 2)
    block = x_buf.shape[0] // 2

    @pl.loop(0, 2)
    def rows_of(r):
        rows = pl.ds(pl.multiple_of(r * block, block), block)
        up, down = up_buf[which], down_buf[which]
        pre = mm(x_buf[rows, :], up)
        square = pre * pre
        tanh = jnp.tanh(GELU_SCALE * (pre * (1.0 + GELU_CUBE * square)))
        half = 0.5 * (1.0 + tanh)
        act = (pre * half).astype(bf16)
        act_ref[0, rows, :] = act
        out_acc[rows, :] += mm(act, down)
        slope = half + (0.5 * GELU_SCALE) * pre * (1.0 - tanh * tanh) * (
            1.0 + (3.0 * GELU_CUBE) * square
        )
        dpre = (mm(dy_buf[rows, :], down, NT) * slope).astype(bf16)
        dpre_ref[0, rows, :] = dpre
        slot_acc[rows, :] += mm(dpre, up, NT)

    @pl.when(step == parts - 1)
    def last():
        for n in range(sources):
            rows = slice(n * size, (n + 1) * size)
            out = out_acc[rows, :].astype(bf16)
            out_ref[n] = out
            slot_ref[n, 0:size, :] = slot_acc[rows, :].astype(bf16)
            dgate = jnp.sum(
                dy_buf[rows, :].astype(f32) * out.astype(f32), axis=1, keepdims=True
            )
            slot_ref[n, size:, :] = jnp.zeros((EXTRA, width), bf16)
            slot_ref[n, size:, 0:size] = three_rows(row_of(dgate))


def run_experts(start, x, dy, weights):
    sources, size, width = x.shape
    size -= EXTRA
    rows = sources * size
    units = weights[0].shape[1]
    parts = len(weights) // 2

    def whole(shape):
        return pl.BlockSpec(shape, lambda g: (0,) * len(shape), pipeline_mode=pl.Buffered(1))

    kept = jax.ShapeDtypeStruct((parts, rows, units), bf16)
    kept_spec = pl.BlockSpec((1, rows, units), lambda g: (g, 0, 0))
    piece = (sources, size, width)
    return pl.pallas_call(
        functools.partial(expert_kernel, start),
        out_shape=[
            jax.ShapeDtypeStruct(piece, bf16), jax.ShapeDtypeStruct(x.shape, bf16), kept, kept
        ],
        grid=(parts,),
        in_specs=[whole(x.shape), whole(dy.shape)]
        + [pl.BlockSpec(memory_space=pl.ANY)] * (2 * parts),
        out_specs=[whole(piece), whole(x.shape), kept_spec, kept_spec],
        scratch_shapes=[
            pltpu.VMEM((rows, width), bf16),
            pltpu.VMEM((rows, width), bf16),
            pltpu.VMEM((2, width, units), bf16),
            pltpu.VMEM((2, units, width), bf16),
            pltpu.VMEM((rows, width), f32),
            pltpu.VMEM((rows, width), f32),
            pltpu.SemaphoreType.DMA((2, 2)),
        ],
        compiler_params=params(60),
        name="experts",
        cost_estimate=cost(27),
    )(x, dy, *weights)


def weight_kernel(dy_ref, x_a, x_b, act_a, act_b, dpre_a, dpre_b, own_out, near_out, far_out, x_turn, dy_turn, gate_buf):
    step = pl.program_id(0)
    experts, capacity, _ = dy_ref.shape

    @pl.when(step == 0)
    def turn():
        begin = 0
        for (start, size), x_ref in zip(halves_of(capacity), (x_a, x_b)):
            cols = slice(begin, begin + experts * size)
            for n in range(experts):
                three = x_ref[n, size:, 0:size].astype(f32)
                gate_buf[0:1, begin : begin + size] = three[0:1] + three[1:2] + three[2:3]
                begin += size
            gate = gate_buf[0:1, cols]
            shape = (experts * size, x_ref.shape[2])
            rows = x_ref[:, 0:size, :].reshape(shape).astype(f32)
            x_turn[:, cols] = (rows.T * gate).astype(bf16)
            rows = dy_ref[:, start : start + size, :].reshape(shape).astype(f32)
            dy_turn[:, cols] = (rows.T * gate).astype(bf16)

    cut = act_a.shape[1]
    up = mm(x_turn[:, :cut], dpre_a[0]) + mm(x_turn[:, cut:], dpre_b[0])
    down = (mm(dy_turn[:, :cut], act_a[0]) + mm(dy_turn[:, cut:], act_b[0])).T
    for j, (out, n) in enumerate(((own_out, 0), (near_out, 0), (far_out, 0), (near_out, 2))):

        @pl.when(step == j)
        def keep(out=out, n=n):
            out[n] = up.astype(out.dtype)
            out[n + 1] = down.astype(out.dtype)


def weight_grads(xs, dy, acts, dpres):
    experts, capacity, width = dy.shape
    parts, _, units = acts[0].shape
    assert units == width

    def whole(*shape):
        return pl.BlockSpec(shape, lambda g: (0,) * len(shape), pipeline_mode=pl.Buffered(1))

    kept = [pl.BlockSpec((1,) + a.shape[1:], lambda g: (g, 0, 0)) for a in (*acts, *dpres)]
    return pl.pallas_call(
        weight_kernel,
        out_shape=[
            jax.ShapeDtypeStruct((2, width, units), f32),
            jax.ShapeDtypeStruct((4, width, units), bf16),
            jax.ShapeDtypeStruct((2, width, units), f32),
        ],
        grid=(parts,),
        in_specs=[whole(*dy.shape)] + [whole(*x.shape) for x in xs] + kept,
        out_specs=[whole(2, width, units), whole(4, width, units), whole(2, width, units)],
        scratch_shapes=[pltpu.VMEM((width, experts * capacity), bf16)] * 2
        + [pltpu.VMEM((8, experts * capacity), f32)],
        compiler_params=params(60),
        name="expert_weight_grads",
        cost_estimate=cost(30),
    )(dy, *xs, *acts, *dpres)


def combine_back_kernel(
    own_ref, hot_a, hot_b, p0a, p1a, p0b, p1b, residual_ref, dy_ref, gates_ref, routes_ref,
    router_ref, gain_ref, w_ref, t0, t1, t2, t3, slot_a, slot_b,
    dres_ref, datt_ref, gout_ref, small_ref, buf_a, buf_b,
):
    experts = router_ref.shape[0]
    table = [0.0] * experts
    for slot, hot, buf in ((slot_a, hot_a, buf_a), (slot_b, hot_b, buf_b)):
        size = slot.shape[1] - EXTRA
        for e in range(experts):
            rows = slice(e * size, (e + 1) * size)
            buf[rows, :] = slot[e, 0:size, :]
            picked = mm(slot[e, size:, 0:size], hot[rows, :])
            table[e] = table[e] + (picked[0:1] + picked[1:2] + picked[2:3])
    table = jnp.concatenate(table, axis=0)
    residual = residual_ref[...]
    count = residual.shape[0]
    scale = lax.rsqrt(jnp.mean(residual * residual, axis=1, keepdims=True) + norm_eps)
    unit = residual * scale
    gain = gain_ref[...]
    expert_row = iota((experts, count), 0)
    routes = [routes_ref[k : k + 1, :] for k in range(2)]
    gates = [gates_ref[k : k + 1, :] for k in range(2)]
    dgates = [
        jnp.sum(jnp.where(expert_row == r, table, 0.0), axis=0, keepdims=True) for r in routes
    ]
    mean = gates[0] * dgates[0] + gates[1] * dgates[1]
    dlogit = sum(
        jnp.where(expert_row == r, g * (d - mean), 0.0) for r, g, d in zip(routes, gates, dgates)
    )
    small_ref[...] = jnp.zeros_like(small_ref)
    small_ref[0:experts, :] = mm(dlogit, unit * gain, precision=precise)
    dnormed = mm(dlogit, router_ref[...], TN, precise)
    for gate, pick_a, pick_b in ((gates[0], p0a, p0b), (gates[1], p1a, p1b)):
        rows = mm(pick_a[...], buf_a[...]) + mm(pick_b[...], buf_b[...])
        dnormed = dnormed + column_of(gate) * rows
    small_ref[experts : experts + 1, :] = jnp.sum(dnormed * unit, axis=0, keepdims=True)
    scaled = dnormed * gain
    dres = dy_ref[...].astype(f32) + scale * (
        scaled - unit * jnp.mean(scaled * unit, axis=1, keepdims=True)
    )
    dres_ref[...] = dres
    branch = dres.astype(bf16)
    datt_ref[...] = mm(w_ref[...], branch, NT).astype(bf16)
    group = t0.shape[0]
    for j, part in enumerate((t0, t1, t2, t3)):
        rows = pl.ds(pl.multiple_of((own_ref[0] ^ j) * group, group), group)
        gout_ref[rows, :] = mm(part[...], branch)


def combine_back(own, slots, hots, picks, residual, dy, gates, routes_t, router_t, gain, w_out, parts):
    count, width = residual.shape
    experts = router_t.shape[0]
    shapes = [
        jax.ShapeDtypeStruct((count, width), f32),
        jax.ShapeDtypeStruct((width, count), bf16),
        jax.ShapeDtypeStruct((width, width), f32),
        jax.ShapeDtypeStruct((experts + 8, width), f32),
    ]
    return pl.pallas_call(
        combine_back_kernel,
        out_shape=shapes,
        in_specs=[smem_spec()] + [vmem_spec()] * 19,
        out_specs=[vmem_spec()] * len(shapes),
        scratch_shapes=[pltpu.VMEM((hot.shape[0], width), bf16) for hot in hots],
        compiler_params=params(60),
        name="combine_back",
        cost_estimate=cost(13),
    )(own, *hots, *picks, residual, dy, gates, routes_t, router_t, gain, w_out, *parts, *slots)


def combine_kernel(p0a, p1a, p0b, p1b, residual_ref, gates_ref, out_a, out_b, y_ref, buf_a, buf_b):
    for out, buf in ((out_a, buf_a), (out_b, buf_b)):
        size = out.shape[1]
        for e in range(out.shape[0]):
            buf[e * size : (e + 1) * size, :] = out[e]
    total = residual_ref[...]
    for k, (pick_a, pick_b) in enumerate(((p0a, p0b), (p1a, p1b))):
        rows = mm(pick_a[...], buf_a[...]) + mm(pick_b[...], buf_b[...])
        total = total + column_of(gates_ref[k : k + 1, :]) * rows
    y_ref[...] = total.astype(bf16)


def combine(outs, picks, residual, gates):
    width = residual.shape[1]
    return pl.pallas_call(
        combine_kernel,
        out_shape=jax.ShapeDtypeStruct(residual.shape, bf16),
        in_specs=[vmem_spec()] * 8,
        out_specs=vmem_spec(),
        scratch_shapes=[pltpu.VMEM((out.shape[0] * out.shape[1], width), bf16) for out in outs],
        compiler_params=params(60),
        name="combine",
        cost_estimate=cost(6),
    )(*picks, residual, gates, *outs)


def spread_kernel(places_ref, d0, d1, d2, w_ref, near_out, last_out, far_out, own_out, d_buf):
    step = pl.program_id(0)
    heads = d_buf.shape[0] // (3 * HEAD_DIM)
    for c, part in enumerate((d0, d1, d2)):
        for t in range(3):
            start = (t * heads + c) * HEAD_DIM
            d_buf[start : start + HEAD_DIM, :] = part[t * HEAD_DIM : (t + 1) * HEAD_DIM, :]
    dn = mm(d_buf[...], w_ref[...], TN)
    for n, out in enumerate((near_out, last_out, far_out, own_out)):

        @pl.when(step == n)
        def keep(out=out):
            out[...] = dn.astype(out.dtype)


def spread(places, parts, w_t):
    rows, row_len = parts[0].shape
    cols, width = w_t.shape
    steps = places.shape[0]
    count = row_len // steps
    tile = pl.BlockSpec((rows, count), lambda g, places: (0, places[g]))

    def whole(shape):
        return pl.BlockSpec(shape, lambda g, places: (0, 0), pipeline_mode=pl.Buffered(1))

    return pl.pallas_call(
        spread_kernel,
        out_shape=[jax.ShapeDtypeStruct((count, width), t) for t in (bf16, bf16, f32, f32)],
        grid_spec=pltpu.PrefetchScalarGridSpec(
            num_scalar_prefetch=1,
            grid=(steps,),
            in_specs=[tile] * 3 + [whole((cols, width))],
            out_specs=[whole((count, width))] * 4,
            scratch_shapes=[pltpu.VMEM((cols, count), bf16)],
        ),
        compiler_params=params(40),
        name="spread_back",
        cost_estimate=cost(8),
    )(places, *parts, w_t)


def fold_kernel(special, taken, moved_ref, *refs):
    given, out_ref = refs[:-1], refs[-1]
    exps, rows, width = out_ref.shape
    sums = moved_ref[0, 0:taken].astype(f32)
    for e in range(1, exps):
        sums = sums + moved_ref[e, 0:taken].astype(f32)
    if special:
        body = taken - 2 * special
        high, mid, _ = split_three(
            sums[body : body + special] + sums[body + special : body + 2 * special]
        )
        sums = jnp.concatenate([sums[:body], high.astype(f32), mid.astype(f32)], axis=0)
    start = given[0].shape[1] if given else 0
    pad = rows - start - taken
    if pad:
        sums = jnp.concatenate([sums, jnp.zeros((pad, width), f32)], axis=0)
    sums = sums.astype(bf16)
    for e in range(exps):
        if given:
            out_ref[e, 0:start] = given[0][e]
        out_ref[e, start:] = sums


def fold(moved, taken, special, given=()):
    exps, _, width = moved.shape
    rows = taken + sum(g.shape[1] for g in given)
    return pl.pallas_call(
        functools.partial(fold_kernel, special, taken),
        out_shape=jax.ShapeDtypeStruct((exps, rows + -rows % 8, width), bf16),
        in_specs=[vmem_spec()] * (1 + len(given)),
        out_specs=vmem_spec(),
        compiler_params=params(40),
        name="fold_sums",
        cost_estimate=cost(2),
    )(moved, *given)


def lay_out_kernel(rows, own_ref, *refs):
    arrays, (w_ref, gain_ref, grad_ref, ggain_ref, b0, b1, b2, sems) = refs[:12], refs[12:]
    hids, exps = b0.shape[0], b0.shape[1]
    bufs = (b0, b1, b2)
    step = pl.program_id(0)
    block = grad_ref.shape[0]

    @pl.when(step == 0)
    def fetch():
        copies = [
            pltpu.make_async_copy(arrays[4 * c + j], bufs[c].at[own_ref[0] ^ j], sems.at[c, j])
            for c in range(3)
            for j in range(hids)
        ]
        for copy in copies:
            copy.start()
        for copy in copies:
            copy.wait()

    cols = pl.ds(pl.multiple_of(step * block, block), block)
    blocks = {}
    for h in range(hids):
        for c, buf in enumerate(bufs):
            pieces = [buf[h, e, 0:rows, cols].astype(f32) for e in range(exps)]
            blocks[h, c] = jnp.concatenate(pieces, axis=0)
    stacked = [
        blocks[h, c][t * HEAD_DIM : (t + 1) * HEAD_DIM]
        for t in range(3)
        for h in range(hids)
        for c in range(3)
    ]
    grad = jnp.concatenate(stacked, axis=0).T
    grad_ref[...] = grad
    total = jnp.sum(grad * w_ref[...].astype(f32), axis=1, keepdims=True)
    ggain_ref[...] = row_of(total) / gain_ref[...]


def lay_out(own, chunks, rows, w_qkv, gain, block=128):
    width, cols = w_qkv.shape
    arrays = [a for chunk in chunks for a in chunk]
    tile = pl.BlockSpec((block, cols), lambda g: (g, 0))
    row = pl.BlockSpec((1, block), lambda g: (0, g))
    return pl.pallas_call(
        functools.partial(lay_out_kernel, rows),
        out_shape=[
            jax.ShapeDtypeStruct((width, cols), f32),
            jax.ShapeDtypeStruct((1, width), f32),
        ],
        grid=(width // block,),
        in_specs=[smem_spec()] + [pl.BlockSpec(memory_space=pl.ANY)] * 12 + [tile, row],
        out_specs=[tile, row],
        scratch_shapes=[pltpu.VMEM((4,) + chunk[0].shape, bf16) for chunk in chunks]
        + [pltpu.SemaphoreType.DMA((3, 4))],
        compiler_params=params(50),
        name="lay_out_qkv",
        cost_estimate=cost(10),
    )(own, *arrays, w_qkv, gain)


def lay_out_rest_kernel(start, own_ref, *refs):
    arrays, (out_ref, buf, sems) = refs[:4], refs[4:]
    hids, exps = buf.shape[0], buf.shape[1]
    rows = out_ref.shape[0] // (hids * exps)
    copies = [
        pltpu.make_async_copy(arrays[j], buf.at[own_ref[0] ^ j], sems.at[j]) for j in range(hids)
    ]
    for copy in copies:
        copy.start()
    for copy in copies:
        copy.wait()
    for h in range(hids):
        for e in range(exps):
            n = h * exps + e
            out_ref[n * rows : (n + 1) * rows, :] = buf[h, e, start : start + rows].astype(f32)


def lay_out_rest(own, arrays, start, width):
    return pl.pallas_call(
        functools.partial(lay_out_rest_kernel, start),
        out_shape=jax.ShapeDtypeStruct((width, width), f32),
        in_specs=[smem_spec()] + [pl.BlockSpec(memory_space=pl.ANY)] * 4,
        out_specs=vmem_spec(),
        scratch_shapes=[pltpu.VMEM((4,) + arrays[0].shape, bf16), pltpu.SemaphoreType.DMA((4,))],
        compiler_params=params(50),
        name="lay_out_w_out",
        cost_estimate=cost(3),
    )(own, *arrays)


def adam_update(weight, gradient, first_moment, second_moment, live_mask):
    first_next = beta_one * first_moment + (1.0 - beta_one) * gradient
    second_next = beta_two * second_moment + (1.0 - beta_two) * gradient * gradient
    first_hat = first_next / (1.0 - beta_one**adam_steps)
    second_hat = second_next / (1.0 - beta_two**adam_steps)
    weight_next = weight - learn_rate * first_hat / (jnp.sqrt(second_hat) + adam_eps)
    return (
        jnp.where(live_mask, weight_next, weight),
        jnp.where(live_mask, first_next, first_moment),
        jnp.where(live_mask, second_next, second_moment),
    )


def tie(value, other):
    return lax.optimization_barrier((value, other))[0]


def exchange(value, axis):
    return lax.all_to_all(value, axis, split_axis=0, concat_axis=0, tiled=True)


def split_sum(value, axis, distance):
    pairs = value.reshape((value.shape[0] // 2, 2) + value.shape[1:])
    low = (lax.axis_index(axis) & distance) == 0
    keep = jnp.where(low, pairs[:, 0], pairs[:, 1])
    give = jnp.where(low, pairs[:, 1], pairs[:, 0]).astype(bf16)
    return keep + swap(give, axis, distance).astype(f32)


def halves(value):
    high = lax.reduce_precision(value, 8, 7)
    return high.astype(bf16), (value - high).astype(bf16)


def pad_rows(value):
    return jnp.pad(value, ((0, 0), (0, -value.shape[1] % 8), (0, 0)))


def gather_hid(value):
    far = swap(value, "hid", 2)
    near = swap(value, "hid", 1)
    return value, near, far, swap(far, "hid", 1)


def body(
    tokens, cotangent, routes, segments, lengths, gain_attn, gain_moe, w_qkv, w_out, router_w,
    router_first, router_second, up_w, down_w, up_first, up_second, down_first, down_second,
):
    exp_count = lax.axis_size("exp")
    hid_count = lax.axis_size("hid")
    hid = lax.axis_index("hid")
    exp_index = lax.axis_index("exp")
    own = jnp.stack([hid, exp_index]).astype(jnp.int32)
    x_own = tokens[0]
    dy = cotangent[0]
    count, width = x_own.shape
    experts = router_w.shape[1]
    frozen_count = experts // 2
    capacity = max(2, 3 * count // experts)
    group = width // hid_count
    heads = group // HEAD_DIM
    is_new = exp_index >= frozen_count

    x_far = swap(x_own, "hid", 2)
    x_near = swap(x_own, "hid", 1)
    routes_t = routes[0].T
    hots, picks, dy_send = make_tables(routes_t, dy, experts, capacity)
    seg_row = segments[0]
    info = jnp.stack(
        [
            jnp.sum((seg_row < 1).astype(jnp.int32)),
            jnp.sum((seg_row < 2).astype(jnp.int32)),
            lengths[0],
        ]
    )
    up_low = up_w[0].astype(bf16)
    down_low = down_w[0].astype(bf16)
    router_t = router_w.T
    x_far, (info, dy_send, up_low, down_low, router_t, routes_t) = lax.optimization_barrier(
        (x_far, (info, dy_send, up_low, down_low, router_t, routes_t))
    )
    x_last = swap(x_far, "hid", 1)
    blocks = (x_own, x_near, x_far, x_last)
    dy_all = exchange(dy_send, "exp")

    up_far = swap(up_low, "hid", 2)
    up_near, down_near = swap(up_low, "hid", 1), swap(down_low, "hid", 1)

    a_one, qkv_t, keys, values, w_t = project_qkv(own, blocks, gain_attn[None], w_qkv)
    out_heads, out_low, logs = attend(info, keys, qkv_t)
    out_low, (up_far, up_near, down_near) = lax.optimization_barrier(
        (out_low, (up_far, up_near, down_near))
    )

    def piece_of(value, j):
        return lax.dynamic_slice_in_dim(value, (hid ^ j) * count, count, 1)

    att_parts = [piece_of(out_low, 0)] + [
        swap(piece_of(out_low, j), "hid", j) for j in range(1, hid_count)
    ]
    att_parts, down_low = lax.optimization_barrier((att_parts, down_low))
    down_far = swap(down_low, "hid", 2)

    residual, gates, *sends = make_dispatch(
        own, att_parts, x_own, w_out, gain_moe[None], router_t, routes_t, hots
    )
    up_far, down_far = tie((up_far, down_far), residual)
    up_last, down_last = swap(up_far, "hid", 1), swap(down_far, "hid", 1)
    weights = (up_low, down_low, up_near, down_near, up_far, down_far, up_last, down_last)
    sends = tie(sends, dy_all)
    x_rows = [exchange(send, "exp") for send in sends]

    starts = [start for start, _ in halves_of(capacity)]
    results = [run_experts(start, x, dy_all, weights) for start, x in zip(starts, x_rows)]
    outs, slots, acts, dpres = zip(*results)
    slot_back = [exchange(slot, "exp") for slot in slots]

    own_part, near_part, far_part = weight_grads(x_rows, dy_all, acts, dpres)
    slot_back, near_part = lax.optimization_barrier((slot_back, near_part))
    near_part = swap(near_part, "hid", 1)

    dres, datt, gout, small = combine_back(
        own, slot_back, hots, picks, residual, dy, gates, routes_t, router_t,
        gain_moe[None], w_out, att_parts,
    )

    datt, near_part = lax.optimization_barrier((datt, near_part))

    def heads_of(value, j):
        return lax.dynamic_slice_in_dim(value, (hid ^ j) * group, group, 0)

    datt_parts = [heads_of(datt, 0)] + [
        swap(heads_of(datt, j), "hid", j) for j in range(1, hid_count)
    ]

    gout, small = tie((gout, small), datt_parts)

    gout = gout.reshape(hid_count, width // hid_count, width)
    for d in (1, 2):
        gout = split_sum(gout, "hid", d)
        small = small + swap(small, "hid", d)
    far_part, gout, small = lax.optimization_barrier((far_part, gout, small))
    far_part = swap((far_part + near_part[2:].astype(f32)).astype(bf16), "hid", 2)
    out_rows = width // (hid_count * exp_count)
    small_rows = -(-(experts + 1) // exp_count)
    missing = max(0, exp_count * small_rows - small.shape[0])
    small = jnp.pad(small, ((0, missing), (0, 0)))[: exp_count * small_rows]
    small = small.reshape(exp_count, small_rows, width)
    gout = gout.reshape(exp_count, out_rows, width).astype(bf16)

    rows = 3 * HEAD_DIM // exp_count
    chunks, dqkv = [], []
    for h in range(heads):
        if h == 1:
            out_first = exchange(tie(outs[0], slot_back), "exp")
            chunks[0] = jnp.concatenate([chunks[0], gout, *halves(small)], axis=1)
            chunks[0], out_first = lax.optimization_barrier((chunks[0], out_first))
            first = exchange(pad_rows(chunks[0]), "exp")
        if h == 2:
            datt_parts, first = lax.optimization_barrier((datt_parts, first))
        dqkv_h, grad_h = attend_back(
            h, exp_count, info, own, keys, values, qkv_t, datt_parts, out_heads, logs, a_one
        )
        dqkv.append(dqkv_h)
        chunks.append(grad_h)
    places = jnp.stack([hid ^ j for j in (1, 3, 2, 0)]).astype(jnp.int32)
    near_dn, last_dn, far_dn, own_dn = spread(places, dqkv, w_t)
    near_dn, last_dn = swap(near_dn, "hid", 1), swap(last_dn, "hid", 1)
    far_dn = swap((far_dn + last_dn.astype(f32)).astype(bf16), "hid", 2)
    dnormed = own_dn + near_dn.astype(f32) + far_dn.astype(f32)
    x = x_own.astype(f32)
    scale = lax.rsqrt(jnp.mean(x * x, axis=-1, keepdims=True) + norm_eps)
    unit = x * scale
    scaled = dnormed * gain_attn
    grad_tokens = (
        dres + scale * (scaled - unit * jnp.mean(scaled * unit, axis=-1, keepdims=True))
    ).astype(bf16)

    first_rows = rows + out_rows + 2 * small_rows
    second = exchange(fold(first, first_rows, small_rows, [chunks[1]]), "exp")
    third = exchange(fold(second, rows, 0, [chunks[2]]), "exp")
    fourth = exchange(fold(third, rows, 0), "exp")
    out_second = exchange(tie(outs[1], fourth), "exp")
    out_tokens = combine((out_first, out_second), picks, residual, gates)
    gathered = [
        gather_hid(value)
        for value in (second[:, rows : 2 * rows + out_rows], third[:, rows : 2 * rows], fourth)
    ]
    grad_qkv, grad_gain_attn = lay_out(own, gathered, rows, w_qkv, gain_attn[None])
    grad_out_proj = lay_out_rest(own, gathered[0], rows, width)
    start = 2 * rows + out_rows
    small = second[:, start : start + small_rows].astype(f32)
    small = small + second[:, start + small_rows : start + 2 * small_rows].astype(f32)
    small = small.reshape(exp_count * small_rows, width)
    far_part = [far_part[0], tie(far_part[1], fourth)]
    grad_up, grad_down = (
        jnp.where(is_new, own_part[n] + near_part[n].astype(f32) + far_part[n].astype(f32), 0.0)
        for n in range(2)
    )
    grad_gain_attn = grad_gain_attn[0]
    grad_gain_moe = small[experts]
    live_columns = (jnp.arange(experts, dtype=jnp.int32) >= frozen_count)[None, :]
    grad_router = jnp.where(live_columns, small[:experts].T, 0.0)
    router_new, router_first_next, router_second_next = adam_update(
        router_w[:, frozen_count:], grad_router[:, frozen_count:], router_first, router_second, True
    )
    router_next = jnp.concatenate([router_w[:, :frozen_count], router_new], axis=1)
    up_next, up_first_next, up_second_next = adam_update(
        up_w[0], grad_up, up_first[0], up_second[0], is_new
    )
    down_next, down_first_next, down_second_next = adam_update(
        down_w[0], grad_down, down_first[0], down_second[0], is_new
    )
    return (
        out_tokens[None],
        grad_tokens[None],
        grad_qkv,
        grad_out_proj,
        grad_gain_attn,
        grad_gain_moe,
        grad_router,
        router_next,
        router_first_next,
        router_second_next,
        grad_up[None],
        grad_down[None],
        up_next[None],
        down_next[None],
        up_first_next[None],
        up_second_next[None],
        down_first_next[None],
        down_second_next[None],
    )


def solution(mesh):
    tok = P("exp", "hid", None)
    up = P("exp", None, "hid")
    return jax.shard_map(
        body,
        mesh=mesh,
        in_specs=(tok, tok, tok, P("exp", None), P("exp")) + (P(),) * 7
        + (up, tok, up, up, tok, tok),
        out_specs=(tok, tok) + (P(),) * 8 + (up, tok, up, tok, up, up, tok, tok),
        check_vma=False,
    )
```

time: 574 us -> 431 us (0.75)
  waiting for transfers between devices: 175 us -> 74.8 us
  local copies, waits for them, and re-layouts: 47.6 us -> 20 us
  starting transfers between devices: 112 us -> 90.1 us
  other arithmetic: 36.1 us -> 47.6 us
  matrix products: 6.8 us -> 0 us
    ppermute x70 -> x33, waiting for transfers between devices: 172 us -> 32.2 us  [swap(): return lax.ppermute(value, axis, [(i, i ^ distance) for i in range(count)])]
    ppermute x70 -> x33, starting transfers between devices: 105 us -> 32.7 us  [swap(): return lax.ppermute(value, axis, [(i, i ^ distance) for i in range(count)])]
    all_to_all x2 -> x11, starting transfers between devices: 6.67 us -> 57.3 us  [exchange(): return lax.all_to_all(value, axis, split_axis=0, concat_axis=0, tiled=True)]
    all_to_all x2 -> x11, waiting for transfers between devices: 2.89 us -> 42.6 us  [exchange(): return lax.all_to_all(value, axis, split_axis=0, concat_axis=0, tiled=True)]
    unnamed x240 -> x84, local copies, waits for them, and re-layouts: 41.4 us -> 9.78 us
    select_n x0 -> x2, other arithmetic: none -> 13.2 us  [the longest x1 7.63 us: adam_update(): jnp.where(live_mask, first_next, first_moment)]
    broadcast_in_dim x2 -> x0, other arithmetic: 7.49 us -> none  [the longest x1 3.86 us: body(): up_first_next[None]]
    dot_general x2 -> x0, matrix products: 6.8 us -> none  [mm(): lax.dot_general(left, right, (contract, ((), ())), preferred_element_type...]
  transfers between devices with their start and end apart: 72 -> 44, of which waited for: 25 -> 16; matrix products, arithmetic and copies ran while one was open for 8% -> 13% of each run, Pallas kernels for 29% -> 44%
where the time goes in v2:
time: 431 us; the launch traced here: 427 us
  Pallas kernels  192 us (45%)
  starting transfers between devices  90.1 us (21%)
  waiting for transfers between devices  74.8 us (17%)
  other arithmetic  47.6 us (11%)
  local copies, waits for them, and re-layouts  20 us (5%)
    all_to_all x11, starting transfers between devices, exchange(): return lax.all_to_all(value, axis, split_axis=0, concat_axis=0, tiled=True)  57.3 us
    pallas_call x2, Pallas kernels, run_experts(): pl.pallas_call(functools.partial(expert_kernel, start), out_shape=[jax.Sh...  49.4 us
    all_to_all x11, waiting for transfers between devices, exchange(): return lax.all_to_all(value, axis, split_axis=0, concat_axis=0, tiled=True)  42.6 us
    pallas_call x3, Pallas kernels, attend_back(): pl.pallas_call(functools.partial(attend_back_kernel, block, head), out_sh...  33.8 us
    ppermute x33, starting transfers between devices, swap(): return lax.ppermute(value, axis, [(i, i ^ distance) for i in range(count)])  32.7 us
    ppermute x33, waiting for transfers between devices, swap(): return lax.ppermute(value, axis, [(i, i ^ distance) for i in range(count)])  32.2 us
    pallas_call x1, Pallas kernels, weight_grads(): pl.pallas_call(weight_kernel, out_shape=[jax.ShapeDtypeStruct((2, width,...  28.1 us
    pallas_call x1, Pallas kernels, attend(): pl.pallas_call(functools.partial(attend_kernel, block), out_shape=[jax.Sh...  17.1 us
  transfers between devices with their start and end apart: 44, of which 16 were waited for; matrix products, arithmetic and copies ran while one was open for 13% of the time, Pallas kernels for 44%

profile of v2, /device:TPU:1, one launch (start us, length us, event | category | flops | bytes accessed | tf_op | source)
XLA Modules:
  0.0 427.2 jit_solution(15773843966573469434)
XLA Ops:
  6.6 5.3 %slot_tables.1 = (bf16[768,512]{1,0:T(8,128)(2,1)}, bf16[768,512]{1,0:T(8,128)(2,1)}, bf16[512,768]{1,0:T(8,128)(2,1)}, bf16[512,768]{1,0:T(8,128)(2,1)}, bf16[5...) custom-call(s32[2,512]{1,0:T(2,128)} %bitcast.105, bf16[512,768]{1,0:T(8,128)(2,1)} %bitcast.103), custom_call_target="tpu_custom_call" | custom-call | flops 1375000064 | bytes 3750000 | tf_op jit(solution)/shard_map/slot_tables/pallas_call | solution.py:126
  15.2 5.0 %collective-permute-done.x2 = bf16[512,768]{1,0:T(8,128)(2,1)S(1)} collective-permute-done((bf16[512,768]{1,0:T(8,128)(2,1)}, bf16[512,768]{1,0:T(8,128)(2,1)S(1)}, u32[]{:S(2)}, u32[]{:S(2)}) %collective-permute-start) | collective-permute-done | bytes 786464 | tf_op jit(solution)/shard_map/ppermute | solution.py:40
  21.1 5.7 %all-to-all-start = ((bf16[8,192,768]{2,1,0:T(8,128)(2,1)}), bf16[8,192,768]{2,1,0:T(8,128)(2,1)S(1)}, u32[]{:S(2)}, u32[]{:S(2)}) async-start(bf16[8,192,768]{2,1,0:T(8,128)(2,1)} %get-tuple-element.130), calls=%async_computation | async-start | bytes 4718592 | tf_op jit(solution)/shard_map/all_to_all | solution.py:903
  32.1 11.2 %norm_qkv.1 = (bf16[2048,768]{1,0:T(8,128)(2,1)}, bf16[576,2048]{1,0:T(8,128)(2,1)}, bf16[2048,192]{1,0:T(8,128)(2,1)}, bf16[2048,192]{1,0:T(8,128)(2,1)}, bf16[576,768]{1,0:T(8,128)(2,1)}) custom-call(s32[2]{0:T(128)} %pad_add_fusion.own_ref, bf16[512,768]{1,0:T(8,128)(2,1)} %bitcast.94, bf16[512,768]{1,0:T(8,128)(2,1)} %collective-permute-done.1.x1, ...), custom_call_target="tpu_custom_call" | custom-call | flops 3024999936 | bytes 8250000 | tf_op jit(solution)/shard_map/norm_qkv/pallas_call | solution.py:184
  43.3 17.1 %attend.1 = (f32[192,2048]{1,0:T(8,128)}, bf16[192,2048]{1,0:T(8,128)(2,1)}, f32[3,1,2048]{2,1,0:T(1,128)}) custom-call(s32[3]{0:T(128)} %pad_add_fusion.1.info_ref, bf16[2048,192]{1,0:T(8,128)(2,1)} %get-tuple-element.111.k_ref, bf16[576,2048]{1,0:T(8,128)(2,1)} %get-tuple-element.112.q_ref.v_ref.kt_ref, bf16[576,2048]{1,0:T(8,128)(2,1)} %get-tuple-element.112.q_ref.v_ref.kt_ref), custom_call_target="tpu_custom_call" | custom-call | flops 4674999808 | bytes 12750000 | tf_op jit(solution)/shard_map/attend/pallas_call | solution.py:271
  69.1 4.5 %collective-permute-done.8.t3 = bf16[192,512]{1,0:T(8,128)(2,1)S(1)} collective-permute-done((bf16[192,512]{1,0:T(8,128)(2,1)S(1)}, bf16[192,512]{1,0:T(8,128)(2,1)S(1)}, u32[]{:S(2)}, u32[]{:S(2)}) %collective-permute-start.8) | collective-permute-done | bytes 196640 | tf_op jit(solution)/shard_map/ppermute | solution.py:40
  74.3 8.0 %project_dispatch.1 = (f32[512,768]{1,0:T(8,128)}, f32[2,512]{1,0:T(2,128)}, bf16[8,104,768]{2,1,0:T(8,128)(2,1)}, bf16[8,104,768]{2,1,0:T(8,128)(2,1)}) custom-call(s32[2]{0:T(128)} %pad_add_fusion.own_ref, bf16[192,512]{1,0:T(8,128)(2,1)} %get-tuple-element.117.t0, bf16[192,512]{1,0:T(8,128)(2,1)} %copy-done.39, bf16[192,512]{1,0:T(8,128)(2,1)} %copy-done.40, ...), custom_call_target="tpu_custom_call" | custom-call | flops 2475000064 | bytes 6750000 | tf_op jit(solution)/shard_map/project_dispatch/pallas_call | solution.py:434
  82.3 6.0 %all-to-all-start.1 = ((bf16[8,104,768]{2,1,0:T(8,128)(2,1)}), bf16[8,104,768]{2,1,0:T(8,128)(2,1)}, u32[]{:S(2)}, u32[]{:S(2)}) async-start(bf16[8,104,768]{2,1,0:T(8,128)(2,1)} %get-tuple-element.131), calls=%async_computation.1 | async-start | bytes 2555904 | tf_op jit(solution)/shard_map/all_to_all | solution.py:903
  89.5 29.7 %all-to-all-done.1.x_ref.x_a = bf16[8,104,768]{2,1,0:T(8,128)(2,1)} async-done(((bf16[8,104,768]{2,1,0:T(8,128)(2,1)}), bf16[8,104,768]{2,1,0:T(8,128)(2,1)}, u32[]{:S(2)}, u32[]{:S(2)}) %all-to-all-start.1) | async-done | bytes 1277984 | tf_op jit(solution)/shard_map/all_to_all | solution.py:903
  119.2 4.7 %all-to-all-start.3 = ((bf16[8,104,768]{2,1,0:T(8,128)(2,1)}), bf16[8,104,768]{2,1,0:T(8,128)(2,1)}, u32[]{:S(2)}, u32[]{:S(2)}) async-start(bf16[8,104,768]{2,1,0:T(8,128)(2,1)} %get-tuple-element.139), calls=%async_computation.3 | async-start | bytes 2555904 | tf_op jit(solution)/shard_map/all_to_all | solution.py:903
  130.3 24.7 %experts.2 = (bf16[8,96,768]{2,1,0:T(8,128)(2,1)}, bf16[8,104,768]{2,1,0:T(8,128)(2,1)}, bf16[4,768,768]{2,1,0:T(8,128)(2,1)}, bf16[4,768,768]{2,1,0:T(8,128)(2,1)}) custom-call(bf16[8,104,768]{2,1,0:T(8,128)(2,1)} %all-to-all-done.1.x_ref.x_a, bf16[8,192,768]{2,1,0:T(8,128)(2,1)} %copy-done.21, bf16[768,768]{1,0:T(8,128)(2,1)} %get-tuple-element.114.refs_0_, ...), custom_call_target="tpu_custom_call" | custom-call | flops 7424999936 | bytes 20250000 | tf_op jit(solution)/shard_map/experts/pallas_call | solution.py:539
  155.0 5.6 %all-to-all-start.2 = ((bf16[8,104,768]{2,1,0:T(8,128)(2,1)}), bf16[8,104,768]{2,1,0:T(8,128)(2,1)S(1)}, u32[]{:S(2)}, u32[]{:S(2)}) async-start(bf16[8,104,768]{2,1,0:T(8,128)(2,1)} %get-tuple-element.138), calls=%async_computation.2 | async-start | bytes 2555904 | tf_op jit(solution)/shard_map/all_to_all | solution.py:903
  160.5 24.7 %experts.3 = (bf16[8,96,768]{2,1,0:T(8,128)(2,1)}, bf16[8,104,768]{2,1,0:T(8,128)(2,1)}, bf16[4,768,768]{2,1,0:T(8,128)(2,1)}, bf16[4,768,768]{2,1,0:T(8,128)(2,1)}) custom-call(bf16[8,104,768]{2,1,0:T(8,128)(2,1)} %all-to-all-done.3.x_ref.x_b, bf16[8,192,768]{2,1,0:T(8,128)(2,1)} %copy-done.21, bf16[768,768]{1,0:T(8,128)(2,1)} %get-tuple-element.114.refs_0_, ...), custom_call_target="tpu_custom_call" | custom-call | flops 7424999936 | bytes 20250000 | tf_op jit(solution)/shard_map/experts/pallas_call | solution.py:539
  185.3 5.4 %all-to-all-done.2.slot_a = bf16[8,104,768]{2,1,0:T(8,128)(2,1)S(1)} async-done(((bf16[8,104,768]{2,1,0:T(8,128)(2,1)}), bf16[8,104,768]{2,1,0:T(8,128)(2,1)S(1)}, u32[]{:S(2)}, u32[]{:S(2)}) %all-to-all-start.2) | async-done | bytes 1277984 | tf_op jit(solution)/shard_map/all_to_all | solution.py:903
  195.0 28.1 %expert_weight_grads.1 = (f32[2,768,768]{2,1,0:T(8,128)}, bf16[4,768,768]{2,1,0:T(8,128)(2,1)}, f32[2,768,768]{2,1,0:T(8,128)}) custom-call(bf16[8,192,768]{2,1,0:T(8,128)(2,1)} %copy-done.21, bf16[8,104,768]{2,1,0:T(8,128)(2,1)} %all-to-all-done.1.x_ref.x_a, bf16[8,104,768]{2,1,0:T(8,128)(2,1)} %all-to-all-done.3.x_ref.x_b, ...), custom_call_target="tpu_custom_call" | custom-call | flops 8249999872 | bytes 22500000 | tf_op jit(solution)/shard_map/expert_weight_grads/pallas_call | solution.py:603
  226.7 12.7 %combine_back.1 = (f32[512,768]{1,0:T(8,128)}, bf16[768,512]{1,0:T(8,128)(2,1)}, f32[768,768]{1,0:T(8,128)}, f32[16,768]{1,0:T(8,128)}) custom-call(s32[2]{0:T(128)} %pad_add_fusion.own_ref, bf16[768,512]{1,0:T(8,128)(2,1)} %get-tuple-element.123.hot_a, bf16[768,512]{1,0:T(8,128)(2,1)} %get-tuple-element.124.hot_b, bf16[512,768]{1,0:T(8,128)(2,1)} %get-tuple-element.104.p0a, ...), custom_call_target="tpu_custom_call" | custom-call | flops 3575000064 | bytes 9750000 | tf_op jit(solution)/shard_map/combine_back/pallas_call | solution.py:680
  249.1 4.7 %collective-permute-done.15.g3 = bf16[192,512]{1,0:T(8,128)(2,1)S(1)} collective-permute-done((bf16[192,512]{1,0:T(8,128)(2,1)S(1)}, bf16[192,512]{1,0:T(8,128)(2,1)S(1)}, u32[]{:S(2)}, u32[]{:S(2)}) %collective-permute-start.15) | collective-permute-done | bytes 196640 | tf_op jit(solution)/shard_map/ppermute | solution.py:40
  259.1 11.2 %attend_back.3 = (bf16[192,2048]{1,0:T(8,128)(2,1)}, bf16[8,24,768]{2,1,0:T(8,128)(2,1)}) custom-call(s32[3]{0:T(128)} %pad_add_fusion.1.info_ref, s32[2]{0:T(128)} %pad_add_fusion.own_ref, bf16[2048,192]{1,0:T(8,128)(2,1)} %get-tuple-element.111.k_ref, bf16[2048,192]{1,0:T(8,128)(2,1)} %get-tuple-element.127.v_ref, ...), custom_call_target="tpu_custom_call" | custom-call | flops 3024999936 | bytes 8250000 | tf_op jit(solution)/shard_map/attend_back/pallas_call | solution.py:337
  271.6 5.5 %all-to-all-done.5.out_a = bf16[8,96,768]{2,1,0:T(8,128)(2,1)} async-done(((bf16[8,96,768]{2,1,0:T(8,128)(2,1)}), bf16[8,96,768]{2,1,0:T(8,128)(2,1)}, u32[]{:S(2)}, u32[]{:S(2)}) %all-to-all-start.5) | async-done | bytes 1179680 | tf_op jit(solution)/shard_map/all_to_all | solution.py:903
  282.2 5.0 %add_convert_fusion = bf16[2,768,768]{2,1,0:T(8,128)(2,1)} fusion(f32[2,768,768]{2,1,0:T(8,128)} %get-tuple-element.188, bf16[4,768,768]{2,1,0:T(8,128)(2,1)} %collective-permute-done.12), kind=kLoop, calls=%fused_computation | loop fusion | flops 3538944 | bytes 9437184 | tf_op jit(solution)/shard_map/convert_element_type | solution.py:1027
  288.5 11.2 %attend_back.4 = (bf16[192,2048]{1,0:T(8,128)(2,1)}, bf16[8,24,768]{2,1,0:T(8,128)(2,1)}) custom-call(s32[3]{0:T(128)} %pad_add_fusion.1.info_ref, s32[2]{0:T(128)} %pad_add_fusion.own_ref, bf16[2048,192]{1,0:T(8,128)(2,1)} %get-tuple-element.111.k_ref, bf16[2048,192]{1,0:T(8,128)(2,1)} %get-tuple-element.127.v_ref, ...), custom_call_target="tpu_custom_call" | custom-call | flops 3024999936 | bytes 8250000 | tf_op jit(solution)/shard_map/attend_back/pallas_call | solution.py:337
  301.7 5.7 %all-to-all-start.7 = ((bf16[8,80,768]{2,1,0:T(8,128)(2,1)}), bf16[8,80,768]{2,1,0:T(8,128)(2,1)S(1)}, u32[]{:S(2)}, u32[]{:S(2)}) async-start(bf16[8,80,768]{2,1,0:T(8,128)(2,1)} %fold_sums.3), calls=%async_computation.7 | async-start | bytes 1966080 | tf_op jit(solution)/shard_map/all_to_all | solution.py:903
  307.5 11.3 %attend_back.5 = (bf16[192,2048]{1,0:T(8,128)(2,1)}, bf16[8,24,768]{2,1,0:T(8,128)(2,1)}) custom-call(s32[3]{0:T(128)} %pad_add_fusion.1.info_ref, s32[2]{0:T(128)} %pad_add_fusion.own_ref, bf16[2048,192]{1,0:T(8,128)(2,1)} %get-tuple-element.111.k_ref, bf16[2048,192]{1,0:T(8,128)(2,1)} %get-tuple-element.127.v_ref, ...), custom_call_target="tpu_custom_call" | custom-call | flops 3024999936 | bytes 8250000 | tf_op jit(solution)/shard_map/attend_back/pallas_call | solution.py:337
  322.2 5.4 %spread_back.1 = (bf16[512,768]{1,0:T(8,128)(2,1)S(1)}, bf16[512,768]{1,0:T(8,128)(2,1)}, f32[512,768]{1,0:T(8,128)S(1)}, f32[512,768]{1,0:T(8,128)S(1)}) custom-call(s32[4]{0:T(128)S(1)} %pad_add_fusion.2.places_ref, bf16[192,2048]{1,0:T(8,128)(2,1)S(1)} %copy-done.5, bf16[192,2048]{1,0:T(8,128)(2,1)S(1)} %copy-done.7, bf16[192,2048]{1,0:T(8,128)(2,1)S(1)} %copy-done.8, ...), custom_call_target="tpu_custom_call" | custom-call | flops 2200000000 | bytes 6000000 | tf_op jit(solution)/shard_map/spread_back/pallas_call | solution.py:743
  339.6 5.5 %fusion.10 = (f32[1,768,768]{2,1,0:T(8,128)}, f32[1,768,768]{2,1,0:T(8,128)}) fusion(f32[1,768,768]{2,1,0:T(8,128)S(1)} %copy-done.14, pred[]{:T(512)S(6)} %ge.11, bf16[2,768,768]{2,1,0:T(8,128)(2,1)} %collective-permute-done.32, bf16[4,768,768]{2,1,0:T(8,128)(2,1)} %collective-permute-done.12, f32[2,768,768]{2,1,0:T(8,128)} %get-tuple-element.186), kind=kLoop, calls=%fused_computation.25 | loop fusion | flops 5898240 | bytes 11796481 | tf_op jit(solution)/shard_map/jit(_where)/select_n | solution.py:894
  346.0 5.5 %all-to-all-start.8 = ((bf16[8,48,768]{2,1,0:T(8,128)(2,1)}), bf16[8,48,768]{2,1,0:T(8,128)(2,1)}, u32[]{:S(2)}, u32[]{:S(2)}) async-start(bf16[8,48,768]{2,1,0:T(8,128)(2,1)} %fold_sums.4), calls=%async_computation.8 | async-start | bytes 1179648 | tf_op jit(solution)/shard_map/all_to_all | solution.py:903
  351.4 7.6 %fusion.7 = (f32[1,768,768]{2,1,0:T(8,128)}, f32[1,768,768]{2,1,0:T(8,128)}) fusion(f32[1,768,768]{2,1,0:T(8,128)} %param.32, f32[1,768,768]{2,1,0:T(8,128)} %get-tuple-element.195, pred[]{:T(512)S(6)} %ge.11, f32[1,768,768]{2,1,0:T(8,128)} %param.30, f32[1,768,768]{2,1,0:T(8,128)} %param.33), kind=kLoop, calls=%fused_computation.22 | loop fusion | flops 8257536 | bytes 14155777 | tf_op jit(solution)/shard_map/jit(_where)/select_n | solution.py:893
  366.6 5.4 %all-to-all-start.9 = ((bf16[8,24,768]{2,1,0:T(8,128)(2,1)}), bf16[8,24,768]{2,1,0:T(8,128)(2,1)S(1)}, u32[]{:S(2)}, u32[]{:S(2)}) async-start(bf16[8,24,768]{2,1,0:T(8,128)(2,1)} %copy-done.2), calls=%async_computation.9 | async-start | bytes 589824 | tf_op jit(solution)/shard_map/all_to_all | solution.py:903
  375.6 4.7 %collective-permute-start.23 = (bf16[8,48,768]{2,1,0:T(8,128)(2,1)S(1)}, bf16[8,48,768]{2,1,0:T(8,128)(2,1)S(1)}, u32[]{:S(2)}, u32[]{:S(2)}) collective-permute-start(bf16[8,48,768]{2,1,0:T(8,128)(2,1)S(1)} %slice.92.refs_0_), channel_id=1, source_target_pairs={{0,1},{1,0},{2,3},{3,2},{4,5},{5,4},{6,7},{7,6},{8,9},{9,8},{10,11... | collective-permute-start | bytes 1769480 | tf_op jit(solution)/shard_map/ppermute | solution.py:40
  380.5 5.7 %all-to-all-start.10 = ((bf16[8,96,768]{2,1,0:T(8,128)(2,1)}), bf16[8,96,768]{2,1,0:T(8,128)(2,1)}, u32[]{:S(2)}, u32[]{:S(2)}) async-start(bf16[8,96,768]{2,1,0:T(8,128)(2,1)} %get-tuple-element.174), calls=%async_computation.10 | async-start | bytes 2359296 | tf_op jit(solution)/shard_map/all_to_all | solution.py:903
  411.2 8.3 %lay_out_qkv.1 = (f32[768,2304]{1,0:T(8,128)}, f32[1,768]{1,0:T(1,128)S(1)}) custom-call(s32[2]{0:T(128)S(1)} %copy-done.3, bf16[8,48,768]{2,1,0:T(8,128)(2,1)S(1)} %slice.92.refs_0_, bf16[8,48,768]{2,1,0:T(8,128)(2,1)S(1)} %collective-permute-done.23.refs_1_, bf16[8,48,768]{2,1,0:T(8,128)(2,1)} %collective-permute-done.24.refs_2_, ...), custom_call_target="tpu_custom_call" | custom-call | flops 2750000128 | bytes 7500000 | tf_op jit(solution)/shard_map/lay_out_qkv/pallas_call | solution.py:838
  420.2 6.5 %combine.1 = bf16[512,768]{1,0:T(8,128)(2,1)} custom-call(bf16[512,768]{1,0:T(8,128)(2,1)} %get-tuple-element.104.p0a, bf16[512,768]{1,0:T(8,128)(2,1)} %get-tuple-element.105.p1a, bf16[512,768]{1,0:T(8,128)(2,1)} %get-tuple-element.106.p0b, bf16[512,768]{1,0:T(8,128)(2,1)} %get-tuple-element.107.p1b, f32[512,768]{1,0:T(8,128)} %get-tuple-element.125.residual_ref, ...), custom_call_target="tpu_custom_call" | custom-call | flops 1650000000 | bytes 4500000 | tf_op jit(solution)/shard_map/combine/pallas_call | solution.py:706
  (201 shorter events, 116.8 us)
Async XLA Ops:
  0.7 19.6 %collective-permute-start = (bf16[512,768]{1,0:T(8,128)(2,1)}, bf16[512,768]{1,0:T(8,128)(2,1)S(1)}, u32[]{:S(2)}, u32[]{:S(2)}) collective-permute-start(bf16[512,768]{1,0:T(8,128)(2,1)} %bitcast.93), channel_id=1, source_target_pairs={{0,2},{1,3},{2,0},{3,1},{4,6},{5,7},{6,4},{7,5},{8,10},{9,11},{10,... | collective-permute-start | bytes 2359304 | tf_op jit(solution)/shard_map/ppermute | solution.py:40
  21.1 61.2 %all-to-all-start = ((bf16[8,192,768]{2,1,0:T(8,128)(2,1)}), bf16[8,192,768]{2,1,0:T(8,128)(2,1)S(1)}, u32[]{:S(2)}, u32[]{:S(2)}) async-start(bf16[8,192,768]{2,1,0:T(8,128)(2,1)} %get-tuple-element.130), calls=%async_computation | async-start | bytes 4718592 | tf_op jit(solution)/shard_map/all_to_all | solution.py:903
  28.8 31.6 %collective-permute-start.3 = (bf16[768,768]{1,0:T(8,128)(2,1)}, bf16[768,768]{1,0:T(8,128)(2,1)}, u32[]{:S(2)}, u32[]{:S(2)}) collective-permute-start(bf16[768,768]{1,0:T(8,128)(2,1)} %get-tuple-element.114.refs_0_), channel_id=1, source_target_pairs={{0,2},{1,3},{2,0},{3,1},{4,6},{5,7},{6,4},{7,5},{8,10},{9,11},{10,... | collective-permute-start | bytes 3538952 | tf_op jit(solution)/shard_map/ppermute | solution.py:40
  30.1 30.4 %collective-permute-start.4 = (bf16[768,768]{1,0:T(8,128)(2,1)}, bf16[768,768]{1,0:T(8,128)(2,1)}, u32[]{:S(2)}, u32[]{:S(2)}) collective-permute-start(bf16[768,768]{1,0:T(8,128)(2,1)} %get-tuple-element.114.refs_0_), channel_id=1, source_target_pairs={{0,1},{1,0},{2,3},{3,2},{4,5},{5,4},{6,7},{7,6},{8,9},{9,8},{10,11... | collective-permute-start | bytes 3538952 | tf_op jit(solution)/shard_map/ppermute | solution.py:40
  30.8 29.7 %collective-permute-start.5 = (bf16[768,768]{1,0:T(8,128)(2,1)}, bf16[768,768]{1,0:T(8,128)(2,1)}, u32[]{:S(2)}, u32[]{:S(2)}) collective-permute-start(bf16[768,768]{1,0:T(8,128)(2,1)} %get-tuple-element.132.refs_1_), channel_id=1, source_target_pairs={{0,1},{1,0},{2,3},{3,2},{4,5},{5,4},{6,7},{7,6},{8,9},{9,8},{10,11... | collective-permute-start | bytes 3538952 | tf_op jit(solution)/shard_map/ppermute | solution.py:40
  63.9 9.7 %collective-permute-start.8 = (bf16[192,512]{1,0:T(8,128)(2,1)S(1)}, bf16[192,512]{1,0:T(8,128)(2,1)S(1)}, u32[]{:S(2)}, u32[]{:S(2)}) collective-permute-start(bf16[192,512]{1,0:T(8,128)(2,1)S(1)} %get-tuple-element.207), channel_id=1, source_target_pairs={{0,3},{1,2},{2,1},{3,0},{4,7},{5,6},{6,5},{7,4},{8,11},{9,10},{10,... | collective-permute-start | bytes 589832 | tf_op jit(solution)/shard_map/ppermute | solution.py:40
  82.3 36.9 %all-to-all-start.1 = ((bf16[8,104,768]{2,1,0:T(8,128)(2,1)}), bf16[8,104,768]{2,1,0:T(8,128)(2,1)}, u32[]{:S(2)}, u32[]{:S(2)}) async-start(bf16[8,104,768]{2,1,0:T(8,128)(2,1)} %get-tuple-element.131), calls=%async_computation.1 | async-start | bytes 2555904 | tf_op jit(solution)/shard_map/all_to_all | solution.py:903
  88.3 35.6 %collective-permute-start.9 = (bf16[768,768]{1,0:T(8,128)(2,1)}, bf16[768,768]{1,0:T(8,128)(2,1)}, u32[]{:S(2)}, u32[]{:S(2)}) collective-permute-start(bf16[768,768]{1,0:T(8,128)(2,1)} %get-tuple-element.132.refs_1_), channel_id=1, source_target_pairs={{0,2},{1,3},{2,0},{3,1},{4,6},{5,7},{6,4},{7,5},{8,10},{9,11},{10,... | collective-permute-start | bytes 3538952 | tf_op jit(solution)/shard_map/ppermute | solution.py:40
  119.2 35.8 %all-to-all-start.3 = ((bf16[8,104,768]{2,1,0:T(8,128)(2,1)}), bf16[8,104,768]{2,1,0:T(8,128)(2,1)}, u32[]{:S(2)}, u32[]{:S(2)}) async-start(bf16[8,104,768]{2,1,0:T(8,128)(2,1)} %get-tuple-element.139), calls=%async_computation.3 | async-start | bytes 2555904 | tf_op jit(solution)/shard_map/all_to_all | solution.py:903
  155.0 35.7 %all-to-all-start.2 = ((bf16[8,104,768]{2,1,0:T(8,128)(2,1)}), bf16[8,104,768]{2,1,0:T(8,128)(2,1)S(1)}, u32[]{:S(2)}, u32[]{:S(2)}) async-start(bf16[8,104,768]{2,1,0:T(8,128)(2,1)} %get-tuple-element.138), calls=%async_computation.2 | async-start | bytes 2555904 | tf_op jit(solution)/shard_map/all_to_all | solution.py:903
  190.7 34.4 %all-to-all-start.4 = ((bf16[8,104,768]{2,1,0:T(8,128)(2,1)}), bf16[8,104,768]{2,1,0:T(8,128)(2,1)S(1)}, u32[]{:S(2)}, u32[]{:S(2)}) async-start(bf16[8,104,768]{2,1,0:T(8,128)(2,1)} %get-tuple-element.140), calls=%async_computation.4 | async-start | bytes 2555904 | tf_op jit(solution)/shard_map/all_to_all | solution.py:903
  225.1 14.3 %collective-permute-start.12 = (bf16[4,768,768]{2,1,0:T(8,128)(2,1)}, bf16[4,768,768]{2,1,0:T(8,128)(2,1)}, u32[]{:S(2)}, u32[]{:S(2)}) collective-permute-start(bf16[4,768,768]{2,1,0:T(8,128)(2,1)} %get-tuple-element.149), channel_id=1, source_target_pairs={{0,1},{1,0},{2,3},{3,2},{4,5},{5,4},{6,7},{7,6},{8,9},{9,8},{10,11... | collective-permute-start | bytes 14155784 | tf_op jit(solution)/shard_map/ppermute | solution.py:40
  243.8 10.0 %collective-permute-start.15 = (bf16[192,512]{1,0:T(8,128)(2,1)S(1)}, bf16[192,512]{1,0:T(8,128)(2,1)S(1)}, u32[]{:S(2)}, u32[]{:S(2)}) collective-permute-start(bf16[192,512]{1,0:T(8,128)(2,1)S(1)} %get-tuple-element.203), channel_id=1, source_target_pairs={{0,3},{1,2},{2,1},{3,0},{4,7},{5,6},{6,5},{7,4},{8,11},{9,10},{10,... | collective-permute-start | bytes 589832 | tf_op jit(solution)/shard_map/ppermute | solution.py:40
  244.2 32.9 %all-to-all-start.5 = ((bf16[8,96,768]{2,1,0:T(8,128)(2,1)}), bf16[8,96,768]{2,1,0:T(8,128)(2,1)}, u32[]{:S(2)}, u32[]{:S(2)}) async-start(bf16[8,96,768]{2,1,0:T(8,128)(2,1)} %get-tuple-element.163), calls=%async_computation.5 | async-start | bytes 2359296 | tf_op jit(solution)/shard_map/all_to_all | solution.py:903
  257.5 12.9 %collective-permute-start.17 = (bf16[1,192,768]{2,1,0:T(8,128)(2,1)S(1)}, bf16[1,192,768]{2,1,0:T(8,128)(2,1)S(1)}, u32[]{:S(2)}, u32[]{:S(2)}) collective-permute-start(bf16[1,192,768]{2,1,0:T(8,128)(2,1)S(1)} %fusion.20), channel_id=1, source_target_pairs={{0,2},{1,3},{2,0},{3,1},{4,6},{5,7},{6,4},{7,5},{8,10},{9,11},{10,... | collective-permute-start | bytes 884744 | tf_op jit(solution)/shard_map/ppermute | solution.py:40
  258.7 11.6 %collective-permute-start.19 = (f32[16,768]{1,0:T(8,128)S(1)}, f32[16,768]{1,0:T(8,128)S(1)}, u32[]{:S(2)}, u32[]{:S(2)}) collective-permute-start(f32[16,768]{1,0:T(8,128)S(1)} %add.135), channel_id=1, source_target_pairs={{0,2},{1,3},{2,0},{3,1},{4,6},{5,7},{6,4},{7,5},{8,10},{9,11},{10,... | collective-permute-start | bytes 147464 | tf_op jit(solution)/shard_map/ppermute | solution.py:40
  278.0 21.7 %all-to-all-start.6 = ((bf16[8,56,768]{2,1,0:T(8,128)(2,1)}), bf16[8,56,768]{2,1,0:T(8,128)(2,1)S(1)}, u32[]{:S(2)}, u32[]{:S(2)}) async-start(bf16[8,56,768]{2,1,0:T(8,128)(2,1)} %pad.4), calls=%async_computation.6 | async-start | bytes 1376256 | tf_op jit(solution)/shard_map/all_to_all | solution.py:903
  287.2 52.4 %collective-permute-start.32 = (bf16[2,768,768]{2,1,0:T(8,128)(2,1)}, bf16[2,768,768]{2,1,0:T(8,128)(2,1)}, u32[]{:S(2)}, u32[]{:S(2)}) collective-permute-start(bf16[2,768,768]{2,1,0:T(8,128)(2,1)} %add_convert_fusion), channel_id=1, source_target_pairs={{0,2},{1,3},{2,0},{3,1},{4,6},{5,7},{6,4},{7,5},{8,10},{9,11},{10,... | collective-permute-start | bytes 7077896 | tf_op jit(solution)/shard_map/ppermute | solution.py:40
  301.7 43.4 %all-to-all-start.7 = ((bf16[8,80,768]{2,1,0:T(8,128)(2,1)}), bf16[8,80,768]{2,1,0:T(8,128)(2,1)S(1)}, u32[]{:S(2)}, u32[]{:S(2)}) async-start(bf16[8,80,768]{2,1,0:T(8,128)(2,1)} %fold_sums.3), calls=%async_computation.7 | async-start | bytes 1966080 | tf_op jit(solution)/shard_map/all_to_all | solution.py:903
  332.7 28.8 %collective-permute-start.20 = (bf16[512,768]{1,0:T(8,128)(2,1)}, bf16[512,768]{1,0:T(8,128)(2,1)}, u32[]{:S(2)}, u32[]{:S(2)}) collective-permute-start(bf16[512,768]{1,0:T(8,128)(2,1)} %copy-done.6), channel_id=1, source_target_pairs={{0,1},{1,0},{2,3},{3,2},{4,5},{5,4},{6,7},{7,6},{8,9},{9,8},{10,11... | collective-permute-start | bytes 2359304 | tf_op jit(solution)/shard_map/ppermute | solution.py:40
  335.8 25.7 %collective-permute-start.22 = (bf16[512,768]{1,0:T(8,128)(2,1)}, bf16[512,768]{1,0:T(8,128)(2,1)}, u32[]{:S(2)}, u32[]{:S(2)}) collective-permute-start(bf16[512,768]{1,0:T(8,128)(2,1)} %add_convert_fusion.1), channel_id=1, source_target_pairs={{0,2},{1,3},{2,0},{3,1},{4,6},{5,7},{6,4},{7,5},{8,10},{9,11},{10,... | collective-permute-start | bytes 2359304 | tf_op jit(solution)/shard_map/ppermute | solution.py:40
  346.0 18.8 %all-to-all-start.8 = ((bf16[8,48,768]{2,1,0:T(8,128)(2,1)}), bf16[8,48,768]{2,1,0:T(8,128)(2,1)}, u32[]{:S(2)}, u32[]{:S(2)}) async-start(bf16[8,48,768]{2,1,0:T(8,128)(2,1)} %fold_sums.4), calls=%async_computation.8 | async-start | bytes 1179648 | tf_op jit(solution)/shard_map/all_to_all | solution.py:903
  363.5 16.8 %collective-permute-start.24 = (bf16[8,48,768]{2,1,0:T(8,128)(2,1)S(1)}, bf16[8,48,768]{2,1,0:T(8,128)(2,1)}, u32[]{:S(2)}, u32[]{:S(2)}) collective-permute-start(bf16[8,48,768]{2,1,0:T(8,128)(2,1)S(1)} %slice.92.refs_0_), channel_id=1, source_target_pairs={{0,2},{1,3},{2,0},{3,1},{4,6},{5,7},{6,4},{7,5},{8,10},{9,11},{10,... | collective-permute-start | bytes 1769480 | tf_op jit(solution)/shard_map/ppermute | solution.py:40
  366.6 13.8 %all-to-all-start.9 = ((bf16[8,24,768]{2,1,0:T(8,128)(2,1)}), bf16[8,24,768]{2,1,0:T(8,128)(2,1)S(1)}, u32[]{:S(2)}, u32[]{:S(2)}) async-start(bf16[8,24,768]{2,1,0:T(8,128)(2,1)} %copy-done.2), calls=%async_computation.9 | async-start | bytes 589824 | tf_op jit(solution)/shard_map/all_to_all | solution.py:903
  375.6 17.3 %collective-permute-start.23 = (bf16[8,48,768]{2,1,0:T(8,128)(2,1)S(1)}, bf16[8,48,768]{2,1,0:T(8,128)(2,1)S(1)}, u32[]{:S(2)}, u32[]{:S(2)}) collective-permute-start(bf16[8,48,768]{2,1,0:T(8,128)(2,1)S(1)} %slice.92.refs_0_), channel_id=1, source_target_pairs={{0,1},{1,0},{2,3},{3,2},{4,5},{5,4},{6,7},{7,6},{8,9},{9,8},{10,11... | collective-permute-start | bytes 1769480 | tf_op jit(solution)/shard_map/ppermute | solution.py:40
  380.4 12.6 %collective-permute-start.25 = (bf16[8,48,768]{2,1,0:T(8,128)(2,1)}, bf16[8,48,768]{2,1,0:T(8,128)(2,1)S(1)}, u32[]{:S(2)}, u32[]{:S(2)}) collective-permute-start(bf16[8,48,768]{2,1,0:T(8,128)(2,1)} %collective-permute-done.24.refs_2_), channel_id=1, source_target_pairs={{0,1},{1,0},{2,3},{3,2},{4,5},{5,4},{6,7},{7,6},{8,9},{9,8},{10,11... | collective-permute-start | bytes 1769480 | tf_op jit(solution)/shard_map/ppermute | solution.py:40
  380.5 39.7 %all-to-all-start.10 = ((bf16[8,96,768]{2,1,0:T(8,128)(2,1)}), bf16[8,96,768]{2,1,0:T(8,128)(2,1)}, u32[]{:S(2)}, u32[]{:S(2)}) async-start(bf16[8,96,768]{2,1,0:T(8,128)(2,1)} %get-tuple-element.174), calls=%async_computation.10 | async-start | bytes 2359296 | tf_op jit(solution)/shard_map/all_to_all | solution.py:903
  387.9 8.5 %collective-permute-start.27 = (bf16[8,24,768]{2,1,0:T(8,128)(2,1)S(1)}, bf16[8,24,768]{2,1,0:T(8,128)(2,1)S(1)}, u32[]{:S(2)}, u32[]{:S(2)}) collective-permute-start(bf16[8,24,768]{2,1,0:T(8,128)(2,1)S(1)} %slice.93.refs_4_), channel_id=1, source_target_pairs={{0,2},{1,3},{2,0},{3,1},{4,6},{5,7},{6,4},{7,5},{8,10},{9,11},{10,... | collective-permute-start | bytes 884744 | tf_op jit(solution)/shard_map/ppermute | solution.py:40
  389.5 21.7 %collective-permute-start.26 = (bf16[8,24,768]{2,1,0:T(8,128)(2,1)S(1)}, bf16[8,24,768]{2,1,0:T(8,128)(2,1)S(1)}, u32[]{:S(2)}, u32[]{:S(2)}) collective-permute-start(bf16[8,24,768]{2,1,0:T(8,128)(2,1)S(1)} %slice.93.refs_4_), channel_id=1, source_target_pairs={{0,1},{1,0},{2,3},{3,2},{4,5},{5,4},{6,7},{7,6},{8,9},{9,8},{10,11... | collective-permute-start | bytes 884744 | tf_op jit(solution)/shard_map/ppermute | solution.py:40
  396.5 14.7 %collective-permute-start.28 = (bf16[8,24,768]{2,1,0:T(8,128)(2,1)S(1)}, bf16[8,24,768]{2,1,0:T(8,128)(2,1)S(1)}, u32[]{:S(2)}, u32[]{:S(2)}) collective-permute-start(bf16[8,24,768]{2,1,0:T(8,128)(2,1)S(1)} %collective-permute-done.27.refs_6_), channel_id=1, source_target_pairs={{0,1},{1,0},{2,3},{3,2},{4,5},{5,4},{6,7},{7,6},{8,9},{9,8},{10,11... | collective-permute-start | bytes 884744 | tf_op jit(solution)/shard_map/ppermute | solution.py:40
  397.9 13.3 %collective-permute-start.29 = (bf16[8,24,768]{2,1,0:T(8,128)(2,1)S(1)}, bf16[8,24,768]{2,1,0:T(8,128)(2,1)S(1)}, u32[]{:S(2)}, u32[]{:S(2)}) collective-permute-start(bf16[8,24,768]{2,1,0:T(8,128)(2,1)S(1)} %all-to-all-done.9.refs_8_), channel_id=1, source_target_pairs={{0,1},{1,0},{2,3},{3,2},{4,5},{5,4},{6,7},{7,6},{8,9},{9,8},{10,11... | collective-permute-start | bytes 884744 | tf_op jit(solution)/shard_map/ppermute | solution.py:40
  397.9 8.2 %collective-permute-start.30 = (bf16[8,24,768]{2,1,0:T(8,128)(2,1)S(1)}, bf16[8,24,768]{2,1,0:T(8,128)(2,1)S(1)}, u32[]{:S(2)}, u32[]{:S(2)}) collective-permute-start(bf16[8,24,768]{2,1,0:T(8,128)(2,1)S(1)} %all-to-all-done.9.refs_8_), channel_id=1, source_target_pairs={{0,2},{1,3},{2,0},{3,1},{4,6},{5,7},{6,4},{7,5},{8,10},{9,11},{10,... | collective-permute-start | bytes 884744 | tf_op jit(solution)/shard_map/ppermute | solution.py:40
  (54 other events, 378.8 us)

commit v3 on v2

--- a/solution.py
+++ b/solution.py
@@ -22,7 +22,7 @@
 bf16 = jnp.bfloat16
 f32 = jnp.float32
 MIB = 1 << 20
-COST_SCALE = 0.25
+COST_SCALE = 0.1
 
 
 def mm(left, right, contract=((1,), (0,)), precision=None):
@@ -53,6 +53,7 @@
 
 
 EXTRA = 8
+LANE_B = 128
 
 
 def three_rows(row):
@@ -130,83 +131,57 @@
         out_specs=[vmem_spec()] * len(shapes),
         compiler_params=params(60),
         name="slot_tables",
-        cost_estimate=cost(5),
+        cost_estimate=cost(0.1),
     )(routes_t, dy)
     return results[0:2], results[2:6], results[6]
 
 
 def qkv_kernel(
-    own_ref, x0, x1, x2, x3, gain_ref, w_ref, a_ref, qkv_ref, k_ref, v_ref, w_buf, x_buf, heads_ref
+    pieces, own_ref, *refs
 ):
-    step = pl.program_id(0)
+    blocks, refs = refs[: 2 * pieces], refs[2 * pieces :]
+    gain_ref, w_ref, a0, a1, q0, q1, k0, k1, v0, v1, w_buf, heads_ref = refs
     width, cols = heads_ref.shape
     third = cols // 3
-
-    @pl.when(step == 0)
-    def turn():
-        for h in range(width // third):
-
-            @pl.when(own_ref[0] == h)
-            def pick(h=h):
-                for t in range(3):
-                    start = t * width + h * third
-                    heads_ref[:, t * third : (t + 1) * third] = w_ref[:, start : start + third]
-
-        w_buf[...] = heads_ref[...].T
-
-    for j, block in enumerate((x0, x1, x2, x3)):
-
-        @pl.when(step == j)
-        def take(block=block):
-            x_buf[...] = block[...].astype(f32)
-
-    x = x_buf[...]
-    scale = lax.rsqrt(jnp.mean(x * x, axis=1, keepdims=True) + norm_eps)
-    a = (x * scale * gain_ref[...]).astype(bf16)
-    a_ref[...] = a
-    qkv_t = mm(w_buf[...], a, NT).astype(bf16)
-    qkv_ref[0:third, :] = qkv_t[0:third, :] * jnp.asarray(0.125, bf16)
-    qkv_ref[third:, :] = qkv_t[third:, :]
-    both = mm(a, heads_ref[:, third:]).astype(bf16)
-    k_ref[...] = both[:, :third]
-    v_ref[...] = both[:, third:]
+    for h in range(width // third):
+
+        @pl.when(own_ref[0] == h)
+        def pick(h=h):
+            for t in range(3):
+                start = t * width + h * third
+                heads_ref[:, t * third : (t + 1) * third] = w_ref[:, start : start + third]
+
+    w_buf[...] = heads_ref[...].T
+    outs = ((a0, q0, k0, v0), (a1, q1, k1, v1))
+    for n, (a_ref, qkv_ref, k_ref, v_ref) in enumerate(outs):
+        x = [x_ref[...] for x_ref in blocks[n * pieces : (n + 1) * pieces]]
+        x = jnp.concatenate(x, axis=0).astype(f32)
+        scale = lax.rsqrt(jnp.mean(x * x, axis=1, keepdims=True) + norm_eps)
+        a = (x * scale * gain_ref[...]).astype(bf16)
+        a_ref[...] = a
+        qkv_t = mm(w_buf[...], a, NT).astype(bf16)
+        qkv_ref[0:third, :] = qkv_t[0:third, :] * jnp.asarray(0.125, bf16)
+        qkv_ref[third:, :] = qkv_t[third:, :]
+        both = mm(a, heads_ref[:, third:]).astype(bf16)
+        k_ref[...] = both[:, :third]
+        v_ref[...] = both[:, third:]
 
 
 def project_qkv(own, blocks, gain, w_qkv):
-    count, width = blocks[0].shape
-    parts = len(blocks)
-    cols = w_qkv.shape[1] // parts
+    pieces = len(blocks) // 2
+    count, width = pieces * blocks[0].shape[0], blocks[0].shape[1]
+    cols = w_qkv.shape[1] // 4
     third = cols // 3
-
-    def whole(shape):
-        return pl.BlockSpec(shape, lambda g, own_ref: (0, 0), pipeline_mode=pl.Buffered(1))
-
+    shapes = [(count, width)] * 2 + [(cols, count)] * 2 + [(count, third)] * 4 + [(cols, width)]
     return pl.pallas_call(
-        qkv_kernel,
-        out_shape=[
-            jax.ShapeDtypeStruct((parts * count, width), bf16),
-            jax.ShapeDtypeStruct((cols, parts * count), bf16),
-            jax.ShapeDtypeStruct((parts * count, third), bf16),
-            jax.ShapeDtypeStruct((parts * count, third), bf16),
-            jax.ShapeDtypeStruct((cols, width), bf16),
-        ],
-        grid_spec=pltpu.PrefetchScalarGridSpec(
-            num_scalar_prefetch=1,
-            grid=(parts,),
-            in_specs=[whole((count, width))] * parts
-            + [whole((1, width)), whole((width, parts * cols))],
-            out_specs=[
-                pl.BlockSpec((count, width), lambda g, own_ref: (own_ref[0] ^ g, 0)),
-                pl.BlockSpec((cols, count), lambda g, own_ref: (0, own_ref[0] ^ g)),
-                pl.BlockSpec((count, third), lambda g, own_ref: (own_ref[0] ^ g, 0)),
-                pl.BlockSpec((count, third), lambda g, own_ref: (own_ref[0] ^ g, 0)),
-                whole((cols, width)),
-            ],
-            scratch_shapes=[pltpu.VMEM((count, width), f32), pltpu.VMEM((width, cols), bf16)],
-        ),
+        functools.partial(qkv_kernel, pieces),
+        out_shape=[jax.ShapeDtypeStruct(shape, bf16) for shape in shapes],
+        in_specs=[smem_spec()] + [vmem_spec()] * (2 * pieces + 2),
+        out_specs=[vmem_spec()] * 9,
+        scratch_shapes=[pltpu.VMEM((width, cols), bf16)],
         compiler_params=params(60),
         name="norm_qkv",
-        cost_estimate=cost(11),
+        cost_estimate=cost(0.1),
     )(own, *blocks, gain, w_qkv)
 
 
@@ -242,14 +217,34 @@
     return parts
 
 
-def attend_kernel(block, info_ref, k_ref, q_ref, v_ref, o_ref, low_ref, log_ref, q_pad):
+def gather_blocks(own_ref, buf, parts, axis):
+    for j, part in enumerate(parts):
+        size = part.shape[axis]
+        where = pl.ds(pl.multiple_of((own_ref[0] ^ j) * size, size), size)
+        if axis:
+            buf[:, where] = part[...]
+        else:
+            buf[where, :] = part[...]
+
+
+def attend_kernel(block, info_ref, own_ref, *refs):
+    (k_parts, q_parts, v_parts), refs = (refs[0:4], refs[4:8], refs[8:12]), refs[12:]
+    o_ref, log_ref, keys_ref = refs[:3]
+    pieces, (q_pad, v_buf, low_buf) = refs[3:7], refs[7:]
     head = pl.program_id(0)
-    row_len = k_ref.shape[0]
+    row_len = keys_ref.shape[0]
+
+    @pl.when(head == 0)
+    def keys():
+        gather_blocks(own_ref, keys_ref, k_parts, 0)
+
     q_pad[...] = jnp.zeros_like(q_pad)
-    q_pad[pl.ds(pl.multiple_of(head * HEAD_DIM, HEAD_DIM), HEAD_DIM), :] = q_ref[...]
+    own_rows = pl.ds(pl.multiple_of(head * HEAD_DIM, HEAD_DIM), HEAD_DIM)
+    gather_blocks(own_ref, q_pad.at[own_rows], q_parts, 1)
+    gather_blocks(own_ref, v_buf, v_parts, 1)
     for i in range(row_len // block):
         cols = slice(i * block, (i + 1) * block)
-        parts = score_parts(info_ref, k_ref, q_pad[:, cols], block, i, row_len)
+        parts = score_parts(info_ref, keys_ref, q_pad[:, cols], block, i, row_len)
         top = functools.reduce(
             jnp.maximum, [jnp.max(s, axis=0, keepdims=True) for _, _, s in parts]
         )
@@ -257,119 +252,138 @@
         for first, last, s in parts:
             p = jnp.exp(s - top)
             total = total + jnp.sum(p, axis=0, keepdims=True)
-            out = out + mm(v_ref[:, first:last], p.astype(bf16))
+            out = out + mm(v_buf[:, first:last], p.astype(bf16))
         out = out / total
         o_ref[:, cols] = out
-        low_ref[:, cols] = out.astype(bf16)
+        low_buf[:, cols] = out.astype(bf16)
         log_ref[0, :, cols] = top + jnp.log(total)
-
-
-def attend(info, keys, qkv_t, block=512):
-    row_len, group = keys.shape
+    for j, piece in enumerate(pieces):
+        size = piece.shape[1]
+        where = pl.ds(pl.multiple_of((own_ref[0] ^ j) * size, size), size)
+        piece[...] = low_buf[:, where]
+
+
+def attend(info, own, k_parts, qkv_parts, block=512):
+    count, group = k_parts[0].shape
+    row_len = count * len(k_parts)
     heads = group // HEAD_DIM
     tile = pl.BlockSpec((HEAD_DIM, row_len), lambda h: (h, 0))
-    return pl.pallas_call(
+    whole = pl.BlockSpec((row_len, group), lambda h: (0, 0))
+    keys = pl.BlockSpec((count, group), lambda h: (0, 0))
+    query = pl.BlockSpec((HEAD_DIM, count), lambda h: (h, 0))
+    value = pl.BlockSpec((HEAD_DIM, count), lambda h: (2 * heads + h, 0))
+    results = pl.pallas_call(
         functools.partial(attend_kernel, block),
         out_shape=[
             jax.ShapeDtypeStruct((group, row_len), f32),
-            jax.ShapeDtypeStruct((group, row_len), bf16),
             jax.ShapeDtypeStruct((heads, 1, row_len), f32),
+            jax.ShapeDtypeStruct((row_len, group), bf16),
+        ]
+        + [jax.ShapeDtypeStruct((group, count), bf16)] * 4,
+        grid=(heads,),
+        in_specs=[smem_spec()] * 2 + [keys] * 4 + [query] * 4 + [value] * 4,
+        out_specs=[tile, pl.BlockSpec((1, 1, row_len), lambda h: (h, 0, 0)), whole] + [query] * 4,
+        scratch_shapes=[
+            pltpu.VMEM((group, row_len), bf16),
+            pltpu.VMEM((HEAD_DIM, row_len), bf16),
+            pltpu.VMEM((HEAD_DIM, row_len), bf16),
         ],
-        grid=(heads,),
-        in_specs=[
-            smem_spec(),
-            pl.BlockSpec((row_len, group), lambda h: (0, 0)),
-            tile,
-            pl.BlockSpec((HEAD_DIM, row_len), lambda h: (2 * heads + h, 0)),
-        ],
-        out_specs=[tile, tile, pl.BlockSpec((1, 1, row_len), lambda h: (h, 0, 0))],
-        scratch_shapes=[pltpu.VMEM((group, row_len), bf16)],
         compiler_params=params(60),
         name="attend",
-        cost_estimate=cost(17),
-    )(info, keys, qkv_t, qkv_t)
-
-
-def attend_back_kernel(
-    block, head, info_ref, own_ref, k_ref, v_ref, q_ref, kt_ref, g0, g1, g2, g3, o_ref, log_ref,
-    a_ref, dqkv_ref, grad_ref, q_pad, g_pad, dk_acc, dv_acc,
-):
+        cost_estimate=cost(0.1),
+    )(info, own, *k_parts, *qkv_parts, *qkv_parts)
+    return results[0], results[1], results[2], results[3:]
+
+
+def attend_back_kernel(block, first_head, info_ref, own_ref, k_ref, *refs):
+    v_parts, q_parts, kt_parts, g_parts, a_parts = (refs[4 * n : 4 * n + 4] for n in range(5))
+    o_ref, log_ref, dqkv_ref, grad_ref = refs[20:24]
+    v_buf, q_pad, g_pad, kt_buf, a_buf, dk_acc, dv_acc = refs[24:]
     row_len = k_ref.shape[0]
-    own_rows = slice(head * HEAD_DIM, (head + 1) * HEAD_DIM)
+    head = first_head + pl.program_id(0)
+    own_rows = pl.ds(pl.multiple_of(head * HEAD_DIM, HEAD_DIM), HEAD_DIM)
     dk_acc[...] = jnp.zeros_like(dk_acc)
     dv_acc[...] = jnp.zeros_like(dv_acc)
     q_pad[...] = jnp.zeros_like(q_pad)
     g_pad[...] = jnp.zeros_like(g_pad)
-    q_pad[own_rows, :] = q_ref[...]
-    for j, part in enumerate((g0, g1, g2, g3)):
-        size = part.shape[1]
-        g_pad[own_rows, pl.ds(pl.multiple_of((own_ref[0] ^ j) * size, size), size)] = part[...]
+
+    @pl.when(pl.program_id(0) == 0)
+    def once():
+        gather_blocks(own_ref, v_buf, v_parts, 0)
+        gather_blocks(own_ref, a_buf, a_parts, 0)
+
+    gather_blocks(own_ref, q_pad.at[own_rows], q_parts, 1)
+    gather_blocks(own_ref, g_pad.at[own_rows], g_parts, 1)
+    gather_blocks(own_ref, kt_buf, kt_parts, 1)
     for i in range(row_len // block):
         cols = slice(i * block, (i + 1) * block)
-        q, g = q_ref[:, cols], g_pad[own_rows, cols]
+        q, g = q_pad[own_rows, cols], g_pad[own_rows, cols]
         g_wide = g_pad[:, cols]
         delta = jnp.sum(g.astype(f32) * o_ref[:, cols], axis=0, keepdims=True)
         log_total = log_ref[0, :, cols]
         dq = 0.0
         for first, last, s in score_parts(info_ref, k_ref, q_pad[:, cols], block, i, row_len):
             p = jnp.exp(s - log_total)
-            dp = mm(v_ref[first:last, :], g_wide)
+            dp = mm(v_buf[first:last, :], g_wide)
             ds = (p * (dp - delta)).astype(bf16)
             dv_acc[:, first:last] += mm(g, p.astype(bf16), NT)
             dk_acc[:, first:last] += mm(q, ds, NT)
-            dq = dq + mm(kt_ref[:, first:last], ds)
+            dq = dq + mm(kt_buf[:, first:last], ds)
         dqkv_ref[0:HEAD_DIM, cols] = (0.125 * dq).astype(bf16)
     dqkv_ref[HEAD_DIM : 2 * HEAD_DIM, :] = dk_acc[...].astype(bf16)
     dqkv_ref[2 * HEAD_DIM :, :] = dv_acc[...].astype(bf16)
-    grad = mm(dqkv_ref[...], a_ref[...])
-    rows = grad_ref.shape[1]
-    for e in range(grad_ref.shape[0]):
-        grad_ref[e] = grad[e * rows : (e + 1) * rows, :].astype(bf16)
-
-
-def attend_back(head, pieces, info, own, keys, values, qkv_t, grads, out, logs, a_one, block=256):
+    grad = mm(dqkv_ref[...], a_buf[...])
+    rows = grad_ref.shape[2]
+    for e in range(grad_ref.shape[1]):
+        grad_ref[0, e] = grad[e * rows : (e + 1) * rows, :].astype(bf16)
+
+
+def attend_back(first, number, pieces, info, own, keys, v_parts, qkv_parts, grads, out, logs, a_parts, block=256):
     row_len, group = keys.shape
     heads = group // HEAD_DIM
-    width = a_one.shape[1]
-    whole = pl.BlockSpec((row_len, group), lambda g: (0, 0))
-    piece = pl.BlockSpec((HEAD_DIM, grads[0].shape[1]), lambda g: (head, 0))
-    tile = pl.BlockSpec((HEAD_DIM, row_len), lambda g: (head, 0))
+    count, width = a_parts[0].shape
+
+    def whole(*shape):
+        return pl.BlockSpec(shape, lambda g: (0,) * len(shape))
+
+    def tile(n):
+        return pl.BlockSpec((HEAD_DIM, count), lambda g: (n + g, 0))
+
     return pl.pallas_call(
-        functools.partial(attend_back_kernel, block, head),
+        functools.partial(attend_back_kernel, block, first),
         out_shape=[
-            jax.ShapeDtypeStruct((3 * HEAD_DIM, row_len), bf16),
-            jax.ShapeDtypeStruct((pieces, 3 * HEAD_DIM // pieces, width), bf16),
+            jax.ShapeDtypeStruct((number * 3 * HEAD_DIM, row_len), bf16),
+            jax.ShapeDtypeStruct((number, pieces, 3 * HEAD_DIM // pieces, width), bf16),
         ],
-        grid=(1,),
-        in_specs=[
-            smem_spec(),
-            smem_spec(),
-            whole,
-            whole,
-            tile,
-            pl.BlockSpec((HEAD_DIM, row_len), lambda g: (heads + head, 0)),
-            piece,
-            piece,
-            piece,
-            piece,
-            tile,
-            pl.BlockSpec((1, 1, row_len), lambda g: (head, 0, 0)),
-            pl.BlockSpec((row_len, width), lambda g: (0, 0)),
+        grid=(number,),
+        in_specs=[smem_spec()] * 2
+        + [whole(row_len, group)]
+        + [whole(count, group)] * 4
+        + [tile(first)] * 4
+        + [tile(heads + first)] * 4
+        + [tile(first)] * 4
+        + [whole(count, width)] * 4
+        + [
+            pl.BlockSpec((HEAD_DIM, row_len), lambda g: (first + g, 0)),
+            pl.BlockSpec((1, 1, row_len), lambda g: (first + g, 0, 0)),
         ],
         out_specs=[
-            pl.BlockSpec((3 * HEAD_DIM, row_len), lambda g: (0, 0)),
-            pl.BlockSpec((pieces, 3 * HEAD_DIM // pieces, width), lambda g: (0, 0, 0)),
+            pl.BlockSpec((3 * HEAD_DIM, row_len), lambda g: (g, 0)),
+            pl.BlockSpec((1, pieces, 3 * HEAD_DIM // pieces, width), lambda g: (g, 0, 0, 0)),
         ],
         scratch_shapes=[
+            pltpu.VMEM((row_len, group), bf16),
             pltpu.VMEM((group, row_len), bf16),
             pltpu.VMEM((group, row_len), bf16),
+            pltpu.VMEM((HEAD_DIM, row_len), bf16),
+            pltpu.VMEM((row_len, width), bf16),
             pltpu.VMEM((HEAD_DIM, row_len), f32),
             pltpu.VMEM((HEAD_DIM, row_len), f32),
         ],
         compiler_params=params(60),
         name="attend_back",
-        cost_estimate=cost(11),
-    )(info, own, keys, values, qkv_t, qkv_t, *grads, out, logs, a_one)
+        cost_estimate=cost(11 * number),
+    )(info, own, keys, *v_parts, *qkv_parts, *qkv_parts, *grads, *a_parts, out, logs)
 
 
 def gates_of(normed, router, route_rows):
@@ -408,8 +422,11 @@
     )
     stacked = jnp.concatenate([piece.astype(f32) for piece in split_three(table)], axis=0)
     stacked = stacked.astype(bf16)
-    for hot, send in ((hot_a, send_a), (hot_b, send_b)):
-        size = send.shape[1] - EXTRA
+    last = send_b.shape[1] - EXTRA
+    for e in range(experts):
+        send_b[e, last:, :] = jnp.zeros((EXTRA, send_b.shape[2]), bf16)
+    for hot, send, lane in ((hot_a, send_a, 0), (hot_b, send_b, LANE_B)):
+        size = hot.shape[0] // experts
         rows = mm(hot[...], a_two).astype(bf16)
         for e in range(experts):
             own_rows = slice(e * size, (e + 1) * size)
@@ -417,8 +434,7 @@
             picked = mm(stacked, hot[own_rows, :], NT)
             three = [picked[k * experts + e : k * experts + e + 1, :] for k in range(3)]
             three = jnp.concatenate(three + [jnp.zeros((EXTRA - 3, size), f32)], axis=0)
-            send[e, size:, :] = jnp.zeros((EXTRA, send.shape[2]), bf16)
-            send[e, size:, 0:size] = three.astype(bf16)
+            send_b[e, last:, lane : lane + size] = three.astype(bf16)
 
 
 def make_dispatch(own, parts, x, w_out, gain, router_t, routes_t, hots):
@@ -428,8 +444,10 @@
         jax.ShapeDtypeStruct((count, width), f32),
         jax.ShapeDtypeStruct((2, count), f32),
     ]
+    sizes = [hot.shape[0] // experts for hot in hots]
     shapes += [
-        jax.ShapeDtypeStruct((experts, hot.shape[0] // experts + EXTRA, width), bf16) for hot in hots
+        jax.ShapeDtypeStruct((experts, sizes[0], width), bf16),
+        jax.ShapeDtypeStruct((experts, sizes[1] + EXTRA, width), bf16),
     ]
     return pl.pallas_call(
         dispatch_kernel,
@@ -438,7 +456,7 @@
         out_specs=[vmem_spec()] * len(shapes),
         compiler_params=params(60),
         name="project_dispatch",
-        cost_estimate=cost(9),
+        cost_estimate=cost(0.1),
     )(own, *parts, x, w_out, gain, router_t, routes_t, *hots)
 
 
@@ -454,11 +472,18 @@
 GELU_CUBE = 0.044715
 
 
-def expert_kernel(start, x_ref, dy_ref, *refs):
+def expert_kernel(half, start, x_ref, dy_ref, *refs):
     weights, refs = refs[:8], refs[8:]
-    out_ref, slot_ref, act_ref, dpre_ref = refs[:4]
-    x_buf, dy_buf, up_buf, down_buf, out_acc, slot_acc, sems = refs[4:]
-    sources, size, width = out_ref.shape
+    if half:
+        carried_ref, refs = refs[0], refs[2:]
+        out_ref, slot_ref, act_ref, dpre_ref = refs[:4]
+        refs = refs[4:]
+    else:
+        out_ref, slot_ref, act_ref, dpre_ref, carry_ref = refs[:5]
+        refs = refs[5:]
+    x_buf, dy_buf, up_buf, down_buf, out_acc, slot_acc, sems = refs
+    sources, width = x_ref.shape[0], x_ref.shape[2]
+    size = x_buf.shape[0] // sources
     step = pl.program_id(0)
     parts = len(weights) // 2
 
@@ -514,18 +539,23 @@
         for n in range(sources):
             rows = slice(n * size, (n + 1) * size)
             out = out_acc[rows, :].astype(bf16)
-            out_ref[n] = out
+            out_ref[n, start : start + size, :] = out
             slot_ref[n, 0:size, :] = slot_acc[rows, :].astype(bf16)
             dgate = jnp.sum(
                 dy_buf[rows, :].astype(f32) * out.astype(f32), axis=1, keepdims=True
             )
-            slot_ref[n, size:, :] = jnp.zeros((EXTRA, width), bf16)
-            slot_ref[n, size:, 0:size] = three_rows(row_of(dgate))
-
-
-def run_experts(start, x, dy, weights):
-    sources, size, width = x.shape
-    size -= EXTRA
+            three = three_rows(row_of(dgate))
+            if half:
+                slot_ref[n, size:, :] = jnp.zeros((EXTRA, width), bf16)
+                slot_ref[n, size:, 0:LANE_B] = carried_ref[n]
+                slot_ref[n, size:, LANE_B : LANE_B + size] = three
+            else:
+                carry_ref[n] = jnp.zeros((EXTRA, LANE_B), bf16)
+                carry_ref[n, :, 0:size] = three
+
+
+def run_experts(half, start, size, x, dy, weights, before):
+    sources, _, width = x.shape
     rows = sources * size
     units = weights[0].shape[1]
     parts = len(weights) // 2
@@ -533,18 +563,23 @@
     def whole(shape):
         return pl.BlockSpec(shape, lambda g: (0,) * len(shape), pipeline_mode=pl.Buffered(1))
 
-    kept = jax.ShapeDtypeStruct((parts, rows, units), bf16)
+    def shaped(*shape):
+        return jax.ShapeDtypeStruct(shape, bf16)
+
+    kept = shaped(parts, rows, units)
     kept_spec = pl.BlockSpec((1, rows, units), lambda g: (g, 0, 0))
-    piece = (sources, size, width)
+    carry = shaped(sources, EXTRA, LANE_B)
+    hbm = pl.BlockSpec(memory_space=pl.ANY)
+    piece = pl.BlockSpec((sources, size, width), lambda g: (0, start // size, 0))
     return pl.pallas_call(
-        functools.partial(expert_kernel, start),
-        out_shape=[
-            jax.ShapeDtypeStruct(piece, bf16), jax.ShapeDtypeStruct(x.shape, bf16), kept, kept
-        ],
+        functools.partial(expert_kernel, half, 0),
+        out_shape=[shaped(*dy.shape), shaped(*x.shape), kept, kept] + ([] if half else [carry]),
         grid=(parts,),
-        in_specs=[whole(x.shape), whole(dy.shape)]
-        + [pl.BlockSpec(memory_space=pl.ANY)] * (2 * parts),
-        out_specs=[whole(piece), whole(x.shape), kept_spec, kept_spec],
+        in_specs=[whole(x.shape), piece]
+        + [hbm] * (2 * parts)
+        + ([whole(carry.shape), hbm] if half else []),
+        out_specs=[piece, whole(x.shape), kept_spec, kept_spec]
+        + ([] if half else [whole(carry.shape)]),
         scratch_shapes=[
             pltpu.VMEM((rows, width), bf16),
             pltpu.VMEM((rows, width), bf16),
@@ -554,41 +589,44 @@
             pltpu.VMEM((rows, width), f32),
             pltpu.SemaphoreType.DMA((2, 2)),
         ],
+        input_output_aliases={2 * parts + 3: 0} if half else {},
         compiler_params=params(60),
         name="experts",
-        cost_estimate=cost(27),
-    )(x, dy, *weights)
-
-
-def weight_kernel(dy_ref, x_a, x_b, act_a, act_b, dpre_a, dpre_b, own_out, near_out, far_out, x_turn, dy_turn, gate_buf):
+        cost_estimate=cost(25),
+    )(x, dy, *weights, *((before[4], before[0]) if half else ()))
+
+
+def weight_kernel(dy_ref, x_a, x_b, act_a, act_b, dpre_a, dpre_b, own_out, near_out, far_up, far_down, x_buf, dy_buf):
     step = pl.program_id(0)
     experts, capacity, _ = dy_ref.shape
 
     @pl.when(step == 0)
-    def turn():
+    def gated():
         begin = 0
-        for (start, size), x_ref in zip(halves_of(capacity), (x_a, x_b)):
-            cols = slice(begin, begin + experts * size)
+        halves = zip(halves_of(capacity), (x_a, x_b), (0, LANE_B))
+        for (start, size), x_ref, lane in halves:
             for n in range(experts):
-                three = x_ref[n, size:, 0:size].astype(f32)
-                gate_buf[0:1, begin : begin + size] = three[0:1] + three[1:2] + three[2:3]
+                rows = slice(begin, begin + size)
                 begin += size
-            gate = gate_buf[0:1, cols]
-            shape = (experts * size, x_ref.shape[2])
-            rows = x_ref[:, 0:size, :].reshape(shape).astype(f32)
-            x_turn[:, cols] = (rows.T * gate).astype(bf16)
-            rows = dy_ref[:, start : start + size, :].reshape(shape).astype(f32)
-            dy_turn[:, cols] = (rows.T * gate).astype(bf16)
+                three = x_b[n, x_b.shape[1] - EXTRA :, lane : lane + size].astype(f32)
+                gate = column_of(three[0:1] + three[1:2] + three[2:3])
+                x_buf[rows, :] = (x_ref[n, 0:size, :].astype(f32) * gate).astype(bf16)
+                dy = dy_ref[n, start : start + size, :].astype(f32)
+                dy_buf[rows, :] = (dy * gate).astype(bf16)
 
     cut = act_a.shape[1]
-    up = mm(x_turn[:, :cut], dpre_a[0]) + mm(x_turn[:, cut:], dpre_b[0])
-    down = (mm(dy_turn[:, :cut], act_a[0]) + mm(dy_turn[:, cut:], act_b[0])).T
-    for j, (out, n) in enumerate(((own_out, 0), (near_out, 0), (far_out, 0), (near_out, 2))):
+    up = mm(x_buf[:cut, :], dpre_a[0], TN) + mm(x_buf[cut:, :], dpre_b[0], TN)
+    down = mm(act_a[0], dy_buf[:cut, :], TN) + mm(act_b[0], dy_buf[cut:, :], TN)
+    for j, (out, n) in enumerate(((own_out, 0), (near_out, 0), (None, 0), (near_out, 2))):
 
         @pl.when(step == j)
         def keep(out=out, n=n):
-            out[n] = up.astype(out.dtype)
-            out[n + 1] = down.astype(out.dtype)
+            if out is None:
+                far_up[...] = up
+                far_down[...] = down
+            else:
+                out[n] = up.astype(out.dtype)
+                out[n + 1] = down.astype(out.dtype)
 
 
 def weight_grads(xs, dy, acts, dpres):
@@ -605,32 +643,33 @@
         out_shape=[
             jax.ShapeDtypeStruct((2, width, units), f32),
             jax.ShapeDtypeStruct((4, width, units), bf16),
-            jax.ShapeDtypeStruct((2, width, units), f32),
+            jax.ShapeDtypeStruct((width, units), f32),
+            jax.ShapeDtypeStruct((units, width), f32),
         ],
         grid=(parts,),
         in_specs=[whole(*dy.shape)] + [whole(*x.shape) for x in xs] + kept,
-        out_specs=[whole(2, width, units), whole(4, width, units), whole(2, width, units)],
-        scratch_shapes=[pltpu.VMEM((width, experts * capacity), bf16)] * 2
-        + [pltpu.VMEM((8, experts * capacity), f32)],
+        out_specs=[whole(2, width, units), whole(4, width, units)] + [whole(width, units)] * 2,
+        scratch_shapes=[pltpu.VMEM((experts * capacity, width), bf16)] * 2,
         compiler_params=params(60),
         name="expert_weight_grads",
-        cost_estimate=cost(30),
+        cost_estimate=cost(25),
     )(dy, *xs, *acts, *dpres)
 
 
 def combine_back_kernel(
     own_ref, hot_a, hot_b, p0a, p1a, p0b, p1b, residual_ref, dy_ref, gates_ref, routes_ref,
-    router_ref, gain_ref, w_ref, t0, t1, t2, t3, slot_a, slot_b,
-    dres_ref, datt_ref, gout_ref, small_ref, buf_a, buf_b,
+    router_ref, gain_ref, w_ref, slot_a, slot_b,
+    dres_ref, branch_ref, small_ref, g0, g1, g2, g3, buf_a, buf_b, datt_buf,
 ):
     experts = router_ref.shape[0]
     table = [0.0] * experts
-    for slot, hot, buf in ((slot_a, hot_a, buf_a), (slot_b, hot_b, buf_b)):
-        size = slot.shape[1] - EXTRA
+    last = slot_b.shape[1] - EXTRA
+    for slot, hot, buf, lane in ((slot_a, hot_a, buf_a, 0), (slot_b, hot_b, buf_b, LANE_B)):
+        size = hot.shape[0] // experts
         for e in range(experts):
             rows = slice(e * size, (e + 1) * size)
             buf[rows, :] = slot[e, 0:size, :]
-            picked = mm(slot[e, size:, 0:size], hot[rows, :])
+            picked = mm(slot_b[e, last:, lane : lane + size], hot[rows, :])
             table[e] = table[e] + (picked[0:1] + picked[1:2] + picked[2:3])
     table = jnp.concatenate(table, axis=0)
     residual = residual_ref[...]
@@ -661,39 +700,61 @@
     )
     dres_ref[...] = dres
     branch = dres.astype(bf16)
-    datt_ref[...] = mm(w_ref[...], branch, NT).astype(bf16)
-    group = t0.shape[0]
-    for j, part in enumerate((t0, t1, t2, t3)):
-        rows = pl.ds(pl.multiple_of((own_ref[0] ^ j) * group, group), group)
-        gout_ref[rows, :] = mm(part[...], branch)
-
-
-def combine_back(own, slots, hots, picks, residual, dy, gates, routes_t, router_t, gain, w_out, parts):
+    branch_ref[...] = branch
+    datt_buf[...] = mm(w_ref[...], branch, NT).astype(bf16)
+    for j, piece in enumerate((g0, g1, g2, g3)):
+        size = piece.shape[0]
+        piece[...] = datt_buf[pl.ds(pl.multiple_of((own_ref[0] ^ j) * size, size), size), :]
+
+
+def combine_back(own, slots, hots, picks, residual, dy, gates, routes_t, router_t, gain, w_out):
     count, width = residual.shape
     experts = router_t.shape[0]
     shapes = [
         jax.ShapeDtypeStruct((count, width), f32),
-        jax.ShapeDtypeStruct((width, count), bf16),
-        jax.ShapeDtypeStruct((width, width), f32),
+        jax.ShapeDtypeStruct((count, width), bf16),
         jax.ShapeDtypeStruct((experts + 8, width), f32),
-    ]
-    return pl.pallas_call(
+    ] + [jax.ShapeDtypeStruct((width // 4, count), bf16)] * 4
+    results = pl.pallas_call(
         combine_back_kernel,
         out_shape=shapes,
-        in_specs=[smem_spec()] + [vmem_spec()] * 19,
+        in_specs=[smem_spec()] + [vmem_spec()] * 15,
         out_specs=[vmem_spec()] * len(shapes),
-        scratch_shapes=[pltpu.VMEM((hot.shape[0], width), bf16) for hot in hots],
+        scratch_shapes=[pltpu.VMEM((hot.shape[0], width), bf16) for hot in hots]
+        + [pltpu.VMEM((width, count), bf16)],
         compiler_params=params(60),
         name="combine_back",
-        cost_estimate=cost(13),
-    )(own, *hots, *picks, residual, dy, gates, routes_t, router_t, gain, w_out, *parts, *slots)
-
-
-def combine_kernel(p0a, p1a, p0b, p1b, residual_ref, gates_ref, out_a, out_b, y_ref, buf_a, buf_b):
-    for out, buf in ((out_a, buf_a), (out_b, buf_b)):
-        size = out.shape[1]
-        for e in range(out.shape[0]):
-            buf[e * size : (e + 1) * size, :] = out[e]
+        cost_estimate=cost(11),
+    )(own, *hots, *picks, residual, dy, gates, routes_t, router_t, gain, w_out, *slots)
+    return results[0], results[1], results[2], results[3:]
+
+
+def out_grad_kernel(t0, t1, t2, t3, branch_ref, keep_ref, give_ref):
+    branch = branch_ref[...]
+    keep_ref[0] = mm(t0[...], branch)
+    keep_ref[1] = mm(t2[...], branch)
+    give_ref[0] = mm(t1[...], branch).astype(bf16)
+    give_ref[1] = mm(t3[...], branch).astype(bf16)
+
+
+def out_grads(parts, branch):
+    shape = (2, parts[0].shape[0], branch.shape[1])
+    return pl.pallas_call(
+        out_grad_kernel,
+        out_shape=[jax.ShapeDtypeStruct(shape, f32), jax.ShapeDtypeStruct(shape, bf16)],
+        in_specs=[vmem_spec()] * 5,
+        out_specs=[vmem_spec()] * 2,
+        compiler_params=params(60),
+        name="w_out_grads",
+        cost_estimate=cost(3),
+    )(*parts, branch)
+
+
+def combine_kernel(p0a, p1a, p0b, p1b, residual_ref, gates_ref, out_ref, y_ref, buf_a, buf_b):
+    experts, capacity, _ = out_ref.shape
+    for (start, size), buf in zip(halves_of(capacity), (buf_a, buf_b)):
+        for e in range(experts):
+            buf[e * size : (e + 1) * size, :] = out_ref[e, start : start + size, :]
     total = residual_ref[...]
     for k, (pick_a, pick_b) in enumerate(((p0a, p0b), (p1a, p1b))):
         rows = mm(pick_a[...], buf_a[...]) + mm(pick_b[...], buf_b[...])
@@ -701,27 +762,29 @@
     y_ref[...] = total.astype(bf16)
 
 
-def combine(outs, picks, residual, gates):
-    width = residual.shape[1]
+def combine(out, picks, residual, gates):
+    experts, capacity, width = out.shape
     return pl.pallas_call(
         combine_kernel,
         out_shape=jax.ShapeDtypeStruct(residual.shape, bf16),
-        in_specs=[vmem_spec()] * 8,
+        in_specs=[vmem_spec()] * 7,
         out_specs=vmem_spec(),
-        scratch_shapes=[pltpu.VMEM((out.shape[0] * out.shape[1], width), bf16) for out in outs],
+        scratch_shapes=[
+            pltpu.VMEM((experts * size, width), bf16) for _, size in halves_of(capacity)
+        ],
         compiler_params=params(60),
         name="combine",
         cost_estimate=cost(6),
-    )(*picks, residual, gates, *outs)
-
-
-def spread_kernel(places_ref, d0, d1, d2, w_ref, near_out, last_out, far_out, own_out, d_buf):
+    )(*picks, residual, gates, out)
+
+
+def spread_kernel(places_ref, d01, d2, w_ref, near_out, last_out, far_out, own_out, d_buf):
     step = pl.program_id(0)
     heads = d_buf.shape[0] // (3 * HEAD_DIM)
-    for c, part in enumerate((d0, d1, d2)):
+    for c, (part, n) in enumerate(((d01, 0), (d01, 3), (d2, 0))):
         for t in range(3):
             start = (t * heads + c) * HEAD_DIM
-            d_buf[start : start + HEAD_DIM, :] = part[t * HEAD_DIM : (t + 1) * HEAD_DIM, :]
+            d_buf[start : start + HEAD_DIM, :] = part[(n + t) * HEAD_DIM : (n + t + 1) * HEAD_DIM, :]
     dn = mm(d_buf[...], w_ref[...], TN)
     for n, out in enumerate((near_out, last_out, far_out, own_out)):
 
@@ -731,11 +794,11 @@
 
 
 def spread(places, parts, w_t):
-    rows, row_len = parts[0].shape
+    row_len = parts[0].shape[1]
     cols, width = w_t.shape
     steps = places.shape[0]
     count = row_len // steps
-    tile = pl.BlockSpec((rows, count), lambda g, places: (0, places[g]))
+    tiles = [pl.BlockSpec((p.shape[0], count), lambda g, places: (0, places[g])) for p in parts]
 
     def whole(shape):
         return pl.BlockSpec(shape, lambda g, places: (0, 0), pipeline_mode=pl.Buffered(1))
@@ -746,7 +809,7 @@
         grid_spec=pltpu.PrefetchScalarGridSpec(
             num_scalar_prefetch=1,
             grid=(steps,),
-            in_specs=[tile] * 3 + [whole((cols, width))],
+            in_specs=tiles + [whole((cols, width))],
             out_specs=[whole((count, width))] * 4,
             scratch_shapes=[pltpu.VMEM((cols, count), bf16)],
         ),
@@ -754,6 +817,37 @@
         name="spread_back",
         cost_estimate=cost(8),
     )(places, *parts, w_t)
+
+
+def pack_kernel(special, g_ref, keep_ref, near_ref, far_ref, small_ref, out_ref):
+    exps, _, width = out_ref.shape
+    rows = g_ref.shape[2]
+    gout = keep_ref[0] + near_ref[0].astype(f32) + far_ref[...].astype(f32)
+    out_rows = gout.shape[0] // exps
+    begin = 2 * rows + out_rows
+    pad = out_ref.shape[1] - begin - 2 * special
+    for e in range(exps):
+        out_ref[e, 0:rows] = g_ref[0, e]
+        out_ref[e, rows : 2 * rows] = g_ref[1, e]
+        high, mid, _ = split_three(small_ref[e * special : (e + 1) * special, :])
+        parts = [gout[e * out_rows : (e + 1) * out_rows], high.astype(f32), mid.astype(f32)]
+        if pad:
+            parts.append(jnp.zeros((pad, width), f32))
+        out_ref[e, 2 * rows :] = jnp.concatenate(parts, axis=0).astype(bf16)
+
+
+def pack(grads, keep, near, far, small, special):
+    _, exps, rows, width = grads.shape
+    total = 2 * rows + keep.shape[1] // exps + 2 * special
+    return pl.pallas_call(
+        functools.partial(pack_kernel, special),
+        out_shape=jax.ShapeDtypeStruct((exps, total + -total % 8, width), bf16),
+        in_specs=[vmem_spec()] * 5,
+        out_specs=vmem_spec(),
+        compiler_params=params(50),
+        name="pack_sums",
+        cost_estimate=cost(2),
+    )(grads, keep, near, far, small)
 
 
 def fold_kernel(special, taken, moved_ref, *refs):
@@ -794,17 +888,16 @@
 
 
 def lay_out_kernel(rows, own_ref, *refs):
-    arrays, (w_ref, gain_ref, grad_ref, ggain_ref, b0, b1, b2, sems) = refs[:12], refs[12:]
+    arrays, (w_ref, gain_ref, grad_ref, ggain_ref, b0, b1, sems) = refs[:8], refs[8:]
     hids, exps = b0.shape[0], b0.shape[1]
-    bufs = (b0, b1, b2)
     step = pl.program_id(0)
     block = grad_ref.shape[0]
 
     @pl.when(step == 0)
     def fetch():
         copies = [
-            pltpu.make_async_copy(arrays[4 * c + j], bufs[c].at[own_ref[0] ^ j], sems.at[c, j])
-            for c in range(3)
+            pltpu.make_async_copy(arrays[4 * c + j], buf.at[own_ref[0] ^ j], sems.at[c, j])
+            for c, buf in enumerate((b0, b1))
             for j in range(hids)
         ]
         for copy in copies:
@@ -815,8 +908,8 @@
     cols = pl.ds(pl.multiple_of(step * block, block), block)
     blocks = {}
     for h in range(hids):
-        for c, buf in enumerate(bufs):
-            pieces = [buf[h, e, 0:rows, cols].astype(f32) for e in range(exps)]
+        for c, (buf, start) in enumerate(((b0, 0), (b0, rows), (b1, 0))):
+            pieces = [buf[h, e, start : start + rows, cols].astype(f32) for e in range(exps)]
             blocks[h, c] = jnp.concatenate(pieces, axis=0)
     stacked = [
         blocks[h, c][t * HEAD_DIM : (t + 1) * HEAD_DIM]
@@ -842,10 +935,10 @@
             jax.ShapeDtypeStruct((1, width), f32),
         ],
         grid=(width // block,),
-        in_specs=[smem_spec()] + [pl.BlockSpec(memory_space=pl.ANY)] * 12 + [tile, row],
+        in_specs=[smem_spec()] + [pl.BlockSpec(memory_space=pl.ANY)] * 8 + [tile, row],
         out_specs=[tile, row],
         scratch_shapes=[pltpu.VMEM((4,) + chunk[0].shape, bf16) for chunk in chunks]
-        + [pltpu.SemaphoreType.DMA((3, 4))],
+        + [pltpu.SemaphoreType.DMA((2, 4))],
         compiler_params=params(50),
         name="lay_out_qkv",
         cost_estimate=cost(10),
@@ -893,6 +986,31 @@
         jnp.where(live_mask, first_next, first_moment),
         jnp.where(live_mask, second_next, second_moment),
     )
+
+
+def expert_update_kernel(live_ref, own_ref, near_ref, far_ref, weight_ref, first_ref, second_ref, *outs):
+    live = live_ref[0] > 0
+    grad = own_ref[0] + near_ref[0].astype(f32) + far_ref[...].astype(f32)
+    grad = jnp.where(live, grad, 0.0)
+    outs[0][...] = grad
+    updated = adam_update(weight_ref[...], grad, first_ref[...], second_ref[...], live)
+    for out, value in zip(outs[1:], updated):
+        out[...] = value
+
+
+def expert_update(live, own, near, number, far, weight, first_moment, second_moment, block=128):
+    tile = pl.BlockSpec((block, weight.shape[1]), lambda g: (g, 0))
+    stacked = pl.BlockSpec((1, block, weight.shape[1]), lambda g: (number, g, 0))
+    return pl.pallas_call(
+        expert_update_kernel,
+        out_shape=[jax.ShapeDtypeStruct(weight.shape, f32)] * 4,
+        grid=(weight.shape[0] // block,),
+        in_specs=[smem_spec(), stacked, stacked] + [tile] * 4,
+        out_specs=[tile] * 4,
+        compiler_params=params(60),
+        name="expert_update",
+        cost_estimate=cost(8),
+    )(live, own, near, far, weight, first_moment, second_moment)
 
 
 def tie(value, other):
@@ -945,7 +1063,8 @@
     heads = group // HEAD_DIM
     is_new = exp_index >= frozen_count
 
-    x_far = swap(x_own, "hid", 2)
+    x_halves = [x_own[: count // 2], x_own[count // 2 :]]
+    x_far = [swap(half, "hid", 2) for half in x_halves]
     x_near = swap(x_own, "hid", 1)
     routes_t = routes[0].T
     hots, picks, dy_send = make_tables(routes_t, dy, experts, capacity)
@@ -960,28 +1079,26 @@
     up_low = up_w[0].astype(bf16)
     down_low = down_w[0].astype(bf16)
     router_t = router_w.T
+    first = project_qkv(own, (x_own, x_near), gain_attn[None], w_qkv)
     x_far, (info, dy_send, up_low, down_low, router_t, routes_t) = lax.optimization_barrier(
         (x_far, (info, dy_send, up_low, down_low, router_t, routes_t))
     )
-    x_last = swap(x_far, "hid", 1)
-    blocks = (x_own, x_near, x_far, x_last)
+    x_last = [swap(half, "hid", 1) for half in x_far]
     dy_all = exchange(dy_send, "exp")
 
     up_far = swap(up_low, "hid", 2)
-    up_near, down_near = swap(up_low, "hid", 1), swap(down_low, "hid", 1)
-
-    a_one, qkv_t, keys, values, w_t = project_qkv(own, blocks, gain_attn[None], w_qkv)
-    out_heads, out_low, logs = attend(info, keys, qkv_t)
-    out_low, (up_far, up_near, down_near) = lax.optimization_barrier(
-        (out_low, (up_far, up_near, down_near))
-    )
-
-    def piece_of(value, j):
-        return lax.dynamic_slice_in_dim(value, (hid ^ j) * count, count, 1)
-
-    att_parts = [piece_of(out_low, 0)] + [
-        swap(piece_of(out_low, j), "hid", j) for j in range(1, hid_count)
-    ]
+    up_near, down_near = (swap(tie(low, x_last), "hid", 1) for low in (up_low, down_low))
+
+    second = project_qkv(own, (*x_far, *x_last), gain_attn[None], w_qkv)
+    w_t = first[8]
+    a_parts, qkv_parts, k_parts, v_parts = (
+        (*first[n : n + 2], *second[n : n + 2]) for n in (0, 2, 4, 6)
+    )
+    out_heads, logs, keys, pieces = attend(info, own, k_parts, qkv_parts)
+    pieces, (up_far, up_near, down_near) = lax.optimization_barrier(
+        (pieces, (up_far, up_near, down_near))
+    )
+    att_parts = [pieces[0]] + [swap(pieces[j], "hid", j) for j in range(1, hid_count)]
     att_parts, down_low = lax.optimization_barrier((att_parts, down_low))
     down_far = swap(down_low, "hid", 2)
 
@@ -994,63 +1111,72 @@
     sends = tie(sends, dy_all)
     x_rows = [exchange(send, "exp") for send in sends]
 
-    starts = [start for start, _ in halves_of(capacity)]
-    results = [run_experts(start, x, dy_all, weights) for start, x in zip(starts, x_rows)]
-    outs, slots, acts, dpres = zip(*results)
+    results = [None]
+    for half, ((start, size), x) in enumerate(zip(halves_of(capacity), x_rows)):
+        results.append(run_experts(half, start, size, x, dy_all, weights, results[-1]))
+    outs = results[2][0]
+    slots, acts, dpres = ([r[n] for r in results[1:]] for n in (1, 2, 3))
     slot_back = [exchange(slot, "exp") for slot in slots]
 
-    own_part, near_part, far_part = weight_grads(x_rows, dy_all, acts, dpres)
+    own_part, near_part, far_up, far_down = weight_grads(x_rows, dy_all, acts, dpres)
     slot_back, near_part = lax.optimization_barrier((slot_back, near_part))
     near_part = swap(near_part, "hid", 1)
 
-    dres, datt, gout, small = combine_back(
-        own, slot_back, hots, picks, residual, dy, gates, routes_t, router_t,
-        gain_moe[None], w_out, att_parts,
-    )
-
-    datt, near_part = lax.optimization_barrier((datt, near_part))
-
-    def heads_of(value, j):
-        return lax.dynamic_slice_in_dim(value, (hid ^ j) * group, group, 0)
-
-    datt_parts = [heads_of(datt, 0)] + [
-        swap(heads_of(datt, j), "hid", j) for j in range(1, hid_count)
-    ]
-
-    gout, small = tie((gout, small), datt_parts)
-
-    gout = gout.reshape(hid_count, width // hid_count, width)
-    for d in (1, 2):
-        gout = split_sum(gout, "hid", d)
-        small = small + swap(small, "hid", d)
-    far_part, gout, small = lax.optimization_barrier((far_part, gout, small))
-    far_part = swap((far_part + near_part[2:].astype(f32)).astype(bf16), "hid", 2)
+    dres, branch, small, datt_parts = combine_back(
+        own, slot_back, hots, picks, residual, dy, gates, routes_t, router_t, gain_moe[None], w_out
+    )
+    out_back = exchange(tie(outs, slot_back), "exp")
+    datt_parts, near_part = lax.optimization_barrier((datt_parts, near_part))
+    datt_parts = [datt_parts[0]] + [swap(datt_parts[j], "hid", j) for j in range(1, hid_count)]
+    gout, gout_near = out_grads(att_parts, branch)
+
     out_rows = width // (hid_count * exp_count)
     small_rows = -(-(experts + 1) // exp_count)
     missing = max(0, exp_count * small_rows - small.shape[0])
-    small = jnp.pad(small, ((0, missing), (0, 0)))[: exp_count * small_rows]
-    small = small.reshape(exp_count, small_rows, width)
-    gout = gout.reshape(exp_count, out_rows, width).astype(bf16)
-
+    small = jnp.pad(small, ((0, missing), (0, 0)))
+    gout_near = swap(gout_near, "hid", 1)
+    small = small + swap(small, "hid", 1)
+    far_up = (far_up + near_part[2].astype(f32)).astype(bf16)
+    far_down = (far_down + near_part[3].astype(f32)).astype(bf16)
+    far_up, far_down = tie((far_up, far_down), datt_parts)
+    far_up = swap(far_up, "hid", 2)
     rows = 3 * HEAD_DIM // exp_count
-    chunks, dqkv = [], []
-    for h in range(heads):
-        if h == 1:
-            out_first = exchange(tie(outs[0], slot_back), "exp")
-            chunks[0] = jnp.concatenate([chunks[0], gout, *halves(small)], axis=1)
-            chunks[0], out_first = lax.optimization_barrier((chunks[0], out_first))
-            first = exchange(pad_rows(chunks[0]), "exp")
-        if h == 2:
-            datt_parts, first = lax.optimization_barrier((datt_parts, first))
-        dqkv_h, grad_h = attend_back(
-            h, exp_count, info, own, keys, values, qkv_t, datt_parts, out_heads, logs, a_one
-        )
-        dqkv.append(dqkv_h)
-        chunks.append(grad_h)
+    given = (info, own, keys, v_parts, qkv_parts, datt_parts, out_heads, logs, a_parts)
+    dqkv_first, grads_first = attend_back(0, heads - 1, exp_count, *given)
+    gout_near, small = tie((gout_near, small), dqkv_first)
+    small = small + swap(small, "hid", 2)
+    gout_far = swap((gout[1] + gout_near[1].astype(f32)).astype(bf16), "hid", 2)
+    packed = pack(grads_first, gout, gout_near, gout_far, small, small_rows)
+    packed, out_back, far_up = lax.optimization_barrier((packed, out_back, far_up))
+    far_down = swap(tie(far_down, (gout_far, small)), "hid", 2)
+    first = exchange(packed, "exp")
+    dqkv_last, grads_last = attend_back(heads - 1, 1, exp_count, *given)
+    dqkv = [dqkv_first, dqkv_last]
+    first_rows = 2 * rows + out_rows + 2 * small_rows
+
+    first_sums = fold(first, first_rows, small_rows, [grads_last[0]])
+    second = exchange(first_sums, "exp")
+
+    dqkv, far_down = tie((dqkv, far_down), first_sums)
     places = jnp.stack([hid ^ j for j in (1, 3, 2, 0)]).astype(jnp.int32)
     near_dn, last_dn, far_dn, own_dn = spread(places, dqkv, w_t)
     near_dn, last_dn = swap(near_dn, "hid", 1), swap(last_dn, "hid", 1)
-    far_dn = swap((far_dn + last_dn.astype(f32)).astype(bf16), "hid", 2)
+    far_dn = (far_dn + last_dn.astype(f32)).astype(bf16)
+    out_back, far_up = tie((out_back, far_up), far_dn)
+    far_dn = swap(far_dn, "hid", 2)
+    start = 3 * rows + out_rows
+    small = second[:, start : start + small_rows].astype(f32)
+    small = small + second[:, start + small_rows : start + 2 * small_rows].astype(f32)
+    small = small.reshape(exp_count * small_rows, width)
+
+    out_tokens = combine(out_back, picks, residual, gates)
+    live = is_new.astype(jnp.int32).reshape(1)
+    grad_up, up_next, up_first_next, up_second_next = expert_update(
+        live, own_part, near_part, 0, far_up, up_w[0], up_first[0], up_second[0]
+    )
+    second, out_tokens, up_next = lax.optimization_barrier((second, out_tokens, up_next))
+    last_sums = fold(second, rows, 0)
+    far_dn, far_down = tie((far_dn, far_down), last_sums)
     dnormed = own_dn + near_dn.astype(f32) + far_dn.astype(f32)
     x = x_own.astype(f32)
     scale = lax.rsqrt(jnp.mean(x * x, axis=-1, keepdims=True) + norm_eps)
@@ -1059,29 +1185,14 @@
     grad_tokens = (
         dres + scale * (scaled - unit * jnp.mean(scaled * unit, axis=-1, keepdims=True))
     ).astype(bf16)
-
-    first_rows = rows + out_rows + 2 * small_rows
-    second = exchange(fold(first, first_rows, small_rows, [chunks[1]]), "exp")
-    third = exchange(fold(second, rows, 0, [chunks[2]]), "exp")
-    fourth = exchange(fold(third, rows, 0), "exp")
-    out_second = exchange(tie(outs[1], fourth), "exp")
-    out_tokens = combine((out_first, out_second), picks, residual, gates)
-    gathered = [
-        gather_hid(value)
-        for value in (second[:, rows : 2 * rows + out_rows], third[:, rows : 2 * rows], fourth)
-    ]
-    grad_qkv, grad_gain_attn = lay_out(own, gathered, rows, w_qkv, gain_attn[None])
-    grad_out_proj = lay_out_rest(own, gathered[0], rows, width)
-    start = 2 * rows + out_rows
-    small = second[:, start : start + small_rows].astype(f32)
-    small = small + second[:, start + small_rows : start + 2 * small_rows].astype(f32)
-    small = small.reshape(exp_count * small_rows, width)
-    far_part = [far_part[0], tie(far_part[1], fourth)]
-    grad_up, grad_down = (
-        jnp.where(is_new, own_part[n] + near_part[n].astype(f32) + far_part[n].astype(f32), 0.0)
-        for n in range(2)
-    )
-    grad_gain_attn = grad_gain_attn[0]
+    third = exchange(last_sums, "exp")
+    gathered = gather_hid(second[:, rows:start])
+    grad_down = own_part[1] + near_part[1].astype(f32) + far_down.astype(f32)
+    grad_down = jnp.where(is_new, grad_down, 0.0)
+    down_next, down_first_next, down_second_next = adam_update(
+        down_w[0], grad_down, down_first[0], down_second[0], is_new
+    )
+    grad_out_proj = lay_out_rest(own, gathered, 2 * rows, width)
     grad_gain_moe = small[experts]
     live_columns = (jnp.arange(experts, dtype=jnp.int32) >= frozen_count)[None, :]
     grad_router = jnp.where(live_columns, small[:experts].T, 0.0)
@@ -1089,12 +1200,13 @@
         router_w[:, frozen_count:], grad_router[:, frozen_count:], router_first, router_second, True
     )
     router_next = jnp.concatenate([router_w[:, :frozen_count], router_new], axis=1)
-    up_next, up_first_next, up_second_next = adam_update(
-        up_w[0], grad_up, up_first[0], up_second[0], is_new
-    )
-    down_next, down_first_next, down_second_next = adam_update(
-        down_w[0], grad_down, down_first[0], down_second[0], is_new
-    )
+    near, far = swap(third, "hid", 1), swap(third, "hid", 2)
+    ready = (grad_out_proj, grad_router, router_next, router_first_next, router_second_next)
+    far, ready = lax.optimization_barrier((far, ready))
+    grad_out_proj, grad_router, router_next, router_first_next, router_second_next = ready
+    gathered = (gathered, (third, near, far, swap(far, "hid", 1)))
+    grad_qkv, grad_gain_attn = lay_out(own, gathered, rows, w_qkv, gain_attn[None])
+    grad_gain_attn = grad_gain_attn[0]
     return (
         out_tokens[None],
         grad_tokens[None],

time: 431 us -> 415 us (0.963)
  starting transfers between devices: 90.1 us -> 71.2 us
  other arithmetic: 47.6 us -> 31.8 us
  waiting for transfers between devices: 74.8 us -> 89.3 us
  Pallas kernels: 192 us -> 201 us
  local copies, waits for them, and re-layouts: 20 us -> 13 us
    select_n x2 -> x0, other arithmetic: 13.2 us -> none  [the longest x1 7.63 us: adam_update(): jnp.where(live_mask, first_next, first_moment)]
    pallas_call x6 -> x9, Pallas kernels: 94.4 us -> 107 us  [the longest x2 48.7 us: run_experts(): pl.pallas_call(functools.partial(expert_kernel, half, 0), out_shape=[shap...]
    ppermute x33, waiting for transfers between devices: 32.2 us -> 43.5 us  [swap(): return lax.ppermute(value, axis, [(i, i ^ distance) for i in range(count)])]
    all_to_all x11 -> x9, starting transfers between devices: 57.3 us -> 46.5 us  [exchange(): return lax.all_to_all(value, axis, split_axis=0, concat_axis=0, tiled=True)]
    ppermute x33, starting transfers between devices: 32.7 us -> 24.7 us  [swap(): return lax.ppermute(value, axis, [(i, i ^ distance) for i in range(count)])]
    all_to_all x11 -> x9, waiting for transfers between devices: 42.6 us -> 45.9 us  [exchange(): return lax.all_to_all(value, axis, split_axis=0, concat_axis=0, tiled=True)]
    unnamed x84 -> x88, local copies, waits for them, and re-layouts: 9.78 us -> 9.78 us
  transfers between devices with their start and end apart: 44 -> 42, of which waited for: 16 -> 19; matrix products, arithmetic and copies ran while one was open for 13% -> 8% of each run, Pallas kernels for 44% -> 47%
where the time goes in v3:
time: 415 us; the launch traced here: 408 us
  Pallas kernels  201 us (48%)
  waiting for transfers between devices  89.3 us (22%)
  starting transfers between devices  71.2 us (17%)
  other arithmetic  31.8 us (8%)
  local copies, waits for them, and re-layouts  13 us (3%)
    pallas_call x2, Pallas kernels, run_experts(): pl.pallas_call(functools.partial(expert_kernel, half, 0), out_shape=[shap...  48.7 us
    all_to_all x9, starting transfers between devices, exchange(): return lax.all_to_all(value, axis, split_axis=0, concat_axis=0, tiled=True)  46.5 us
    all_to_all x9, waiting for transfers between devices, exchange(): return lax.all_to_all(value, axis, split_axis=0, concat_axis=0, tiled=True)  45.9 us
    ppermute x33, waiting for transfers between devices, swap(): return lax.ppermute(value, axis, [(i, i ^ distance) for i in range(count)])  43.5 us
    pallas_call x2, Pallas kernels, attend_back(): pl.pallas_call(functools.partial(attend_back_kernel, block, first), out_s...  31 us
    pallas_call x1, Pallas kernels, weight_grads(): pl.pallas_call(weight_kernel, out_shape=[jax.ShapeDtypeStruct((2, width,...  26.9 us
    ppermute x33, starting transfers between devices, swap(): return lax.ppermute(value, axis, [(i, i ^ distance) for i in range(count)])  24.7 us
    pallas_call x1, Pallas kernels, attend(): pl.pallas_call(functools.partial(attend_kernel, block), out_shape=[jax.Sh...  17.5 us
  transfers between devices with their start and end apart: 42, of which 19 were waited for; matrix products, arithmetic and copies ran while one was open for 8% of the time, Pallas kernels for 47%

profile of v3, /device:TPU:1, one launch (start us, length us, event | category | flops | bytes accessed | tf_op | source)
XLA Modules:
  0.0 408.1 jit_solution(17784841521751893275)
XLA Ops:
  6.2 5.1 %slot_tables.1 = (bf16[768,512]{1,0:T(8,128)(2,1)}, bf16[768,512]{1,0:T(8,128)(2,1)}, bf16[512,768]{1,0:T(8,128)(2,1)}, bf16[512,768]{1,0:T(8,128)(2,1)}, bf16[5...) custom-call(s32[2,512]{1,0:T(2,128)} %bitcast.93, bf16[512,768]{1,0:T(8,128)(2,1)} %bitcast.86), custom_call_target="tpu_custom_call" | custom-call | flops 11000000 | bytes 30000 | tf_op jit(solution)/shard_map/slot_tables/pallas_call | solution.py:127
  16.5 4.9 %collective-permute-done.1.refs_1_ = bf16[256,768]{1,0:T(8,128)(2,1)S(1)} collective-permute-done((bf16[256,768]{1,0:T(8,128)(2,1)S(1)}, bf16[256,768]{1,0:T(8,128)(2,1)S(1)}, u32[]{:S(2)}, u32[]{:S(2)}) %collective-permute-start.1) | collective-permute-done | bytes 393248 | tf_op jit(solution)/shard_map/ppermute | solution.py:40
  22.1 5.6 %all-to-all-start = ((bf16[8,192,768]{2,1,0:T(8,128)(2,1)}), bf16[8,192,768]{2,1,0:T(8,128)(2,1)S(1)}, u32[]{:S(2)}, u32[]{:S(2)}) async-start(bf16[8,192,768]{2,1,0:T(8,128)(2,1)} %get-tuple-element.193), calls=%async_computation | async-start | bytes 4718592 | tf_op jit(solution)/shard_map/all_to_all | solution.py:1021
  33.8 6.3 %norm_qkv.3 = (bf16[512,768]{1,0:T(8,128)(2,1)}, bf16[512,768]{1,0:T(8,128)(2,1)}, bf16[576,512]{1,0:T(8,128)(2,1)}, bf16[576,512]{1,0:T(8,128)(2,1)}, bf16[512,...) custom-call(s32[2]{0:T(128)} %pad_add_fusion.1.own_ref, ...), custom_call_target="tpu_custom_call" | custom-call | flops 11000000 | bytes 30000 | tf_op jit(solution)/shard_map/norm_qkv/pallas_call | solution.py:176
  40.1 6.5 %norm_qkv.2 = (bf16[512,768]{1,0:T(8,128)(2,1)}, bf16[512,768]{1,0:T(8,128)(2,1)}, bf16[576,512]{1,0:T(8,128)(2,1)}, bf16[576,512]{1,0:T(8,128)(2,1)}, bf16[512,...) custom-call(s32[2]{0:T(128)} %pad_add_fusion.1.own_ref, ...), custom_call_target="tpu_custom_call" | custom-call | flops 11000000 | bytes 30000 | tf_op jit(solution)/shard_map/norm_qkv/pallas_call | solution.py:176
  46.6 17.5 %attend.1 = (f32[192,2048]{1,0:T(8,128)}, f32[3,1,2048]{2,1,0:T(1,128)}, bf16[2048,192]{1,0:T(8,128)(2,1)}, bf16[192,512]{1,0:T(8,128)(2,1)}, bf16[192,512]{1,0:...) custom-call(s32[3]{0:T(128)} %pad_add_fusion.info_ref, s32[2]{0:T(128)} %pad_add_fusion.1.own_ref, ...), custom_call_target="tpu_custom_call" | custom-call | flops 11000000 | bytes 30000 | tf_op jit(solution)/shard_map/attend/pallas_call | solution.py:275
  70.5 4.8 %collective-permute-done.10.t3 = bf16[192,512]{1,0:T(8,128)(2,1)S(1)} collective-permute-done((bf16[192,512]{1,0:T(8,128)(2,1)}, bf16[192,512]{1,0:T(8,128)(2,1)S(1)}, u32[]{:S(2)}, u32[]{:S(2)}) %collective-permute-start.10) | collective-permute-done | bytes 196640 | tf_op jit(solution)/shard_map/ppermute | solution.py:40
  76.0 8.1 %project_dispatch.1 = (f32[512,768]{1,0:T(8,128)}, f32[2,512]{1,0:T(2,128)}, bf16[8,96,768]{2,1,0:T(8,128)(2,1)}, bf16[8,104,768]{2,1,0:T(8,128)(2,1)}) custom-call(s32[2]{0:T(128)} %pad_add_fusion.1.own_ref, bf16[192,512]{1,0:T(8,128)(2,1)} %get-tuple-element.183.t0, bf16[192,512]{1,0:T(8,128)(2,1)} %copy-done.29, bf16[192,512]{1,0:T(8,128)(2,1)} %copy-done.30, ...), custom_call_target="tpu_custom_call" | custom-call | flops 11000000 | bytes 30000 | tf_op jit(solution)/shard_map/project_dispatch/pallas_call | solution.py:452
  84.1 6.0 %all-to-all-start.1 = ((bf16[8,96,768]{2,1,0:T(8,128)(2,1)}), bf16[8,96,768]{2,1,0:T(8,128)(2,1)}, u32[]{:S(2)}, u32[]{:S(2)}) async-start(bf16[8,96,768]{2,1,0:T(8,128)(2,1)} %get-tuple-element.194), calls=%async_computation.1 | async-start | bytes 2359296 | tf_op jit(solution)/shard_map/all_to_all | solution.py:1021
  91.3 27.7 %all-to-all-done.1.x_ref.x_a = bf16[8,96,768]{2,1,0:T(8,128)(2,1)} async-done(((bf16[8,96,768]{2,1,0:T(8,128)(2,1)}), bf16[8,96,768]{2,1,0:T(8,128)(2,1)}, u32[]{:S(2)}, u32[]{:S(2)}) %all-to-all-start.1) | async-done | bytes 1179680 | tf_op jit(solution)/shard_map/all_to_all | solution.py:1021
  119.0 4.7 %all-to-all-start.3 = ((bf16[8,104,768]{2,1,0:T(8,128)(2,1)}), bf16[8,104,768]{2,1,0:T(8,128)(2,1)}, u32[]{:S(2)}, u32[]{:S(2)}) async-start(bf16[8,104,768]{2,1,0:T(8,128)(2,1)} %get-tuple-element.202), calls=%async_computation.3 | async-start | bytes 2555904 | tf_op jit(solution)/shard_map/all_to_all | solution.py:1021
  129.9 24.3 %experts.2 = (bf16[8,192,768]{2,1,0:T(8,128)(2,1)}, bf16[8,96,768]{2,1,0:T(8,128)(2,1)}, bf16[4,768,768]{2,1,0:T(8,128)(2,1)}, bf16[4,768,768]{2,1,0:T(8,128)(2,1)}, bf16[8,8,128]{2,1,0:T(8,128)(2,1)}) custom-call(bf16[8,96,768]{2,1,0:T(8,128)(2,1)} %all-to-all-done.1.x_ref.x_a, bf16[8,192,768]{2,1,0:T(8,128)(2,1)} %copy-done.13, ...), custom_call_target="tpu_custom_call" | custom-call | flops 2750000128 | bytes 7500000 | tf_op jit(solution)/shard_map/experts/pallas_call | solution.py:574
  154.2 5.7 %all-to-all-start.2 = ((bf16[8,96,768]{2,1,0:T(8,128)(2,1)}), bf16[8,96,768]{2,1,0:T(8,128)(2,1)S(1)}, u32[]{:S(2)}, u32[]{:S(2)}) async-start(bf16[8,96,768]{2,1,0:T(8,128)(2,1)} %get-tuple-element.201), calls=%async_computation.2 | async-start | bytes 2359296 | tf_op jit(solution)/shard_map/all_to_all | solution.py:1021
  159.9 24.4 %experts.3 = (bf16[8,192,768]{2,1,0:T(8,128)(2,1)}, bf16[8,104,768]{2,1,0:T(8,128)(2,1)}, bf16[4,768,768]{2,1,0:T(8,128)(2,1)}, bf16[4,768,768]{2,1,0:T(8,128)(2,1)}) custom-call(bf16[8,104,768]{2,1,0:T(8,128)(2,1)} %all-to-all-done.3.x_ref.x_b, bf16[8,192,768]{2,1,0:T(8,128)(2,1)} %copy-done.13, ...), custom_call_target="tpu_custom_call", output_to_operand_aliasing={{0}: (11, {})} | custom-call | flops 2750000128 | bytes 7500000 | tf_op jit(solution)/shard_map/experts/pallas_call | solution.py:574
  189.0 4.3 %all-to-all-start.4 = ((bf16[8,104,768]{2,1,0:T(8,128)(2,1)}), bf16[8,104,768]{2,1,0:T(8,128)(2,1)S(1)}, u32[]{:S(2)}, u32[]{:S(2)}) async-start(bf16[8,104,768]{2,1,0:T(8,128)(2,1)} %get-tuple-element.205), calls=%async_computation.4 | async-start | bytes 2555904 | tf_op jit(solution)/shard_map/all_to_all | solution.py:1021
  193.3 26.9 %expert_weight_grads.1 = (f32[2,768,768]{2,1,0:T(8,128)}, bf16[4,768,768]{2,1,0:T(8,128)(2,1)}, f32[768,768]{1,0:T(8,128)}, f32[768,768]{1,0:T(8,128)}) custom-call(bf16[8,192,768]{2,1,0:T(8,128)(2,1)} %copy-done.13, bf16[8,96,768]{2,1,0:T(8,128)(2,1)} %all-to-all-done.1.x_ref.x_a, bf16[8,104,768]{2,1,0:T(8,128)(2,1)} %all-to-all-done.3.x_ref.x_b, ...), custom_call_target="tpu_custom_call" | custom-call | flops 2750000128 | bytes 7500000 | tf_op jit(solution)/shard_map/expert_weight_grads/pallas_call | solution.py:641
  229.1 11.6 %combine_back.1 = (f32[512,768]{1,0:T(8,128)}, bf16[512,768]{1,0:T(8,128)(2,1)}, f32[16,768]{1,0:T(8,128)}, bf16[192,512]{1,0:T(8,128)(2,1)}, bf16[192,512]{1,0:...) custom-call(s32[2]{0:T(128)} %pad_add_fusion.1.own_ref, bf16[768,512]{1,0:T(8,128)(2,1)} %get-tuple-element.165.hot_a, ...), custom_call_target="tpu_custom_call" | custom-call | flops 1210000000 | bytes 3300000 | tf_op jit(solution)/shard_map/combine_back/pallas_call | solution.py:718
  243.3 5.0 %fusion.2 = (bf16[768,768]{1,0:T(8,128)(2,1)}, bf16[768,768]{1,0:T(8,128)(2,1)}) fusion(f32[768,768]{1,0:T(8,128)} %get-tuple-element.240, bf16[4,768,768]{2,1,0:T(8,128)(2,1)} %collective-permute-done.14.near_ref, f32[768,768]{1,0:T(8,128)} %get-tuple-element.238), kind=kLoop, calls=%fused_computation.5 | loop fusion | flops 3538944 | bytes 9437184 | tf_op jit(solution)/shard_map/convert_element_type | solution.py:1140
  248.4 4.6 %collective-permute-done.17.refs_15_ = bf16[192,512]{1,0:T(8,128)(2,1)} collective-permute-done((bf16[192,512]{1,0:T(8,128)(2,1)}, bf16[192,512]{1,0:T(8,128)(2,1)}, u32[]{:S(2)}, u32[]{:S(2)}) %collective-permute-start.17) | collective-permute-done | bytes 196640 | tf_op jit(solution)/shard_map/ppermute | solution.py:40
  260.0 19.6 %attend_back.2 = (bf16[384,2048]{1,0:T(8,128)(2,1)}, bf16[2,8,24,768]{3,2,1,0:T(8,128)(2,1)}) custom-call(s32[3]{0:T(128)} %pad_add_fusion.info_ref, s32[2]{0:T(128)} %pad_add_fusion.1.own_ref, bf16[2048,192]{1,0:T(8,128)(2,1)} %get-tuple-element.160.k_ref, bf16[512,192]{1,0:T(8,128)(2,1)} %get-tuple-element.161.refs_0_, ...), custom_call_target="tpu_custom_call" | custom-call | flops 2420000000 | bytes 6600000 | tf_op jit(solution)/shard_map/attend_back/pallas_call | solution.py:352
  281.2 7.9 %collective-permute-done.21 = f32[16,768]{1,0:T(8,128)S(1)} collective-permute-done((f32[16,768]{1,0:T(8,128)}, f32[16,768]{1,0:T(8,128)S(1)}, u32[]{:S(2)}, u32[]{:S(2)}) %collective-permute-start.21) | collective-permute-done | bytes 49184 | tf_op jit(solution)/shard_map/ppermute | solution.py:40
  292.1 6.0 %all-to-all-start.6 = ((bf16[8,80,768]{2,1,0:T(8,128)(2,1)}), bf16[8,80,768]{2,1,0:T(8,128)(2,1)S(1)}, u32[]{:S(2)}, u32[]{:S(2)}) async-start(bf16[8,80,768]{2,1,0:T(8,128)(2,1)} %pack_sums.1), calls=%async_computation.6 | async-start | bytes 1966080 | tf_op jit(solution)/shard_map/all_to_all | solution.py:1021
  298.4 11.4 %attend_back.3 = (bf16[192,2048]{1,0:T(8,128)(2,1)}, bf16[1,8,24,768]{3,2,1,0:T(8,128)(2,1)}) custom-call(s32[3]{0:T(128)} %pad_add_fusion.info_ref, s32[2]{0:T(128)} %pad_add_fusion.1.own_ref, bf16[2048,192]{1,0:T(8,128)(2,1)} %get-tuple-element.160.k_ref, bf16[512,192]{1,0:T(8,128)(2,1)} %get-tuple-element.161.refs_0_, ...), custom_call_target="tpu_custom_call" | custom-call | flops 1210000000 | bytes 3300000 | tf_op jit(solution)/shard_map/attend_back/pallas_call | solution.py:352
  309.8 11.3 %all-to-all-done.6.moved_ref = bf16[8,80,768]{2,1,0:T(8,128)(2,1)S(1)} async-done(((bf16[8,80,768]{2,1,0:T(8,128)(2,1)}), bf16[8,80,768]{2,1,0:T(8,128)(2,1)S(1)}, u32[]{:S(2)}, u32[]{:S(2)}) %all-to-all-start.6) | async-done | bytes 983072 | tf_op jit(solution)/shard_map/all_to_all | solution.py:1021
  323.3 5.0 %all-to-all-start.7 = ((bf16[8,104,768]{2,1,0:T(8,128)(2,1)}), bf16[8,104,768]{2,1,0:T(8,128)(2,1)S(1)}, u32[]{:S(2)}, u32[]{:S(2)}) async-start(bf16[8,104,768]{2,1,0:T(8,128)(2,1)} %fold_sums.2), calls=%async_computation.7 | async-start | bytes 2555904 | tf_op jit(solution)/shard_map/all_to_all | solution.py:1021
  330.7 4.5 %spread_back.1 = (bf16[512,768]{1,0:T(8,128)(2,1)S(1)}, bf16[512,768]{1,0:T(8,128)(2,1)S(1)}, f32[512,768]{1,0:T(8,128)S(1)}, f32[512,768]{1,0:T(8,128)S(1)}) custom-call(s32[4]{0:T(128)S(1)} %pad_add_fusion.2.places_ref, bf16[384,2048]{1,0:T(8,128)(2,1)S(1)} %copy-done.9, bf16[192,2048]{1,0:T(8,128)(2,1)S(1)} %copy-done.12, bf16[576,768]{1,0:T(8,128)(2,1)S(1)} %copy-done.10), custom_call_target="tpu_custom_call" | custom-call | flops 880000000 | bytes 2400000 | tf_op jit(solution)/shard_map/spread_back/pallas_call | solution.py:806
  341.6 6.6 %combine.1 = bf16[512,768]{1,0:T(8,128)(2,1)} custom-call(bf16[512,768]{1,0:T(8,128)(2,1)} %get-tuple-element.167.p0a, bf16[512,768]{1,0:T(8,128)(2,1)} %get-tuple-element.168.p1a, bf16[512,768]{1,0:T(8,128)(2,1)} %get-tuple-element.169.p0b, bf16[512,768]{1,0:T(8,128)(2,1)} %get-tuple-element.170.p1b, f32[512,768]{1,0:T(8,128)} %get-tuple-element.189.residual_ref, ...), custom_call_target="tpu_custom_call" | custom-call | flops 660000000 | bytes 1800000 | tf_op jit(solution)/shard_map/combine/pallas_call | solution.py:767
  348.2 9.9 %expert_update.1 = (f32[768,768]{1,0:T(8,128)}, f32[768,768]{1,0:T(8,128)}, f32[768,768]{1,0:T(8,128)}, f32[768,768]{1,0:T(8,128)}) custom-call(s32[1]{0:T(128)} %bitcast.20.live_ref, f32[2,768,768]{2,1,0:T(8,128)} %get-tuple-element.255.own_ref, bf16[4,768,768]{2,1,0:T(8,128)(2,1)} %collective-permute-done.14.near_ref, ...), custom_call_target="tpu_custom_call" | custom-call | flops 880000000 | bytes 2400000 | tf_op jit(solution)/shard_map/expert_update/pallas_call | solution.py:1004
  361.1 5.1 %all-to-all-start.8 = ((bf16[8,24,768]{2,1,0:T(8,128)(2,1)}), bf16[8,24,768]{2,1,0:T(8,128)(2,1)S(1)}, u32[]{:S(2)}, u32[]{:S(2)}) async-start(bf16[8,24,768]{2,1,0:T(8,128)(2,1)} %copy-done.4), calls=%async_computation.8 | async-start | bytes 589824 | tf_op jit(solution)/shard_map/all_to_all | solution.py:1021
  366.2 5.4 %fusion.4 = (f32[1,768,768]{2,1,0:T(8,128)}, f32[768,768]{1,0:T(8,128)S(1)}) fusion(f32[1,768,768]{2,1,0:T(8,128)} %param.35, pred[]{:T(512)S(6)} %ge.10, bf16[768,768]{1,0:T(8,128)(2,1)} %collective-permute-done.23, bf16[4,768,768]{2,1,0:T(8,128)(2,1)} %collective-permute-done.14.near_ref, f32[2,768,768]{2,1,0:T(8,128)} %get-tuple-element.255.own_ref), kind=kLoop, calls=%fused_computation.10 | loop fusion | flops 5898240 | bytes 11796481 | tf_op jit(solution)/shard_map/broadcast_in_dim | solution.py:1228
  375.7 5.6 %collective-permute-done.28.refs_2_ = bf16[8,72,768]{2,1,0:T(8,128)(2,1)} collective-permute-done((bf16[8,72,768]{2,1,0:T(8,128)(2,1)S(1)}, bf16[8,72,768]{2,1,0:T(8,128)(2,1)}, u32[]{:S(2)}, u32[]{:S(2)}) %collective-permute-start.28) | collective-permute-done | bytes 884768 | tf_op jit(solution)/shard_map/ppermute | solution.py:40
  398.5 8.6 %lay_out_qkv.1 = (f32[768,2304]{1,0:T(8,128)}, f32[1,768]{1,0:T(1,128)S(1)}) custom-call(s32[2]{0:T(128)S(1)} %copy-done.8, bf16[8,72,768]{2,1,0:T(8,128)(2,1)S(1)} %slice.65.refs_0_, bf16[8,72,768]{2,1,0:T(8,128)(2,1)S(1)} %collective-permute-done.27.refs_1_, bf16[8,72,768]{2,1,0:T(8,128)(2,1)} %collective-permute-done.28.refs_2_, ...), custom_call_target="tpu_custom_call" | custom-call | flops 1100000000 | bytes 3000000 | tf_op jit(solution)/shard_map/lay_out_qkv/pallas_call | solution.py:931
  (191 shorter events, 95.1 us)
Async XLA Ops:
  2.0 14.5 %collective-permute-start = (bf16[256,768]{1,0:T(8,128)(2,1)S(1)}, bf16[256,768]{1,0:T(8,128)(2,1)S(1)}, u32[]{:S(2)}, u32[]{:S(2)}) collective-permute-start(bf16[256,768]{1,0:T(8,128)(2,1)S(1)} %get-tuple-element.290), channel_id=1, source_target_pairs={{0,2},{1,3},{2,0},{3,1},{4,6},{5,7},{6,4},{7,5},{8,10},{9,11},{10,... | collective-permute-start | bytes 1179656 | tf_op jit(solution)/shard_map/ppermute | solution.py:40
  4.1 17.3 %collective-permute-start.1 = (bf16[256,768]{1,0:T(8,128)(2,1)S(1)}, bf16[256,768]{1,0:T(8,128)(2,1)S(1)}, u32[]{:S(2)}, u32[]{:S(2)}) collective-permute-start(bf16[256,768]{1,0:T(8,128)(2,1)S(1)} %get-tuple-element.289), channel_id=1, source_target_pairs={{0,2},{1,3},{2,0},{3,1},{4,6},{5,7},{6,4},{7,5},{8,10},{9,11},{10,... | collective-permute-start | bytes 1179656 | tf_op jit(solution)/shard_map/ppermute | solution.py:40
  22.1 62.0 %all-to-all-start = ((bf16[8,192,768]{2,1,0:T(8,128)(2,1)}), bf16[8,192,768]{2,1,0:T(8,128)(2,1)S(1)}, u32[]{:S(2)}, u32[]{:S(2)}) async-start(bf16[8,192,768]{2,1,0:T(8,128)(2,1)} %get-tuple-element.193), calls=%async_computation | async-start | bytes 4718592 | tf_op jit(solution)/shard_map/all_to_all | solution.py:1021
  29.7 34.4 %collective-permute-start.5 = (bf16[768,768]{1,0:T(8,128)(2,1)}, bf16[768,768]{1,0:T(8,128)(2,1)}, u32[]{:S(2)}, u32[]{:S(2)}) collective-permute-start(bf16[768,768]{1,0:T(8,128)(2,1)} %get-tuple-element.176.refs_0_), channel_id=1, source_target_pairs={{0,2},{1,3},{2,0},{3,1},{4,6},{5,7},{6,4},{7,5},{8,10},{9,11},{10,... | collective-permute-start | bytes 3538952 | tf_op jit(solution)/shard_map/ppermute | solution.py:40
  31.8 32.3 %collective-permute-start.6 = (bf16[768,768]{1,0:T(8,128)(2,1)}, bf16[768,768]{1,0:T(8,128)(2,1)}, u32[]{:S(2)}, u32[]{:S(2)}) collective-permute-start(bf16[768,768]{1,0:T(8,128)(2,1)} %get-tuple-element.176.refs_0_), channel_id=1, source_target_pairs={{0,1},{1,0},{2,3},{3,2},{4,5},{5,4},{6,7},{7,6},{8,9},{9,8},{10,11... | collective-permute-start | bytes 3538952 | tf_op jit(solution)/shard_map/ppermute | solution.py:40
  32.1 32.0 %collective-permute-start.7 = (bf16[768,768]{1,0:T(8,128)(2,1)}, bf16[768,768]{1,0:T(8,128)(2,1)}, u32[]{:S(2)}, u32[]{:S(2)}) collective-permute-start(bf16[768,768]{1,0:T(8,128)(2,1)} %get-tuple-element.195.refs_1_), channel_id=1, source_target_pairs={{0,1},{1,0},{2,3},{3,2},{4,5},{5,4},{6,7},{7,6},{8,9},{9,8},{10,11... | collective-permute-start | bytes 3538952 | tf_op jit(solution)/shard_map/ppermute | solution.py:40
  32.3 7.8 %collective-permute-start.2 = (bf16[512,768]{1,0:T(8,128)(2,1)S(1)}, bf16[512,768]{1,0:T(8,128)(2,1)}, u32[]{:S(2)}, u32[]{:S(2)}) collective-permute-start(bf16[512,768]{1,0:T(8,128)(2,1)S(1)} %bitcast.83), channel_id=1, source_target_pairs={{0,1},{1,0},{2,3},{3,2},{4,5},{5,4},{6,7},{7,6},{8,9},{9,8},{10,11... | collective-permute-start | bytes 2359304 | tf_op jit(solution)/shard_map/ppermute | solution.py:40
  65.5 9.8 %collective-permute-start.10 = (bf16[192,512]{1,0:T(8,128)(2,1)}, bf16[192,512]{1,0:T(8,128)(2,1)S(1)}, u32[]{:S(2)}, u32[]{:S(2)}) collective-permute-start(bf16[192,512]{1,0:T(8,128)(2,1)} %get-tuple-element.182), channel_id=1, source_target_pairs={{0,3},{1,2},{2,1},{3,0},{4,7},{5,6},{6,5},{7,4},{8,11},{9,10},{10,... | collective-permute-start | bytes 589832 | tf_op jit(solution)/shard_map/ppermute | solution.py:40
  84.1 35.0 %all-to-all-start.1 = ((bf16[8,96,768]{2,1,0:T(8,128)(2,1)}), bf16[8,96,768]{2,1,0:T(8,128)(2,1)}, u32[]{:S(2)}, u32[]{:S(2)}) async-start(bf16[8,96,768]{2,1,0:T(8,128)(2,1)} %get-tuple-element.194), calls=%async_computation.1 | async-start | bytes 2359296 | tf_op jit(solution)/shard_map/all_to_all | solution.py:1021
  90.1 33.7 %collective-permute-start.11 = (bf16[768,768]{1,0:T(8,128)(2,1)S(1)}, bf16[768,768]{1,0:T(8,128)(2,1)}, u32[]{:S(2)}, u32[]{:S(2)}) collective-permute-start(bf16[768,768]{1,0:T(8,128)(2,1)S(1)} %copy-done.17), channel_id=1, source_target_pairs={{0,2},{1,3},{2,0},{3,1},{4,6},{5,7},{6,4},{7,5},{8,10},{9,11},{10,... | collective-permute-start | bytes 3538952 | tf_op jit(solution)/shard_map/ppermute | solution.py:40
  119.0 35.2 %all-to-all-start.3 = ((bf16[8,104,768]{2,1,0:T(8,128)(2,1)}), bf16[8,104,768]{2,1,0:T(8,128)(2,1)}, u32[]{:S(2)}, u32[]{:S(2)}) async-start(bf16[8,104,768]{2,1,0:T(8,128)(2,1)} %get-tuple-element.202), calls=%async_computation.3 | async-start | bytes 2555904 | tf_op jit(solution)/shard_map/all_to_all | solution.py:1021
  154.2 33.8 %all-to-all-start.2 = ((bf16[8,96,768]{2,1,0:T(8,128)(2,1)}), bf16[8,96,768]{2,1,0:T(8,128)(2,1)S(1)}, u32[]{:S(2)}, u32[]{:S(2)}) async-start(bf16[8,96,768]{2,1,0:T(8,128)(2,1)} %get-tuple-element.201), calls=%async_computation.2 | async-start | bytes 2359296 | tf_op jit(solution)/shard_map/all_to_all | solution.py:1021
  189.0 34.4 %all-to-all-start.4 = ((bf16[8,104,768]{2,1,0:T(8,128)(2,1)}), bf16[8,104,768]{2,1,0:T(8,128)(2,1)S(1)}, u32[]{:S(2)}, u32[]{:S(2)}) async-start(bf16[8,104,768]{2,1,0:T(8,128)(2,1)} %get-tuple-element.205), calls=%async_computation.4 | async-start | bytes 2555904 | tf_op jit(solution)/shard_map/all_to_all | solution.py:1021
  223.3 17.4 %collective-permute-start.14 = (bf16[4,768,768]{2,1,0:T(8,128)(2,1)}, bf16[4,768,768]{2,1,0:T(8,128)(2,1)}, u32[]{:S(2)}, u32[]{:S(2)}) collective-permute-start(bf16[4,768,768]{2,1,0:T(8,128)(2,1)} %get-tuple-element.217), channel_id=1, source_target_pairs={{0,1},{1,0},{2,3},{3,2},{4,5},{5,4},{6,7},{7,6},{8,9},{9,8},{10,11... | collective-permute-start | bytes 14155784 | tf_op jit(solution)/shard_map/ppermute | solution.py:40
  225.0 67.1 %all-to-all-start.5 = ((bf16[8,192,768]{2,1,0:T(8,128)(2,1)}), bf16[8,192,768]{2,1,0:T(8,128)(2,1)S(1)}, u32[]{:S(2)}, u32[]{:S(2)}) async-start(bf16[8,192,768]{2,1,0:T(8,128)(2,1)} %get-tuple-element.237), calls=%async_computation.5 | async-start | bytes 4718592 | tf_op jit(solution)/shard_map/all_to_all | solution.py:1021
  240.7 7.6 %collective-permute-start.15 = (bf16[192,512]{1,0:T(8,128)(2,1)}, bf16[192,512]{1,0:T(8,128)(2,1)}, u32[]{:S(2)}, u32[]{:S(2)}) collective-permute-start(bf16[192,512]{1,0:T(8,128)(2,1)} %get-tuple-element.219), channel_id=1, source_target_pairs={{0,1},{1,0},{2,3},{3,2},{4,5},{5,4},{6,7},{7,6},{8,9},{9,8},{10,11... | collective-permute-start | bytes 589832 | tf_op jit(solution)/shard_map/ppermute | solution.py:40
  241.6 6.8 %collective-permute-start.16 = (bf16[192,512]{1,0:T(8,128)(2,1)}, bf16[192,512]{1,0:T(8,128)(2,1)}, u32[]{:S(2)}, u32[]{:S(2)}) collective-permute-start(bf16[192,512]{1,0:T(8,128)(2,1)} %get-tuple-element.220), channel_id=1, source_target_pairs={{0,2},{1,3},{2,0},{3,1},{4,6},{5,7},{6,4},{7,5},{8,10},{9,11},{10,... | collective-permute-start | bytes 589832 | tf_op jit(solution)/shard_map/ppermute | solution.py:40
  242.8 10.1 %collective-permute-start.17 = (bf16[192,512]{1,0:T(8,128)(2,1)}, bf16[192,512]{1,0:T(8,128)(2,1)}, u32[]{:S(2)}, u32[]{:S(2)}) collective-permute-start(bf16[192,512]{1,0:T(8,128)(2,1)} %get-tuple-element.221), channel_id=1, source_target_pairs={{0,3},{1,2},{2,1},{3,0},{4,7},{5,6},{6,5},{7,4},{8,11},{9,10},{10,... | collective-permute-start | bytes 589832 | tf_op jit(solution)/shard_map/ppermute | solution.py:40
  252.9 39.1 %collective-permute-start.22 = (bf16[768,768]{1,0:T(8,128)(2,1)}, bf16[768,768]{1,0:T(8,128)(2,1)}, u32[]{:S(2)}, u32[]{:S(2)}) collective-permute-start(bf16[768,768]{1,0:T(8,128)(2,1)} %get-tuple-element.241), channel_id=1, source_target_pairs={{0,2},{1,3},{2,0},{3,1},{4,6},{5,7},{6,4},{7,5},{8,10},{9,11},{10,... | collective-permute-start | bytes 3538952 | tf_op jit(solution)/shard_map/ppermute | solution.py:40
  257.3 22.3 %collective-permute-start.18 = (bf16[2,192,768]{2,1,0:T(8,128)(2,1)}, bf16[2,192,768]{2,1,0:T(8,128)(2,1)S(1)}, u32[]{:S(2)}, u32[]{:S(2)}) collective-permute-start(bf16[2,192,768]{2,1,0:T(8,128)(2,1)} %get-tuple-element.231), channel_id=1, source_target_pairs={{0,1},{1,0},{2,3},{3,2},{4,5},{5,4},{6,7},{7,6},{8,9},{9,8},{10,11... | collective-permute-start | bytes 1769480 | tf_op jit(solution)/shard_map/ppermute | solution.py:40
  279.7 10.2 %collective-permute-start.20 = (bf16[192,768]{1,0:T(8,128)(2,1)S(1)}, bf16[192,768]{1,0:T(8,128)(2,1)S(1)}, u32[]{:S(2)}, u32[]{:S(2)}) collective-permute-start(bf16[192,768]{1,0:T(8,128)(2,1)S(1)} %fusion.17), channel_id=1, source_target_pairs={{0,2},{1,3},{2,0},{3,1},{4,6},{5,7},{6,4},{7,5},{8,10},{9,11},{10,... | collective-permute-start | bytes 884744 | tf_op jit(solution)/shard_map/ppermute | solution.py:40
  280.0 9.0 %collective-permute-start.21 = (f32[16,768]{1,0:T(8,128)}, f32[16,768]{1,0:T(8,128)S(1)}, u32[]{:S(2)}, u32[]{:S(2)}) collective-permute-start(f32[16,768]{1,0:T(8,128)} %add.75), channel_id=1, source_target_pairs={{0,2},{1,3},{2,0},{3,1},{4,6},{5,7},{6,4},{7,5},{8,10},{9,11},{10,... | collective-permute-start | bytes 147464 | tf_op jit(solution)/shard_map/ppermute | solution.py:40
  292.1 29.1 %all-to-all-start.6 = ((bf16[8,80,768]{2,1,0:T(8,128)(2,1)}), bf16[8,80,768]{2,1,0:T(8,128)(2,1)S(1)}, u32[]{:S(2)}, u32[]{:S(2)}) async-start(bf16[8,80,768]{2,1,0:T(8,128)(2,1)} %pack_sums.1), calls=%async_computation.6 | async-start | bytes 1966080 | tf_op jit(solution)/shard_map/all_to_all | solution.py:1021
  298.0 30.3 %collective-permute-start.23 = (bf16[768,768]{1,0:T(8,128)(2,1)}, bf16[768,768]{1,0:T(8,128)(2,1)}, u32[]{:S(2)}, u32[]{:S(2)}) collective-permute-start(bf16[768,768]{1,0:T(8,128)(2,1)} %get-tuple-element.248), channel_id=1, source_target_pairs={{0,2},{1,3},{2,0},{3,1},{4,6},{5,7},{6,4},{7,5},{8,10},{9,11},{10,... | collective-permute-start | bytes 3538952 | tf_op jit(solution)/shard_map/ppermute | solution.py:40
  323.3 34.9 %all-to-all-start.7 = ((bf16[8,104,768]{2,1,0:T(8,128)(2,1)}), bf16[8,104,768]{2,1,0:T(8,128)(2,1)S(1)}, u32[]{:S(2)}, u32[]{:S(2)}) async-start(bf16[8,104,768]{2,1,0:T(8,128)(2,1)} %fold_sums.2), calls=%async_computation.7 | async-start | bytes 2555904 | tf_op jit(solution)/shard_map/all_to_all | solution.py:1021
  340.3 25.9 %collective-permute-start.26 = (bf16[512,768]{1,0:T(8,128)(2,1)}, bf16[512,768]{1,0:T(8,128)(2,1)}, u32[]{:S(2)}, u32[]{:S(2)}) collective-permute-start(bf16[512,768]{1,0:T(8,128)(2,1)} %add_convert_fusion), channel_id=1, source_target_pairs={{0,2},{1,3},{2,0},{3,1},{4,6},{5,7},{6,4},{7,5},{8,10},{9,11},{10,... | collective-permute-start | bytes 2359304 | tf_op jit(solution)/shard_map/ppermute | solution.py:40
  340.8 42.6 %collective-permute-start.25 = (bf16[512,768]{1,0:T(8,128)(2,1)}, bf16[512,768]{1,0:T(8,128)(2,1)}, u32[]{:S(2)}, u32[]{:S(2)}) collective-permute-start(bf16[512,768]{1,0:T(8,128)(2,1)} %copy-done.11), channel_id=1, source_target_pairs={{0,1},{1,0},{2,3},{3,2},{4,5},{5,4},{6,7},{7,6},{8,9},{9,8},{10,11... | collective-permute-start | bytes 2359304 | tf_op jit(solution)/shard_map/ppermute | solution.py:40
  358.2 29.2 %collective-permute-start.27 = (bf16[8,72,768]{2,1,0:T(8,128)(2,1)S(1)}, bf16[8,72,768]{2,1,0:T(8,128)(2,1)S(1)}, u32[]{:S(2)}, u32[]{:S(2)}) collective-permute-start(bf16[8,72,768]{2,1,0:T(8,128)(2,1)S(1)} %slice.65.refs_0_), channel_id=1, source_target_pairs={{0,1},{1,0},{2,3},{3,2},{4,5},{5,4},{6,7},{7,6},{8,9},{9,8},{10,11... | collective-permute-start | bytes 2654216 | tf_op jit(solution)/shard_map/ppermute | solution.py:40
  360.0 21.3 %collective-permute-start.28 = (bf16[8,72,768]{2,1,0:T(8,128)(2,1)S(1)}, bf16[8,72,768]{2,1,0:T(8,128)(2,1)}, u32[]{:S(2)}, u32[]{:S(2)}) collective-permute-start(bf16[8,72,768]{2,1,0:T(8,128)(2,1)S(1)} %slice.65.refs_0_), channel_id=1, source_target_pairs={{0,2},{1,3},{2,0},{3,1},{4,6},{5,7},{6,4},{7,5},{8,10},{9,11},{10,... | collective-permute-start | bytes 2654216 | tf_op jit(solution)/shard_map/ppermute | solution.py:40
  361.1 25.0 %all-to-all-start.8 = ((bf16[8,24,768]{2,1,0:T(8,128)(2,1)}), bf16[8,24,768]{2,1,0:T(8,128)(2,1)S(1)}, u32[]{:S(2)}, u32[]{:S(2)}) async-start(bf16[8,24,768]{2,1,0:T(8,128)(2,1)} %copy-done.4), calls=%async_computation.8 | async-start | bytes 589824 | tf_op jit(solution)/shard_map/all_to_all | solution.py:1021
  386.1 8.7 %collective-permute-start.31 = (bf16[8,24,768]{2,1,0:T(8,128)(2,1)S(1)}, bf16[8,24,768]{2,1,0:T(8,128)(2,1)S(1)}, u32[]{:S(2)}, u32[]{:S(2)}) collective-permute-start(bf16[8,24,768]{2,1,0:T(8,128)(2,1)S(1)} %all-to-all-done.8.refs_4_), channel_id=1, source_target_pairs={{0,2},{1,3},{2,0},{3,1},{4,6},{5,7},{6,4},{7,5},{8,10},{9,11},{10,... | collective-permute-start | bytes 884744 | tf_op jit(solution)/shard_map/ppermute | solution.py:40
  387.1 11.4 %collective-permute-start.30 = (bf16[8,24,768]{2,1,0:T(8,128)(2,1)S(1)}, bf16[8,24,768]{2,1,0:T(8,128)(2,1)S(1)}, u32[]{:S(2)}, u32[]{:S(2)}) collective-permute-start(bf16[8,24,768]{2,1,0:T(8,128)(2,1)S(1)} %all-to-all-done.8.refs_4_), channel_id=1, source_target_pairs={{0,1},{1,0},{2,3},{3,2},{4,5},{5,4},{6,7},{7,6},{8,9},{9,8},{10,11... | collective-permute-start | bytes 884744 | tf_op jit(solution)/shard_map/ppermute | solution.py:40
  (54 other events, 371.7 us)

commit v4 on v3

--- a/solution.py
+++ b/solution.py
@@ -334,8 +334,8 @@
     dqkv_ref[2 * HEAD_DIM :, :] = dv_acc[...].astype(bf16)
     grad = mm(dqkv_ref[...], a_buf[...])
     rows = grad_ref.shape[2]
-    for e in range(grad_ref.shape[1]):
-        grad_ref[0, e] = grad[e * rows : (e + 1) * rows, :].astype(bf16)
+    for e in range(grad_ref.shape[0]):
+        grad_ref[e, 0] = grad[e * rows : (e + 1) * rows, :].astype(bf16)
 
 
 def attend_back(first, number, pieces, info, own, keys, v_parts, qkv_parts, grads, out, logs, a_parts, block=256):
@@ -353,7 +353,7 @@
         functools.partial(attend_back_kernel, block, first),
         out_shape=[
             jax.ShapeDtypeStruct((number * 3 * HEAD_DIM, row_len), bf16),
-            jax.ShapeDtypeStruct((number, pieces, 3 * HEAD_DIM // pieces, width), bf16),
+            jax.ShapeDtypeStruct((pieces, number, 3 * HEAD_DIM // pieces, width), bf16),
         ],
         grid=(number,),
         in_specs=[smem_spec()] * 2
@@ -369,7 +369,7 @@
         ],
         out_specs=[
             pl.BlockSpec((3 * HEAD_DIM, row_len), lambda g: (g, 0)),
-            pl.BlockSpec((1, pieces, 3 * HEAD_DIM // pieces, width), lambda g: (g, 0, 0, 0)),
+            pl.BlockSpec((pieces, 1, 3 * HEAD_DIM // pieces, width), lambda g: (0, g, 0, 0)),
         ],
         scratch_shapes=[
             pltpu.VMEM((row_len, group), bf16),
@@ -819,76 +819,70 @@
     )(places, *parts, w_t)
 
 
-def pack_kernel(special, g_ref, keep_ref, near_ref, far_ref, small_ref, out_ref):
-    exps, _, width = out_ref.shape
-    rows = g_ref.shape[2]
-    gout = keep_ref[0] + near_ref[0].astype(f32) + far_ref[...].astype(f32)
-    out_rows = gout.shape[0] // exps
-    begin = 2 * rows + out_rows
-    pad = out_ref.shape[1] - begin - 2 * special
-    for e in range(exps):
-        out_ref[e, 0:rows] = g_ref[0, e]
-        out_ref[e, rows : 2 * rows] = g_ref[1, e]
-        high, mid, _ = split_three(small_ref[e * special : (e + 1) * special, :])
-        parts = [gout[e * out_rows : (e + 1) * out_rows], high.astype(f32), mid.astype(f32)]
-        if pad:
-            parts.append(jnp.zeros((pad, width), f32))
-        out_ref[e, 2 * rows :] = jnp.concatenate(parts, axis=0).astype(bf16)
-
-
-def pack(grads, keep, near, far, small, special):
-    _, exps, rows, width = grads.shape
-    total = 2 * rows + keep.shape[1] // exps + 2 * special
-    return pl.pallas_call(
-        functools.partial(pack_kernel, special),
-        out_shape=jax.ShapeDtypeStruct((exps, total + -total % 8, width), bf16),
-        in_specs=[vmem_spec()] * 5,
-        out_specs=vmem_spec(),
-        compiler_params=params(50),
-        name="pack_sums",
-        cost_estimate=cost(2),
-    )(grads, keep, near, far, small)
-
-
-def fold_kernel(special, taken, moved_ref, *refs):
-    given, out_ref = refs[:-1], refs[-1]
+def mix_kernel(taken, special, moved_ref, grad_ref, keep_ref, near_ref, far_ref, small_ref, out_ref):
     exps, rows, width = out_ref.shape
     sums = moved_ref[0, 0:taken].astype(f32)
     for e in range(1, exps):
         sums = sums + moved_ref[e, 0:taken].astype(f32)
-    if special:
-        body = taken - 2 * special
-        high, mid, _ = split_three(
-            sums[body : body + special] + sums[body + special : body + 2 * special]
-        )
-        sums = jnp.concatenate([sums[:body], high.astype(f32), mid.astype(f32)], axis=0)
-    start = given[0].shape[1] if given else 0
-    pad = rows - start - taken
-    if pad:
-        sums = jnp.concatenate([sums, jnp.zeros((pad, width), f32)], axis=0)
-    sums = sums.astype(bf16)
+    gout = keep_ref[0] + near_ref[0].astype(f32) + far_ref[...].astype(f32)
+    out_rows = gout.shape[0] // exps
+    pad = rows - taken - grad_ref.shape[2] - out_rows - 2 * special
     for e in range(exps):
-        if given:
-            out_ref[e, 0:start] = given[0][e]
-        out_ref[e, start:] = sums
-
-
-def fold(moved, taken, special, given=()):
+        high, mid, _ = split_three(small_ref[e * special : (e + 1) * special, :])
+        parts = [sums, grad_ref[e, 0].astype(f32), gout[e * out_rows : (e + 1) * out_rows]]
+        parts += [high.astype(f32), mid.astype(f32)]
+        if pad:
+            parts.append(jnp.zeros((pad, width), f32))
+        out_ref[e] = jnp.concatenate(parts, axis=0).astype(bf16)
+
+
+def mix(moved, taken, grad, keep, near, far, small, special):
+    exps, _, rows, width = grad.shape
+    total = taken + rows + keep.shape[1] // exps + 2 * special
+    return pl.pallas_call(
+        functools.partial(mix_kernel, taken, special),
+        out_shape=jax.ShapeDtypeStruct((exps, total + -total % 8, width), bf16),
+        in_specs=[vmem_spec()] * 6,
+        out_specs=vmem_spec(),
+        compiler_params=params(50),
+        name="mix_sums",
+        cost_estimate=cost(2),
+    )(moved, grad, keep, near, far, small)
+
+
+def fold_kernel(start, taken, special, moved_ref, out_ref):
+    exps, rows, width = out_ref.shape
+    sums = moved_ref[0, start : start + taken].astype(f32)
+    for e in range(1, exps):
+        sums = sums + moved_ref[e, start : start + taken].astype(f32)
+    body = taken - 2 * special
+    high, mid, _ = split_three(
+        sums[body : body + special] + sums[body + special : body + 2 * special]
+    )
+    parts = [sums[:body], high.astype(f32), mid.astype(f32)]
+    if rows > taken:
+        parts.append(jnp.zeros((rows - taken, width), f32))
+    sums = jnp.concatenate(parts, axis=0).astype(bf16)
+    for e in range(exps):
+        out_ref[e] = sums
+
+
+def fold(moved, start, taken, special):
     exps, _, width = moved.shape
-    rows = taken + sum(g.shape[1] for g in given)
     return pl.pallas_call(
-        functools.partial(fold_kernel, special, taken),
-        out_shape=jax.ShapeDtypeStruct((exps, rows + -rows % 8, width), bf16),
-        in_specs=[vmem_spec()] * (1 + len(given)),
+        functools.partial(fold_kernel, start, taken, special),
+        out_shape=jax.ShapeDtypeStruct((exps, taken + -taken % 8, width), bf16),
+        in_specs=[vmem_spec()],
         out_specs=vmem_spec(),
         compiler_params=params(40),
         name="fold_sums",
         cost_estimate=cost(2),
-    )(moved, *given)
-
-
-def lay_out_kernel(rows, own_ref, *refs):
-    arrays, (w_ref, gain_ref, grad_ref, ggain_ref, b0, b1, sems) = refs[:8], refs[8:]
+    )(moved)
+
+
+def lay_out_kernel(rows, out_rows, small_rows, own_ref, *refs):
+    arrays, refs = refs[:8], refs[8:]
+    w_ref, gain_ref, grad_ref, ggain_ref, gout_ref, small_ref, b0, b1, sems = refs
     hids, exps = b0.shape[0], b0.shape[1]
     step = pl.program_id(0)
     block = grad_ref.shape[0]
@@ -921,58 +915,47 @@
     grad_ref[...] = grad
     total = jnp.sum(grad * w_ref[...].astype(f32), axis=1, keepdims=True)
     ggain_ref[...] = row_of(total) / gain_ref[...]
-
-
-def lay_out(own, chunks, rows, w_qkv, gain, block=128):
+    for h in range(hids):
+        for e in range(exps):
+            n = h * exps + e
+            piece = b1[h, e, rows : rows + out_rows, cols]
+            gout_ref[n * out_rows : (n + 1) * out_rows, :] = piece.astype(f32)
+    start = rows + out_rows
+    for e in range(exps):
+        total = 0.0
+        for h in range(hids):
+            high = b1[h, e, start : start + small_rows, cols].astype(f32)
+            low = b1[h, e, start + small_rows : start + 2 * small_rows, cols].astype(f32)
+            total = total + (high + low)
+        small_ref[e * small_rows : (e + 1) * small_rows, :] = total
+
+
+def lay_out(own, chunks, rows, out_rows, small_rows, w_qkv, gain, block=256):
     width, cols = w_qkv.shape
+    smalls = chunks[0][0].shape[0] * small_rows
     arrays = [a for chunk in chunks for a in chunk]
     tile = pl.BlockSpec((block, cols), lambda g: (g, 0))
     row = pl.BlockSpec((1, block), lambda g: (0, g))
     return pl.pallas_call(
-        functools.partial(lay_out_kernel, rows),
+        functools.partial(lay_out_kernel, rows, out_rows, small_rows),
         out_shape=[
             jax.ShapeDtypeStruct((width, cols), f32),
             jax.ShapeDtypeStruct((1, width), f32),
+            jax.ShapeDtypeStruct((width, width), f32),
+            jax.ShapeDtypeStruct((smalls, width), f32),
         ],
         grid=(width // block,),
         in_specs=[smem_spec()] + [pl.BlockSpec(memory_space=pl.ANY)] * 8 + [tile, row],
-        out_specs=[tile, row],
+        out_specs=[
+            tile, row, pl.BlockSpec((width, block), lambda g: (0, g)),
+            pl.BlockSpec((smalls, block), lambda g: (0, g)),
+        ],
         scratch_shapes=[pltpu.VMEM((4,) + chunk[0].shape, bf16) for chunk in chunks]
         + [pltpu.SemaphoreType.DMA((2, 4))],
         compiler_params=params(50),
-        name="lay_out_qkv",
+        name="lay_out_sums",
         cost_estimate=cost(10),
     )(own, *arrays, w_qkv, gain)
-
-
-def lay_out_rest_kernel(start, own_ref, *refs):
-    arrays, (out_ref, buf, sems) = refs[:4], refs[4:]
-    hids, exps = buf.shape[0], buf.shape[1]
-    rows = out_ref.shape[0] // (hids * exps)
-    copies = [
-        pltpu.make_async_copy(arrays[j], buf.at[own_ref[0] ^ j], sems.at[j]) for j in range(hids)
-    ]
-    for copy in copies:
-        copy.start()
-    for copy in copies:
-        copy.wait()
-    for h in range(hids):
-        for e in range(exps):
-            n = h * exps + e
-            out_ref[n * rows : (n + 1) * rows, :] = buf[h, e, start : start + rows].astype(f32)
-
-
-def lay_out_rest(own, arrays, start, width):
-    return pl.pallas_call(
-        functools.partial(lay_out_rest_kernel, start),
-        out_shape=jax.ShapeDtypeStruct((width, width), f32),
-        in_specs=[smem_spec()] + [pl.BlockSpec(memory_space=pl.ANY)] * 4,
-        out_specs=vmem_spec(),
-        scratch_shapes=[pltpu.VMEM((4,) + arrays[0].shape, bf16), pltpu.SemaphoreType.DMA((4,))],
-        compiler_params=params(50),
-        name="lay_out_w_out",
-        cost_estimate=cost(3),
-    )(own, *arrays)
 
 
 def adam_update(weight, gradient, first_moment, second_moment, live_mask):
@@ -1135,7 +1118,6 @@
     missing = max(0, exp_count * small_rows - small.shape[0])
     small = jnp.pad(small, ((0, missing), (0, 0)))
     gout_near = swap(gout_near, "hid", 1)
-    small = small + swap(small, "hid", 1)
     far_up = (far_up + near_part[2].astype(f32)).astype(bf16)
     far_down = (far_down + near_part[3].astype(f32)).astype(bf16)
     far_up, far_down = tie((far_up, far_down), datt_parts)
@@ -1143,18 +1125,17 @@
     rows = 3 * HEAD_DIM // exp_count
     given = (info, own, keys, v_parts, qkv_parts, datt_parts, out_heads, logs, a_parts)
     dqkv_first, grads_first = attend_back(0, heads - 1, exp_count, *given)
-    gout_near, small = tie((gout_near, small), dqkv_first)
-    small = small + swap(small, "hid", 2)
+    gout_near = tie(gout_near, dqkv_first)
     gout_far = swap((gout[1] + gout_near[1].astype(f32)).astype(bf16), "hid", 2)
-    packed = pack(grads_first, gout, gout_near, gout_far, small, small_rows)
-    packed, out_back, far_up = lax.optimization_barrier((packed, out_back, far_up))
-    far_down = swap(tie(far_down, (gout_far, small)), "hid", 2)
-    first = exchange(packed, "exp")
+    grads_first, out_back, far_up, gout_far = lax.optimization_barrier(
+        (grads_first, out_back, far_up, gout_far)
+    )
+    far_down = swap(tie(far_down, gout_far), "hid", 2)
+    first = exchange(pad_rows(grads_first.reshape(exp_count, -1, width)), "exp")
     dqkv_last, grads_last = attend_back(heads - 1, 1, exp_count, *given)
     dqkv = [dqkv_first, dqkv_last]
-    first_rows = 2 * rows + out_rows + 2 * small_rows
-
-    first_sums = fold(first, first_rows, small_rows, [grads_last[0]])
+    known = (heads - 1) * rows
+    first_sums = mix(first, known, grads_last, gout, gout_near, gout_far, small, small_rows)
     second = exchange(first_sums, "exp")
 
     dqkv, far_down = tie((dqkv, far_down), first_sums)
@@ -1162,21 +1143,17 @@
     near_dn, last_dn, far_dn, own_dn = spread(places, dqkv, w_t)
     near_dn, last_dn = swap(near_dn, "hid", 1), swap(last_dn, "hid", 1)
     far_dn = (far_dn + last_dn.astype(f32)).astype(bf16)
-    out_back, far_up = tie((out_back, far_up), far_dn)
+    out_back = tie(out_back, far_dn)
     far_dn = swap(far_dn, "hid", 2)
-    start = 3 * rows + out_rows
-    small = second[:, start : start + small_rows].astype(f32)
-    small = small + second[:, start + small_rows : start + 2 * small_rows].astype(f32)
-    small = small.reshape(exp_count * small_rows, width)
 
     out_tokens = combine(out_back, picks, residual, gates)
+    second, out_tokens = lax.optimization_barrier((second, out_tokens))
+    last_sums = fold(second, known, rows + out_rows + 2 * small_rows, small_rows)
+    far_dn, far_up = tie((far_dn, far_up), last_sums)
     live = is_new.astype(jnp.int32).reshape(1)
     grad_up, up_next, up_first_next, up_second_next = expert_update(
         live, own_part, near_part, 0, far_up, up_w[0], up_first[0], up_second[0]
     )
-    second, out_tokens, up_next = lax.optimization_barrier((second, out_tokens, up_next))
-    last_sums = fold(second, rows, 0)
-    far_dn, far_down = tie((far_dn, far_down), last_sums)
     dnormed = own_dn + near_dn.astype(f32) + far_dn.astype(f32)
     x = x_own.astype(f32)
     scale = lax.rsqrt(jnp.mean(x * x, axis=-1, keepdims=True) + norm_eps)
@@ -1186,13 +1163,18 @@
         dres + scale * (scaled - unit * jnp.mean(scaled * unit, axis=-1, keepdims=True))
     ).astype(bf16)
     third = exchange(last_sums, "exp")
-    gathered = gather_hid(second[:, rows:start])
+    third, grad_tokens, up_next = lax.optimization_barrier((third, grad_tokens, up_next))
+    far_down = tie(far_down, third)
+    gathered = gather_hid(second[:, :known])
     grad_down = own_part[1] + near_part[1].astype(f32) + far_down.astype(f32)
     grad_down = jnp.where(is_new, grad_down, 0.0)
     down_next, down_first_next, down_second_next = adam_update(
         down_w[0], grad_down, down_first[0], down_second[0], is_new
     )
-    grad_out_proj = lay_out_rest(own, gathered, 2 * rows, width)
+    gathered = (gathered, gather_hid(third))
+    grad_qkv, grad_gain_attn, grad_out_proj, small = lay_out(
+        own, gathered, rows, out_rows, small_rows, w_qkv, gain_attn[None]
+    )
     grad_gain_moe = small[experts]
     live_columns = (jnp.arange(experts, dtype=jnp.int32) >= frozen_count)[None, :]
     grad_router = jnp.where(live_columns, small[:experts].T, 0.0)
@@ -1200,12 +1182,6 @@
         router_w[:, frozen_count:], grad_router[:, frozen_count:], router_first, router_second, True
     )
     router_next = jnp.concatenate([router_w[:, :frozen_count], router_new], axis=1)
-    near, far = swap(third, "hid", 1), swap(third, "hid", 2)
-    ready = (grad_out_proj, grad_router, router_next, router_first_next, router_second_next)
-    far, ready = lax.optimization_barrier((far, ready))
-    grad_out_proj, grad_router, router_next, router_first_next, router_second_next = ready
-    gathered = (gathered, (third, near, far, swap(far, "hid", 1)))
-    grad_qkv, grad_gain_attn = lay_out(own, gathered, rows, w_qkv, gain_attn[None])
     grad_gain_attn = grad_gain_attn[0]
     return (
         out_tokens[None],

time: 415 us -> 410 us (0.988)
    all_to_all x9, waiting for transfers between devices: 45.9 us -> 41.5 us  [exchange(): return lax.all_to_all(value, axis, split_axis=0, concat_axis=0, tiled=True)]
    pallas_call x5 -> x3, Pallas kernels: 14.8 us -> 10.7 us  [the longest x1 8.5 us: lay_out(): pl.pallas_call(functools.partial(lay_out_kernel, rows, out_rows, small_ro...]
    ppermute x33 -> x31, starting transfers between devices: 24.7 us -> 27.9 us  [swap(): return lax.ppermute(value, axis, [(i, i ^ distance) for i in range(count)])]
    ppermute x33 -> x31, waiting for transfers between devices: 43.5 us -> 45.4 us  [swap(): return lax.ppermute(value, axis, [(i, i ^ distance) for i in range(count)])]
    unnamed x88 -> x78, local copies, waits for them, and re-layouts: 9.78 us -> 8.1 us
  transfers between devices with their start and end apart: 42 -> 40, of which waited for: 19 -> 20; matrix products, arithmetic and copies ran while one was open for 8% -> 8% of each run, Pallas kernels for 47% -> 47%
where the time goes in v4:
time: 410 us; the launch traced here: 404 us
  Pallas kernels  198 us (48%)
  waiting for transfers between devices  86.9 us (21%)
  starting transfers between devices  74.5 us (18%)
  other arithmetic  30.8 us (8%)
  local copies, waits for them, and re-layouts  12.1 us (3%)
    pallas_call x2, Pallas kernels, run_experts(): pl.pallas_call(functools.partial(expert_kernel, half, 0), out_shape=[shap...  48.7 us
    all_to_all x9, starting transfers between devices, exchange(): return lax.all_to_all(value, axis, split_axis=0, concat_axis=0, tiled=True)  46.6 us
    ppermute x31, waiting for transfers between devices, swap(): return lax.ppermute(value, axis, [(i, i ^ distance) for i in range(count)])  45.4 us
    all_to_all x9, waiting for transfers between devices, exchange(): return lax.all_to_all(value, axis, split_axis=0, concat_axis=0, tiled=True)  41.5 us
    pallas_call x2, Pallas kernels, attend_back(): pl.pallas_call(functools.partial(attend_back_kernel, block, first), out_s...  31 us
    ppermute x31, starting transfers between devices, swap(): return lax.ppermute(value, axis, [(i, i ^ distance) for i in range(count)])  27.9 us
    pallas_call x1, Pallas kernels, weight_grads(): pl.pallas_call(weight_kernel, out_shape=[jax.ShapeDtypeStruct((2, width,...  26.9 us
    pallas_call x1, Pallas kernels, attend(): pl.pallas_call(functools.partial(attend_kernel, block), out_shape=[jax.Sh...  17.5 us
  transfers between devices with their start and end apart: 40, of which 20 were waited for; matrix products, arithmetic and copies ran while one was open for 8% of the time, Pallas kernels for 47%

profile of v4, /device:TPU:1, one launch (start us, length us, event | category | flops | bytes accessed | tf_op | source)
XLA Modules:
  0.0 403.9 jit_solution(15013768962962962917)
XLA Ops:
  6.2 5.1 %slot_tables.1 = (bf16[768,512]{1,0:T(8,128)(2,1)}, bf16[768,512]{1,0:T(8,128)(2,1)}, bf16[512,768]{1,0:T(8,128)(2,1)}, bf16[512,768]{1,0:T(8,128)(2,1)}, bf16[5...) custom-call(s32[2,512]{1,0:T(2,128)} %bitcast.93, bf16[512,768]{1,0:T(8,128)(2,1)} %bitcast.84), custom_call_target="tpu_custom_call" | custom-call | flops 11000000 | bytes 30000 | tf_op jit(solution)/shard_map/slot_tables/pallas_call | solution.py:127
  16.6 4.8 %collective-permute-done.1.refs_1_ = bf16[256,768]{1,0:T(8,128)(2,1)S(1)} collective-permute-done((bf16[256,768]{1,0:T(8,128)(2,1)S(1)}, bf16[256,768]{1,0:T(8,128)(2,1)S(1)}, u32[]{:S(2)}, u32[]{:S(2)}) %collective-permute-start.1) | collective-permute-done | bytes 393248 | tf_op jit(solution)/shard_map/ppermute | solution.py:40
  22.1 5.6 %all-to-all-start = ((bf16[8,192,768]{2,1,0:T(8,128)(2,1)}), bf16[8,192,768]{2,1,0:T(8,128)(2,1)S(1)}, u32[]{:S(2)}, u32[]{:S(2)}) async-start(bf16[8,192,768]{2,1,0:T(8,128)(2,1)} %get-tuple-element.191), calls=%async_computation | async-start | bytes 4718592 | tf_op jit(solution)/shard_map/all_to_all | solution.py:1004
  33.8 6.3 %norm_qkv.3 = (bf16[512,768]{1,0:T(8,128)(2,1)}, bf16[512,768]{1,0:T(8,128)(2,1)}, bf16[576,512]{1,0:T(8,128)(2,1)}, bf16[576,512]{1,0:T(8,128)(2,1)}, bf16[512,...) custom-call(s32[2]{0:T(128)} %pad_add_fusion.1.own_ref, ...), custom_call_target="tpu_custom_call" | custom-call | flops 11000000 | bytes 30000 | tf_op jit(solution)/shard_map/norm_qkv/pallas_call | solution.py:176
  40.1 6.5 %norm_qkv.2 = (bf16[512,768]{1,0:T(8,128)(2,1)}, bf16[512,768]{1,0:T(8,128)(2,1)}, bf16[576,512]{1,0:T(8,128)(2,1)}, bf16[576,512]{1,0:T(8,128)(2,1)}, bf16[512,...) custom-call(s32[2]{0:T(128)} %pad_add_fusion.1.own_ref, ...), custom_call_target="tpu_custom_call" | custom-call | flops 11000000 | bytes 30000 | tf_op jit(solution)/shard_map/norm_qkv/pallas_call | solution.py:176
  46.6 17.5 %attend.1 = (f32[192,2048]{1,0:T(8,128)}, f32[3,1,2048]{2,1,0:T(1,128)}, bf16[2048,192]{1,0:T(8,128)(2,1)}, bf16[192,512]{1,0:T(8,128)(2,1)}, bf16[192,512]{1,0:...) custom-call(s32[3]{0:T(128)} %pad_add_fusion.info_ref, s32[2]{0:T(128)} %pad_add_fusion.1.own_ref, ...), custom_call_target="tpu_custom_call" | custom-call | flops 11000000 | bytes 30000 | tf_op jit(solution)/shard_map/attend/pallas_call | solution.py:275
  70.6 4.8 %collective-permute-done.10.t3 = bf16[192,512]{1,0:T(8,128)(2,1)S(1)} collective-permute-done((bf16[192,512]{1,0:T(8,128)(2,1)}, bf16[192,512]{1,0:T(8,128)(2,1)S(1)}, u32[]{:S(2)}, u32[]{:S(2)}) %collective-permute-start.10) | collective-permute-done | bytes 196640 | tf_op jit(solution)/shard_map/ppermute | solution.py:40
  76.0 8.1 %project_dispatch.1 = (f32[512,768]{1,0:T(8,128)}, f32[2,512]{1,0:T(2,128)}, bf16[8,96,768]{2,1,0:T(8,128)(2,1)}, bf16[8,104,768]{2,1,0:T(8,128)(2,1)}) custom-call(s32[2]{0:T(128)} %pad_add_fusion.1.own_ref, bf16[192,512]{1,0:T(8,128)(2,1)} %get-tuple-element.181.t0, bf16[192,512]{1,0:T(8,128)(2,1)} %copy-done.21, bf16[192,512]{1,0:T(8,128)(2,1)} %copy-done.22, ...), custom_call_target="tpu_custom_call" | custom-call | flops 11000000 | bytes 30000 | tf_op jit(solution)/shard_map/project_dispatch/pallas_call | solution.py:452
  84.1 6.0 %all-to-all-start.1 = ((bf16[8,96,768]{2,1,0:T(8,128)(2,1)}), bf16[8,96,768]{2,1,0:T(8,128)(2,1)}, u32[]{:S(2)}, u32[]{:S(2)}) async-start(bf16[8,96,768]{2,1,0:T(8,128)(2,1)} %get-tuple-element.192), calls=%async_computation.1 | async-start | bytes 2359296 | tf_op jit(solution)/shard_map/all_to_all | solution.py:1004
  91.4 27.7 %all-to-all-done.1.x_ref.x_a = bf16[8,96,768]{2,1,0:T(8,128)(2,1)} async-done(((bf16[8,96,768]{2,1,0:T(8,128)(2,1)}), bf16[8,96,768]{2,1,0:T(8,128)(2,1)}, u32[]{:S(2)}, u32[]{:S(2)}) %all-to-all-start.1) | async-done | bytes 1179680 | tf_op jit(solution)/shard_map/all_to_all | solution.py:1004
  119.0 4.8 %all-to-all-start.3 = ((bf16[8,104,768]{2,1,0:T(8,128)(2,1)}), bf16[8,104,768]{2,1,0:T(8,128)(2,1)}, u32[]{:S(2)}, u32[]{:S(2)}) async-start(bf16[8,104,768]{2,1,0:T(8,128)(2,1)} %get-tuple-element.200), calls=%async_computation.3 | async-start | bytes 2555904 | tf_op jit(solution)/shard_map/all_to_all | solution.py:1004
  129.9 24.3 %experts.2 = (bf16[8,192,768]{2,1,0:T(8,128)(2,1)}, bf16[8,96,768]{2,1,0:T(8,128)(2,1)}, bf16[4,768,768]{2,1,0:T(8,128)(2,1)}, bf16[4,768,768]{2,1,0:T(8,128)(2,1)}, bf16[8,8,128]{2,1,0:T(8,128)(2,1)}) custom-call(bf16[8,96,768]{2,1,0:T(8,128)(2,1)} %all-to-all-done.1.x_ref.x_a, bf16[8,192,768]{2,1,0:T(8,128)(2,1)} %copy-done.8, ...), custom_call_target="tpu_custom_call" | custom-call | flops 2750000128 | bytes 7500000 | tf_op jit(solution)/shard_map/experts/pallas_call | solution.py:574
  154.2 5.7 %all-to-all-start.2 = ((bf16[8,96,768]{2,1,0:T(8,128)(2,1)}), bf16[8,96,768]{2,1,0:T(8,128)(2,1)S(1)}, u32[]{:S(2)}, u32[]{:S(2)}) async-start(bf16[8,96,768]{2,1,0:T(8,128)(2,1)} %get-tuple-element.199), calls=%async_computation.2 | async-start | bytes 2359296 | tf_op jit(solution)/shard_map/all_to_all | solution.py:1004
  159.9 24.4 %experts.3 = (bf16[8,192,768]{2,1,0:T(8,128)(2,1)}, bf16[8,104,768]{2,1,0:T(8,128)(2,1)}, bf16[4,768,768]{2,1,0:T(8,128)(2,1)}, bf16[4,768,768]{2,1,0:T(8,128)(2,1)}) custom-call(bf16[8,104,768]{2,1,0:T(8,128)(2,1)} %all-to-all-done.3.x_ref.x_b, bf16[8,192,768]{2,1,0:T(8,128)(2,1)} %copy-done.8, ...), custom_call_target="tpu_custom_call", output_to_operand_aliasing={{0}: (11, {})} | custom-call | flops 2750000128 | bytes 7500000 | tf_op jit(solution)/shard_map/experts/pallas_call | solution.py:574
  188.0 4.3 %all-to-all-start.4 = ((bf16[8,104,768]{2,1,0:T(8,128)(2,1)}), bf16[8,104,768]{2,1,0:T(8,128)(2,1)S(1)}, u32[]{:S(2)}, u32[]{:S(2)}) async-start(bf16[8,104,768]{2,1,0:T(8,128)(2,1)} %get-tuple-element.203), calls=%async_computation.4 | async-start | bytes 2555904 | tf_op jit(solution)/shard_map/all_to_all | solution.py:1004
  192.3 26.9 %expert_weight_grads.1 = (f32[2,768,768]{2,1,0:T(8,128)}, bf16[4,768,768]{2,1,0:T(8,128)(2,1)}, f32[768,768]{1,0:T(8,128)}, f32[768,768]{1,0:T(8,128)}) custom-call(bf16[8,192,768]{2,1,0:T(8,128)(2,1)} %copy-done.8, bf16[8,96,768]{2,1,0:T(8,128)(2,1)} %all-to-all-done.1.x_ref.x_a, bf16[8,104,768]{2,1,0:T(8,128)(2,1)} %all-to-all-done.3.x_ref.x_b, ...), custom_call_target="tpu_custom_call" | custom-call | flops 2750000128 | bytes 7500000 | tf_op jit(solution)/shard_map/expert_weight_grads/pallas_call | solution.py:641
  224.0 4.6 %all-to-all-start.5 = ((bf16[8,192,768]{2,1,0:T(8,128)(2,1)}), bf16[8,192,768]{2,1,0:T(8,128)(2,1)}, u32[]{:S(2)}, u32[]{:S(2)}) async-start(bf16[8,192,768]{2,1,0:T(8,128)(2,1)} %get-tuple-element.228), calls=%async_computation.5 | async-start | bytes 4718592 | tf_op jit(solution)/shard_map/all_to_all | solution.py:1004
  228.6 11.8 %combine_back.1 = (f32[512,768]{1,0:T(8,128)}, bf16[512,768]{1,0:T(8,128)(2,1)}, f32[16,768]{1,0:T(8,128)}, bf16[192,512]{1,0:T(8,128)(2,1)}, bf16[192,512]{1,0:...) custom-call(s32[2]{0:T(128)} %pad_add_fusion.1.own_ref, bf16[768,512]{1,0:T(8,128)(2,1)} %get-tuple-element.163.hot_a, ...), custom_call_target="tpu_custom_call" | custom-call | flops 1210000000 | bytes 3300000 | tf_op jit(solution)/shard_map/combine_back/pallas_call | solution.py:718
  248.2 4.7 %collective-permute-done.17.refs_15_ = bf16[192,512]{1,0:T(8,128)(2,1)S(1)} collective-permute-done((bf16[192,512]{1,0:T(8,128)(2,1)}, bf16[192,512]{1,0:T(8,128)(2,1)S(1)}, u32[]{:S(2)}, u32[]{:S(2)}) %collective-permute-start.17) | collective-permute-done | bytes 196640 | tf_op jit(solution)/shard_map/ppermute | solution.py:40
  257.4 19.6 %attend_back.2 = (bf16[384,2048]{1,0:T(8,128)(2,1)}, bf16[8,2,24,768]{3,2,1,0:T(8,128)(2,1)}) custom-call(s32[3]{0:T(128)} %pad_add_fusion.info_ref, s32[2]{0:T(128)} %pad_add_fusion.1.own_ref, bf16[2048,192]{1,0:T(8,128)(2,1)} %get-tuple-element.158.k_ref, bf16[512,192]{1,0:T(8,128)(2,1)} %get-tuple-element.159.refs_0_, ...), custom_call_target="tpu_custom_call" | custom-call | flops 2420000000 | bytes 6600000 | tf_op jit(solution)/shard_map/attend_back/pallas_call | solution.py:352
  281.4 5.7 %collective-permute-done.20.far_ref = bf16[192,768]{1,0:T(8,128)(2,1)S(1)} collective-permute-done((bf16[192,768]{1,0:T(8,128)(2,1)S(1)}, bf16[192,768]{1,0:T(8,128)(2,1)S(1)}, u32[]{:S(2)}, u32[]{:S(2)}) %collective-permute-start.20) | collective-permute-done | bytes 294944 | tf_op jit(solution)/shard_map/ppermute | solution.py:40
  287.1 5.8 %all-to-all-start.6 = ((bf16[8,48,768]{2,1,0:T(8,128)(2,1)}), bf16[8,48,768]{2,1,0:T(8,128)(2,1)S(1)}, u32[]{:S(2)}, u32[]{:S(2)}) async-start(bf16[8,48,768]{2,1,0:T(8,128)(2,1)} %bitcast.90), calls=%async_computation.6 | async-start | bytes 1179648 | tf_op jit(solution)/shard_map/all_to_all | solution.py:1004
  294.3 11.4 %attend_back.3 = (bf16[192,2048]{1,0:T(8,128)(2,1)}, bf16[8,1,24,768]{3,2,1,0:T(8,128)(2,1)}) custom-call(s32[3]{0:T(128)} %pad_add_fusion.info_ref, s32[2]{0:T(128)} %pad_add_fusion.1.own_ref, bf16[2048,192]{1,0:T(8,128)(2,1)} %get-tuple-element.158.k_ref, bf16[512,192]{1,0:T(8,128)(2,1)} %get-tuple-element.159.refs_0_, ...), custom_call_target="tpu_custom_call" | custom-call | flops 1210000000 | bytes 3300000 | tf_op jit(solution)/shard_map/attend_back/pallas_call | solution.py:352
  309.8 5.1 %all-to-all-start.7 = ((bf16[8,104,768]{2,1,0:T(8,128)(2,1)}), bf16[8,104,768]{2,1,0:T(8,128)(2,1)S(1)}, u32[]{:S(2)}, u32[]{:S(2)}) async-start(bf16[8,104,768]{2,1,0:T(8,128)(2,1)} %mix_sums.1), calls=%async_computation.7 | async-start | bytes 2555904 | tf_op jit(solution)/shard_map/all_to_all | solution.py:1004
  314.9 4.9 %collective-permute-done.21 = bf16[768,768]{1,0:T(8,128)(2,1)} collective-permute-done((bf16[768,768]{1,0:T(8,128)(2,1)}, bf16[768,768]{1,0:T(8,128)(2,1)}, u32[]{:S(2)}, u32[]{:S(2)}) %collective-permute-start.21) | collective-permute-done | bytes 1179680 | tf_op jit(solution)/shard_map/ppermute | solution.py:40
  323.6 5.4 %spread_back.1 = (bf16[512,768]{1,0:T(8,128)(2,1)}, bf16[512,768]{1,0:T(8,128)(2,1)S(1)}, f32[512,768]{1,0:T(8,128)S(1)}, f32[512,768]{1,0:T(8,128)S(1)}) custom-call(s32[4]{0:T(128)S(1)} %pad_add_fusion.2.places_ref, bf16[384,2048]{1,0:T(8,128)(2,1)S(1)} %copy-done.5, bf16[192,2048]{1,0:T(8,128)(2,1)S(1)} %copy-done.7, bf16[576,768]{1,0:T(8,128)(2,1)S(1)} %copy-done.6), custom_call_target="tpu_custom_call" | custom-call | flops 880000000 | bytes 2400000 | tf_op jit(solution)/shard_map/spread_back/pallas_call | solution.py:806
  337.1 6.6 %combine.1 = bf16[512,768]{1,0:T(8,128)(2,1)} custom-call(bf16[512,768]{1,0:T(8,128)(2,1)} %get-tuple-element.165.p0a, bf16[512,768]{1,0:T(8,128)(2,1)} %get-tuple-element.166.p1a, bf16[512,768]{1,0:T(8,128)(2,1)} %get-tuple-element.167.p0b, bf16[512,768]{1,0:T(8,128)(2,1)} %get-tuple-element.168.p1b, f32[512,768]{1,0:T(8,128)} %get-tuple-element.187.residual_ref, ...), custom_call_target="tpu_custom_call" | custom-call | flops 660000000 | bytes 1800000 | tf_op jit(solution)/shard_map/combine/pallas_call | solution.py:767
  345.8 4.8 %all-to-all-start.8 = ((bf16[8,56,768]{2,1,0:T(8,128)(2,1)}), bf16[8,56,768]{2,1,0:T(8,128)(2,1)S(1)}, u32[]{:S(2)}, u32[]{:S(2)}) async-start(bf16[8,56,768]{2,1,0:T(8,128)(2,1)} %fold_sums.1), calls=%async_computation.8 | async-start | bytes 1376256 | tf_op jit(solution)/shard_map/all_to_all | solution.py:1004
  356.3 9.9 %expert_update.1 = (f32[768,768]{1,0:T(8,128)}, f32[768,768]{1,0:T(8,128)}, f32[768,768]{1,0:T(8,128)}, f32[768,768]{1,0:T(8,128)}) custom-call(s32[1]{0:T(128)} %bitcast.21.live_ref, f32[2,768,768]{2,1,0:T(8,128)} %get-tuple-element.259.own_ref, bf16[4,768,768]{2,1,0:T(8,128)(2,1)} %collective-permute-done.14.near_ref, ...), custom_call_target="tpu_custom_call" | custom-call | flops 880000000 | bytes 2400000 | tf_op jit(solution)/shard_map/expert_update/pallas_call | solution.py:987
  372.4 5.3 %fusion.4 = (f32[1,768,768]{2,1,0:T(8,128)}, f32[768,768]{1,0:T(8,128)S(1)}) fusion(f32[1,768,768]{2,1,0:T(8,128)} %param.35, pred[]{:T(512)S(6)} %ge.10, bf16[768,768]{1,0:T(8,128)(2,1)} %collective-permute-done.21, bf16[4,768,768]{2,1,0:T(8,128)(2,1)} %collective-permute-done.14.near_ref, f32[2,768,768]{2,1,0:T(8,128)} %get-tuple-element.259.own_ref), kind=kLoop, calls=%fused_computation.10 | loop fusion | flops 5898240 | bytes 11796481 | tf_op jit(solution)/shard_map/broadcast_in_dim | solution.py:1204
  377.6 7.6 %collective-permute-done.29.refs_6_ = bf16[8,56,768]{2,1,0:T(8,128)(2,1)S(1)} collective-permute-done((bf16[8,56,768]{2,1,0:T(8,128)(2,1)S(1)}, bf16[8,56,768]{2,1,0:T(8,128)(2,1)S(1)}, u32[]{:S(2)}, u32[]{:S(2)}) %collective-permute-start.29) | collective-permute-done | bytes 688160 | tf_op jit(solution)/shard_map/ppermute | solution.py:40
  392.4 8.5 %lay_out_sums.1 = (f32[768,2304]{1,0:T(8,128)}, f32[1,768]{1,0:T(1,128)S(1)}, f32[768,768]{1,0:T(8,128)}, f32[16,768]{1,0:T(8,128)S(1)}) custom-call(s32[2]{0:T(128)S(1)} %copy-done.4, bf16[8,48,768]{2,1,0:T(8,128)(2,1)} %slice.56.refs_0_, bf16[8,48,768]{2,1,0:T(8,128)(2,1)S(1)} %collective-permute-done.25.refs_1_, ...), custom_call_target="tpu_custom_call" | custom-call | flops 1100000000 | bytes 3000000 | tf_op jit(solution)/shard_map/lay_out_sums/pallas_call | solution.py:939
  (169 shorter events, 97.6 us)
Async XLA Ops:
  2.0 14.6 %collective-permute-start = (bf16[256,768]{1,0:T(8,128)(2,1)S(1)}, bf16[256,768]{1,0:T(8,128)(2,1)S(1)}, u32[]{:S(2)}, u32[]{:S(2)}) collective-permute-start(bf16[256,768]{1,0:T(8,128)(2,1)S(1)} %get-tuple-element.286), channel_id=1, source_target_pairs={{0,2},{1,3},{2,0},{3,1},{4,6},{5,7},{6,4},{7,5},{8,10},{9,11},{10,... | collective-permute-start | bytes 1179656 | tf_op jit(solution)/shard_map/ppermute | solution.py:40
  4.1 17.3 %collective-permute-start.1 = (bf16[256,768]{1,0:T(8,128)(2,1)S(1)}, bf16[256,768]{1,0:T(8,128)(2,1)S(1)}, u32[]{:S(2)}, u32[]{:S(2)}) collective-permute-start(bf16[256,768]{1,0:T(8,128)(2,1)S(1)} %get-tuple-element.285), channel_id=1, source_target_pairs={{0,2},{1,3},{2,0},{3,1},{4,6},{5,7},{6,4},{7,5},{8,10},{9,11},{10,... | collective-permute-start | bytes 1179656 | tf_op jit(solution)/shard_map/ppermute | solution.py:40
  22.1 62.0 %all-to-all-start = ((bf16[8,192,768]{2,1,0:T(8,128)(2,1)}), bf16[8,192,768]{2,1,0:T(8,128)(2,1)S(1)}, u32[]{:S(2)}, u32[]{:S(2)}) async-start(bf16[8,192,768]{2,1,0:T(8,128)(2,1)} %get-tuple-element.191), calls=%async_computation | async-start | bytes 4718592 | tf_op jit(solution)/shard_map/all_to_all | solution.py:1004
  29.7 34.4 %collective-permute-start.5 = (bf16[768,768]{1,0:T(8,128)(2,1)}, bf16[768,768]{1,0:T(8,128)(2,1)}, u32[]{:S(2)}, u32[]{:S(2)}) collective-permute-start(bf16[768,768]{1,0:T(8,128)(2,1)} %get-tuple-element.174.refs_0_), channel_id=1, source_target_pairs={{0,2},{1,3},{2,0},{3,1},{4,6},{5,7},{6,4},{7,5},{8,10},{9,11},{10,... | collective-permute-start | bytes 3538952 | tf_op jit(solution)/shard_map/ppermute | solution.py:40
  31.8 32.4 %collective-permute-start.6 = (bf16[768,768]{1,0:T(8,128)(2,1)}, bf16[768,768]{1,0:T(8,128)(2,1)}, u32[]{:S(2)}, u32[]{:S(2)}) collective-permute-start(bf16[768,768]{1,0:T(8,128)(2,1)} %get-tuple-element.174.refs_0_), channel_id=1, source_target_pairs={{0,1},{1,0},{2,3},{3,2},{4,5},{5,4},{6,7},{7,6},{8,9},{9,8},{10,11... | collective-permute-start | bytes 3538952 | tf_op jit(solution)/shard_map/ppermute | solution.py:40
  32.1 32.0 %collective-permute-start.7 = (bf16[768,768]{1,0:T(8,128)(2,1)}, bf16[768,768]{1,0:T(8,128)(2,1)}, u32[]{:S(2)}, u32[]{:S(2)}) collective-permute-start(bf16[768,768]{1,0:T(8,128)(2,1)} %get-tuple-element.193.refs_1_), channel_id=1, source_target_pairs={{0,1},{1,0},{2,3},{3,2},{4,5},{5,4},{6,7},{7,6},{8,9},{9,8},{10,11... | collective-permute-start | bytes 3538952 | tf_op jit(solution)/shard_map/ppermute | solution.py:40
  32.3 7.8 %collective-permute-start.2 = (bf16[512,768]{1,0:T(8,128)(2,1)S(1)}, bf16[512,768]{1,0:T(8,128)(2,1)}, u32[]{:S(2)}, u32[]{:S(2)}) collective-permute-start(bf16[512,768]{1,0:T(8,128)(2,1)S(1)} %bitcast.81), channel_id=1, source_target_pairs={{0,1},{1,0},{2,3},{3,2},{4,5},{5,4},{6,7},{7,6},{8,9},{9,8},{10,11... | collective-permute-start | bytes 2359304 | tf_op jit(solution)/shard_map/ppermute | solution.py:40
  65.5 9.8 %collective-permute-start.10 = (bf16[192,512]{1,0:T(8,128)(2,1)}, bf16[192,512]{1,0:T(8,128)(2,1)S(1)}, u32[]{:S(2)}, u32[]{:S(2)}) collective-permute-start(bf16[192,512]{1,0:T(8,128)(2,1)} %get-tuple-element.180), channel_id=1, source_target_pairs={{0,3},{1,2},{2,1},{3,0},{4,7},{5,6},{6,5},{7,4},{8,11},{9,10},{10,... | collective-permute-start | bytes 589832 | tf_op jit(solution)/shard_map/ppermute | solution.py:40
  84.1 34.9 %all-to-all-start.1 = ((bf16[8,96,768]{2,1,0:T(8,128)(2,1)}), bf16[8,96,768]{2,1,0:T(8,128)(2,1)}, u32[]{:S(2)}, u32[]{:S(2)}) async-start(bf16[8,96,768]{2,1,0:T(8,128)(2,1)} %get-tuple-element.192), calls=%async_computation.1 | async-start | bytes 2359296 | tf_op jit(solution)/shard_map/all_to_all | solution.py:1004
  90.1 33.7 %collective-permute-start.11 = (bf16[768,768]{1,0:T(8,128)(2,1)S(1)}, bf16[768,768]{1,0:T(8,128)(2,1)}, u32[]{:S(2)}, u32[]{:S(2)}) collective-permute-start(bf16[768,768]{1,0:T(8,128)(2,1)S(1)} %copy-done.10), channel_id=1, source_target_pairs={{0,2},{1,3},{2,0},{3,1},{4,6},{5,7},{6,4},{7,5},{8,10},{9,11},{10,... | collective-permute-start | bytes 3538952 | tf_op jit(solution)/shard_map/ppermute | solution.py:40
  119.0 35.2 %all-to-all-start.3 = ((bf16[8,104,768]{2,1,0:T(8,128)(2,1)}), bf16[8,104,768]{2,1,0:T(8,128)(2,1)}, u32[]{:S(2)}, u32[]{:S(2)}) async-start(bf16[8,104,768]{2,1,0:T(8,128)(2,1)} %get-tuple-element.200), calls=%async_computation.3 | async-start | bytes 2555904 | tf_op jit(solution)/shard_map/all_to_all | solution.py:1004
  154.2 33.8 %all-to-all-start.2 = ((bf16[8,96,768]{2,1,0:T(8,128)(2,1)}), bf16[8,96,768]{2,1,0:T(8,128)(2,1)S(1)}, u32[]{:S(2)}, u32[]{:S(2)}) async-start(bf16[8,96,768]{2,1,0:T(8,128)(2,1)} %get-tuple-element.199), calls=%async_computation.2 | async-start | bytes 2359296 | tf_op jit(solution)/shard_map/all_to_all | solution.py:1004
  188.0 34.4 %all-to-all-start.4 = ((bf16[8,104,768]{2,1,0:T(8,128)(2,1)}), bf16[8,104,768]{2,1,0:T(8,128)(2,1)S(1)}, u32[]{:S(2)}, u32[]{:S(2)}) async-start(bf16[8,104,768]{2,1,0:T(8,128)(2,1)} %get-tuple-element.203), calls=%async_computation.4 | async-start | bytes 2555904 | tf_op jit(solution)/shard_map/all_to_all | solution.py:1004
  222.4 18.0 %collective-permute-start.14 = (bf16[4,768,768]{2,1,0:T(8,128)(2,1)}, bf16[4,768,768]{2,1,0:T(8,128)(2,1)}, u32[]{:S(2)}, u32[]{:S(2)}) collective-permute-start(bf16[4,768,768]{2,1,0:T(8,128)(2,1)} %get-tuple-element.215), channel_id=1, source_target_pairs={{0,1},{1,0},{2,3},{3,2},{4,5},{5,4},{6,7},{7,6},{8,9},{9,8},{10,11... | collective-permute-start | bytes 14155784 | tf_op jit(solution)/shard_map/ppermute | solution.py:40
  224.0 57.5 %all-to-all-start.5 = ((bf16[8,192,768]{2,1,0:T(8,128)(2,1)}), bf16[8,192,768]{2,1,0:T(8,128)(2,1)}, u32[]{:S(2)}, u32[]{:S(2)}) async-start(bf16[8,192,768]{2,1,0:T(8,128)(2,1)} %get-tuple-element.228), calls=%async_computation.5 | async-start | bytes 4718592 | tf_op jit(solution)/shard_map/all_to_all | solution.py:1004
  240.3 7.1 %collective-permute-start.15 = (bf16[192,512]{1,0:T(8,128)(2,1)}, bf16[192,512]{1,0:T(8,128)(2,1)S(1)}, u32[]{:S(2)}, u32[]{:S(2)}) collective-permute-start(bf16[192,512]{1,0:T(8,128)(2,1)} %get-tuple-element.217), channel_id=1, source_target_pairs={{0,1},{1,0},{2,3},{3,2},{4,5},{5,4},{6,7},{7,6},{8,9},{9,8},{10,11... | collective-permute-start | bytes 589832 | tf_op jit(solution)/shard_map/ppermute | solution.py:40
  241.4 6.8 %collective-permute-start.16 = (bf16[192,512]{1,0:T(8,128)(2,1)}, bf16[192,512]{1,0:T(8,128)(2,1)S(1)}, u32[]{:S(2)}, u32[]{:S(2)}) collective-permute-start(bf16[192,512]{1,0:T(8,128)(2,1)} %get-tuple-element.218), channel_id=1, source_target_pairs={{0,2},{1,3},{2,0},{3,1},{4,6},{5,7},{6,4},{7,5},{8,10},{9,11},{10,... | collective-permute-start | bytes 589832 | tf_op jit(solution)/shard_map/ppermute | solution.py:40
  242.7 10.2 %collective-permute-start.17 = (bf16[192,512]{1,0:T(8,128)(2,1)}, bf16[192,512]{1,0:T(8,128)(2,1)S(1)}, u32[]{:S(2)}, u32[]{:S(2)}) collective-permute-start(bf16[192,512]{1,0:T(8,128)(2,1)} %get-tuple-element.219), channel_id=1, source_target_pairs={{0,3},{1,2},{2,1},{3,0},{4,7},{5,6},{6,5},{7,4},{8,11},{9,10},{10,... | collective-permute-start | bytes 589832 | tf_op jit(solution)/shard_map/ppermute | solution.py:40
  252.9 34.2 %collective-permute-start.18 = (bf16[768,768]{1,0:T(8,128)(2,1)}, bf16[768,768]{1,0:T(8,128)(2,1)}, u32[]{:S(2)}, u32[]{:S(2)}) collective-permute-start(bf16[768,768]{1,0:T(8,128)(2,1)} %get-tuple-element.232), channel_id=1, source_target_pairs={{0,2},{1,3},{2,0},{3,1},{4,6},{5,7},{6,4},{7,5},{8,10},{9,11},{10,... | collective-permute-start | bytes 3538952 | tf_op jit(solution)/shard_map/ppermute | solution.py:40
  257.3 19.8 %collective-permute-start.19 = (bf16[2,192,768]{2,1,0:T(8,128)(2,1)}, bf16[2,192,768]{2,1,0:T(8,128)(2,1)S(1)}, u32[]{:S(2)}, u32[]{:S(2)}) collective-permute-start(bf16[2,192,768]{2,1,0:T(8,128)(2,1)} %get-tuple-element.235), channel_id=1, source_target_pairs={{0,1},{1,0},{2,3},{3,2},{4,5},{5,4},{6,7},{7,6},{8,9},{9,8},{10,11... | collective-permute-start | bytes 1769480 | tf_op jit(solution)/shard_map/ppermute | solution.py:40
  277.1 10.0 %collective-permute-start.20 = (bf16[192,768]{1,0:T(8,128)(2,1)S(1)}, bf16[192,768]{1,0:T(8,128)(2,1)S(1)}, u32[]{:S(2)}, u32[]{:S(2)}) collective-permute-start(bf16[192,768]{1,0:T(8,128)(2,1)S(1)} %fusion.16), channel_id=1, source_target_pairs={{0,2},{1,3},{2,0},{3,1},{4,6},{5,7},{6,4},{7,5},{8,10},{9,11},{10,... | collective-permute-start | bytes 884744 | tf_op jit(solution)/shard_map/ppermute | solution.py:40
  287.1 20.5 %all-to-all-start.6 = ((bf16[8,48,768]{2,1,0:T(8,128)(2,1)}), bf16[8,48,768]{2,1,0:T(8,128)(2,1)S(1)}, u32[]{:S(2)}, u32[]{:S(2)}) async-start(bf16[8,48,768]{2,1,0:T(8,128)(2,1)} %bitcast.90), calls=%async_computation.6 | async-start | bytes 1179648 | tf_op jit(solution)/shard_map/all_to_all | solution.py:1004
  293.0 26.9 %collective-permute-start.21 = (bf16[768,768]{1,0:T(8,128)(2,1)}, bf16[768,768]{1,0:T(8,128)(2,1)}, u32[]{:S(2)}, u32[]{:S(2)}) collective-permute-start(bf16[768,768]{1,0:T(8,128)(2,1)} %get-tuple-element.245), channel_id=1, source_target_pairs={{0,2},{1,3},{2,0},{3,1},{4,6},{5,7},{6,4},{7,5},{8,10},{9,11},{10,... | collective-permute-start | bytes 3538952 | tf_op jit(solution)/shard_map/ppermute | solution.py:40
  309.8 35.1 %all-to-all-start.7 = ((bf16[8,104,768]{2,1,0:T(8,128)(2,1)}), bf16[8,104,768]{2,1,0:T(8,128)(2,1)S(1)}, u32[]{:S(2)}, u32[]{:S(2)}) async-start(bf16[8,104,768]{2,1,0:T(8,128)(2,1)} %mix_sums.1), calls=%async_computation.7 | async-start | bytes 2555904 | tf_op jit(solution)/shard_map/all_to_all | solution.py:1004
  333.8 19.1 %collective-permute-start.24 = (bf16[512,768]{1,0:T(8,128)(2,1)}, bf16[512,768]{1,0:T(8,128)(2,1)}, u32[]{:S(2)}, u32[]{:S(2)}) collective-permute-start(bf16[512,768]{1,0:T(8,128)(2,1)} %add_convert_fusion), channel_id=1, source_target_pairs={{0,2},{1,3},{2,0},{3,1},{4,6},{5,7},{6,4},{7,5},{8,10},{9,11},{10,... | collective-permute-start | bytes 2359304 | tf_op jit(solution)/shard_map/ppermute | solution.py:40
  335.0 19.1 %collective-permute-start.23 = (bf16[512,768]{1,0:T(8,128)(2,1)}, bf16[512,768]{1,0:T(8,128)(2,1)}, u32[]{:S(2)}, u32[]{:S(2)}) collective-permute-start(bf16[512,768]{1,0:T(8,128)(2,1)} %get-tuple-element.256), channel_id=1, source_target_pairs={{0,1},{1,0},{2,3},{3,2},{4,5},{5,4},{6,7},{7,6},{8,9},{9,8},{10,11... | collective-permute-start | bytes 2359304 | tf_op jit(solution)/shard_map/ppermute | solution.py:40
  345.8 23.9 %all-to-all-start.8 = ((bf16[8,56,768]{2,1,0:T(8,128)(2,1)}), bf16[8,56,768]{2,1,0:T(8,128)(2,1)S(1)}, u32[]{:S(2)}, u32[]{:S(2)}) async-start(bf16[8,56,768]{2,1,0:T(8,128)(2,1)} %fold_sums.1), calls=%async_computation.8 | async-start | bytes 1376256 | tf_op jit(solution)/shard_map/all_to_all | solution.py:1004
  352.9 19.0 %collective-permute-start.26 = (bf16[8,48,768]{2,1,0:T(8,128)(2,1)}, bf16[8,48,768]{2,1,0:T(8,128)(2,1)S(1)}, u32[]{:S(2)}, u32[]{:S(2)}) collective-permute-start(bf16[8,48,768]{2,1,0:T(8,128)(2,1)} %slice.56.refs_0_), channel_id=1, source_target_pairs={{0,2},{1,3},{2,0},{3,1},{4,6},{5,7},{6,4},{7,5},{8,10},{9,11},{10,... | collective-permute-start | bytes 1769480 | tf_op jit(solution)/shard_map/ppermute | solution.py:40
  369.7 15.4 %collective-permute-start.29 = (bf16[8,56,768]{2,1,0:T(8,128)(2,1)S(1)}, bf16[8,56,768]{2,1,0:T(8,128)(2,1)S(1)}, u32[]{:S(2)}, u32[]{:S(2)}) collective-permute-start(bf16[8,56,768]{2,1,0:T(8,128)(2,1)S(1)} %all-to-all-done.8.refs_4_), channel_id=1, source_target_pairs={{0,2},{1,3},{2,0},{3,1},{4,6},{5,7},{6,4},{7,5},{8,10},{9,11},{10,... | collective-permute-start | bytes 2064392 | tf_op jit(solution)/shard_map/ppermute | solution.py:40
  370.0 21.5 %collective-permute-start.25 = (bf16[8,48,768]{2,1,0:T(8,128)(2,1)}, bf16[8,48,768]{2,1,0:T(8,128)(2,1)S(1)}, u32[]{:S(2)}, u32[]{:S(2)}) collective-permute-start(bf16[8,48,768]{2,1,0:T(8,128)(2,1)} %slice.56.refs_0_), channel_id=1, source_target_pairs={{0,1},{1,0},{2,3},{3,2},{4,5},{5,4},{6,7},{7,6},{8,9},{9,8},{10,11... | collective-permute-start | bytes 1769480 | tf_op jit(solution)/shard_map/ppermute | solution.py:40
  371.8 19.7 %collective-permute-start.27 = (bf16[8,48,768]{2,1,0:T(8,128)(2,1)S(1)}, bf16[8,48,768]{2,1,0:T(8,128)(2,1)S(1)}, u32[]{:S(2)}, u32[]{:S(2)}) collective-permute-start(bf16[8,48,768]{2,1,0:T(8,128)(2,1)S(1)} %collective-permute-done.26.refs_2_), channel_id=1, source_target_pairs={{0,1},{1,0},{2,3},{3,2},{4,5},{5,4},{6,7},{7,6},{8,9},{9,8},{10,11... | collective-permute-start | bytes 1769480 | tf_op jit(solution)/shard_map/ppermute | solution.py:40
  371.9 19.6 %collective-permute-start.28 = (bf16[8,56,768]{2,1,0:T(8,128)(2,1)S(1)}, bf16[8,56,768]{2,1,0:T(8,128)(2,1)S(1)}, u32[]{:S(2)}, u32[]{:S(2)}) collective-permute-start(bf16[8,56,768]{2,1,0:T(8,128)(2,1)S(1)} %all-to-all-done.8.refs_4_), channel_id=1, source_target_pairs={{0,1},{1,0},{2,3},{3,2},{4,5},{5,4},{6,7},{7,6},{8,9},{9,8},{10,11... | collective-permute-start | bytes 2064392 | tf_op jit(solution)/shard_map/ppermute | solution.py:40
  (47 other events, 394.7 us)

commit v5 on v4

--- a/solution.py
+++ b/solution.py
@@ -137,21 +137,26 @@
 
 
 def qkv_kernel(
-    pieces, own_ref, *refs
+    pieces, turned, own_ref, *refs
 ):
     blocks, refs = refs[: 2 * pieces], refs[2 * pieces :]
-    gain_ref, w_ref, a0, a1, q0, q1, k0, k1, v0, v1, w_buf, heads_ref = refs
-    width, cols = heads_ref.shape
-    third = cols // 3
-    for h in range(width // third):
-
-        @pl.when(own_ref[0] == h)
-        def pick(h=h):
-            for t in range(3):
-                start = t * width + h * third
-                heads_ref[:, t * third : (t + 1) * third] = w_ref[:, start : start + third]
-
-    w_buf[...] = heads_ref[...].T
+    gain_ref, w_ref, a0, a1, q0, q1, k0, k1, v0, v1 = refs[:10]
+    if turned:
+        w_buf = w_ref
+    else:
+        w_buf, heads_ref = refs[10:]
+        width, cols = heads_ref.shape
+        part = cols // 3
+        for h in range(width // part):
+
+            @pl.when(own_ref[0] == h)
+            def pick(h=h):
+                for t in range(3):
+                    start = t * width + h * part
+                    heads_ref[:, t * part : (t + 1) * part] = w_ref[:, start : start + part]
+
+        w_buf[...] = heads_ref[...].T
+    third = w_buf.shape[0] // 3
     outs = ((a0, q0, k0, v0), (a1, q1, k1, v1))
     for n, (a_ref, qkv_ref, k_ref, v_ref) in enumerate(outs):
         x = [x_ref[...] for x_ref in blocks[n * pieces : (n + 1) * pieces]]
@@ -162,23 +167,24 @@
         qkv_t = mm(w_buf[...], a, NT).astype(bf16)
         qkv_ref[0:third, :] = qkv_t[0:third, :] * jnp.asarray(0.125, bf16)
         qkv_ref[third:, :] = qkv_t[third:, :]
-        both = mm(a, heads_ref[:, third:]).astype(bf16)
+        both = mm(a, w_buf[third:, :], NT).astype(bf16)
         k_ref[...] = both[:, :third]
         v_ref[...] = both[:, third:]
 
 
-def project_qkv(own, blocks, gain, w_qkv):
+def project_qkv(own, blocks, gain, w_qkv, turned=False):
     pieces = len(blocks) // 2
     count, width = pieces * blocks[0].shape[0], blocks[0].shape[1]
-    cols = w_qkv.shape[1] // 4
+    cols = w_qkv.shape[0] if turned else w_qkv.shape[1] // 4
     third = cols // 3
-    shapes = [(count, width)] * 2 + [(cols, count)] * 2 + [(count, third)] * 4 + [(cols, width)]
+    shapes = [(count, width)] * 2 + [(cols, count)] * 2 + [(count, third)] * 4
+    shapes += [] if turned else [(cols, width)]
     return pl.pallas_call(
-        functools.partial(qkv_kernel, pieces),
+        functools.partial(qkv_kernel, pieces, turned),
         out_shape=[jax.ShapeDtypeStruct(shape, bf16) for shape in shapes],
         in_specs=[smem_spec()] + [vmem_spec()] * (2 * pieces + 2),
-        out_specs=[vmem_spec()] * 9,
-        scratch_shapes=[pltpu.VMEM((width, cols), bf16)],
+        out_specs=[vmem_spec()] * len(shapes),
+        scratch_shapes=[] if turned else [pltpu.VMEM((width, cols), bf16)],
         compiler_params=params(60),
         name="norm_qkv",
         cost_estimate=cost(0.1),
@@ -1046,8 +1052,7 @@
     heads = group // HEAD_DIM
     is_new = exp_index >= frozen_count
 
-    x_halves = [x_own[: count // 2], x_own[count // 2 :]]
-    x_far = [swap(half, "hid", 2) for half in x_halves]
+    x_far = [swap(x_own, "hid", 2)]
     x_near = swap(x_own, "hid", 1)
     routes_t = routes[0].T
     hots, picks, dy_send = make_tables(routes_t, dy, experts, capacity)
@@ -1063,8 +1068,10 @@
     down_low = down_w[0].astype(bf16)
     router_t = router_w.T
     first = project_qkv(own, (x_own, x_near), gain_attn[None], w_qkv)
-    x_far, (info, dy_send, up_low, down_low, router_t, routes_t) = lax.optimization_barrier(
-        (x_far, (info, dy_send, up_low, down_low, router_t, routes_t))
+    x_far, (x_near, info, dy_send, up_low, down_low, router_t, routes_t) = (
+        lax.optimization_barrier(
+            (x_far, (x_near, info, dy_send, up_low, down_low, router_t, routes_t))
+        )
     )
     x_last = [swap(half, "hid", 1) for half in x_far]
     dy_all = exchange(dy_send, "exp")
@@ -1072,8 +1079,8 @@
     up_far = swap(up_low, "hid", 2)
     up_near, down_near = (swap(tie(low, x_last), "hid", 1) for low in (up_low, down_low))
 
-    second = project_qkv(own, (*x_far, *x_last), gain_attn[None], w_qkv)
     w_t = first[8]
+    second = project_qkv(own, (*x_far, *x_last), gain_attn[None], w_t, True)
     a_parts, qkv_parts, k_parts, v_parts = (
         (*first[n : n + 2], *second[n : n + 2]) for n in (0, 2, 4, 6)
     )

time: 410 us -> 410 us (level)
    unnamed x78 -> x72, local copies, waits for them, and re-layouts: 8.1 us -> 10.4 us
    ppermute x31 -> x29, starting transfers between devices: 27.9 us -> 28.5 us  [swap(): return lax.ppermute(value, axis, [(i, i ^ distance) for i in range(count)])]
    ppermute x31 -> x29, waiting for transfers between devices: 45.4 us -> 45.7 us  [swap(): return lax.ppermute(value, axis, [(i, i ^ distance) for i in range(count)])]
  transfers between devices with their start and end apart: 40 -> 38, of which waited for: 20 -> 19; matrix products, arithmetic and copies ran while one was open for 8% -> 8% of each run, Pallas kernels for 47% -> 47%
where the time goes in v5:
time: 410 us; the launch traced here: 403 us
  Pallas kernels  197 us (48%)
  waiting for transfers between devices  85.7 us (21%)
  starting transfers between devices  74.4 us (18%)
  other arithmetic  31 us (8%)
  local copies, waits for them, and re-layouts  13 us (3%)
    pallas_call x2, Pallas kernels, run_experts(): pl.pallas_call(functools.partial(expert_kernel, half, 0), out_shape=[shap...  48.6 us
    all_to_all x9, starting transfers between devices, exchange(): return lax.all_to_all(value, axis, split_axis=0, concat_axis=0, tiled=True)  45.9 us
    ppermute x29, waiting for transfers between devices, swap(): return lax.ppermute(value, axis, [(i, i ^ distance) for i in range(count)])  45.7 us
    all_to_all x9, waiting for transfers between devices, exchange(): return lax.all_to_all(value, axis, split_axis=0, concat_axis=0, tiled=True)  40 us
    pallas_call x2, Pallas kernels, attend_back(): pl.pallas_call(functools.partial(attend_back_kernel, block, first), out_s...  31.4 us
    ppermute x29, starting transfers between devices, swap(): return lax.ppermute(value, axis, [(i, i ^ distance) for i in range(count)])  28.5 us
    pallas_call x1, Pallas kernels, weight_grads(): pl.pallas_call(weight_kernel, out_shape=[jax.ShapeDtypeStruct((2, width,...  26.9 us
    pallas_call x1, Pallas kernels, attend(): pl.pallas_call(functools.partial(attend_kernel, block), out_shape=[jax.Sh...  18.1 us
  transfers between devices with their start and end apart: 38, of which 19 were waited for; matrix products, arithmetic and copies ran while one was open for 8% of the time, Pallas kernels for 47%

profile of v5, /device:TPU:1, one launch (start us, length us, event | category | flops | bytes accessed | tf_op | source)
XLA Modules:
  0.0 402.7 jit_solution(12156184478475492923)
XLA Ops:
  4.4 5.1 %slot_tables.1 = (bf16[768,512]{1,0:T(8,128)(2,1)}, bf16[768,512]{1,0:T(8,128)(2,1)}, bf16[512,768]{1,0:T(8,128)(2,1)}, bf16[512,768]{1,0:T(8,128)(2,1)}, bf16[5...) custom-call(s32[2,512]{1,0:T(2,128)} %bitcast.90, bf16[512,768]{1,0:T(8,128)(2,1)} %bitcast.81), custom_call_target="tpu_custom_call" | custom-call | flops 11000000 | bytes 30000 | tf_op jit(solution)/shard_map/slot_tables/pallas_call | solution.py:127
  21.4 5.5 %all-to-all-start = ((bf16[8,192,768]{2,1,0:T(8,128)(2,1)}), bf16[8,192,768]{2,1,0:T(8,128)(2,1)S(1)}, u32[]{:S(2)}, u32[]{:S(2)}) async-start(bf16[8,192,768]{2,1,0:T(8,128)(2,1)} %get-tuple-element.190), calls=%async_computation | async-start | bytes 4718592 | tf_op jit(solution)/shard_map/all_to_all | solution.py:1010
  33.3 6.3 %norm_qkv.2 = (bf16[512,768]{1,0:T(8,128)(2,1)}, bf16[512,768]{1,0:T(8,128)(2,1)}, bf16[576,512]{1,0:T(8,128)(2,1)}, bf16[576,512]{1,0:T(8,128)(2,1)}, bf16[512,...) custom-call(s32[2]{0:T(128)} %pad_add_fusion.1.own_ref, ...), custom_call_target="tpu_custom_call" | custom-call | flops 11000000 | bytes 30000 | tf_op jit(solution)/shard_map/norm_qkv/pallas_call | solution.py:182
  39.6 4.8 %norm_qkv.3 = (bf16[512,768]{1,0:T(8,128)(2,1)}, bf16[512,768]{1,0:T(8,128)(2,1)}, bf16[576,512]{1,0:T(8,128)(2,1)}, bf16[576,512]{1,0:T(8,128)(2,1)}, bf16[512,...) custom-call(s32[2]{0:T(128)} %pad_add_fusion.1.own_ref, ...), custom_call_target="tpu_custom_call" | custom-call | flops 11000000 | bytes 30000 | tf_op jit(solution)/shard_map/norm_qkv/pallas_call | solution.py:182
  44.4 18.1 %attend.1 = (f32[192,2048]{1,0:T(8,128)}, f32[3,1,2048]{2,1,0:T(1,128)}, bf16[2048,192]{1,0:T(8,128)(2,1)}, bf16[192,512]{1,0:T(8,128)(2,1)}, bf16[192,512]{1,0:...) custom-call(s32[3]{0:T(128)} %pad_add_fusion.info_ref, s32[2]{0:T(128)} %pad_add_fusion.1.own_ref, ...), custom_call_target="tpu_custom_call" | custom-call | flops 11000000 | bytes 30000 | tf_op jit(solution)/shard_map/attend/pallas_call | solution.py:281
  69.2 4.7 %collective-permute-done.8.t3 = bf16[192,512]{1,0:T(8,128)(2,1)} collective-permute-done((bf16[192,512]{1,0:T(8,128)(2,1)}, bf16[192,512]{1,0:T(8,128)(2,1)}, u32[]{:S(2)}, u32[]{:S(2)}) %collective-permute-start.8) | collective-permute-done | bytes 196640 | tf_op jit(solution)/shard_map/ppermute | solution.py:40
  73.9 8.0 %project_dispatch.1 = (f32[512,768]{1,0:T(8,128)}, f32[2,512]{1,0:T(2,128)}, bf16[8,96,768]{2,1,0:T(8,128)(2,1)}, bf16[8,104,768]{2,1,0:T(8,128)(2,1)}) custom-call(s32[2]{0:T(128)} %pad_add_fusion.1.own_ref, bf16[192,512]{1,0:T(8,128)(2,1)} %get-tuple-element.180.t0, bf16[192,512]{1,0:T(8,128)(2,1)} %copy-done.20, bf16[192,512]{1,0:T(8,128)(2,1)} %copy-done.21, ...), custom_call_target="tpu_custom_call" | custom-call | flops 11000000 | bytes 30000 | tf_op jit(solution)/shard_map/project_dispatch/pallas_call | solution.py:458
  81.9 6.0 %all-to-all-start.1 = ((bf16[8,96,768]{2,1,0:T(8,128)(2,1)}), bf16[8,96,768]{2,1,0:T(8,128)(2,1)}, u32[]{:S(2)}, u32[]{:S(2)}) async-start(bf16[8,96,768]{2,1,0:T(8,128)(2,1)} %get-tuple-element.191), calls=%async_computation.1 | async-start | bytes 2359296 | tf_op jit(solution)/shard_map/all_to_all | solution.py:1010
  89.2 27.4 %all-to-all-done.1.x_ref.x_a = bf16[8,96,768]{2,1,0:T(8,128)(2,1)} async-done(((bf16[8,96,768]{2,1,0:T(8,128)(2,1)}), bf16[8,96,768]{2,1,0:T(8,128)(2,1)}, u32[]{:S(2)}, u32[]{:S(2)}) %all-to-all-start.1) | async-done | bytes 1179680 | tf_op jit(solution)/shard_map/all_to_all | solution.py:1010
  116.6 4.5 %all-to-all-start.3 = ((bf16[8,104,768]{2,1,0:T(8,128)(2,1)}), bf16[8,104,768]{2,1,0:T(8,128)(2,1)}, u32[]{:S(2)}, u32[]{:S(2)}) async-start(bf16[8,104,768]{2,1,0:T(8,128)(2,1)} %get-tuple-element.199), calls=%async_computation.3 | async-start | bytes 2555904 | tf_op jit(solution)/shard_map/all_to_all | solution.py:1010
  127.5 24.3 %experts.2 = (bf16[8,192,768]{2,1,0:T(8,128)(2,1)}, bf16[8,96,768]{2,1,0:T(8,128)(2,1)}, bf16[4,768,768]{2,1,0:T(8,128)(2,1)}, bf16[4,768,768]{2,1,0:T(8,128)(2,1)}, bf16[8,8,128]{2,1,0:T(8,128)(2,1)}) custom-call(bf16[8,96,768]{2,1,0:T(8,128)(2,1)} %all-to-all-done.1.x_ref.x_a, bf16[8,192,768]{2,1,0:T(8,128)(2,1)} %copy-done.8, ...), custom_call_target="tpu_custom_call" | custom-call | flops 2750000128 | bytes 7500000 | tf_op jit(solution)/shard_map/experts/pallas_call | solution.py:580
  151.8 5.7 %all-to-all-start.2 = ((bf16[8,96,768]{2,1,0:T(8,128)(2,1)}), bf16[8,96,768]{2,1,0:T(8,128)(2,1)S(1)}, u32[]{:S(2)}, u32[]{:S(2)}) async-start(bf16[8,96,768]{2,1,0:T(8,128)(2,1)} %get-tuple-element.198), calls=%async_computation.2 | async-start | bytes 2359296 | tf_op jit(solution)/shard_map/all_to_all | solution.py:1010
  157.5 24.4 %experts.3 = (bf16[8,192,768]{2,1,0:T(8,128)(2,1)}, bf16[8,104,768]{2,1,0:T(8,128)(2,1)}, bf16[4,768,768]{2,1,0:T(8,128)(2,1)}, bf16[4,768,768]{2,1,0:T(8,128)(2,1)}) custom-call(bf16[8,104,768]{2,1,0:T(8,128)(2,1)} %all-to-all-done.3.x_ref.x_b, bf16[8,192,768]{2,1,0:T(8,128)(2,1)} %copy-done.8, ...), custom_call_target="tpu_custom_call", output_to_operand_aliasing={{0}: (11, {})} | custom-call | flops 2750000128 | bytes 7500000 | tf_op jit(solution)/shard_map/experts/pallas_call | solution.py:580
  185.5 4.3 %all-to-all-start.4 = ((bf16[8,104,768]{2,1,0:T(8,128)(2,1)}), bf16[8,104,768]{2,1,0:T(8,128)(2,1)S(1)}, u32[]{:S(2)}, u32[]{:S(2)}) async-start(bf16[8,104,768]{2,1,0:T(8,128)(2,1)} %get-tuple-element.202), calls=%async_computation.4 | async-start | bytes 2555904 | tf_op jit(solution)/shard_map/all_to_all | solution.py:1010
  189.9 26.9 %expert_weight_grads.1 = (f32[2,768,768]{2,1,0:T(8,128)}, bf16[4,768,768]{2,1,0:T(8,128)(2,1)}, f32[768,768]{1,0:T(8,128)}, f32[768,768]{1,0:T(8,128)}) custom-call(bf16[8,192,768]{2,1,0:T(8,128)(2,1)} %copy-done.8, bf16[8,96,768]{2,1,0:T(8,128)(2,1)} %all-to-all-done.1.x_ref.x_a, bf16[8,104,768]{2,1,0:T(8,128)(2,1)} %all-to-all-done.3.x_ref.x_b, ...), custom_call_target="tpu_custom_call" | custom-call | flops 2750000128 | bytes 7500000 | tf_op jit(solution)/shard_map/expert_weight_grads/pallas_call | solution.py:647
  221.5 4.6 %all-to-all-start.5 = ((bf16[8,192,768]{2,1,0:T(8,128)(2,1)}), bf16[8,192,768]{2,1,0:T(8,128)(2,1)}, u32[]{:S(2)}, u32[]{:S(2)}) async-start(bf16[8,192,768]{2,1,0:T(8,128)(2,1)} %get-tuple-element.227), calls=%async_computation.5 | async-start | bytes 4718592 | tf_op jit(solution)/shard_map/all_to_all | solution.py:1010
  226.1 11.8 %combine_back.1 = (f32[512,768]{1,0:T(8,128)}, bf16[512,768]{1,0:T(8,128)(2,1)}, f32[16,768]{1,0:T(8,128)}, bf16[192,512]{1,0:T(8,128)(2,1)}, bf16[192,512]{1,0:...) custom-call(s32[2]{0:T(128)} %pad_add_fusion.1.own_ref, bf16[768,512]{1,0:T(8,128)(2,1)} %get-tuple-element.162.hot_a, ...), custom_call_target="tpu_custom_call" | custom-call | flops 1210000000 | bytes 3300000 | tf_op jit(solution)/shard_map/combine_back/pallas_call | solution.py:724
  240.7 4.2 %fusion.2 = (bf16[768,768]{1,0:T(8,128)(2,1)}, bf16[768,768]{1,0:T(8,128)(2,1)}) fusion(f32[768,768]{1,0:T(8,128)} %get-tuple-element.230, bf16[4,768,768]{2,1,0:T(8,128)(2,1)} %collective-permute-done.12.near_ref, f32[768,768]{1,0:T(8,128)S(1)} %copy-done.18), kind=kLoop, calls=%fused_computation.5 | loop fusion | flops 3538944 | bytes 9437184 | tf_op jit(solution)/shard_map/convert_element_type | solution.py:1129
  245.8 4.7 %collective-permute-done.15.refs_15_ = bf16[192,512]{1,0:T(8,128)(2,1)S(1)} collective-permute-done((bf16[192,512]{1,0:T(8,128)(2,1)}, bf16[192,512]{1,0:T(8,128)(2,1)S(1)}, u32[]{:S(2)}, u32[]{:S(2)}) %collective-permute-start.15) | collective-permute-done | bytes 196640 | tf_op jit(solution)/shard_map/ppermute | solution.py:40
  255.7 19.9 %attend_back.2 = (bf16[384,2048]{1,0:T(8,128)(2,1)}, bf16[8,2,24,768]{3,2,1,0:T(8,128)(2,1)}) custom-call(s32[3]{0:T(128)} %pad_add_fusion.info_ref, s32[2]{0:T(128)} %pad_add_fusion.1.own_ref, bf16[2048,192]{1,0:T(8,128)(2,1)} %get-tuple-element.157.k_ref, bf16[512,192]{1,0:T(8,128)(2,1)} %get-tuple-element.158.refs_0_, ...), custom_call_target="tpu_custom_call" | custom-call | flops 2420000000 | bytes 6600000 | tf_op jit(solution)/shard_map/attend_back/pallas_call | solution.py:358
  278.8 6.6 %collective-permute-done.18.far_ref = bf16[192,768]{1,0:T(8,128)(2,1)S(1)} collective-permute-done((bf16[192,768]{1,0:T(8,128)(2,1)S(1)}, bf16[192,768]{1,0:T(8,128)(2,1)S(1)}, u32[]{:S(2)}, u32[]{:S(2)}) %collective-permute-start.18) | collective-permute-done | bytes 294944 | tf_op jit(solution)/shard_map/ppermute | solution.py:40
  286.4 5.6 %all-to-all-start.6 = ((bf16[8,48,768]{2,1,0:T(8,128)(2,1)}), bf16[8,48,768]{2,1,0:T(8,128)(2,1)S(1)}, u32[]{:S(2)}, u32[]{:S(2)}) async-start(bf16[8,48,768]{2,1,0:T(8,128)(2,1)} %bitcast.87), calls=%async_computation.6 | async-start | bytes 1179648 | tf_op jit(solution)/shard_map/all_to_all | solution.py:1010
  293.3 11.4 %attend_back.3 = (bf16[192,2048]{1,0:T(8,128)(2,1)}, bf16[8,1,24,768]{3,2,1,0:T(8,128)(2,1)}) custom-call(s32[3]{0:T(128)} %pad_add_fusion.info_ref, s32[2]{0:T(128)} %pad_add_fusion.1.own_ref, bf16[2048,192]{1,0:T(8,128)(2,1)} %get-tuple-element.157.k_ref, bf16[512,192]{1,0:T(8,128)(2,1)} %get-tuple-element.158.refs_0_, ...), custom_call_target="tpu_custom_call" | custom-call | flops 1210000000 | bytes 3300000 | tf_op jit(solution)/shard_map/attend_back/pallas_call | solution.py:358
  308.9 5.1 %all-to-all-start.7 = ((bf16[8,104,768]{2,1,0:T(8,128)(2,1)}), bf16[8,104,768]{2,1,0:T(8,128)(2,1)S(1)}, u32[]{:S(2)}, u32[]{:S(2)}) async-start(bf16[8,104,768]{2,1,0:T(8,128)(2,1)} %mix_sums.1), calls=%async_computation.7 | async-start | bytes 2555904 | tf_op jit(solution)/shard_map/all_to_all | solution.py:1010
  314.0 4.9 %collective-permute-done.19 = bf16[768,768]{1,0:T(8,128)(2,1)} collective-permute-done((bf16[768,768]{1,0:T(8,128)(2,1)}, bf16[768,768]{1,0:T(8,128)(2,1)}, u32[]{:S(2)}, u32[]{:S(2)}) %collective-permute-start.19) | collective-permute-done | bytes 1179680 | tf_op jit(solution)/shard_map/ppermute | solution.py:40
  322.6 5.4 %spread_back.1 = (bf16[512,768]{1,0:T(8,128)(2,1)}, bf16[512,768]{1,0:T(8,128)(2,1)S(1)}, f32[512,768]{1,0:T(8,128)S(1)}, f32[512,768]{1,0:T(8,128)S(1)}) custom-call(s32[4]{0:T(128)S(1)} %pad_add_fusion.2.places_ref, bf16[384,2048]{1,0:T(8,128)(2,1)S(1)} %copy-done.6, bf16[192,2048]{1,0:T(8,128)(2,1)S(1)} %copy-done.7, bf16[576,768]{1,0:T(8,128)(2,1)S(1)} %copy-done.1), custom_call_target="tpu_custom_call" | custom-call | flops 880000000 | bytes 2400000 | tf_op jit(solution)/shard_map/spread_back/pallas_call | solution.py:812
  336.1 6.6 %combine.1 = bf16[512,768]{1,0:T(8,128)(2,1)} custom-call(bf16[512,768]{1,0:T(8,128)(2,1)} %get-tuple-element.164.p0a, bf16[512,768]{1,0:T(8,128)(2,1)} %get-tuple-element.165.p1a, bf16[512,768]{1,0:T(8,128)(2,1)} %get-tuple-element.166.p0b, bf16[512,768]{1,0:T(8,128)(2,1)} %get-tuple-element.167.p1b, f32[512,768]{1,0:T(8,128)} %get-tuple-element.186.residual_ref, ...), custom_call_target="tpu_custom_call" | custom-call | flops 660000000 | bytes 1800000 | tf_op jit(solution)/shard_map/combine/pallas_call | solution.py:773
  344.9 4.7 %all-to-all-start.8 = ((bf16[8,56,768]{2,1,0:T(8,128)(2,1)}), bf16[8,56,768]{2,1,0:T(8,128)(2,1)S(1)}, u32[]{:S(2)}, u32[]{:S(2)}) async-start(bf16[8,56,768]{2,1,0:T(8,128)(2,1)} %fold_sums.1), calls=%async_computation.8 | async-start | bytes 1376256 | tf_op jit(solution)/shard_map/all_to_all | solution.py:1010
  355.3 9.9 %expert_update.1 = (f32[768,768]{1,0:T(8,128)}, f32[768,768]{1,0:T(8,128)}, f32[768,768]{1,0:T(8,128)}, f32[768,768]{1,0:T(8,128)}) custom-call(s32[1]{0:T(128)} %bitcast.19.live_ref, f32[2,768,768]{2,1,0:T(8,128)} %get-tuple-element.257.own_ref, bf16[4,768,768]{2,1,0:T(8,128)(2,1)} %collective-permute-done.12.near_ref, bf16[768,768]{1,0:T(8,128)(2,1)} %copy-done.19, ...), custom_call_target="tpu_custom_call" | custom-call | flops 880000000 | bytes 2400000 | tf_op jit(solution)/shard_map/expert_update/pallas_call | solution.py:993
  371.4 5.3 %fusion.4 = (f32[1,768,768]{2,1,0:T(8,128)}, f32[768,768]{1,0:T(8,128)S(1)}) fusion(f32[1,768,768]{2,1,0:T(8,128)} %param.35, pred[]{:T(512)S(6)} %ge.10, bf16[768,768]{1,0:T(8,128)(2,1)} %collective-permute-done.19, bf16[4,768,768]{2,1,0:T(8,128)(2,1)} %collective-permute-done.12.near_ref, f32[2,768,768]{2,1,0:T(8,128)} %get-tuple-element.257.own_ref), kind=kLoop, calls=%fused_computation.10 | loop fusion | flops 5898240 | bytes 11796481 | tf_op jit(solution)/shard_map/broadcast_in_dim | solution.py:1211
  376.7 7.6 %collective-permute-done.27.refs_6_ = bf16[8,56,768]{2,1,0:T(8,128)(2,1)S(1)} collective-permute-done((bf16[8,56,768]{2,1,0:T(8,128)(2,1)S(1)}, bf16[8,56,768]{2,1,0:T(8,128)(2,1)S(1)}, u32[]{:S(2)}, u32[]{:S(2)}) %collective-permute-start.27) | collective-permute-done | bytes 688160 | tf_op jit(solution)/shard_map/ppermute | solution.py:40
  391.4 8.5 %lay_out_sums.1 = (f32[768,2304]{1,0:T(8,128)}, f32[1,768]{1,0:T(1,128)S(1)}, f32[768,768]{1,0:T(8,128)}, f32[16,768]{1,0:T(8,128)S(1)}) custom-call(s32[2]{0:T(128)S(1)} %copy-done.5, bf16[8,48,768]{2,1,0:T(8,128)(2,1)} %slice.40.refs_0_, bf16[8,48,768]{2,1,0:T(8,128)(2,1)S(1)} %collective-permute-done.23.refs_1_, ...), custom_call_target="tpu_custom_call" | custom-call | flops 1100000000 | bytes 3000000 | tf_op jit(solution)/shard_map/lay_out_sums/pallas_call | solution.py:945
  (158 shorter events, 98.2 us)
Async XLA Ops:
  0.7 19.6 %collective-permute-start = (bf16[512,768]{1,0:T(8,128)(2,1)}, bf16[512,768]{1,0:T(8,128)(2,1)S(1)}, u32[]{:S(2)}, u32[]{:S(2)}) collective-permute-start(bf16[512,768]{1,0:T(8,128)(2,1)} %bitcast.75), channel_id=1, source_target_pairs={{0,2},{1,3},{2,0},{3,1},{4,6},{5,7},{6,4},{7,5},{8,10},{9,11},{10,... | collective-permute-start | bytes 2359304 | tf_op jit(solution)/shard_map/ppermute | solution.py:40
  2.8 17.5 %collective-permute-start.1 = (bf16[512,768]{1,0:T(8,128)(2,1)}, bf16[512,768]{1,0:T(8,128)(2,1)S(1)}, u32[]{:S(2)}, u32[]{:S(2)}) collective-permute-start(bf16[512,768]{1,0:T(8,128)(2,1)} %bitcast.76), channel_id=1, source_target_pairs={{0,1},{1,0},{2,3},{3,2},{4,5},{5,4},{6,7},{7,6},{8,9},{9,8},{10,11... | collective-permute-start | bytes 2359304 | tf_op jit(solution)/shard_map/ppermute | solution.py:40
  21.4 60.6 %all-to-all-start = ((bf16[8,192,768]{2,1,0:T(8,128)(2,1)}), bf16[8,192,768]{2,1,0:T(8,128)(2,1)S(1)}, u32[]{:S(2)}, u32[]{:S(2)}) async-start(bf16[8,192,768]{2,1,0:T(8,128)(2,1)} %get-tuple-element.190), calls=%async_computation | async-start | bytes 4718592 | tf_op jit(solution)/shard_map/all_to_all | solution.py:1010
  28.7 33.8 %collective-permute-start.3 = (bf16[768,768]{1,0:T(8,128)(2,1)}, bf16[768,768]{1,0:T(8,128)(2,1)}, u32[]{:S(2)}, u32[]{:S(2)}) collective-permute-start(bf16[768,768]{1,0:T(8,128)(2,1)} %get-tuple-element.173.refs_0_), channel_id=1, source_target_pairs={{0,2},{1,3},{2,0},{3,1},{4,6},{5,7},{6,4},{7,5},{8,10},{9,11},{10,... | collective-permute-start | bytes 3538952 | tf_op jit(solution)/shard_map/ppermute | solution.py:40
  31.7 30.8 %collective-permute-start.4 = (bf16[768,768]{1,0:T(8,128)(2,1)}, bf16[768,768]{1,0:T(8,128)(2,1)}, u32[]{:S(2)}, u32[]{:S(2)}) collective-permute-start(bf16[768,768]{1,0:T(8,128)(2,1)} %get-tuple-element.173.refs_0_), channel_id=1, source_target_pairs={{0,1},{1,0},{2,3},{3,2},{4,5},{5,4},{6,7},{7,6},{8,9},{9,8},{10,11... | collective-permute-start | bytes 3538952 | tf_op jit(solution)/shard_map/ppermute | solution.py:40
  32.1 30.4 %collective-permute-start.5 = (bf16[768,768]{1,0:T(8,128)(2,1)S(1)}, bf16[768,768]{1,0:T(8,128)(2,1)}, u32[]{:S(2)}, u32[]{:S(2)}) collective-permute-start(bf16[768,768]{1,0:T(8,128)(2,1)S(1)} %get-tuple-element.192.refs_1_), channel_id=1, source_target_pairs={{0,1},{1,0},{2,3},{3,2},{4,5},{5,4},{6,7},{7,6},{8,9},{9,8},{10,11... | collective-permute-start | bytes 3538952 | tf_op jit(solution)/shard_map/ppermute | solution.py:40
  62.8 6.4 %collective-permute-start.7 = (bf16[192,512]{1,0:T(8,128)(2,1)}, bf16[192,512]{1,0:T(8,128)(2,1)S(1)}, u32[]{:S(2)}, u32[]{:S(2)}) collective-permute-start(bf16[192,512]{1,0:T(8,128)(2,1)} %get-tuple-element.178), channel_id=1, source_target_pairs={{0,2},{1,3},{2,0},{3,1},{4,6},{5,7},{6,4},{7,5},{8,10},{9,11},{10,... | collective-permute-start | bytes 589832 | tf_op jit(solution)/shard_map/ppermute | solution.py:40
  64.0 9.9 %collective-permute-start.8 = (bf16[192,512]{1,0:T(8,128)(2,1)}, bf16[192,512]{1,0:T(8,128)(2,1)}, u32[]{:S(2)}, u32[]{:S(2)}) collective-permute-start(bf16[192,512]{1,0:T(8,128)(2,1)} %get-tuple-element.179), channel_id=1, source_target_pairs={{0,3},{1,2},{2,1},{3,0},{4,7},{5,6},{6,5},{7,4},{8,11},{9,10},{10,... | collective-permute-start | bytes 589832 | tf_op jit(solution)/shard_map/ppermute | solution.py:40
  81.9 34.6 %all-to-all-start.1 = ((bf16[8,96,768]{2,1,0:T(8,128)(2,1)}), bf16[8,96,768]{2,1,0:T(8,128)(2,1)}, u32[]{:S(2)}, u32[]{:S(2)}) async-start(bf16[8,96,768]{2,1,0:T(8,128)(2,1)} %get-tuple-element.191), calls=%async_computation.1 | async-start | bytes 2359296 | tf_op jit(solution)/shard_map/all_to_all | solution.py:1010
  87.9 33.1 %collective-permute-start.9 = (bf16[768,768]{1,0:T(8,128)(2,1)S(1)}, bf16[768,768]{1,0:T(8,128)(2,1)}, u32[]{:S(2)}, u32[]{:S(2)}) collective-permute-start(bf16[768,768]{1,0:T(8,128)(2,1)S(1)} %get-tuple-element.192.refs_1_), channel_id=1, source_target_pairs={{0,2},{1,3},{2,0},{3,1},{4,6},{5,7},{6,4},{7,5},{8,10},{9,11},{10,... | collective-permute-start | bytes 3538952 | tf_op jit(solution)/shard_map/ppermute | solution.py:40
  116.6 35.2 %all-to-all-start.3 = ((bf16[8,104,768]{2,1,0:T(8,128)(2,1)}), bf16[8,104,768]{2,1,0:T(8,128)(2,1)}, u32[]{:S(2)}, u32[]{:S(2)}) async-start(bf16[8,104,768]{2,1,0:T(8,128)(2,1)} %get-tuple-element.199), calls=%async_computation.3 | async-start | bytes 2555904 | tf_op jit(solution)/shard_map/all_to_all | solution.py:1010
  151.8 33.8 %all-to-all-start.2 = ((bf16[8,96,768]{2,1,0:T(8,128)(2,1)}), bf16[8,96,768]{2,1,0:T(8,128)(2,1)S(1)}, u32[]{:S(2)}, u32[]{:S(2)}) async-start(bf16[8,96,768]{2,1,0:T(8,128)(2,1)} %get-tuple-element.198), calls=%async_computation.2 | async-start | bytes 2359296 | tf_op jit(solution)/shard_map/all_to_all | solution.py:1010
  185.5 34.4 %all-to-all-start.4 = ((bf16[8,104,768]{2,1,0:T(8,128)(2,1)}), bf16[8,104,768]{2,1,0:T(8,128)(2,1)S(1)}, u32[]{:S(2)}, u32[]{:S(2)}) async-start(bf16[8,104,768]{2,1,0:T(8,128)(2,1)} %get-tuple-element.202), calls=%async_computation.4 | async-start | bytes 2555904 | tf_op jit(solution)/shard_map/all_to_all | solution.py:1010
  219.9 18.0 %collective-permute-start.12 = (bf16[4,768,768]{2,1,0:T(8,128)(2,1)}, bf16[4,768,768]{2,1,0:T(8,128)(2,1)}, u32[]{:S(2)}, u32[]{:S(2)}) collective-permute-start(bf16[4,768,768]{2,1,0:T(8,128)(2,1)} %get-tuple-element.214), channel_id=1, source_target_pairs={{0,1},{1,0},{2,3},{3,2},{4,5},{5,4},{6,7},{7,6},{8,9},{9,8},{10,11... | collective-permute-start | bytes 14155784 | tf_op jit(solution)/shard_map/ppermute | solution.py:40
  221.5 57.3 %all-to-all-start.5 = ((bf16[8,192,768]{2,1,0:T(8,128)(2,1)}), bf16[8,192,768]{2,1,0:T(8,128)(2,1)}, u32[]{:S(2)}, u32[]{:S(2)}) async-start(bf16[8,192,768]{2,1,0:T(8,128)(2,1)} %get-tuple-element.227), calls=%async_computation.5 | async-start | bytes 4718592 | tf_op jit(solution)/shard_map/all_to_all | solution.py:1010
  237.9 7.1 %collective-permute-start.13 = (bf16[192,512]{1,0:T(8,128)(2,1)}, bf16[192,512]{1,0:T(8,128)(2,1)S(1)}, u32[]{:S(2)}, u32[]{:S(2)}) collective-permute-start(bf16[192,512]{1,0:T(8,128)(2,1)} %get-tuple-element.216), channel_id=1, source_target_pairs={{0,1},{1,0},{2,3},{3,2},{4,5},{5,4},{6,7},{7,6},{8,9},{9,8},{10,11... | collective-permute-start | bytes 589832 | tf_op jit(solution)/shard_map/ppermute | solution.py:40
  239.0 6.8 %collective-permute-start.14 = (bf16[192,512]{1,0:T(8,128)(2,1)}, bf16[192,512]{1,0:T(8,128)(2,1)S(1)}, u32[]{:S(2)}, u32[]{:S(2)}) collective-permute-start(bf16[192,512]{1,0:T(8,128)(2,1)} %get-tuple-element.217), channel_id=1, source_target_pairs={{0,2},{1,3},{2,0},{3,1},{4,6},{5,7},{6,4},{7,5},{8,10},{9,11},{10,... | collective-permute-start | bytes 589832 | tf_op jit(solution)/shard_map/ppermute | solution.py:40
  240.3 10.2 %collective-permute-start.15 = (bf16[192,512]{1,0:T(8,128)(2,1)}, bf16[192,512]{1,0:T(8,128)(2,1)S(1)}, u32[]{:S(2)}, u32[]{:S(2)}) collective-permute-start(bf16[192,512]{1,0:T(8,128)(2,1)} %get-tuple-element.218), channel_id=1, source_target_pairs={{0,3},{1,2},{2,1},{3,0},{4,7},{5,6},{6,5},{7,4},{8,11},{9,10},{10,... | collective-permute-start | bytes 589832 | tf_op jit(solution)/shard_map/ppermute | solution.py:40
  251.2 34.2 %collective-permute-start.16 = (bf16[768,768]{1,0:T(8,128)(2,1)}, bf16[768,768]{1,0:T(8,128)(2,1)S(1)}, u32[]{:S(2)}, u32[]{:S(2)}) collective-permute-start(bf16[768,768]{1,0:T(8,128)(2,1)} %get-tuple-element.231), channel_id=1, source_target_pairs={{0,2},{1,3},{2,0},{3,1},{4,6},{5,7},{6,4},{7,5},{8,10},{9,11},{10,... | collective-permute-start | bytes 3538952 | tf_op jit(solution)/shard_map/ppermute | solution.py:40
  255.6 20.1 %collective-permute-start.17 = (bf16[2,192,768]{2,1,0:T(8,128)(2,1)}, bf16[2,192,768]{2,1,0:T(8,128)(2,1)S(1)}, u32[]{:S(2)}, u32[]{:S(2)}) collective-permute-start(bf16[2,192,768]{2,1,0:T(8,128)(2,1)} %get-tuple-element.234), channel_id=1, source_target_pairs={{0,1},{1,0},{2,3},{3,2},{4,5},{5,4},{6,7},{7,6},{8,9},{9,8},{10,11... | collective-permute-start | bytes 1769480 | tf_op jit(solution)/shard_map/ppermute | solution.py:40
  275.7 9.7 %collective-permute-start.18 = (bf16[192,768]{1,0:T(8,128)(2,1)S(1)}, bf16[192,768]{1,0:T(8,128)(2,1)S(1)}, u32[]{:S(2)}, u32[]{:S(2)}) collective-permute-start(bf16[192,768]{1,0:T(8,128)(2,1)S(1)} %fusion.16), channel_id=1, source_target_pairs={{0,2},{1,3},{2,0},{3,1},{4,6},{5,7},{6,4},{7,5},{8,10},{9,11},{10,... | collective-permute-start | bytes 884744 | tf_op jit(solution)/shard_map/ppermute | solution.py:40
  286.4 20.2 %all-to-all-start.6 = ((bf16[8,48,768]{2,1,0:T(8,128)(2,1)}), bf16[8,48,768]{2,1,0:T(8,128)(2,1)S(1)}, u32[]{:S(2)}, u32[]{:S(2)}) async-start(bf16[8,48,768]{2,1,0:T(8,128)(2,1)} %bitcast.87), calls=%async_computation.6 | async-start | bytes 1179648 | tf_op jit(solution)/shard_map/all_to_all | solution.py:1010
  292.0 26.9 %collective-permute-start.19 = (bf16[768,768]{1,0:T(8,128)(2,1)}, bf16[768,768]{1,0:T(8,128)(2,1)}, u32[]{:S(2)}, u32[]{:S(2)}) collective-permute-start(bf16[768,768]{1,0:T(8,128)(2,1)} %get-tuple-element.244), channel_id=1, source_target_pairs={{0,2},{1,3},{2,0},{3,1},{4,6},{5,7},{6,4},{7,5},{8,10},{9,11},{10,... | collective-permute-start | bytes 3538952 | tf_op jit(solution)/shard_map/ppermute | solution.py:40
  308.9 35.1 %all-to-all-start.7 = ((bf16[8,104,768]{2,1,0:T(8,128)(2,1)}), bf16[8,104,768]{2,1,0:T(8,128)(2,1)S(1)}, u32[]{:S(2)}, u32[]{:S(2)}) async-start(bf16[8,104,768]{2,1,0:T(8,128)(2,1)} %mix_sums.1), calls=%async_computation.7 | async-start | bytes 2555904 | tf_op jit(solution)/shard_map/all_to_all | solution.py:1010
  332.8 19.1 %collective-permute-start.22 = (bf16[512,768]{1,0:T(8,128)(2,1)}, bf16[512,768]{1,0:T(8,128)(2,1)}, u32[]{:S(2)}, u32[]{:S(2)}) collective-permute-start(bf16[512,768]{1,0:T(8,128)(2,1)} %add_convert_fusion), channel_id=1, source_target_pairs={{0,2},{1,3},{2,0},{3,1},{4,6},{5,7},{6,4},{7,5},{8,10},{9,11},{10,... | collective-permute-start | bytes 2359304 | tf_op jit(solution)/shard_map/ppermute | solution.py:40
  334.1 19.1 %collective-permute-start.21 = (bf16[512,768]{1,0:T(8,128)(2,1)}, bf16[512,768]{1,0:T(8,128)(2,1)}, u32[]{:S(2)}, u32[]{:S(2)}) collective-permute-start(bf16[512,768]{1,0:T(8,128)(2,1)} %get-tuple-element.254), channel_id=1, source_target_pairs={{0,1},{1,0},{2,3},{3,2},{4,5},{5,4},{6,7},{7,6},{8,9},{9,8},{10,11... | collective-permute-start | bytes 2359304 | tf_op jit(solution)/shard_map/ppermute | solution.py:40
  344.9 23.9 %all-to-all-start.8 = ((bf16[8,56,768]{2,1,0:T(8,128)(2,1)}), bf16[8,56,768]{2,1,0:T(8,128)(2,1)S(1)}, u32[]{:S(2)}, u32[]{:S(2)}) async-start(bf16[8,56,768]{2,1,0:T(8,128)(2,1)} %fold_sums.1), calls=%async_computation.8 | async-start | bytes 1376256 | tf_op jit(solution)/shard_map/all_to_all | solution.py:1010
  351.9 19.0 %collective-permute-start.24 = (bf16[8,48,768]{2,1,0:T(8,128)(2,1)}, bf16[8,48,768]{2,1,0:T(8,128)(2,1)S(1)}, u32[]{:S(2)}, u32[]{:S(2)}) collective-permute-start(bf16[8,48,768]{2,1,0:T(8,128)(2,1)} %slice.40.refs_0_), channel_id=1, source_target_pairs={{0,2},{1,3},{2,0},{3,1},{4,6},{5,7},{6,4},{7,5},{8,10},{9,11},{10,... | collective-permute-start | bytes 1769480 | tf_op jit(solution)/shard_map/ppermute | solution.py:40
  368.8 15.4 %collective-permute-start.27 = (bf16[8,56,768]{2,1,0:T(8,128)(2,1)S(1)}, bf16[8,56,768]{2,1,0:T(8,128)(2,1)S(1)}, u32[]{:S(2)}, u32[]{:S(2)}) collective-permute-start(bf16[8,56,768]{2,1,0:T(8,128)(2,1)S(1)} %all-to-all-done.8.refs_4_), channel_id=1, source_target_pairs={{0,2},{1,3},{2,0},{3,1},{4,6},{5,7},{6,4},{7,5},{8,10},{9,11},{10,... | collective-permute-start | bytes 2064392 | tf_op jit(solution)/shard_map/ppermute | solution.py:40
  369.0 21.5 %collective-permute-start.23 = (bf16[8,48,768]{2,1,0:T(8,128)(2,1)}, bf16[8,48,768]{2,1,0:T(8,128)(2,1)S(1)}, u32[]{:S(2)}, u32[]{:S(2)}) collective-permute-start(bf16[8,48,768]{2,1,0:T(8,128)(2,1)} %slice.40.refs_0_), channel_id=1, source_target_pairs={{0,1},{1,0},{2,3},{3,2},{4,5},{5,4},{6,7},{7,6},{8,9},{9,8},{10,11... | collective-permute-start | bytes 1769480 | tf_op jit(solution)/shard_map/ppermute | solution.py:40
  370.9 19.7 %collective-permute-start.25 = (bf16[8,48,768]{2,1,0:T(8,128)(2,1)S(1)}, bf16[8,48,768]{2,1,0:T(8,128)(2,1)S(1)}, u32[]{:S(2)}, u32[]{:S(2)}) collective-permute-start(bf16[8,48,768]{2,1,0:T(8,128)(2,1)S(1)} %collective-permute-done.24.refs_2_), channel_id=1, source_target_pairs={{0,1},{1,0},{2,3},{3,2},{4,5},{5,4},{6,7},{7,6},{8,9},{9,8},{10,11... | collective-permute-start | bytes 1769480 | tf_op jit(solution)/shard_map/ppermute | solution.py:40
  371.0 19.6 %collective-permute-start.26 = (bf16[8,56,768]{2,1,0:T(8,128)(2,1)S(1)}, bf16[8,56,768]{2,1,0:T(8,128)(2,1)S(1)}, u32[]{:S(2)}, u32[]{:S(2)}) collective-permute-start(bf16[8,56,768]{2,1,0:T(8,128)(2,1)S(1)} %all-to-all-done.8.refs_4_), channel_id=1, source_target_pairs={{0,1},{1,0},{2,3},{3,2},{4,5},{5,4},{6,7},{7,6},{8,9},{9,8},{10,11... | collective-permute-start | bytes 2064392 | tf_op jit(solution)/shard_map/ppermute | solution.py:40
  (42 other events, 408.9 us)
